TPU v7x, 32 devices: a whole 2x2x4 slice. The times are simulated.
32 devices in a mesh: rows: 16 (over z, x, core), tp: 2 (over y).
Axes of the slice: x: 2, y: 2, z: 4, core: 2. Of those that a mesh axis runs over, the one named last changes fastest.
Arguments:
- section_rows: bfloat16 [51200, 1024], P(('rows', 'tp')), may hold values from -100 to 100
- window_mask: int32 [51200], P('rows'), may hold values from 0 to 1, as said below
- cotangent: bfloat16 [51200, 512], P(('rows', 'tp')), may hold values from -6 to 6
- merge_weight: bfloat16 [1024, 512], P('tp'), may hold values from -0.1875 to 0.1875
- merge_gain: bfloat16 [1024], P('tp'), may hold values from 0.099609375 to 1.8984375
- merge_bias: bfloat16 [1024], P('tp'), may hold values from -3 to 3
- norm1_gain: float32 [512], replicated, may hold values from 0.1 to 1.9
- norm1_bias: float32 [512], replicated, may hold values from -3 to 3
- qkv_weight: bfloat16 [3, 512, 512], P(None, None, 'tp'), may hold values from -0.25 to 0.25
- qv_bias: float32 [2, 512], P(None, 'tp'), may hold values from -3 to 3
- bias_table: float32 [361, 16], P(None, 'tp'), may hold values from -4 to 4
- proj_weight: bfloat16 [512, 512], P('tp'), may hold values from -1 to 1
- proj_bias: float32 [512], replicated, may hold values from -3 to 3
- norm2_gain: float32 [512], replicated, may hold values from 0.1 to 1.9
- norm2_bias: float32 [512], replicated, may hold values from -3 to 3
- up_weight: bfloat16 [512, 2048], P(None, 'tp'), may hold values from -0.25 to 0.25
- up_bias: float32 [2048], P('tp'), may hold values from -3 to 3
- down_weight: bfloat16 [2048, 512], P('tp'), may hold values from -0.125 to 0.125
- down_bias: float32 [512], replicated, may hold values from -3 to 3
Outputs:
- block_out: bfloat16 [51200, 512], P(('rows', 'tp'))
- section_rows_grad: bfloat16 [51200, 1024], P(('rows', 'tp'))
- merge_weight_grad: float32 [1024, 512], P('tp')
- merge_gain_grad: float32 [1024], P('tp')
- merge_bias_grad: float32 [1024], P('tp')
- norm1_gain_grad: float32 [512], replicated
- norm1_bias_grad: float32 [512], replicated
- qkv_weight_grad: float32 [3, 512, 512], P(None, None, 'tp')
- qv_bias_grad: float32 [2, 512], P(None, 'tp')
- bias_table_grad: float32 [361, 16], P(None, 'tp')
- proj_weight_grad: float32 [512, 512], P('tp')
- proj_bias_grad: float32 [512], replicated
- norm2_gain_grad: float32 [512], replicated
- norm2_bias_grad: float32 [512], replicated
- up_weight_grad: float32 [512, 2048], P(None, 'tp')
- up_bias_grad: float32 [2048], P('tp')
- down_weight_grad: float32 [2048, 512], P('tp')
- down_bias_grad: float32 [512], replicated
Inputs may be any that keep to these rules, and one draw needn't show every extreme that they name: `window_mask`: 1 marks a real patch; in every window of 10 x 10 patches the padded patches fill whole trailing columns, and a window may be padded throughout.
All inputs are finite; a program needn't handle non-finite values.
Results may differ from a plain program's by a relative error of at most 0.019.
Values may be sent and summed in bfloat16 or wider, within the bound.
No kernel may reach another device: no remote copies, remote signals or barrier semaphores. Data moves between devices by JAX's collectives and lax.ppermute only.
A program may use at most 256 MiB of HBM per device.

v0:
```python
from functools import partial
import math

import jax
import jax.numpy as jnp
from jax import lax
from jax.experimental import pallas as pl
from jax.experimental.pallas import tpu as pltpu
from jax.sharding import PartitionSpec as P

MERGE_IN = 1024
D = 512
HEADS = 16
HEAD_DIM = 32
FFN = 2048
WINDOW = 10
AREA = WINDOW * WINDOW
SIDE = 2 * WINDOW - 1
EPSILON = 1e-05
MASKED_SCORE = -1e30
EXACT = lax.Precision.HIGHEST
SCALING = 1.0 / math.sqrt(HEAD_DIM)
GROUP = 4
ROWS = GROUP * AREA
KEYS = 112
QUERIES = 128
QUADS = 4
QUAD = 4 * HEAD_DIM
LANES = 4 * QUERIES

bf16 = jnp.bfloat16
f32 = jnp.float32


def mm(a, b):
    return jnp.dot(a, b, preferred_element_type=f32)


def mm_t(a, b):
    return lax.dot_general(a, b, (((1,), (1,)), ((), ())), preferred_element_type=f32)


def t_mm(a, b):
    return lax.dot_general(a, b, (((0,), (0,)), ((), ())), preferred_element_type=f32)


def normalize(values):
    center = jnp.mean(values, axis=-1, keepdims=True)
    spread = jnp.mean(values * values, axis=-1, keepdims=True) - center * center
    inverse = lax.rsqrt(spread + EPSILON)
    return (values - center) * inverse, inverse


def norm_back(grad_hat, normed, inverse):
    first_mean = jnp.mean(grad_hat, axis=-1, keepdims=True)
    second_mean = jnp.mean(grad_hat * normed, axis=-1, keepdims=True)
    return inverse * (grad_hat - first_mean - normed * second_mean)


def column_sum(values):
    return jnp.sum(values, axis=0, keepdims=True)


def head_masks():
    lane = lax.broadcasted_iota(jnp.int32, (1, QUAD), 1) // HEAD_DIM
    return [(lane == head).astype(f32).astype(bf16) for head in range(4)]


def spread_heads(rows, masks):
    return jnp.concatenate([rows * mask for mask in masks], axis=0)


def kernel_call(body, grid, in_specs, out_specs, out_shape, scratch=(), flops=0, moved=0, room=32, cost=None):
    return pl.pallas_call(
        body,
        grid=grid,
        in_specs=in_specs,
        out_specs=out_specs,
        out_shape=out_shape,
        scratch_shapes=list(scratch),
        compiler_params=pltpu.CompilerParams(
            dimension_semantics=("arbitrary",) * len(grid), vmem_limit_bytes=room * 1024 * 1024
        ),
        cost_estimate=cost or COST,
    )


def whole(shape):
    return pl.BlockSpec(shape, lambda *_: (0,) * len(shape), pipeline_mode=pl.Buffered(1))


def by_rows(rows, columns):
    return pl.BlockSpec((rows, columns), lambda i: (i, 0))


def by_windows(shape):
    return pl.BlockSpec((GROUP,) + shape, lambda i: (i,) + (0,) * len(shape))


SCALARS = pl.BlockSpec(memory_space=pltpu.SMEM)
RESIDENT = pl.BlockSpec(memory_space=pltpu.VMEM)
ANYWHERE = pl.BlockSpec(memory_space=pl.ANY)


def in_hbm(array):
    return pltpu.with_memory_space_constraint(array, pltpu.HBM)


FEED_PACK = 1024
QKV_PACK = 384
PROJ_PACK = 128
MERGE_PACK = 256
STAGE_ROOM = 16
COST = pl.CostEstimate(flops=1, bytes_accessed=1, transcendentals=0)
LONG = pl.CostEstimate(flops=10**12, bytes_accessed=1, transcendentals=0)
SUMS = 16
PARAMS = 16


def shape_of(shape, dtype):
    return jax.ShapeDtypeStruct(shape, dtype)


def split(rows):
    high = rows.astype(bf16).astype(f32)
    return jnp.concatenate([high, rows - high], axis=0).astype(bf16)


def joined(pair):
    half = pair.shape[0] // 2
    return pair[:half].astype(f32) + pair[half:].astype(f32)


def both_shards(tp, mine, other, axis):
    return jnp.where(
        tp == 0, jnp.concatenate([mine, other], axis=axis), jnp.concatenate([other, mine], axis=axis)
    )


def pack_merge_body(place, merge_ref, out_ref):
    out_ref[...] = merge_ref[pl.ds(pl.multiple_of(256 * place[0], 256), 256), :]


def pack_params_body(
    place, after, merge_ref, qv_ref, up_bias_ref, table_ref, params_ref, out_ref, merge_s, qv_s, up_bias_s, table_s, sems
):
    pairs = ((merge_ref, merge_s), (qv_ref, qv_s), (up_bias_ref, up_bias_s), (table_ref, table_s))
    copies = [pltpu.make_async_copy(source, target, sems.at[index]) for index, (source, target) in enumerate(pairs)]
    for copy in copies:
        copy.start()
    params_ref[...] = jnp.zeros_like(params_ref)
    for copy in copies:
        copy.wait()
    params_ref[0:1, :] = merge_s[:, 0:512]
    params_ref[1:2, :] = merge_s[:, 512:1024]
    params_ref[2:3, 0:256] = qv_s[0:1, :]
    params_ref[2:3, 256:512] = qv_s[1:2, :]
    params_ref[3:4, :] = up_bias_s[:, 0:512]
    params_ref[4:5, :] = up_bias_s[:, 512:1024]
    params_ref[8:16, 0 : SIDE * SIDE] = table_s[...]
    out_ref[...] = split(params_ref[...])


def pack_params(place, after, merge, qv, up_bias, table):
    operands = [in_hbm(array) for array in (merge, qv, up_bias, table)]
    return pl.pallas_call(
        pack_params_body,
        in_specs=[SCALARS] + [ANYWHERE] * 5,
        out_specs=[RESIDENT] * 2,
        out_shape=[shape_of((PARAMS, D), f32), shape_of((2 * PARAMS, D), bf16)],
        scratch_shapes=[pltpu.VMEM(array.shape, f32) for array in operands] + [pltpu.SemaphoreType.DMA((4,))],
        cost_estimate=COST,
    )(place, after, *operands)


def plain_call(body, outs, operands, room=16, scratch=(), flops=0):
    return pl.pallas_call(
        body,
        in_specs=[SCALARS] + [pl.BlockSpec(memory_space=pltpu.VMEM)] * (len(operands) - 1),
        out_specs=[pl.BlockSpec(memory_space=pltpu.VMEM)] * len(outs),
        out_shape=outs,
        scratch_shapes=list(scratch),
        compiler_params=pltpu.CompilerParams(vmem_limit_bytes=room * 1024 * 1024),
        cost_estimate=COST,
    )(*operands)


def pack_qkv_body(place, qkv_ref, proj_ref, out):
    core = place[0]
    for side in range(2):
        rows = pl.ds(pl.multiple_of(768 * core + 384 * side, 128), 384)
        out[0:384, 256 * side : 256 * side + 256] = qkv_ref[rows, :]
    out[384:512, :] = proj_ref[pl.ds(pl.multiple_of(128 * core, 128), 128), :]


def pack_feed_body(place, up_ref, down_ref, out):
    half = pl.ds(pl.multiple_of(512 * place[0], 512), 512)
    out[0:512, :] = down_ref[half, :]
    out[512:1024, :] = up_ref[:, half]


def plain_call_after(body, outs, place, after, operands, room=16, scratch=(), flops=0, cost=COST):
    after = after if isinstance(after, tuple) else (after,)

    def without_after(place, *refs):
        return body(place, *refs[len(after) :])

    return pl.pallas_call(
        without_after,
        in_specs=[SCALARS] + [pl.BlockSpec(memory_space=pl.ANY)] * len(after) + [pl.BlockSpec(memory_space=pltpu.VMEM)] * len(operands),
        out_specs=[pl.BlockSpec(memory_space=pltpu.VMEM)] * len(outs),
        out_shape=outs,
        scratch_shapes=list(scratch),
        compiler_params=pltpu.CompilerParams(vmem_limit_bytes=room * 1024 * 1024),
        cost_estimate=cost,
    )(place, *after, *operands)


def masks_body(place, window_ref, mask_ref, live_ref, stage):
    windows = mask_ref.shape[0]
    shards = window_ref.shape[1] // (windows * AREA)
    stage[...] = jnp.zeros_like(stage)
    for window in range(windows):
        patch = window_ref[:, AREA * window : AREA * (window + 1)]
        for shard in range(1, shards):
            begin = AREA * (windows * shard + window)
            patch = jnp.where(place[3] == shard, window_ref[:, begin : begin + AREA], patch)
        stage[window : window + 1, 0:AREA] = patch
    patches = jnp.minimum(stage[...], 1).astype(f32)
    live = jnp.max(patches, axis=1, keepdims=True)
    inside = lax.broadcasted_iota(jnp.int32, (windows, QUERIES), 1) < AREA
    keep = jnp.logical_and(jnp.maximum(patches, 1.0 - live) > 0.5, inside)
    added = jnp.where(keep, 0.0, MASKED_SCORE)
    for window in range(windows):
        mask_ref[window] = added[window : window + 1, :]
        live_ref[AREA * window : AREA * (window + 1), :] = jnp.broadcast_to(live[window : window + 1, :], (AREA, 1))


def masks_of(place, after, window_mask, count):
    windows = count // AREA
    return plain_call_after(
        masks_body,
        [shape_of((windows, 1, QUERIES), f32), shape_of((count, 1), f32)],
        place,
        after,
        (window_mask[None],),
        scratch=[pltpu.VMEM((windows, QUERIES), jnp.int32)],
    )


def section_norm_body(after, rows_ref, hat_ref, inverse_ref, rows_s, sems):
    steps = rows_s.shape[0] // ROWS
    copies = []
    for step in range(steps):
        here = slice(ROWS * step, ROWS * (step + 1))
        copies.append(pltpu.make_async_copy(rows_ref.at[here, :], rows_s.at[here, :], sems.at[step]))
        copies[step].start()
    for step in range(steps):
        here = slice(ROWS * step, ROWS * (step + 1))
        copies[step].wait()
        hat, inverse = normalize(rows_s[here, :].astype(f32))
        hat_ref[here, :] = hat.astype(bf16)
        inverse_ref[here, :] = inverse


def section_norm(after, rows):
    count = rows.shape[0]
    return kernel_call(
        section_norm_body,
        (1,),
        [ANYWHERE, ANYWHERE],
        [RESIDENT, RESIDENT],
        [pltpu.VMEM((count, MERGE_IN), bf16), shape_of((count, 1), f32)],
        [pltpu.VMEM((count, MERGE_IN), bf16), pltpu.SemaphoreType.DMA((count // ROWS,))],
        room=16,
    )(after, in_hbm(rows))


def turn_body(after, first_ref, hat_ref, first_out, hat_out, hat_copy):
    columns = first_out.shape[0]
    first_out[...] = first_ref[:, pl.ds(pl.multiple_of(columns * pl.program_id(0), 128), columns)].T
    columns = hat_out.shape[0]
    hat = hat_ref[:, pl.ds(pl.multiple_of(columns * pl.program_id(0), 128), columns)]
    hat_out[...] = hat.T
    hat_copy[...] = hat


def turn(after, first, hat):
    count = hat.shape[0]
    steps = 4
    return kernel_call(
        turn_body,
        (steps,),
        [ANYWHERE, RESIDENT, RESIDENT],
        [
            pl.BlockSpec((D // steps, count), lambda i: (i, 0)),
            pl.BlockSpec((MERGE_IN // steps, count), lambda i: (i, 0)),
            pl.BlockSpec((count, MERGE_IN // steps), lambda i: (0, i)),
        ],
        [pltpu.HBM((D, count), bf16), pltpu.HBM((MERGE_IN, count), bf16), pltpu.HBM((count, MERGE_IN), bf16)],
        room=16,
    )(after, first, hat)


def gain_rows(tp, params, others):
    return both_shards(tp, params[0:1], others[0:1], 1), both_shards(tp, params[1:2], others[1:2], 1)


def merge_body(
    place, hat_ref, own_ref, near_ref, far_ref, params_ref, others_ref, rows_ref,
    merged_ref, first_ref, merge_ref, params_out_ref, column_ref,
    merge_s, shift_s, gain_s,
):

    @pl.when(pl.program_id(0) == 0)
    def _():
        core, tp = place[0], place[3]
        merge_s[pl.ds(pl.multiple_of(512 * tp, 512), 512), :] = own_ref[...]
        other = 512 * (1 - tp)
        merge_s[pl.ds(pl.multiple_of(other + 256 * core, 256), 256), :] = near_ref[...]
        merge_s[pl.ds(pl.multiple_of(other + 256 * (1 - core), 256), 256), :] = far_ref[...]
        merge_ref[...] = merge_s[...]
        params = params_ref[...]
        others = joined(others_ref[...])
        gain, bias = gain_rows(tp, params, others)
        gain_s[...] = gain.astype(bf16)
        shift_s[...] = mm(jnp.broadcast_to(bias, (16, MERGE_IN)).astype(bf16), merge_s[...])[0:1]
        params_out_ref[0:1, 0:1024] = gain
        params_out_ref[0:1, 1024:2048] = bias
        params_out_ref[1:2, 0:512] = both_shards(tp, params[2:3, 0:256], others[2:3, 0:256], 1)
        params_out_ref[1:2, 512:1024] = both_shards(tp, params[2:3, 256:512], others[2:3, 256:512], 1)
        params_out_ref[1:2, 1024:2048] = jnp.zeros((1, 1024), f32)
        params_out_ref[2:3, :] = both_shards(
            tp,
            jnp.concatenate([params[3:4], params[4:5]], axis=1),
            jnp.concatenate([others[3:4], others[4:5]], axis=1),
            1,
        )
        params_out_ref[3:8, :] = jnp.zeros((5, 2048), f32)
        params_out_ref[8:24, 0:512] = both_shards(tp, params[8:16], others[8:16], 0)
        params_out_ref[8:24, 512:2048] = jnp.zeros((16, 1536), f32)
        column_ref[...] = jnp.broadcast_to(gain, (128, MERGE_IN)).T

    here = pl.ds(pl.multiple_of(pl.program_id(0) * ROWS, 16), ROWS)
    merged = mm(hat_ref[here, :] * gain_s[...], merge_s[...]) + shift_s[...]
    merged_ref[...] = merged
    hat, _ = normalize(merged)
    first_ref[here, :] = (hat * rows_ref[0:1, :] + rows_ref[1:2, :]).astype(bf16)


def merge_rows(place, hat, own, near, far, params, others, rows):
    count = hat.shape[0]
    return kernel_call(
        merge_body,
        (count // ROWS,),
        [
            SCALARS, RESIDENT, RESIDENT, RESIDENT, RESIDENT, RESIDENT, RESIDENT, whole((2, D)),
        ],
        [by_rows(ROWS, D), RESIDENT, whole((MERGE_IN, D)), RESIDENT, whole((MERGE_IN, 128))],
        [
            pltpu.HBM((count, D), f32), pltpu.VMEM((count, D), bf16), pltpu.HBM((MERGE_IN, D), bf16),
            shape_of((24, 2048), f32), pltpu.HBM((MERGE_IN, 128), f32),
        ],
        [pltpu.VMEM((MERGE_IN, D), bf16), pltpu.VMEM((1, D), f32), pltpu.VMEM((1, MERGE_IN), bf16)],
        flops=2 * count * D * MERGE_IN,
        moved=count * 10 * D + 4 * D * MERGE_IN,
        room=24,
    )(place, hat, own, near, far, params, others, rows)


def value_blocks(values, masks):
    return [jnp.concatenate([values * mask, jnp.broadcast_to(mask, (QUERIES, QUAD))], axis=1) for mask in masks]


def turned_products(turned, scores):
    parts = []
    for pair in range(2):
        both = mm(turned[64 * pair : 64 * pair + 64], scores[:, 256 * pair : 256 * pair + 256])
        parts += [both[0:32, 0:128], both[32:64, 128:256]]
    return jnp.concatenate(parts, axis=0).T


def attend_body(
    place, first_ref, own_ref, near_ref, far_ref, params_ref, position_ref, mask_ref,
    qkv_out_ref, weights_ref, attended_ref, padded_ref, inverse_ref, qkv_ref,
    stage, mixed,
):
    @pl.when(pl.program_id(0) == 0)
    def _():
        core, tp = place[0], place[3]
        other = pl.ds(pl.multiple_of(256 * (1 - tp), 256), 256)
        qkv_ref[:, pl.ds(pl.multiple_of(256 * tp, 256), 256)] = own_ref[...]
        for ref, half in ((near_ref, core), (far_ref, 1 - core)):
            for side in range(2):
                rows = pl.ds(pl.multiple_of(768 * half + 384 * side, 128), 384)
                qkv_ref[rows, other] = ref[0:384, 256 * side : 256 * side + 256]

    here = pl.ds(pl.multiple_of(pl.program_id(0) * ROWS, 16), ROWS)
    stage[pl.ds(0, ROWS), :] = first_ref[here, :].astype(f32)
    stage[pl.ds(ROWS, 32), :] = jnp.zeros((32, D), f32)
    padded = jnp.concatenate(
        [stage[pl.ds(AREA * w, QUERIES), :].astype(bf16) for w in range(GROUP)], axis=0
    )
    queries = (SCALING * (mm(padded, qkv_ref[0:512, :]) + params_ref[1:2, 0:512])).astype(bf16)
    keys = mm(padded, qkv_ref[512:1024, :]).astype(bf16)
    values = (mm(padded, qkv_ref[1024:1536, :]) + params_ref[1:2, 512:1024]).astype(bf16)
    for w in range(GROUP):
        block = slice(QUERIES * w, QUERIES * (w + 1))
        qkv_out_ref[w, :, 0:D] = queries[block]
        qkv_out_ref[w, :, D : 2 * D] = keys[block]
        qkv_out_ref[w, :, 2 * D :] = values[block]
    masks = head_masks()
    for w in range(GROUP):
        mask = mask_ref[w]
        for quad in range(QUADS):
            columns = slice(QUAD * quad, QUAD * (quad + 1))
            rows = QUERIES * w
            spread = spread_heads(keys[rows : rows + QUERIES, columns], masks)
            scores = mm_t(queries[rows : rows + KEYS, columns], spread)
            raised = []
            for head in range(4):
                lanes = slice(QUERIES * head, QUERIES * (head + 1))
                part = scores[:, lanes] + position_ref[quad, :, lanes] + mask
                raised.append(jnp.exp(part - jnp.max(part, axis=1, keepdims=True)).astype(bf16))
            weights = jnp.concatenate(raised, axis=1)
            weights_ref[w, quad] = weights
            blocks = value_blocks(values[rows : rows + QUERIES, columns], masks)
            out = mm(weights, jnp.concatenate(blocks, axis=0))
            inverse = 1.0 / out[:, QUAD:]
            both = out[:, :QUAD] * inverse
            inverse_ref[w, :, columns] = inverse
            padded_ref[w, :, columns] = both.astype(bf16)
            mixed[pl.ds(AREA * w, AREA), columns] = both[0:AREA]
    attended_ref[...] = mixed[...].astype(bf16)


def attend(place, first, own, near, far, params, position, mask):
    count = first.shape[0]
    windows = count // AREA
    return kernel_call(
        attend_body,
        (count // ROWS,),
        [
            SCALARS, RESIDENT, RESIDENT, RESIDENT, RESIDENT, RESIDENT, RESIDENT, by_windows((1, QUERIES)),
        ],
        [
            by_windows((QUERIES, 3 * D)), by_windows((QUADS, KEYS, LANES)), by_rows(ROWS, D),
            by_windows((KEYS, D)), by_windows((KEYS, D)), RESIDENT,
        ],
        [
            pltpu.HBM((windows, QUERIES, 3 * D), bf16), pltpu.HBM((windows, QUADS, KEYS, LANES), bf16),
            pltpu.HBM((count, D), bf16), pltpu.HBM((windows, KEYS, D), bf16), pltpu.HBM((windows, KEYS, D), f32),
            shape_of((3 * D, D), bf16),
        ],
        [pltpu.VMEM((ROWS + 32, D), f32), pltpu.VMEM((ROWS, D), f32)],
        flops=2 * count * D * (3 * D + 4 * AREA),
        moved=count * 10 * D + windows * QUADS * KEYS * LANES * 2,
        room=20,
    )(place, first, own, near, far, params, position, mask)


def gelu_parts(t):
    chance = 0.5 * lax.erf(t * math.sqrt(0.5)) + 0.5
    density = jnp.exp(t * t * -0.5) * (1.0 / math.sqrt(2.0 * math.pi))
    return t * chance, chance + t * density


TILE = 512
FEED_ROWS = 400
OWN_ROOM = 18
OTHER_ROOM = 12
AB_ROOM = 20
NEAR_ROOM = 20


def feed_tile(up, down, bias, second_ref, turned_ref, branch_ref, total_s, back_s, active_s, raise_s, target, first):
    sums = jnp.zeros((1, TILE), f32)
    for begin in range(0, second_ref.shape[0], FEED_ROWS):
        here = slice(begin, begin + FEED_ROWS)
        value, slope = gelu_parts(mm(second_ref[here, :], up) + bias)
        active = value.astype(bf16)
        grad_raised = (mm_t(branch_ref[here, :], down) * slope).astype(bf16)
        active_s[here, :] = active
        raise_s[here, :] = grad_raised
        sums += column_sum(grad_raised.astype(f32))
        out = mm(active, down)
        back = mm_t(grad_raised, up)
        if first:
            total_s[here, :] = out
            back_s[here, :] = back
        else:
            total_s[here, :] += out
            back_s[here, :] += back
    target[0:512, :] = t_mm(active_s[...], branch_ref[...]).astype(bf16)
    target[512:1024, :] = mm(turned_ref[...], raise_s[...]).astype(bf16)
    return sums


def feed_own_body(
    place, attended_ref, merged_ref, cotangent_ref, live_ref, proj_bias, norm_gain, norm_bias, params_ref,
    proj_own, near_ref, far_ref, up_own, down_own,
    residual_ref, total_ref, back_ref, second_ref, turned_ref, branch_ref, send_ref, sums_ref, proj_ref,
    active_s, raise_s,
):
    step = pl.program_id(0)
    blocks = pl.num_programs(0) - 1
    core, tp = place[0], place[3]

    @pl.when(step == 0)
    def _():
        proj_ref[pl.ds(pl.multiple_of(256 * tp, 256), 256), :] = proj_own[...]
        for ref, which in ((near_ref, core), (far_ref, 1 - core)):
            proj_ref[pl.ds(pl.multiple_of(256 * (1 - tp) + 128 * which, 128), 128), :] = ref[384:512, :]
        sums_ref[...] = jnp.zeros_like(sums_ref)

    @pl.when(step < blocks)
    def _():
        here = pl.ds(pl.multiple_of(step * ROWS, 16), ROWS)
        residual = merged_ref[...] + mm(attended_ref[...], proj_ref[...]) + proj_bias[...]
        residual_ref[here, :] = residual
        hat, _ = normalize(residual)
        second_ref[here, :] = (hat * norm_gain[...] + norm_bias[...]).astype(bf16)
        branch = cotangent_ref[...].astype(f32) * live_ref[...]
        branch_ref[here, :] = branch.astype(bf16)
        sums_ref[7:8, :] += column_sum(branch)

    @pl.when(step == blocks)
    def _():
        turned_ref[...] = second_ref[...].T
        shard = 2 * tp + 1 - core
        units = pl.ds(pl.multiple_of(TILE * (1 - core), TILE), TILE)
        bias = params_ref[2:3, pl.ds(pl.multiple_of(TILE * shard, TILE), TILE)]
        sums_ref[pl.ds(shard, 1), :] = feed_tile(
            up_own[:, units], down_own[units, :], bias, second_ref, turned_ref, branch_ref, total_ref, back_ref,
            active_s, raise_s, send_ref, True,
        )


def feed_own(
    place, attended, merged, cotangent, live, proj_bias, gain, bias, down_bias, params, proj, near, far, up, down
):
    count = attended.shape[0]
    blocks = count // ROWS

    def taken(columns):
        return pl.BlockSpec((ROWS, columns), lambda i: (jnp.minimum(i, blocks - 1), 0))

    return kernel_call(
        feed_own_body,
        (blocks + 1,),
        [
            SCALARS, taken(D), taken(D), taken(D), taken(1), RESIDENT, RESIDENT, RESIDENT, RESIDENT, RESIDENT, RESIDENT, RESIDENT,
            RESIDENT, RESIDENT,
        ],
        [RESIDENT] * 9,
        [pltpu.VMEM((count, D), f32)] * 3
        + [pltpu.VMEM((count, D), bf16), pltpu.VMEM((D, count), bf16), pltpu.VMEM((count, D), bf16)]
        + [pltpu.VMEM((FEED_PACK, D), bf16), shape_of((8, D), f32), shape_of((D, D), bf16)],
        [pltpu.VMEM((count, TILE), bf16)] * 2,
        room=OWN_ROOM,
    )(
        place, in_hbm(attended), in_hbm(merged), in_hbm(cotangent), in_hbm(live), proj_bias, gain, bias, params, proj,
        near, far, up, down,
    )


def feed_middle_body(
    own, place, second_ref, turned_ref, branch_ref, total_in, back_in, params_ref, sums_in, *refs
):
    weights, (total_ref, back_ref, target_ref, sums_ref, active_s, raise_s) = refs[:-6], refs[-6:]
    core, tp = place[0], place[3]
    sums_ref[...] = sums_in[...]
    if own:
        shard = 2 * tp + core
        units = pl.ds(pl.multiple_of(TILE * core, TILE), TILE)
        up, down = weights[0][:, units], weights[1][units, :]
    else:
        shard = 2 * (1 - tp) + 1 - core
        up, down = weights[0][512:1024, :], weights[0][0:512, :]
    bias = params_ref[2:3, pl.ds(pl.multiple_of(TILE * shard, TILE), TILE)]
    sums_ref[pl.ds(shard, 1), :] = feed_tile(
        up, down, bias, second_ref, turned_ref, branch_ref, total_ref, back_ref, active_s, raise_s, target_ref, False
    )


def feed_middle(own, place, second, turned, branch, total, back, params, sums, weights, cost=COST):
    count = second.shape[0]
    return pl.pallas_call(
        partial(feed_middle_body, own),
        in_specs=[SCALARS] + [RESIDENT] * (7 + len(weights)),
        out_specs=[RESIDENT] * 4,
        out_shape=[pltpu.VMEM((count, D), f32)] * 2 + [pltpu.VMEM((FEED_PACK, D), bf16), shape_of((8, D), f32)],
        scratch_shapes=[pltpu.VMEM((count, TILE), bf16)] * 2,
        input_output_aliases={4: 0, 5: 1},
        compiler_params=pltpu.CompilerParams(vmem_limit_bytes=OTHER_ROOM * 1024 * 1024),
        cost_estimate=cost,
    )(place, second, turned, branch, total, back, params, sums, *weights)


def feed_near_body(
    place, residual_ref, second_ref, turned_ref, branch_ref, total_in, back_in, down_bias, norm_gain, params_ref,
    sums_in, near_ref, attended_ref,
    out_ref, grad_residual_ref, attn_ref, keep_ref, proj_send, proj_keep, sums_ref,
    total_s, back_s, active_s, raise_s, attended_s, proj_s, sem,
):
    step = pl.program_id(0)
    core, tp = place[0], place[3]
    fetch = pltpu.make_async_copy(attended_ref, attended_s, sem)

    @pl.when(step == 0)
    def _():
        fetch.start()
        sums_ref[...] = sums_in[...]
        shard = 2 * (1 - tp) + core
        bias = params_ref[2:3, pl.ds(pl.multiple_of(TILE * shard, TILE), TILE)]
        sums_ref[pl.ds(shard, 1), :] = feed_tile(
            near_ref[512:1024, :], near_ref[0:512, :], bias, second_ref, turned_ref, branch_ref, total_s, back_s,
            active_s, raise_s, keep_ref, True,
        )

    @pl.when(step >= 1)
    def _():
        here = pl.ds(pl.multiple_of((step - 1) * ROWS, 16), ROWS)
        residual = residual_ref[here, :]
        out_ref[...] = (residual + down_bias[...] + total_in[here, :] + total_s[here, :]).astype(bf16)
        hat, inverse = normalize(residual)
        grad_second = back_in[here, :] + back_s[here, :]
        grad_residual = branch_ref[here, :].astype(f32) + norm_back(grad_second * norm_gain[...], hat, inverse)
        grad_residual_ref[here, :] = grad_residual
        attn_ref[here, :] = grad_residual.astype(bf16)
        sums_ref[4:5, :] += column_sum(grad_residual)
        sums_ref[5:6, :] += column_sum(grad_second * hat)
        sums_ref[6:7, :] += column_sum(grad_second)

    @pl.when(step == pl.num_programs(0) - 1)
    def _():
        fetch.wait()
        proj_s[...] = t_mm(attended_s[...], attn_ref[...]).astype(bf16)
        for target, half in ((proj_send, 1 - core), (proj_keep, core)):
            for other in range(2):
                shard = jnp.where(other == 0, tp, 1 - tp)
                rows = pl.ds(pl.multiple_of(256 * shard + 128 * half, 128), 128)
                target[PROJ_PACK * other : PROJ_PACK * (other + 1), :] = proj_s[rows, :]


def feed_near(place, residual, second, turned, branch, total, back, down_bias, gain, params, sums, near, attended):
    count = residual.shape[0]
    blocks = count // ROWS

    def given(columns):
        return pl.BlockSpec((ROWS, columns), lambda i: (jnp.maximum(i - 1, 0), 0))

    return kernel_call(
        feed_near_body,
        (blocks + 1,),
        [SCALARS] + [RESIDENT] * 9 + [whole((8, D)), RESIDENT]
        + [pl.BlockSpec(memory_space=pl.ANY)],
        [given(D)] + [RESIDENT] * 5 + [whole((8, D))],
        [pltpu.HBM((count, D), bf16), pltpu.VMEM((count, D), f32), pltpu.VMEM((count, D), bf16)]
        + [pltpu.VMEM((FEED_PACK, D), bf16)] + [pltpu.VMEM((2 * PROJ_PACK, D), bf16)] * 2
        + [shape_of((8, D), f32)],
        [pltpu.VMEM((count, D), f32)] * 2 + [pltpu.VMEM((count, TILE), bf16)] * 2
        + [pltpu.VMEM((count, D), bf16), pltpu.VMEM((D, D), bf16), pltpu.SemaphoreType.DMA],
        room=NEAR_ROOM,
    )(
        place, residual, second, turned, branch, total, back, down_bias, gain, params, sums, near, in_hbm(attended)
    )


def attend_back_body(
    after, attn_ref, qkv_in_ref, weights_ref, padded_ref, inverse_ref, proj_ref,
    merged_ref, grad_residual_ref, qkv_ref, rows_ref,
    stack_ref, low_ref, sums_ref, vectors_ref, position_ref,
    stage, grads,
):
    @pl.when(pl.program_id(0) == 0)
    def _():
        vectors_ref[...] = jnp.zeros_like(vectors_ref)
        sums_ref[...] = jnp.zeros_like(sums_ref)
        position_ref[...] = jnp.zeros_like(position_ref)

    here = pl.ds(pl.multiple_of(pl.program_id(0) * ROWS, 16), ROWS)
    stage[pl.ds(0, ROWS), :] = attn_ref[here, :].astype(f32)
    stage[pl.ds(ROWS, 32), :] = jnp.zeros((32, D), f32)
    real = lax.broadcasted_iota(jnp.int32, (KEYS, 1), 0) < AREA
    padded = jnp.concatenate(
        [jnp.where(real, stage[pl.ds(AREA * w, KEYS), :], 0.0).astype(bf16) for w in range(GROUP)], axis=0
    )
    grad_attended = mm_t(padded, proj_ref[...])
    masks = head_masks()
    empty = jnp.zeros((QUERIES - KEYS, QUAD), bf16)
    kept = {}
    for w in range(GROUP):
        for quad in range(QUADS):
            columns = slice(QUAD * quad, QUAD * (quad + 1))
            values = qkv_in_ref[w, :, 2 * D + QUAD * quad : 2 * D + QUAD * (quad + 1)]
            grad = grad_attended[KEYS * w : KEYS * (w + 1), columns] * inverse_ref[w, :, columns]
            low = grad.astype(bf16)
            taken = (grad * padded_ref[w, :, columns].astype(f32)).astype(bf16)
            both = jnp.concatenate([low, -taken], axis=1)
            change = jnp.concatenate([mm_t(both, block) for block in value_blocks(values, masks)], axis=1)
            grad_scores = (weights_ref[w, quad].astype(f32) * change).astype(bf16)
            position_ref[quad] += grad_scores.astype(f32)
            kept[w, quad] = (low, grad_scores)
    for w in range(GROUP):
        to = pl.ds(AREA * w, AREA)
        for quad in range(QUADS):
            low, grad_scores = kept[w, quad]
            queries = qkv_in_ref[w, :, QUAD * quad : QUAD * (quad + 1)]
            keys = qkv_in_ref[w, :, D + QUAD * quad : D + QUAD * (quad + 1)]
            grad_queries = mm(grad_scores, spread_heads(keys, masks)) * SCALING
            grad_keys = turned_products(queries.T[:, :KEYS], grad_scores)
            grad_values = turned_products(jnp.concatenate([low, empty], axis=0).T[:, :KEYS], weights_ref[w, quad])
            for part, grad in enumerate((grad_queries, grad_keys, grad_values)):
                grads[to, D * part + QUAD * quad : D * part + QUAD * (quad + 1)] = grad[0:AREA]
    stack = grads[...].astype(bf16)
    stack_ref[here, :] = stack
    sums_ref[...] += column_sum(stack.astype(f32))
    grad_first = (
        mm_t(stack[:, 0:D], qkv_ref[0:D, :])
        + mm_t(stack[:, D : 2 * D], qkv_ref[D : 2 * D, :])
        + mm_t(stack[:, 2 * D :], qkv_ref[2 * D :, :])
    )
    normed, inverse = normalize(merged_ref[...])
    grad_merged = grad_residual_ref[here, :] + norm_back(grad_first * rows_ref[0:1, :], normed, inverse)
    low = grad_merged.astype(bf16)
    low_ref[here, :] = low
    vectors_ref[0:1, :] += column_sum(grad_first * normed)
    vectors_ref[1:2, :] += column_sum(grad_first)
    vectors_ref[2:3, :] += column_sum(low.astype(f32))


def attend_back(after, attn, qkv_in, weights, padded, inverse, proj, merged, grad_residual, qkv, rows):
    count = attn.shape[0]
    return kernel_call(
        attend_back_body,
        (count // ROWS,),
        [
            ANYWHERE, RESIDENT, by_windows((QUERIES, 3 * D)), by_windows((QUADS, KEYS, LANES)),
            by_windows((KEYS, D)), by_windows((KEYS, D)), RESIDENT, by_rows(ROWS, D), RESIDENT, RESIDENT, RESIDENT,
        ],
        [RESIDENT] * 5,
        [
            pltpu.VMEM((count, 3 * D), bf16), pltpu.VMEM((count, D), bf16), shape_of((1, 3 * D), f32),
            shape_of((8, D), f32), shape_of((QUADS, KEYS, LANES), f32),
        ],
        [pltpu.VMEM((ROWS + 32, D), f32), pltpu.VMEM((ROWS, 3 * D), f32)],
        room=AB_ROOM,
    )(
        after, attn, *[in_hbm(array) for array in (qkv_in, weights, padded, inverse)], proj, in_hbm(merged),
        grad_residual, qkv, rows,
    )


def qkv_back_body(place, after, turned_ref, stack_ref, send_ref, keep_ref, qkv_s):
    part = pl.program_id(0)
    core, tp = place[0], place[3]
    qkv_s[...] = mm(turned_ref[...], stack_ref[:, pl.ds(pl.multiple_of(D * part, D), D)]).astype(bf16)
    for target, half in ((send_ref, 1 - core), (keep_ref, core)):
        for other in range(2):
            shard = jnp.where(other == 0, tp, 1 - tp)
            base = QKV_PACK * other
            rows = pl.ds(pl.multiple_of(256 * half, 256), 256)
            columns = pl.ds(pl.multiple_of(256 * shard, 256), 256)

            @pl.when(part < 2)
            def _():
                target[base : base + 256, pl.ds(pl.multiple_of(256 * part, 256), 256)] = qkv_s[rows, columns]

            @pl.when(part == 2)
            def _():
                block = qkv_s[rows, columns]
                target[base + 256 : base + 384, 0:256] = block[0:128]
                target[base + 256 : base + 384, 256:512] = block[128:256]


def qkv_back(place, after, turned, stack):
    count = stack.shape[0]
    return kernel_call(
        qkv_back_body,
        (3,),
        [
            SCALARS, ANYWHERE, RESIDENT, RESIDENT,
        ],
        [RESIDENT, RESIDENT],
        [pltpu.VMEM((2 * QKV_PACK, D), bf16), pltpu.VMEM((2 * QKV_PACK, D), bf16)],
        [pltpu.VMEM((D, D), bf16)],
        room=12,
    )(place, after, turned, stack)


def merge_back_body(
    place, after, low_ref, turned_ref, merge_ref, params_ref, column_ref, feed_sums_ref, qkv_sums_ref, vectors_ref,
    position_ref,
    send_ref, keep_ref,
    fold_s, all_s, raw_s,
):
    core, tp = place[0], place[3]
    total = vectors_ref[2:3, :]
    pair = jnp.concatenate([split(total), jnp.zeros((14, D), bf16)], axis=0)
    ones = jnp.ones((16, D), bf16)
    raw_s[...] = mm(turned_ref[...], low_ref[...])
    all_s[...] = jnp.zeros_like(all_s)
    all_s[0:2, :] = vectors_ref[0:2, :]
    all_s[2:6, :] = feed_sums_ref[4:8, :]
    all_s[6:7, :] = qkv_sums_ref[:, 0:D]
    all_s[7:8, :] = qkv_sums_ref[:, 2 * D :]
    all_s[8:12, :] = feed_sums_ref[0:4, :]
    all_s[16:32, 0:384] = fold_place(position_ref, fold_s)
    for tile in range(2):
        rows = slice(512 * tile, 512 * (tile + 1))
        merge = merge_ref[rows, :]
        scaled = raw_s[rows, :] * merge.astype(f32)
        scaled_high = scaled.astype(bf16)
        scaled_rest = (scaled - scaled_high.astype(f32)).astype(bf16)
        all_s[12 + tile : 13 + tile, :] = (mm_t(ones, scaled_high) + mm_t(ones, scaled_rest))[0:1]
        all_s[14 + tile : 15 + tile, :] = column_sum(mm_t(pair, merge))
    for target, half in ((send_ref, 1 - core), (keep_ref, core)):
        for other in range(2):
            begin = pl.multiple_of(512 * jnp.where(other == 0, tp, 1 - tp) + 256 * half, 256)
            bias = jnp.broadcast_to(params_ref[0:1, pl.ds(1024 + begin, 256)], (16, 256)).astype(bf16)
            gain = column_ref[pl.ds(begin, 256), 0:1]
            block = raw_s[pl.ds(begin, 256), :] * gain + t_mm(bias, pair)
            target[MERGE_PACK * other : MERGE_PACK * (other + 1), :] = block.astype(bf16)
        target[2 * MERGE_PACK :, :] = split(all_s[pl.ds(pl.multiple_of(SUMS * half, SUMS), SUMS), :])


def merge_back(place, after, low, turned, merge, params, column, feed_sums, sums, vectors, position):
    pack = 2 * MERGE_PACK + 2 * SUMS
    return pl.pallas_call(
        merge_back_body,
        in_specs=[SCALARS, ANYWHERE] + [RESIDENT] * 9,
        out_specs=[RESIDENT] * 2,
        out_shape=[pltpu.VMEM((pack, D), bf16), pltpu.VMEM((pack, D), bf16)],
        scratch_shapes=[
            pltpu.VMEM((HEADS, KEYS, 256), f32), pltpu.VMEM((32, D), f32), pltpu.VMEM((MERGE_IN, D), f32),
        ],
        compiler_params=pltpu.CompilerParams(vmem_limit_bytes=20 * 1024 * 1024),
        cost_estimate=COST,
    )(place, after, low, turned, merge, params, column, feed_sums, sums, vectors, position)


def section_back_body(after, low_ref, hat_ref, inverse_ref, merge_ref, params_ref, out_ref, token_ref):
    token_ref[...] = jnp.zeros_like(token_ref)
    scaled = mm_t(low_ref[...], merge_ref[...]) * params_ref[0:1, 0:MERGE_IN]
    out_ref[...] = norm_back(scaled, hat_ref[...].astype(f32), inverse_ref[...]).astype(bf16)


def section_back(after, low, hat, inverse, merge, params):
    count = low.shape[0]
    return kernel_call(
        section_back_body,
        (count // ROWS,),
        [
            pl.BlockSpec(memory_space=pl.ANY), by_rows(ROWS, D), by_rows(ROWS, MERGE_IN), by_rows(ROWS, 1),
            whole((MERGE_IN, D)), whole((24, 2048)),
        ],
        [by_rows(ROWS, MERGE_IN), whole((8, 128))],
        [pltpu.HBM((count, MERGE_IN), bf16), shape_of((8, 128), f32)],
        flops=2 * count * D * MERGE_IN,
        moved=count * 5 * MERGE_IN,
        room=24,
    )(after, in_hbm(low), in_hbm(hat), inverse, merge, params)


def spread_matrix():
    place = lax.broadcasted_iota(jnp.int32, (QUERIES, 256), 0)
    lane = lax.broadcasted_iota(jnp.int32, (QUERIES, 256), 1)
    target = place + (SIDE - WINDOW) * (place // WINDOW)
    return jnp.logical_and(lane == target, place < AREA).astype(f32)


def expand_body(params_ref, place_ref, stage_s):
    spread = spread_matrix().astype(bf16)
    for head in range(HEADS):
        stage = stage_s.at[head]
        stage[96:KEYS, :] = jnp.zeros((KEYS - 96, 256), f32)
        line = params_ref[8 + head : 9 + head, 0:384]
        lines = jnp.concatenate(
            [pltpu.roll(line, (384 - (WINDOW - 1) * (SIDE + 1) + x) % 384, 1) for x in range(WINDOW)]
            + [jnp.zeros((6, 384), f32)],
            axis=0,
        )
        for y in range(WINDOW):
            moved = pltpu.roll(lines, SIDE * y, 1) if y else lines
            stage[pl.ds(WINDOW * y, WINDOW), :] = moved[0:WINDOW, 0:256]
        rows = stage[...]
        high = rows.astype(bf16)
        rest = rows - high.astype(f32)
        middle = rest.astype(bf16)
        low = (rest - middle.astype(f32)).astype(bf16)
        block = mm_t(high, spread) + mm_t(middle, spread) + mm_t(low, spread)
        block = jnp.concatenate([block, jnp.zeros((QUERIES - KEYS, QUERIES), f32)], axis=0).T[:KEYS]
        place_ref[head // 4, :, QUERIES * (head % 4) : QUERIES * (head % 4 + 1)] = block


def expand(params):
    return kernel_call(
        expand_body,
        (1,),
        [whole((24, 2048))],
        whole((QUADS, KEYS, LANES)),
        shape_of((QUADS, KEYS, LANES), f32),
        [pltpu.VMEM((HEADS, KEYS, 256), f32)],
        room=24,
    )(params)


def fold_place(place_ref, stage_s):
    spread = spread_matrix().astype(bf16)
    lines = []
    for head in range(HEADS):
        stage = stage_s.at[head]
        rows = place_ref[head // 4, :, QUERIES * (head % 4) : QUERIES * (head % 4 + 1)]
        rows = jnp.concatenate([rows, jnp.zeros((QUERIES - KEYS, QUERIES), f32)], axis=0).T[:KEYS]
        high = rows.astype(bf16)
        rest = (rows - high.astype(f32)).astype(bf16)
        stage[...] = mm(high, spread) + mm(rest, spread)
        total = jnp.zeros((WINDOW, 384), f32)
        for y in range(WINDOW):
            part = jnp.concatenate(
                [stage[pl.ds(WINDOW * y, WINDOW), :], jnp.zeros((WINDOW, 128), f32)], axis=1
            )
            total += pltpu.roll(part, SIDE * (WINDOW - 1 - y), 1) if y < WINDOW - 1 else part
        line = total[WINDOW - 1 : WINDOW, :]
        for x in range(WINDOW - 1):
            line += pltpu.roll(total[x : x + 1, :], WINDOW - 1 - x, 1)
        lines.append(line)
    return jnp.concatenate(lines, axis=0)


class Ring:
    def __init__(self, place, rows_size):
        self.place = place
        self.rows_size = rows_size
        self.along = rows_size // 4

    def to(self, array, bits):
        return lax.ppermute(array, "rows", [(i, i ^ bits) for i in range(self.rows_size)])

    def core(self, array):
        return self.to(array, 1)

    def x(self, array):
        return self.to(array, 2)

    def z(self, array, step):
        return self.to(array, 4 * step)

    def y(self, array):
        return lax.ppermute(array, "tp", [(0, 1), (1, 0)])

    def xy(self, array):
        pairs = [(2 * i + t, 2 * (i ^ 2) + 1 - t) for i in range(self.rows_size) for t in range(2)]
        return lax.ppermute(array, ("rows", "tp"), pairs)


def rows_of(array, begin, rows):
    return lax.dynamic_slice_in_dim(array, begin, rows, 0).astype(f32)


def stage(body, place, after, rows, *operands, cost=COST, scratch=()):
    return plain_call_after(
        body, [pltpu.VMEM((count, D), bf16) for count in rows], place, after, operands, room=STAGE_ROOM, cost=cost,
        scratch=scratch,
    )


def added(refs, begin, rows):
    here = pl.ds(pl.multiple_of(begin, 16), rows)
    total = refs[0][here, :].astype(f32)
    for ref in refs[1:]:
        total = total + ref[here, :].astype(f32)
    return total


def part(ref, begin, rows):
    return ref.at[begin : begin + rows, :]


def feed_first_body(
    place, own_keep, own_got, other_keep, other_got, proj_keep, proj_got, down_y, up_x
):
    down_y[0:512, :] = added((other_keep, other_got), 0, 512).astype(bf16)
    down_y[512:640, :] = added((proj_keep, proj_got), 128, 128).astype(bf16)
    begin = 512 + 256 * (1 - place[1])
    up_x[0:256, :] = added((own_keep, own_got), begin, 256).astype(bf16)
    up_x[256:512, :] = added((other_keep, other_got), begin, 256).astype(bf16)


def feed_second_body(
    place, own_keep, own_got, other_keep, other_got, proj_keep, proj_got, down_shard, up_got, down_x, up_y, kept
):
    x = place[1]
    for target, side in ((down_x, 1 - x), (kept, x)):
        target[0:256, :] = added((own_keep, own_got, down_shard), 256 * side, 256).astype(bf16)
        proj = (proj_keep, proj_got, part(down_shard, 512, 128))
        target[256:320, :] = added(proj, 64 * side, 64).astype(bf16)
    begin = 512 + 256 * x
    up_y[...] = (added((other_keep, other_got), begin, 256) + up_got[256:512, :].astype(f32)).astype(bf16)
    kept[320:576, :] = (added((own_keep, own_got), begin, 256) + up_got[0:256, :].astype(f32)).astype(bf16)


def feed_third_body(place, kept, down_got, up_shard, *outs):
    for step, out in enumerate(outs):
        to = place[2] ^ step
        offset = 0
        for ref, got, begin, size in ((kept, down_got, 0, 256), (kept, down_got, 256, 64), (kept, up_shard, 320, 256)):
            span = size // len(outs)
            mine = part(ref, begin, size)
            theirs = part(got, begin if got is down_got else 0, size)
            out[offset : offset + span, :] = added((mine, theirs), to * span, span).astype(bf16)
            offset += span


def total_body(place, *refs):
    refs[-1][...] = added(refs[:-1], 0, refs[-1].shape[0]).astype(bf16)


def beside_body(place, *refs):
    rows = refs[0].shape[0]
    for index, ref in enumerate(refs[:-1]):
        refs[-1][rows * index : rows * (index + 1), :] = ref[...]


def last_first_body(place, keep, got, qkv_keep, qkv_got, to_y, to_x, to_both, kept, sums_s):
    x = place[1]
    sums_s[...] = joined(keep[512:544, :]) + joined(got[512:544, :])
    for target, other, side in ((to_y, 1, x), (to_x, 0, 1 - x), (to_both, 1, 1 - x), (kept, 0, x)):
        target[0:192, :] = added((qkv_keep, qkv_got), QKV_PACK * other + 192 * side, 192).astype(bf16)
        target[192:320, :] = added((keep, got), MERGE_PACK * other + 128 * side, 128).astype(bf16)
        target[320:336, :] = split(sums_s[pl.ds(pl.multiple_of(8 * side, 8), 8), :])


def last_second_body(place, *refs):
    blocks, outs = refs[:4], refs[4:]
    vectors = split(sum(joined(ref[320:336, :]) for ref in blocks))
    wide, narrow = 192 // len(outs), 128 // len(outs)
    for step, out in enumerate(outs):
        to = place[2] ^ step
        out[0:wide, :] = added(blocks, to * wide, wide).astype(bf16)
        out[wide : wide + narrow, :] = added(blocks, 192 + to * narrow, narrow).astype(bf16)
        out[wide + narrow :, :] = vectors


def merge_total_body(place, *refs):
    blocks, (out, vectors) = refs[:-2], refs[-2:]
    rows = out.shape[0]
    out[...] = added(blocks, 0, rows).astype(bf16)
    vectors[...] = split(sum(joined(ref[rows : rows + 16, :]) for ref in blocks))


def last_beside_body(place, vectors, *refs):
    rows = refs[0].shape[0]
    for index, ref in enumerate(refs[:-1]):
        refs[-1][rows * index : rows * (index + 1), :] = ref[...]
    refs[-1][rows * (len(refs) - 1) :, :] = vectors[...]


def in_order(place, near, far, stage, rows, along):
    piece = sum(rows) // 2 // along
    for side, ref in ((place[1], near), (1 - place[1], far)):
        for step in range(along):
            begin, offset = 0, piece * step
            for size in rows:
                span = size // 2 // along
                to = begin + side * (size // 2) + (place[2] ^ step) * span
                stage[pl.ds(pl.multiple_of(to, 16), span), :] = ref[offset : offset + span, :]
                begin += size
                offset += span


def feed_unpack_body(along, place, near, far, core_near, core_far, down_ref, up_ref, proj_ref, token_ref, stage):
    token_ref[...] = jnp.zeros_like(token_ref)
    for target, mine, beside in ((place[0], near, far), (1 - place[0], core_near, core_far)):
        in_order(place, mine, beside, stage, (512, PROJ_PACK, 512), along)
        wide = pl.ds(pl.multiple_of(512 * target, 512), 512)
        down_ref[wide, :] = stage[0:512, :].astype(f32)
        proj_ref[pl.ds(pl.multiple_of(128 * target, 128), 128), :] = stage[512:640, :].astype(f32)
        up_ref[:, wide] = stage[640:1152, :].astype(f32)


def feed_unpack(along, place, after, parts):
    return plain_call_after(
        partial(feed_unpack_body, along),
        [pltpu.HBM((FFN // 2, D), f32), pltpu.HBM((D, FFN // 2), f32), pltpu.HBM((D // 2, D), f32), shape_of((8, 128), f32)],
        place,
        after,
        parts,
        scratch=[pltpu.VMEM((FEED_PACK + PROJ_PACK, D), bf16)],
        room=24,
    )


def last_unpack_body(along, place, mine, other, qkv_ref, merge_ref, *refs):
    vectors, stage, all_s = refs[:-2], refs[-2], refs[-1]
    half = mine.shape[0] // 2
    rows = half - 16
    for target, ref in ((place[0], mine), (1 - place[0], other)):
        near, far = ref.at[0:half, :], ref.at[half:, :]
        in_order(place, near, far, stage, (QKV_PACK, MERGE_PACK), along)
        for side, ref in ((place[1], near), (1 - place[1], far)):
            all_s[pl.ds(pl.multiple_of(SUMS * target + 8 * side, 8), 8), :] = joined(ref[rows:, :])
        begin = pl.multiple_of(256 * target, 256)
        for part in range(2):
            qkv_ref[part, pl.ds(begin, 256), :] = stage[0:256, 256 * part : 256 * part + 256].astype(f32)
        qkv_ref[2, pl.ds(begin, 128), :] = stage[256:384, 0:256].astype(f32)
        qkv_ref[2, pl.ds(begin + 128, 128), :] = stage[256:384, 256:512].astype(f32)
        merge_ref[pl.ds(begin, 256), :] = stage[384:640, :].astype(f32)
    write_vectors(place[3], all_s, vectors)


VECTORS = [(1, D)] * 6 + [(2, D // 2), (1, FFN // 2), (1, MERGE_IN // 2), (1, MERGE_IN // 2), (HEADS // 2, SIDE * SIDE)]


def write_vectors(tp, sums, refs):
    for row in range(6):
        refs[row][...] = sums[row : row + 1, :]
    columns = pl.ds(pl.multiple_of(256 * tp, 256), 256)
    refs[6][...] = sums[6:8, columns]
    refs[7][:, 0:512] = sums[pl.ds(8 + 2 * tp, 1), :]
    refs[7][:, 512:1024] = sums[pl.ds(9 + 2 * tp, 1), :]
    refs[8][...] = sums[pl.ds(12 + tp, 1), :]
    refs[9][...] = sums[pl.ds(14 + tp, 1), :]
    refs[10][...] = sums[pl.ds(pl.multiple_of(16 + 8 * tp, 8), 8), 0 : SIDE * SIDE]


def last_unpack(along, place, mine, other):
    outs = plain_call(
        partial(last_unpack_body, along),
        [pltpu.HBM(shape, f32) if shape[-2] >= 128 else shape_of(shape, f32) for shape in [(3, D, D // 2), (MERGE_IN // 2, D)] + VECTORS],
        (place, mine, other),
        scratch=[pltpu.VMEM((QKV_PACK + MERGE_PACK, D), bf16), pltpu.VMEM((2 * SUMS, D), f32)],
    )
    return outs[0], outs[1], outs[2:]


def fetch_by_tp(ring, piece_of):
    near = ring.y(piece_of)
    return near, ring.core(near)


def plain_pieces(tp_size, weights, params):
    merge, qkv, proj, up, down = [
        lax.all_gather(array, "tp", axis=axis, tiled=True) for array, axis in zip(weights, (0, 2, 0, 1, 0))
    ]
    gain, bias, qv, up_bias, table = [
        lax.all_gather(array, "tp", axis=axis, tiled=True) for array, axis in zip(params, (0, 0, 1, 0, 1))
    ]

    def shard(array, axis, which):
        size = array.shape[axis] // 2
        return lax.slice_in_dim(array, which * size, (which + 1) * size, axis=axis)

    def rows_of(which):
        rows = jnp.zeros((PARAMS, D), f32)
        rows = rows.at[0].set(shard(gain.astype(f32), 0, which)).at[1].set(shard(bias.astype(f32), 0, which))
        rows = rows.at[2].set(shard(qv, 1, which).reshape(-1)).at[3:5].set(shard(up_bias, 0, which).reshape(2, D))
        return rows.at[8:16, : SIDE * SIDE].set(shard(table, 1, which).T)

    merge_other = shard(merge, 0, 1)
    qkv_other = shard(qkv, 2, 1).reshape(3 * D, 256)
    proj_other, up_other, down_other = shard(proj, 0, 1), shard(up, 1, 1), shard(down, 0, 1)

    def qkv_piece(half):
        rows = qkv_other[768 * half : 768 * half + 768]
        return jnp.concatenate(
            [jnp.concatenate([rows[:384], rows[384:]], axis=1), proj_other[128 * half : 128 * half + 128]], axis=0
        )

    def feed_piece(half):
        tile = slice(512 * half, 512 * half + 512)
        return jnp.concatenate([down_other[tile], up_other[:, tile]], axis=0)

    own = (
        shard(merge, 0, 0), shard(qkv, 2, 0).reshape(3 * D, 256), shard(proj, 0, 0), shard(up, 1, 0), shard(down, 0, 0)
    )
    return own, (rows_of(0), split(rows_of(1))), (merge_other[:256], merge_other[256:]), (qkv_piece(0), qkv_piece(1)), (feed_piece(0), feed_piece(1))


def sum_plainly(tp_size, feed_packs, proj_packs, qkv_packs, merge_packs):
    feed_packs, proj_packs, qkv_packs, merge_packs = lax.psum(
        (feed_packs, proj_packs, qkv_packs, merge_packs), ("rows", "tp")
    )
    own_send, own_keep, other_send, other_keep = feed_packs
    order = [own_keep, own_send, other_keep, other_send]
    down = jnp.concatenate([block[0:512] for block in order], axis=0)
    up = jnp.concatenate([block[512:1024] for block in order], axis=1)

    def blocks(packs, size):
        send, keep = packs
        return [keep[:size], send[:size], keep[size : 2 * size], send[size : 2 * size]]

    def qkv_rows(block):
        return jnp.stack(
            [block[0:256, 0:256], block[0:256, 256:512], jnp.concatenate([block[256:384, 0:256], block[256:384, 256:512]])]
        )

    order = blocks(qkv_packs, QKV_PACK)
    qkv = jnp.concatenate(
        [jnp.concatenate([qkv_rows(order[2 * shard + half]) for half in range(2)], axis=1) for shard in range(2)], axis=2
    )
    proj = jnp.concatenate(blocks(proj_packs, PROJ_PACK), axis=0)
    merge = jnp.concatenate(blocks(merge_packs, MERGE_PACK), axis=0)
    sums = jnp.concatenate([joined(merge_packs[1][2 * MERGE_PACK :]), joined(merge_packs[0][2 * MERGE_PACK :])], axis=0)
    index = lax.axis_index("tp")

    def own(array, axis):
        size = array.shape[axis] // tp_size
        return lax.dynamic_slice_in_dim(array, index * size, size, axis).astype(f32)

    vectors = [sums[row] for row in range(6)] + [
        own(sums[6:8], 1), own(sums[8:12].reshape(-1), 0), own(sums[12:14].reshape(-1), 0),
        own(sums[14:16].reshape(-1), 0), own(sums[16:32, : SIDE * SIDE], 0),
    ]
    return own(down, 0), own(up, 1), own(qkv, 2), own(proj, 0), own(merge, 0), vectors


def per_device(
    rows_size, tp_size,
    section_rows, window_mask, cotangent, merge_weight, merge_gain, merge_bias, norm1_gain, norm1_bias,
    qkv_weight, qv_bias, bias_table, proj_weight, proj_bias, norm2_gain, norm2_bias,
    up_weight, up_bias, down_weight, down_bias,
):
    fast = tp_size == 2 and rows_size in (8, 16)
    count = cotangent.shape[0]
    index, tp = lax.axis_index("rows"), lax.axis_index("tp")
    place = jnp.stack([index & 1, (index >> 1) & 1, index >> 2, tp]).astype(jnp.int32)
    ring = Ring(place, rows_size)
    if fast:
        flat_qkv = qkv_weight.reshape(3 * D, D // 2)
        (merge_piece,) = plain_call(pack_merge_body, [shape_of((256, D), bf16)], (place, merge_weight))
        merge_near = ring.y(merge_piece)
        params, piece = pack_params(
            place, merge_piece, jnp.concatenate([merge_gain, merge_bias]).astype(f32)[None], qv_bias, up_bias[None], bias_table.T
        )
        others = ring.y(piece)
        mask, live = masks_of(place, piece, window_mask, count)
        hat, inverse = section_norm(mask, section_rows)
        (qkv_piece,) = plain_call_after(
            pack_qkv_body, [shape_of((QKV_PACK + PROJ_PACK, D), bf16)], place, (others, merge_near, hat), (flat_qkv, proj_weight)
        )
        qkv_near = ring.y(qkv_piece)
        merge_far = ring.core(merge_near)
        kernel_place = place
    else:
        (merge_weight, flat_qkv, proj_weight, up_weight, down_weight), (params, others), merge_pair, qkv_pair, feed_pair = plain_pieces(
            tp_size,
            (merge_weight, qkv_weight, proj_weight, up_weight, down_weight),
            (merge_gain, merge_bias, qv_bias, up_bias, bias_table),
        )
        (merge_near, merge_far), (qkv_near, qkv_far), (feed_near_piece, feed_far_piece) = merge_pair, qkv_pair, feed_pair
        kernel_place = jnp.zeros_like(place)
        hat, inverse = section_norm(params, section_rows)
        own_mask = lax.dynamic_slice_in_dim(window_mask, tp * count, count, 0)
        mask, live = masks_of(kernel_place, params, own_mask, count)

    merged, first, merge_full, params, column = merge_rows(
        kernel_place, hat, merge_weight, merge_near, merge_far, params, others, jnp.stack([norm1_gain, norm1_bias])
    )
    position = expand(params)
    turned_first, turned_hat, hat = turn(position, first, hat)
    if fast:
        (feed_piece,) = plain_call_after(
            pack_feed_body, [shape_of((FEED_PACK, D), bf16)], place, (position, qkv_near), (up_weight, down_weight)
        )
        qkv_far = ring.core(qkv_near)
        feed_near_piece = ring.y(feed_piece)
        feed_far_piece = ring.core(feed_near_piece)
    qkv_rows, weights, attended, padded, inverse_sums, qkv_full = attend(
        kernel_place, first, flat_qkv, qkv_near, qkv_far, params, position, mask
    )
    rows = [row[None] for row in (proj_bias, norm2_gain, norm2_bias, down_bias)]
    residual, total, back, second, turned, branch, own_send, feed_sums, proj_full = feed_own(
        kernel_place, attended, merged, cotangent, live, *rows, params, proj_weight, qkv_near, qkv_far,
        up_weight, down_weight,
    )
    total, back, own_keep, feed_sums = feed_middle(
        True, kernel_place, second, turned, branch, total, back, params, feed_sums, (up_weight, down_weight), LONG
    )
    total, back, other_send, feed_sums = feed_middle(
        False, kernel_place, second, turned, branch, total, back, params, feed_sums, (feed_far_piece,)
    )
    block_out, grad_residual, attn, other_keep, proj_send, proj_keep, feed_sums = feed_near(
        kernel_place, residual, second, turned, branch, total, back, rows[3], rows[1], params, feed_sums, feed_near_piece,
        attended,
    )
    after = feed_sums
    if fast:
        own_got, other_got, proj_got = ring.core(own_send), ring.core(other_send), ring.core(proj_send)
        feed_keeps = (own_keep, own_got, other_keep, other_got, proj_keep, proj_got)
        down_y, up_x = stage(feed_first_body, place, feed_sums, (640, 512), *feed_keeps)
        down_shard, up_got = ring.y(down_y), ring.x(up_x)
        after = up_x
    stack, low, sums, vectors, position_grad = attend_back(
        after, attn, qkv_rows, weights, padded, inverse_sums, proj_full, merged, grad_residual, qkv_full,
        norm1_gain[None],
    )
    after = sums
    if fast:
        down_x, up_y, feed_kept = stage(
            feed_second_body, place, sums, (320, 256, 576), *feed_keeps, down_shard, up_got
        )
        down_got, up_shard = ring.x(down_x), ring.y(up_y)
        after = up_y
    qkv_send, qkv_keep = qkv_back(kernel_place, after, turned_first, stack)
    after = sums
    if fast:
        along = ring.along
        qkv_got = ring.core(qkv_send)
        span = 576 // along
        feed_parts = stage(
            feed_third_body, place, qkv_send, (span,) * along, feed_kept, down_got, up_shard, cost=LONG
        )
        feed_got = [ring.z(feed_parts[step], step) for step in range(1, along)]
        after = feed_parts[0]
    merge_send, merge_keep = merge_back(
        kernel_place, after, low, turned_hat, merge_full, params, column, feed_sums, sums, vectors, position_grad
    )
    if fast:
        merge_got = ring.core(merge_send)
        (feed_total,) = stage(total_body, place, merge_send, (span,), feed_parts[0], *feed_got, cost=LONG)
        feed_all = [feed_total] + [ring.z(feed_total, step) for step in range(1, along)]
        to_y, to_x, to_both, last_kept = stage(
            last_first_body, place, feed_total, (336,) * 4, merge_keep, merge_got, qkv_keep, qkv_got,
            scratch=[pltpu.VMEM((SUMS, D), f32)],
        )
        last_span = 320 // along
        last_parts = stage(
            last_second_body, place, to_y, (last_span + 16,) * along,
            last_kept, ring.y(to_y), ring.x(to_x), ring.xy(to_both),
        )
        last_got = [ring.z(last_parts[step], step) for step in range(1, along)]
        (feed_mine,) = stage(beside_body, place, last_parts[0], (span * along,), *feed_all)
        feed_beside = ring.x(feed_mine)
        last_total, vectors = stage(
            merge_total_body, place, feed_mine, (last_span, 16), *([last_parts[0]] + last_got), cost=LONG
        )
        last_all = [last_total] + [ring.z(last_total, step) for step in range(1, along)]
        section_grad, token = section_back(last_total, low, hat, inverse, merge_full, params)
        (last_near,) = stage(
            last_beside_body, place, (token, feed_beside), (336,), vectors, *last_all, cost=LONG
        )
        last_far = ring.x(last_near)
        feed_cores = ring.core(feed_mine), ring.core(feed_beside)
        down_grad, up_grad, proj_grad, token = feed_unpack(
            along, place, last_near, (feed_mine, feed_beside, *feed_cores)
        )
        (last_half,) = stage(beside_body, place, token, (672,), last_near, last_far)
        qkv_grad, merge_grad, vectors = last_unpack(along, place, last_half, ring.core(last_half))
    else:
        section_grad, _ = section_back(low, low, hat, inverse, merge_full, params)
        down_grad, up_grad, qkv_grad, proj_grad, merge_grad, vectors = sum_plainly(
            tp_size, (own_send, own_keep, other_send, other_keep), (proj_send, proj_keep), (qkv_send, qkv_keep),
            (merge_send, merge_keep),
        )
    norm1_gain_grad, norm1_bias_grad, proj_bias_grad, norm2_gain_grad, norm2_bias_grad, down_bias_grad = [
        row.reshape(D) for row in vectors[0:6]
    ]
    qv_grad, up_bias_grad, gain_grad, bias_grad, table_grad = vectors[6:]
    return (
        block_out, section_grad, merge_grad, gain_grad.reshape(-1), bias_grad.reshape(-1),
        norm1_gain_grad, norm1_bias_grad, qkv_grad, qv_grad, table_grad.T, proj_grad, proj_bias_grad,
        norm2_gain_grad, norm2_bias_grad, up_grad, up_bias_grad.reshape(-1), down_grad, down_bias_grad,
    )


def solution(mesh):
    rows_size, tp_size = mesh.shape["rows"], mesh.shape["tp"]
    both = ("rows", "tp")
    return jax.shard_map(
        partial(per_device, rows_size, tp_size),
        mesh=mesh,
        in_specs=(
            P(both, None), P("rows"), P(both, None), P("tp", None), P("tp"), P("tp"), P(), P(),
            P(None, None, "tp"), P(None, "tp"), P(None, "tp"), P("tp", None), P(), P(), P(),
            P(None, "tp"), P("tp"), P("tp", None), P(),
        ),
        out_specs=(
            P(both, None), P(both, None), P("tp", None), P("tp"), P("tp"), P(), P(),
            P(None, None, "tp"), P(None, "tp"), P(None, "tp"), P("tp", None), P(), P(), P(),
            P(None, "tp"), P("tp"), P("tp", None), P(),
        ),
        check_vma=False,
    )
```

profile of v0, /device:TPU:0, one launch (start us, length us, event | category | flops | bytes accessed | tf_op | source)
XLA Modules:
  0.0 202.0 jit_solution(14140410140198724722)
XLA Ops:
  0.8 1.1 copy-done.16
  2.4 3.0 %collective-permute-start = (bf16[256,512]{1,0:T(8,128)(2,1)S(1)}, bf16[256,512]{1,0:T(8,128)(2,1)S(1)}, u32[]{:S(2)}, u32[]{:S(2)}) collective-permute-start(bf16[256,512]{1,0:T(8,128)(2,1)S(1)} %shard_map.322.after), channel_id=1, source_target_pairs={{0,1},{1,0},{2,3},{3,2},{4,5},{5,4},{6,7},{7,6},{8,9},{9,8},{10,11... | collective-permute-start | bytes 786440 | tf_op jit(solution)/shard_map/ppermute | solution.py:951
  5.5 0.7 concatenate.14
  6.2 0.7 concatenate.15
  6.8 0.6 maximum_convert_fusion.merge_ref
  7.4 2.1 %shard_map.323 = (f32[16,512]{1,0:T(8,128)}, bf16[32,512]{1,0:T(8,128)(2,1)}) custom-call(s32[4]{0:T(128)} %copy-done.23, bf16[256,512]{1,0:T(8,128)(2,1)} %copy-done.19, f32[1,1024]{1,0:T(1,128)} %maximum_convert_fusion.merge_ref, f32[2,256]{1,0:T(2,128)} %qv_ref.1, f32[1,1024]{1,0:T(1,128)} %bitcast.33, f32[8,361]{1,0:T(8,128)} %bitcast.32), custom_call_target="tpu_custom_call" | custom-call | flops 1 | bytes 1 | tf_op jit(solution)/shard_map/pallas_call | solution.py:166
  9.6 0.7 broadcast_in_dim.21.refs_1_
  10.4 0.6 copy-done.24
  11.0 0.8 copy-done.27
  11.8 0.8 shard_map.324
  12.6 3.3 %shard_map.325 = (bf16[1600,1024]{1,0:T(8,128)(2,1)S(1)}, f32[1600,1]{1,0:T(8,128)S(1)}) custom-call(f32[16,1,128]{2,1,0:T(1,128)S(1)} %get-tuple-element.110.after.mask_ref, bf16[1600,1024]{1,0:T(8,128)(2,1)} %rows_ref.1), custom_call_target="tpu_custom_call" | custom-call | flops 1 | bytes 1 | tf_op jit(solution)/shard_map/pallas_call | solution.py:268
  16.7 2.1 %collective-permute-start.3 = (bf16[512,512]{1,0:T(8,128)(2,1)S(1)}, bf16[512,512]{1,0:T(8,128)(2,1)S(1)}, u32[]{:S(2)}, u32[]{:S(2)}) collective-permute-start(bf16[512,512]{1,0:T(8,128)(2,1)S(1)} %shard_map.327), channel_id=1, source_target_pairs={{0,1},{1,0},{2,3},{3,2},{4,5},{5,4},{6,7},{7,6},{8,9},{9,8},{10,11... | collective-permute-start | bytes 1572872 | tf_op jit(solution)/shard_map/ppermute | solution.py:951
  18.8 1.5 collective-permute-done.1.far_ref
  20.3 5.3 %shard_map.326 = (f32[1600,512]{1,0:T(8,128)}, bf16[1600,512]{1,0:T(8,128)(2,1)S(1)}, bf16[1024,512]{1,0:T(8,128)(2,1)}, f32[24,2048]{1,0:T(8,128)S(1)}, f32[1024,128]{1,0:T(8,128)}) custom-call(s32[4]{0:T(128)S(1)} %copy-done.25, bf16[1600,1024]{1,0:T(8,128)(2,1)S(1)} %get-tuple-element.111.hat_ref.refs_2_, bf16[512,512]{1,0:T(8,128)(2,1)S(1)} %copy-done.17, ...), custom_call_target="tpu_custom_call" | custom-call | flops 1 | bytes 1 | tf_op jit(solution)/shard_map/pallas_call | solution.py:353
  25.6 3.4 %shard_map.328.position_ref.refs_0_.after = f32[4,112,512]{2,1,0:T(8,128)S(1)} custom-call(f32[24,2048]{1,0:T(8,128)S(1)} %get-tuple-element.114.params_ref), custom_call_target="tpu_custom_call" | custom-call | flops 1 | bytes 1 | tf_op jit(solution)/shard_map/pallas_call | solution.py:898
  29.0 1.1 collective-permute-done.3.near_ref.refs_1_
  30.2 0.6 shard_map.332
  30.8 1.8 collective-permute-start.5
  32.6 1.9 collective-permute-done.4.far_ref
  34.5 12.5 %shard_map.329 = (bf16[16,128,1536]{2,1,0:T(8,128)(2,1)}, bf16[16,4,112,512]{3,2,1,0:T(8,128)(2,1)}, bf16[1600,512]{1,0:T(8,128)(2,1)}, bf16[16,112,512]{2,1,0:T...) custom-call(s32[4]{0:T(128)S(1)} %copy-done.25, ...), custom_call_target="tpu_custom_call" | custom-call | flops 1 | bytes 1 | tf_op jit(solution)/shard_map/pallas_call | solution.py:440
  47.1 12.4 %shard_map.330 = (f32[1600,512]{1,0:T(8,128)S(1)}, f32[1600,512]{1,0:T(8,128)S(1)}, f32[1600,512]{1,0:T(8,128)S(1)}, bf16[1600,512]{1,0:T(8,128)(2,1)S(1)}, bf16...) custom-call(s32[4]{0:T(128)S(1)} %copy-done.25, ...), custom_call_target="tpu_custom_call" | custom-call | flops 1 | bytes 1 | tf_op jit(solution)/shard_map/pallas_call | solution.py:548
  60.1 6.9 %shard_map.331 = (f32[1600,512]{1,0:T(8,128)S(1)}, f32[1600,512]{1,0:T(8,128)S(1)}, bf16[1024,512]{1,0:T(8,128)(2,1)S(1)}, f32[8,512]{1,0:T(8,128)S(1)}) custom-call(s32[4]{0:T(128)S(1)} %copy-done.25, bf16[1600,512]{1,0:T(8,128)(2,1)S(1)} %get-tuple-element.119.second_ref, ...), custom_call_target="tpu_custom_call", output_to_operand_aliasing={{0}: (4, {}), {1}: (5, {})} | custom-call | flops 999999995904 | bytes 1 | tf_op jit(solution)/shard_map/pallas_call | solution.py:588
  67.0 7.6 %shard_map.333 = (f32[1600,512]{1,0:T(8,128)S(1)}, f32[1600,512]{1,0:T(8,128)S(1)}, bf16[1024,512]{1,0:T(8,128)(2,1)S(1)}, f32[8,512]{1,0:T(8,128)S(1)}) custom-call(s32[4]{0:T(128)S(1)} %copy-done.25, bf16[1600,512]{1,0:T(8,128)(2,1)S(1)} %get-tuple-element.119.second_ref, ...), custom_call_target="tpu_custom_call", output_to_operand_aliasing={{0}: (4, {}), {1}: (5, {})} | custom-call | flops 1 | bytes 1 | tf_op jit(solution)/shard_map/pallas_call | solution.py:588
  74.8 13.3 %shard_map.334 = (bf16[1600,512]{1,0:T(8,128)(2,1)}, f32[1600,512]{1,0:T(8,128)S(1)}, bf16[1600,512]{1,0:T(8,128)(2,1)S(1)}, bf16[1024,512]{1,0:T(8,128)(2,1)S(1...) custom-call(s32[4]{0:T(128)S(1)} %copy-done.25, ...), custom_call_target="tpu_custom_call" | custom-call | flops 1 | bytes 1 | tf_op jit(solution)/shard_map/pallas_call | solution.py:653
  88.6 1.2 collective-permute-done.9.refs_6_
  89.8 1.5 shard_map.335
  91.7 1.7 collective-permute-start.11
  93.4 18.9 %shard_map.336 = (bf16[1600,1536]{1,0:T(8,128)(2,1)S(1)}, bf16[1600,512]{1,0:T(8,128)(2,1)S(1)}, f32[1,1536]{1,0:T(1,128)S(1)}, f32[8,512]{1,0:T(8,128)S(1)}, f32[4,112,512]{2,1,0:T(8,128)S(1)}) custom-call(bf16[512,512]{1,0:T(8,128)(2,1)S(1)} %get-tuple-element.139.after, bf16[1600,512]{1,0:T(8,128)(2,1)S(1)} %get-tuple-element.140.attn_ref, ...), custom_call_target="tpu_custom_call" | custom-call | flops 1 | bytes 1 | tf_op jit(solution)/shard_map/pallas_call | solution.py:735
  112.4 2.3 %shard_map.337 = (bf16[320,512]{1,0:T(8,128)(2,1)S(1)}, bf16[256,512]{1,0:T(8,128)(2,1)S(1)}, bf16[576,512]{1,0:T(8,128)(2,1)S(1)}) custom-call(s32[4]{0:T(128)S(1)} %copy-done.25, f32[1,1536]{1,0:T(1,128)S(1)} %get-tuple-element.148.refs_0_.qkv_sums_ref, bf16[1024,512]{1,0:T(8,128)(2,1)S(1)} %get-tuple-element.133.refs_1_, ...), custom_call_target="tpu_custom_call" | custom-call | flops 1 | bytes 1 | tf_op jit(solution)/shard_map/pallas_call | solution.py:208
  115.1 1.7 collective-permute-start.13
  116.8 3.9 %shard_map.338 = (bf16[512,1600]{1,0:T(8,128)(2,1)}, bf16[1024,1600]{1,0:T(8,128)(2,1)}, bf16[1600,1024]{1,0:T(8,128)(2,1)}) custom-call(f32[4,112,512]{2,1,0:T(8,128)S(1)} %copy-done.3, bf16[1600,512]{1,0:T(8,128)(2,1)S(1)} %copy-done.9, bf16[1600,1024]{1,0:T(8,128)(2,1)S(1)} %copy-done.1), custom_call_target="tpu_custom_call" | custom-call | flops 1 | bytes 1 | tf_op jit(solution)/shard_map/pallas_call | solution.py:291
  120.8 1.5 copy-done.18
  122.2 5.1 %shard_map.339 = (bf16[768,512]{1,0:T(8,128)(2,1)}, bf16[768,512]{1,0:T(8,128)(2,1)S(1)}) custom-call(s32[4]{0:T(128)S(1)} %copy-done.25, bf16[256,512]{1,0:T(8,128)(2,1)S(1)} %get-tuple-element.150.after, bf16[512,1600]{1,0:T(8,128)(2,1)S(1)} %copy-done.18, bf16[1600,1536]{1,0:T(8,128)(2,1)S(1)} %get-tuple-element.152.stack_ref), custom_call_target="tpu_custom_call" | custom-call | flops 1 | bytes 1 | tf_op jit(solution)/shard_map/pallas_call | solution.py:779
  127.4 0.7 shard_map.340
  128.1 1.6 collective-permute-start.14
  129.7 2.6 %collective-permute-start.15 = (bf16[144,512]{1,0:T(8,128)(2,1)S(1)}, bf16[144,512]{1,0:T(8,128)(2,1)S(1)}, u32[]{:S(2)}, u32[]{:S(2)}) collective-permute-start(bf16[144,512]{1,0:T(8,128)(2,1)S(1)} %get-tuple-element.165), channel_id=1, source_target_pairs={{0,16},{2,18},{4,20},{6,22},{8,24},{10,26},{12,28},{14,30},{16,0},... | collective-permute-start | bytes 442376 | tf_op jit(solution)/shard_map/ppermute | solution.py:939
  132.6 5.1 %shard_map.341 = (bf16[544,512]{1,0:T(8,128)(2,1)}, bf16[544,512]{1,0:T(8,128)(2,1)S(1)}) custom-call(s32[4]{0:T(128)S(1)} %copy-done.25, bf16[144,512]{1,0:T(8,128)(2,1)S(1)} %get-tuple-element.156.after.refs_1_, bf16[1600,512]{1,0:T(8,128)(2,1)S(1)} %get-tuple-element.157.low_ref, bf16[1024,1600]{1,0:T(8,128)(2,1)S(1)} %copy-done.14, ...), custom_call_target="tpu_custom_call" | custom-call | flops 1 | bytes 1 | tf_op jit(solution)/shard_map/pallas_call | solution.py:830
  138.2 5.1 %collective-permute-done.15.refs_3_ = bf16[144,512]{1,0:T(8,128)(2,1)S(1)} collective-permute-done((bf16[144,512]{1,0:T(8,128)(2,1)S(1)}, bf16[144,512]{1,0:T(8,128)(2,1)S(1)}, u32[]{:S(2)}, u32[]{:S(2)}) %collective-permute-start.15) | collective-permute-done | bytes 147488 | tf_op jit(solution)/shard_map/ppermute | solution.py:939
  143.3 0.6 shard_map.342.refs_0_.refs_1_
  143.9 1.8 shard_map.343
  145.7 1.2 collective-permute-start.19
  146.9 0.9 collective-permute-start.20
  147.8 1.5 collective-permute-start.21
  149.3 2.1 %collective-permute-start.22 = (bf16[144,512]{1,0:T(8,128)(2,1)S(1)}, bf16[144,512]{1,0:T(8,128)(2,1)S(1)}, u32[]{:S(2)}, u32[]{:S(2)}) collective-permute-start(bf16[144,512]{1,0:T(8,128)(2,1)S(1)} %shard_map.342.refs_0_.refs_1_), channel_id=1, source_target_pairs={{0,8},{2,10},{4,12},{6,14},{8,0},{10,2},{12,4},{14,6},{16,24},{18,... | collective-permute-start | bytes 442376 | tf_op jit(solution)/shard_map/ppermute | solution.py:939
  151.4 1.0 collective-permute-start.23
  152.4 4.3 %collective-permute-done.19.refs_2_ = bf16[336,512]{1,0:T(8,128)(2,1)S(1)} collective-permute-done((bf16[336,512]{1,0:T(8,128)(2,1)S(1)}, bf16[336,512]{1,0:T(8,128)(2,1)S(1)}, u32[]{:S(2)}, u32[]{:S(2)}) %collective-permute-start.19) | collective-permute-done | bytes 344096 | tf_op jit(solution)/shard_map/ppermute | solution.py:951
  156.7 1.6 collective-permute-start.24
  158.3 2.7 %collective-permute-done.21.refs_4_ = bf16[336,512]{1,0:T(8,128)(2,1)S(1)} collective-permute-done((bf16[336,512]{1,0:T(8,128)(2,1)S(1)}, bf16[336,512]{1,0:T(8,128)(2,1)S(1)}, u32[]{:S(2)}, u32[]{:S(2)}) %collective-permute-start.21) | collective-permute-done | bytes 344096 | tf_op jit(solution)/shard_map/ppermute | solution.py:955
  161.0 0.7 shard_map.344
  161.7 3.7 %collective-permute-start.25 = (bf16[96,512]{1,0:T(8,128)(2,1)S(1)}, bf16[96,512]{1,0:T(8,128)(2,1)S(1)}, u32[]{:S(2)}, u32[]{:S(2)}) collective-permute-start(bf16[96,512]{1,0:T(8,128)(2,1)S(1)} %get-tuple-element.174), channel_id=1, source_target_pairs={{0,8},{2,10},{4,12},{6,14},{8,0},{10,2},{12,4},{14,6},{16,24},{18,... | collective-permute-start | bytes 294920 | tf_op jit(solution)/shard_map/ppermute | solution.py:939
  165.4 1.5 collective-permute-start.26
  166.9 1.4 collective-permute-start.27
  168.3 1.4 shard_map.345.refs_0_.refs_1_
  169.7 1.5 collective-permute-start.28
  171.2 2.4 %collective-permute-done.26.refs_3_ = bf16[96,512]{1,0:T(8,128)(2,1)S(1)} collective-permute-done((bf16[96,512]{1,0:T(8,128)(2,1)S(1)}, bf16[96,512]{1,0:T(8,128)(2,1)S(1)}, u32[]{:S(2)}, u32[]{:S(2)}) %collective-permute-start.26) | collective-permute-done | bytes 98336 | tf_op jit(solution)/shard_map/ppermute | solution.py:939
  174.3 1.7 collective-permute-start.29
  176.0 1.4 collective-permute-start.30
  177.4 1.3 collective-permute-start.31
  178.7 6.8 %shard_map.347 = (bf16[1600,1024]{1,0:T(8,128)(2,1)}, f32[8,128]{1,0:T(8,128)S(1)}) custom-call(bf16[80,512]{1,0:T(8,128)(2,1)S(1)} %get-tuple-element.177.after.refs_3_, bf16[1600,512]{1,0:T(8,128)(2,1)} %copy-done.7, bf16[1600,1024]{1,0:T(8,128)(2,1)} %get-tuple-element.178.hat_ref, f32[1600,1]{1,0:T(8,128)S(1)} %get-tuple-element.179.inverse_ref, ...), custom_call_target="tpu_custom_call" | custom-call | flops 1 | bytes 1 | tf_op jit(solution)/shard_map/pallas_call | solution.py:851
  186.6 1.6 collective-permute-start.34
  188.2 4.2 %shard_map.349 = (f32[1024,512]{1,0:T(8,128)}, f32[512,1024]{1,0:T(8,128)}, f32[256,512]{1,0:T(8,128)}, f32[8,128]{1,0:T(8,128)S(1)}) custom-call(s32[4]{0:T(128)S(1)} %copy-done.25, bf16[336,512]{1,0:T(8,128)(2,1)S(1)} %shard_map.348.refs_0_.refs_1_, bf16[576,512]{1,0:T(8,128)(2,1)} %shard_map.345.refs_0_.refs_1_, ...), custom_call_target="tpu_custom_call" | custom-call | flops 1 | bytes 1 | tf_op jit(solution)/shard_map/pallas_call | solution.py:208
  192.4 4.3 %collective-permute-done.34.refs_2_ = bf16[336,512]{1,0:T(8,128)(2,1)S(1)} collective-permute-done((bf16[336,512]{1,0:T(8,128)(2,1)S(1)}, bf16[336,512]{1,0:T(8,128)(2,1)S(1)}, u32[]{:S(2)}, u32[]{:S(2)}) %collective-permute-start.34) | collective-permute-done | bytes 344096 | tf_op jit(solution)/shard_map/ppermute | solution.py:939
  197.4 2.1 %collective-permute-done.35.other = bf16[672,512]{1,0:T(8,128)(2,1)S(1)} collective-permute-done((bf16[672,512]{1,0:T(8,128)(2,1)S(1)}, bf16[672,512]{1,0:T(8,128)(2,1)S(1)}, u32[]{:S(2)}, u32[]{:S(2)}) %collective-permute-start.35) | collective-permute-done | bytes 688160 | tf_op jit(solution)/shard_map/ppermute | solution.py:939
  199.5 2.3 %shard_map.351 = (f32[3,512,256]{2,1,0:T(8,128)}, f32[512,512]{1,0:T(8,128)}, f32[1,512]{1,0:T(1,128)}, f32[1,512]{1,0:T(1,128)}, f32[1,512]{1,0:T(1,128)}, /*in...) custom-call(s32[4]{0:T(128)S(1)} %copy-done.25, ...), custom_call_target="tpu_custom_call" | custom-call | flops 1 | bytes 1 | tf_op jit(solution)/shard_map/pallas_call | solution.py:177
  (114 shorter events, 6.6 us)
Async XLA Ops:
  0.7 15.4 %copy-start.15 = (bf16[3,512,256]{2,1,0:T(8,128)(2,1)S(1)}, bf16[3,512,256]{2,1,0:T(8,128)(2,1)}, u32[]{:S(2)}) copy-start(bf16[3,512,256]{2,1,0:T(8,128)(2,1)} %param.27) | copy-start | bytes 2359300
  1.8 5.6 %copy-start.23 = (s32[4]{0:T(128)}, s32[4]{0:T(128)S(1)}, u32[]{:S(2)}) copy-start(s32[4]{0:T(128)S(1)} %pad_add_fusion.place) | copy-start | bytes 52
  1.9 14.2 %copy-start.20 = (bf16[256,512]{1,0:T(8,128)(2,1)S(1)}, bf16[256,512]{1,0:T(8,128)(2,1)}, u32[]{:S(2)}) copy-start(bf16[256,512]{1,0:T(8,128)(2,1)} %proj_own.1) | copy-start | bytes 786436
  2.4 5.0 %copy-start.19 = (bf16[256,512]{1,0:T(8,128)(2,1)}, bf16[256,512]{1,0:T(8,128)(2,1)S(1)}, u32[]{:S(2)}) copy-start(bf16[256,512]{1,0:T(8,128)(2,1)S(1)} %shard_map.322.after) | copy-start | bytes 786436
  2.4 13.6 %collective-permute-start = (bf16[256,512]{1,0:T(8,128)(2,1)S(1)}, bf16[256,512]{1,0:T(8,128)(2,1)S(1)}, u32[]{:S(2)}, u32[]{:S(2)}) collective-permute-start(bf16[256,512]{1,0:T(8,128)(2,1)S(1)} %shard_map.322.after), channel_id=1, source_target_pairs={{0,1},{1,0},{2,3},{3,2},{4,5},{5,4},{6,7},{7,6},{8,9},{9,8},{10,11... | collective-permute-start | bytes 786440 | tf_op jit(solution)/shard_map/ppermute | solution.py:951
  9.5 6.5 %copy-start.25 = (s32[4]{0:T(128)S(1)}, s32[4]{0:T(128)}, u32[]{:S(2)}) copy-start(s32[4]{0:T(128)} %copy-done.23) | copy-start | bytes 52
  9.5 6.5 %collective-permute-start.2 = (bf16[32,512]{1,0:T(8,128)(2,1)}, bf16[32,512]{1,0:T(8,128)(2,1)S(1)}, u32[]{:S(2)}, u32[]{:S(2)}) collective-permute-start(bf16[32,512]{1,0:T(8,128)(2,1)} %get-tuple-element.109.refs_0_), channel_id=1, source_target_pairs={{0,1},{1,0},{2,3},{3,2},{4,5},{5,4},{6,7},{7,6},{8,9},{9,8},{10,11... | collective-permute-start | bytes 98312 | tf_op jit(solution)/shard_map/ppermute | solution.py:951
  16.0 9.6 %copy-start = (bf16[1600,1024]{1,0:T(8,128)(2,1)}, bf16[1600,1024]{1,0:T(8,128)(2,1)S(1)}, u32[]{:S(2)}) copy-start(bf16[1600,1024]{1,0:T(8,128)(2,1)S(1)} %get-tuple-element.111.hat_ref.refs_2_) | copy-start | bytes 9830404
  16.0 4.3 %copy-start.17 = (bf16[512,512]{1,0:T(8,128)(2,1)S(1)}, bf16[512,512]{1,0:T(8,128)(2,1)}, u32[]{:S(2)}) copy-start(bf16[512,512]{1,0:T(8,128)(2,1)} %own_ref.1) | copy-start | bytes 1572868
  16.0 4.3 %copy-start.26 = (f32[16,512]{1,0:T(8,128)S(1)}, f32[16,512]{1,0:T(8,128)}, u32[]{:S(2)}) copy-start(f32[16,512]{1,0:T(8,128)} %get-tuple-element.112.params_ref) | copy-start | bytes 98308
  16.7 13.5 %copy-start.10 = (bf16[512,1024]{1,0:T(8,128)(2,1)S(1)}, bf16[512,1024]{1,0:T(8,128)(2,1)}, u32[]{:S(2)}) copy-start(bf16[512,1024]{1,0:T(8,128)(2,1)} %refs_2_.1) | copy-start | bytes 3145732
  16.7 13.5 %copy-start.11 = (bf16[1024,512]{1,0:T(8,128)(2,1)S(1)}, bf16[1024,512]{1,0:T(8,128)(2,1)}, u32[]{:S(2)}) copy-start(bf16[1024,512]{1,0:T(8,128)(2,1)} %refs_3_.1) | copy-start | bytes 3145732
  16.7 13.4 %collective-permute-start.3 = (bf16[512,512]{1,0:T(8,128)(2,1)S(1)}, bf16[512,512]{1,0:T(8,128)(2,1)S(1)}, u32[]{:S(2)}, u32[]{:S(2)}) collective-permute-start(bf16[512,512]{1,0:T(8,128)(2,1)S(1)} %shard_map.327), channel_id=1, source_target_pairs={{0,1},{1,0},{2,3},{3,2},{4,5},{5,4},{6,7},{7,6},{8,9},{9,8},{10,11... | collective-permute-start | bytes 1572872 | tf_op jit(solution)/shard_map/ppermute | solution.py:951
  18.8 1.5 collective-permute-start.1
  25.6 21.4 %copy-start.8 = (bf16[1600,512]{1,0:T(8,128)(2,1)}, bf16[1600,512]{1,0:T(8,128)(2,1)S(1)}, u32[]{:S(2)}) copy-start(bf16[1600,512]{1,0:T(8,128)(2,1)S(1)} %get-tuple-element.113.first_ref) | copy-start | bytes 4915204
  25.6 49.2 %copy-start.4 = (f32[24,2048]{1,0:T(8,128)}, f32[24,2048]{1,0:T(8,128)S(1)}, u32[]{:S(2)}) copy-start(f32[24,2048]{1,0:T(8,128)S(1)} %get-tuple-element.114.params_ref) | copy-start | bytes 589828
  29.0 18.0 %copy-start.2 = (f32[4,112,512]{2,1,0:T(8,128)}, f32[4,112,512]{2,1,0:T(8,128)S(1)}, u32[]{:S(2)}) copy-start(f32[4,112,512]{2,1,0:T(8,128)S(1)} %shard_map.328.position_ref.refs_0_.after) | copy-start | bytes 2752516
  30.8 16.3 %copy-start.28 = (f32[512]{0:T(512)S(1)}, f32[512]{0:T(512)}, u32[]{:S(2)}) copy-start(f32[512]{0:T(512)} %param.32) | copy-start | bytes 6148
  30.8 16.3 %copy-start.32 = (f32[512]{0:T(512)S(1)}, f32[512]{0:T(512)}, u32[]{:S(2)}) copy-start(f32[512]{0:T(512)} %param.31) | copy-start | bytes 6148
  30.8 16.3 %copy-start.33 = (f32[512]{0:T(512)S(1)}, f32[512]{0:T(512)}, u32[]{:S(2)}) copy-start(f32[512]{0:T(512)} %param.33) | copy-start | bytes 6148
  30.8 28.9 %collective-permute-start.5 = (bf16[1024,512]{1,0:T(8,128)(2,1)S(1)}, bf16[1024,512]{1,0:T(8,128)(2,1)}, u32[]{:S(2)}, u32[]{:S(2)}) collective-permute-start(bf16[1024,512]{1,0:T(8,128)(2,1)S(1)} %shard_map.332), channel_id=1, source_target_pairs={{0,1},{1,0},{2,3},{3,2},{4,5},{5,4},{6,7},{7,6},{8,9},{9,8},{10,11... | collective-permute-start | bytes 3145736 | tf_op jit(solution)/shard_map/ppermute | solution.py:951
  32.6 1.9 collective-permute-start.4
  59.5 29.2 %collective-permute-start.7 = (bf16[1024,512]{1,0:T(8,128)(2,1)}, bf16[1024,512]{1,0:T(8,128)(2,1)}, u32[]{:S(2)}, u32[]{:S(2)}) collective-permute-start(bf16[1024,512]{1,0:T(8,128)(2,1)} %get-tuple-element.134), channel_id=1, source_target_pairs={{0,2},{2,0},{4,6},{6,4},{8,10},{10,8},{12,14},{14,12},{16,18},{18,... | collective-permute-start | bytes 3145736 | tf_op jit(solution)/shard_map/ppermute | solution.py:939
  59.7 7.3 %collective-permute-start.6 = (bf16[1024,512]{1,0:T(8,128)(2,1)}, bf16[1024,512]{1,0:T(8,128)(2,1)}, u32[]{:S(2)}, u32[]{:S(2)}) collective-permute-start(bf16[1024,512]{1,0:T(8,128)(2,1)} %collective-permute-done.5.near_ref), channel_id=1, source_target_pairs={{0,2},{2,0},{4,6},{6,4},{8,10},{10,8},{12,14},{14,12},{16,18},{18,... | collective-permute-start | bytes 3145736 | tf_op jit(solution)/shard_map/ppermute | solution.py:939
  67.0 7.9 %copy-start.31 = (f32[512]{0:T(512)S(1)}, f32[512]{0:T(512)}, u32[]{:S(2)}) copy-start(f32[512]{0:T(512)} %param.37) | copy-start | bytes 6148
  74.6 15.1 %collective-permute-start.8 = (bf16[1024,512]{1,0:T(8,128)(2,1)S(1)}, bf16[1024,512]{1,0:T(8,128)(2,1)S(1)}, u32[]{:S(2)}, u32[]{:S(2)}) collective-permute-start(bf16[1024,512]{1,0:T(8,128)(2,1)S(1)} %get-tuple-element.136), channel_id=1, source_target_pairs={{0,2},{2,0},{4,6},{6,4},{8,10},{10,8},{12,14},{14,12},{16,18},{18,... | collective-permute-start | bytes 3145736 | tf_op jit(solution)/shard_map/ppermute | solution.py:939
  88.2 5.2 %copy-start.30 = (f32[512]{0:T(512)S(1)}, f32[512]{0:T(512)}, u32[]{:S(2)}) copy-start(f32[512]{0:T(512)} %param.25) | copy-start | bytes 6148
  88.2 1.6 collective-permute-start.9
  91.3 21.1 %collective-permute-start.10 = (bf16[640,512]{1,0:T(8,128)(2,1)S(1)}, bf16[640,512]{1,0:T(8,128)(2,1)S(1)}, u32[]{:S(2)}, u32[]{:S(2)}) collective-permute-start(bf16[640,512]{1,0:T(8,128)(2,1)S(1)} %get-tuple-element.149), channel_id=1, source_target_pairs={{0,1},{1,0},{2,3},{3,2},{4,5},{5,4},{6,7},{7,6},{8,9},{9,8},{10,11... | collective-permute-start | bytes 1966088 | tf_op jit(solution)/shard_map/ppermute | solution.py:951
  91.7 20.7 %collective-permute-start.11 = (bf16[512,512]{1,0:T(8,128)(2,1)S(1)}, bf16[512,512]{1,0:T(8,128)(2,1)S(1)}, u32[]{:S(2)}, u32[]{:S(2)}) collective-permute-start(bf16[512,512]{1,0:T(8,128)(2,1)S(1)} %get-tuple-element.139.after), channel_id=1, source_target_pairs={{0,4},{2,6},{4,0},{6,2},{8,12},{10,14},{12,8},{14,10},{16,20},{18,... | collective-permute-start | bytes 1572872 | tf_op jit(solution)/shard_map/ppermute | solution.py:939
  112.3 20.2 %copy-start.7 = (bf16[1600,512]{1,0:T(8,128)(2,1)}, bf16[1600,512]{1,0:T(8,128)(2,1)S(1)}, u32[]{:S(2)}) copy-start(bf16[1600,512]{1,0:T(8,128)(2,1)S(1)} %get-tuple-element.157.low_ref) | copy-start | bytes 4915204
  112.3 4.5 %copy-start.1 = (bf16[1600,1024]{1,0:T(8,128)(2,1)S(1)}, bf16[1600,1024]{1,0:T(8,128)(2,1)}, u32[]{:S(2)}) copy-start(bf16[1600,1024]{1,0:T(8,128)(2,1)} %copy-done) | copy-start | bytes 9830404
  112.4 4.5 %copy-start.3 = (f32[4,112,512]{2,1,0:T(8,128)S(1)}, f32[4,112,512]{2,1,0:T(8,128)}, u32[]{:S(2)}) copy-start(f32[4,112,512]{2,1,0:T(8,128)} %copy-done.2) | copy-start | bytes 2752516
  112.4 4.5 %copy-start.9 = (bf16[1600,512]{1,0:T(8,128)(2,1)S(1)}, bf16[1600,512]{1,0:T(8,128)(2,1)}, u32[]{:S(2)}) copy-start(bf16[1600,512]{1,0:T(8,128)(2,1)} %copy-done.8) | copy-start | bytes 4915204
  114.7 12.7 %collective-permute-start.12 = (bf16[320,512]{1,0:T(8,128)(2,1)S(1)}, bf16[320,512]{1,0:T(8,128)(2,1)S(1)}, u32[]{:S(2)}, u32[]{:S(2)}) collective-permute-start(bf16[320,512]{1,0:T(8,128)(2,1)S(1)} %get-tuple-element.155), channel_id=1, source_target_pairs={{0,4},{2,6},{4,0},{6,2},{8,12},{10,14},{12,8},{14,10},{16,20},{18,... | collective-permute-start | bytes 983048 | tf_op jit(solution)/shard_map/ppermute | solution.py:939
  115.1 12.3 %collective-permute-start.13 = (bf16[256,512]{1,0:T(8,128)(2,1)S(1)}, bf16[256,512]{1,0:T(8,128)(2,1)S(1)}, u32[]{:S(2)}, u32[]{:S(2)}) collective-permute-start(bf16[256,512]{1,0:T(8,128)(2,1)S(1)} %get-tuple-element.150.after), channel_id=1, source_target_pairs={{0,1},{1,0},{2,3},{3,2},{4,5},{5,4},{6,7},{7,6},{8,9},{9,8},{10,11... | collective-permute-start | bytes 786440 | tf_op jit(solution)/shard_map/ppermute | solution.py:951
  127.4 5.2 %copy-start.5 = (f32[24,2048]{1,0:T(8,128)S(1)}, f32[24,2048]{1,0:T(8,128)}, u32[]{:S(2)}) copy-start(f32[24,2048]{1,0:T(8,128)} %copy-done.4) | copy-start | bytes 589828
  127.4 5.2 %copy-start.12 = (bf16[1024,512]{1,0:T(8,128)(2,1)S(1)}, bf16[1024,512]{1,0:T(8,128)(2,1)}, u32[]{:S(2)}) copy-start(bf16[1024,512]{1,0:T(8,128)(2,1)} %get-tuple-element.159.merge_ref) | copy-start | bytes 3145732
  127.4 5.2 %copy-start.14 = (bf16[1024,1600]{1,0:T(8,128)(2,1)S(1)}, bf16[1024,1600]{1,0:T(8,128)(2,1)}, u32[]{:S(2)}) copy-start(bf16[1024,1600]{1,0:T(8,128)(2,1)} %get-tuple-element.158.turned_ref) | copy-start | bytes 9830404
  127.4 5.2 %copy-start.22 = (f32[1024,128]{1,0:T(8,128)S(1)}, f32[1024,128]{1,0:T(8,128)}, u32[]{:S(2)}) copy-start(f32[1024,128]{1,0:T(8,128)} %get-tuple-element.160.column_ref) | copy-start | bytes 1572868
  128.1 10.1 %collective-permute-start.14 = (bf16[144,512]{1,0:T(8,128)(2,1)S(1)}, bf16[144,512]{1,0:T(8,128)(2,1)S(1)}, u32[]{:S(2)}, u32[]{:S(2)}) collective-permute-start(bf16[144,512]{1,0:T(8,128)(2,1)S(1)} %get-tuple-element.164), channel_id=1, source_target_pairs={{0,8},{2,10},{4,12},{6,14},{8,0},{10,2},{12,4},{14,6},{16,24},{18,... | collective-permute-start | bytes 442376 | tf_op jit(solution)/shard_map/ppermute | solution.py:939
  129.7 13.5 %collective-permute-start.15 = (bf16[144,512]{1,0:T(8,128)(2,1)S(1)}, bf16[144,512]{1,0:T(8,128)(2,1)S(1)}, u32[]{:S(2)}, u32[]{:S(2)}) collective-permute-start(bf16[144,512]{1,0:T(8,128)(2,1)S(1)} %get-tuple-element.165), channel_id=1, source_target_pairs={{0,16},{2,18},{4,20},{6,22},{8,24},{10,26},{12,28},{14,30},{16,0},... | collective-permute-start | bytes 442376 | tf_op jit(solution)/shard_map/ppermute | solution.py:939
  132.3 10.9 %collective-permute-start.16 = (bf16[144,512]{1,0:T(8,128)(2,1)S(1)}, bf16[144,512]{1,0:T(8,128)(2,1)S(1)}, u32[]{:S(2)}, u32[]{:S(2)}) collective-permute-start(bf16[144,512]{1,0:T(8,128)(2,1)S(1)} %get-tuple-element.166), channel_id=1, source_target_pairs={{0,24},{2,26},{4,28},{6,30},{8,16},{10,18},{12,20},{14,22},{16,8},... | collective-permute-start | bytes 442376 | tf_op jit(solution)/shard_map/ppermute | solution.py:939
  132.6 11.4 %collective-permute-start.18 = (bf16[768,512]{1,0:T(8,128)(2,1)}, bf16[768,512]{1,0:T(8,128)(2,1)}, u32[]{:S(2)}, u32[]{:S(2)}) collective-permute-start(bf16[768,512]{1,0:T(8,128)(2,1)} %get-tuple-element.153.refs_0_), channel_id=1, source_target_pairs={{0,2},{2,0},{4,6},{6,4},{8,10},{10,8},{12,14},{14,12},{16,18},{18,... | collective-permute-start | bytes 2359304 | tf_op jit(solution)/shard_map/ppermute | solution.py:939
  137.7 6.2 %collective-permute-start.17 = (bf16[544,512]{1,0:T(8,128)(2,1)}, bf16[544,512]{1,0:T(8,128)(2,1)}, u32[]{:S(2)}, u32[]{:S(2)}) collective-permute-start(bf16[544,512]{1,0:T(8,128)(2,1)} %get-tuple-element.163.refs_0_), channel_id=1, source_target_pairs={{0,2},{2,0},{4,6},{6,4},{8,10},{10,8},{12,14},{14,12},{16,18},{18,... | collective-permute-start | bytes 1671176 | tf_op jit(solution)/shard_map/ppermute | solution.py:939
  145.7 11.0 %collective-permute-start.19 = (bf16[336,512]{1,0:T(8,128)(2,1)S(1)}, bf16[336,512]{1,0:T(8,128)(2,1)S(1)}, u32[]{:S(2)}, u32[]{:S(2)}) collective-permute-start(bf16[336,512]{1,0:T(8,128)(2,1)S(1)} %get-tuple-element.169.refs_0_), channel_id=1, source_target_pairs={{0,1},{1,0},{2,3},{3,2},{4,5},{5,4},{6,7},{7,6},{8,9},{9,8},{10,11... | collective-permute-start | bytes 1032200 | tf_op jit(solution)/shard_map/ppermute | solution.py:951
  146.9 11.4 %collective-permute-start.20 = (bf16[336,512]{1,0:T(8,128)(2,1)S(1)}, bf16[336,512]{1,0:T(8,128)(2,1)S(1)}, u32[]{:S(2)}, u32[]{:S(2)}) collective-permute-start(bf16[336,512]{1,0:T(8,128)(2,1)S(1)} %get-tuple-element.171), channel_id=1, source_target_pairs={{0,4},{2,6},{4,0},{6,2},{8,12},{10,14},{12,8},{14,10},{16,20},{18,... | collective-permute-start | bytes 1032200 | tf_op jit(solution)/shard_map/ppermute | solution.py:939
  147.8 13.2 %collective-permute-start.21 = (bf16[336,512]{1,0:T(8,128)(2,1)S(1)}, bf16[336,512]{1,0:T(8,128)(2,1)S(1)}, u32[]{:S(2)}, u32[]{:S(2)}) collective-permute-start(bf16[336,512]{1,0:T(8,128)(2,1)S(1)} %get-tuple-element.172), channel_id=1, source_target_pairs={{0,5},{1,4},{2,7},{3,6},{4,1},{5,0},{6,3},{7,2},{8,13},{9,12},{10,... | collective-permute-start | bytes 1032200 | tf_op jit(solution)/shard_map/ppermute | solution.py:955
  149.3 17.7 %collective-permute-start.22 = (bf16[144,512]{1,0:T(8,128)(2,1)S(1)}, bf16[144,512]{1,0:T(8,128)(2,1)S(1)}, u32[]{:S(2)}, u32[]{:S(2)}) collective-permute-start(bf16[144,512]{1,0:T(8,128)(2,1)S(1)} %shard_map.342.refs_0_.refs_1_), channel_id=1, source_target_pairs={{0,8},{2,10},{4,12},{6,14},{8,0},{10,2},{12,4},{14,6},{16,24},{18,... | collective-permute-start | bytes 442376 | tf_op jit(solution)/shard_map/ppermute | solution.py:939
  151.4 16.9 %collective-permute-start.23 = (bf16[144,512]{1,0:T(8,128)(2,1)S(1)}, bf16[144,512]{1,0:T(8,128)(2,1)S(1)}, u32[]{:S(2)}, u32[]{:S(2)}) collective-permute-start(bf16[144,512]{1,0:T(8,128)(2,1)S(1)} %shard_map.342.refs_0_.refs_1_), channel_id=1, source_target_pairs={{0,16},{2,18},{4,20},{6,22},{8,24},{10,26},{12,28},{14,30},{16,0},... | collective-permute-start | bytes 442376 | tf_op jit(solution)/shard_map/ppermute | solution.py:939
  156.7 11.6 %collective-permute-start.24 = (bf16[144,512]{1,0:T(8,128)(2,1)S(1)}, bf16[144,512]{1,0:T(8,128)(2,1)S(1)}, u32[]{:S(2)}, u32[]{:S(2)}) collective-permute-start(bf16[144,512]{1,0:T(8,128)(2,1)S(1)} %shard_map.342.refs_0_.refs_1_), channel_id=1, source_target_pairs={{0,24},{2,26},{4,28},{6,30},{8,16},{10,18},{12,20},{14,22},{16,8},... | collective-permute-start | bytes 442376 | tf_op jit(solution)/shard_map/ppermute | solution.py:939
  161.7 9.5 %collective-permute-start.25 = (bf16[96,512]{1,0:T(8,128)(2,1)S(1)}, bf16[96,512]{1,0:T(8,128)(2,1)S(1)}, u32[]{:S(2)}, u32[]{:S(2)}) collective-permute-start(bf16[96,512]{1,0:T(8,128)(2,1)S(1)} %get-tuple-element.174), channel_id=1, source_target_pairs={{0,8},{2,10},{4,12},{6,14},{8,0},{10,2},{12,4},{14,6},{16,24},{18,... | collective-permute-start | bytes 294920 | tf_op jit(solution)/shard_map/ppermute | solution.py:939
  165.4 8.2 %collective-permute-start.26 = (bf16[96,512]{1,0:T(8,128)(2,1)S(1)}, bf16[96,512]{1,0:T(8,128)(2,1)S(1)}, u32[]{:S(2)}, u32[]{:S(2)}) collective-permute-start(bf16[96,512]{1,0:T(8,128)(2,1)S(1)} %get-tuple-element.175), channel_id=1, source_target_pairs={{0,16},{2,18},{4,20},{6,22},{8,24},{10,26},{12,28},{14,30},{16,0},... | collective-permute-start | bytes 294920 | tf_op jit(solution)/shard_map/ppermute | solution.py:939
  166.9 6.7 %collective-permute-start.27 = (bf16[96,512]{1,0:T(8,128)(2,1)S(1)}, bf16[96,512]{1,0:T(8,128)(2,1)S(1)}, u32[]{:S(2)}, u32[]{:S(2)}) collective-permute-start(bf16[96,512]{1,0:T(8,128)(2,1)S(1)} %get-tuple-element.176), channel_id=1, source_target_pairs={{0,24},{2,26},{4,28},{6,30},{8,16},{10,18},{12,20},{14,22},{16,8},... | collective-permute-start | bytes 294920 | tf_op jit(solution)/shard_map/ppermute | solution.py:939
  169.7 15.8 %collective-permute-start.28 = (bf16[576,512]{1,0:T(8,128)(2,1)}, bf16[576,512]{1,0:T(8,128)(2,1)}, u32[]{:S(2)}, u32[]{:S(2)}) collective-permute-start(bf16[576,512]{1,0:T(8,128)(2,1)} %shard_map.345.refs_0_.refs_1_), channel_id=1, source_target_pairs={{0,4},{2,6},{4,0},{6,2},{8,12},{10,14},{12,8},{14,10},{16,20},{18,... | collective-permute-start | bytes 1769480 | tf_op jit(solution)/shard_map/ppermute | solution.py:939
  173.7 5.1 %copy-start.6 = (f32[24,2048]{1,0:T(8,128)S(1)}, f32[24,2048]{1,0:T(8,128)}, u32[]{:S(2)}) copy-start(f32[24,2048]{1,0:T(8,128)} %copy-done.4) | copy-start | bytes 589828
  173.7 5.1 %copy-start.13 = (bf16[1024,512]{1,0:T(8,128)(2,1)S(1)}, bf16[1024,512]{1,0:T(8,128)(2,1)}, u32[]{:S(2)}) copy-start(bf16[1024,512]{1,0:T(8,128)(2,1)} %get-tuple-element.159.merge_ref) | copy-start | bytes 3145732
  174.3 11.8 %collective-permute-start.29 = (bf16[80,512]{1,0:T(8,128)(2,1)S(1)}, bf16[80,512]{1,0:T(8,128)(2,1)S(1)}, u32[]{:S(2)}, u32[]{:S(2)}) collective-permute-start(bf16[80,512]{1,0:T(8,128)(2,1)S(1)} %get-tuple-element.177.after.refs_3_), channel_id=1, source_target_pairs={{0,8},{2,10},{4,12},{6,14},{8,0},{10,2},{12,4},{14,6},{16,24},{18,... | collective-permute-start | bytes 245768 | tf_op jit(solution)/shard_map/ppermute | solution.py:939
  176.0 10.1 %collective-permute-start.30 = (bf16[80,512]{1,0:T(8,128)(2,1)S(1)}, bf16[80,512]{1,0:T(8,128)(2,1)S(1)}, u32[]{:S(2)}, u32[]{:S(2)}) collective-permute-start(bf16[80,512]{1,0:T(8,128)(2,1)S(1)} %get-tuple-element.177.after.refs_3_), channel_id=1, source_target_pairs={{0,16},{2,18},{4,20},{6,22},{8,24},{10,26},{12,28},{14,30},{16,0},... | collective-permute-start | bytes 245768 | tf_op jit(solution)/shard_map/ppermute | solution.py:939
  177.4 8.7 %collective-permute-start.31 = (bf16[80,512]{1,0:T(8,128)(2,1)S(1)}, bf16[80,512]{1,0:T(8,128)(2,1)S(1)}, u32[]{:S(2)}, u32[]{:S(2)}) collective-permute-start(bf16[80,512]{1,0:T(8,128)(2,1)S(1)} %get-tuple-element.177.after.refs_3_), channel_id=1, source_target_pairs={{0,24},{2,26},{4,28},{6,30},{8,16},{10,18},{12,20},{14,22},{16,8},... | collective-permute-start | bytes 245768 | tf_op jit(solution)/shard_map/ppermute | solution.py:939
  178.7 9.5 %collective-permute-start.32 = (bf16[576,512]{1,0:T(8,128)(2,1)}, bf16[576,512]{1,0:T(8,128)(2,1)}, u32[]{:S(2)}, u32[]{:S(2)}) collective-permute-start(bf16[576,512]{1,0:T(8,128)(2,1)} %shard_map.345.refs_0_.refs_1_), channel_id=1, source_target_pairs={{0,2},{2,0},{4,6},{6,4},{8,10},{10,8},{12,14},{14,12},{16,18},{18,... | collective-permute-start | bytes 1769480 | tf_op jit(solution)/shard_map/ppermute | solution.py:939
  185.6 2.7 %collective-permute-start.33 = (bf16[576,512]{1,0:T(8,128)(2,1)}, bf16[576,512]{1,0:T(8,128)(2,1)}, u32[]{:S(2)}, u32[]{:S(2)}) collective-permute-start(bf16[576,512]{1,0:T(8,128)(2,1)} %collective-permute-done.28.refs_1_.refs_2_), channel_id=1, source_target_pairs={{0,2},{2,0},{4,6},{6,4},{8,10},{10,8},{12,14},{14,12},{16,18},{18,... | collective-permute-start | bytes 1769480 | tf_op jit(solution)/shard_map/ppermute | solution.py:939
  186.6 10.1 %collective-permute-start.34 = (bf16[336,512]{1,0:T(8,128)(2,1)S(1)}, bf16[336,512]{1,0:T(8,128)(2,1)S(1)}, u32[]{:S(2)}, u32[]{:S(2)}) collective-permute-start(bf16[336,512]{1,0:T(8,128)(2,1)S(1)} %shard_map.348.refs_0_.refs_1_), channel_id=1, source_target_pairs={{0,4},{2,6},{4,0},{6,2},{8,12},{10,14},{12,8},{14,10},{16,20},{18,... | collective-permute-start | bytes 1032200 | tf_op jit(solution)/shard_map/ppermute | solution.py:939
  197.3 2.2 %collective-permute-start.35 = (bf16[672,512]{1,0:T(8,128)(2,1)S(1)}, bf16[672,512]{1,0:T(8,128)(2,1)S(1)}, u32[]{:S(2)}, u32[]{:S(2)}) collective-permute-start(bf16[672,512]{1,0:T(8,128)(2,1)S(1)} %shard_map.350.mine), channel_id=1, source_target_pairs={{0,2},{2,0},{4,6},{6,4},{8,10},{10,8},{12,14},{14,12},{16,18},{18,... | collective-permute-start | bytes 2064392 | tf_op jit(solution)/shard_map/ppermute | solution.py:939
  (7 other events, 13.6 us)
where the time goes:
time: 205 us; the launch traced here: 202 us
  Pallas kernels  127 us (62%)
  starting transfers between devices  40.3 us (20%)
  waiting for transfers between devices  26.7 us (13%)
  local copies, waits for them, and re-layouts  6.21 us (3%)
    ppermute x28, starting transfers between devices, to(): lax.ppermute(array, 'rows', [(i, i ^ bits) for i in range(self.rows_size)])  28.6 us
    pallas_call x1, Pallas kernels, attend_back(): kernel_call(attend_back_body, (count // ROWS,), [ANYWHERE, RESIDENT, by_w...  18.9 us
    ppermute x28, waiting for transfers between devices, to(): lax.ppermute(array, 'rows', [(i, i ^ bits) for i in range(self.rows_size)])  18.5 us
    pallas_call x14, Pallas kernels, plain_call_after(): pl.pallas_call(without_after, in_specs=[SCALARS] + [pl.BlockSpec(memory_s...  17 us
    pallas_call x2, Pallas kernels, feed_middle(): pl.pallas_call(partial(feed_middle_body, own), in_specs=[SCALARS] + [RESI...  14.5 us
    pallas_call x1, Pallas kernels, feed_near(): kernel_call(feed_near_body, (blocks + 1,), [SCALARS] + [RESIDENT] * 9 + [...  13.3 us
    pallas_call x1, Pallas kernels, attend(): kernel_call(attend_body, (count // ROWS,), [SCALARS, RESIDENT, RESIDENT,...  12.5 us
    pallas_call x1, Pallas kernels, feed_own(): kernel_call(feed_own_body, (blocks + 1,), [SCALARS, taken(D), taken(D), t...  12.4 us
  transfers between devices with their start and end apart: 36, of which 10 were waited for; matrix products, arithmetic and copies ran while one was open for 1% of the time, Pallas kernels for 57%

commit v1 on v0

--- a/solution.py
+++ b/solution.py
@@ -137,22 +137,39 @@
     )
 
 
-def pack_merge_body(place, merge_ref, out_ref):
-    out_ref[...] = merge_ref[pl.ds(pl.multiple_of(256 * place[0], 256), 256), :]
+def pack_merge_body(place, merge_ref, out_ref, sem):
+    half = pl.ds(pl.multiple_of(256 * place[0], 256), 256)
+    copy = pltpu.make_async_copy(merge_ref.at[half, :], out_ref, sem)
+    copy.start()
+    copy.wait()
+
+
+def pack_merge(place, merge):
+    return pl.pallas_call(
+        pack_merge_body,
+        in_specs=[SCALARS, ANYWHERE],
+        out_specs=RESIDENT,
+        out_shape=pltpu.VMEM((256, D), bf16),
+        scratch_shapes=[pltpu.SemaphoreType.DMA],
+        cost_estimate=COST,
+    )(place, in_hbm(merge))
 
 
 def pack_params_body(
-    place, after, merge_ref, qv_ref, up_bias_ref, table_ref, params_ref, out_ref, merge_s, qv_s, up_bias_s, table_s, sems
+    place, after, gain_ref, bias_ref, qv_ref, up_bias_ref, table_ref,
+    params_ref, out_ref, gain_s, bias_s, qv_s, up_bias_s, table_s, sems,
 ):
-    pairs = ((merge_ref, merge_s), (qv_ref, qv_s), (up_bias_ref, up_bias_s), (table_ref, table_s))
+    pairs = (
+        (gain_ref, gain_s), (bias_ref, bias_s), (qv_ref, qv_s), (up_bias_ref, up_bias_s), (table_ref, table_s)
+    )
     copies = [pltpu.make_async_copy(source, target, sems.at[index]) for index, (source, target) in enumerate(pairs)]
     for copy in copies:
         copy.start()
     params_ref[...] = jnp.zeros_like(params_ref)
     for copy in copies:
         copy.wait()
-    params_ref[0:1, :] = merge_s[:, 0:512]
-    params_ref[1:2, :] = merge_s[:, 512:1024]
+    params_ref[0:1, :] = gain_s[...].astype(f32).reshape(1, D)
+    params_ref[1:2, :] = bias_s[...].astype(f32).reshape(1, D)
     params_ref[2:3, 0:256] = qv_s[0:1, :]
     params_ref[2:3, 256:512] = qv_s[1:2, :]
     params_ref[3:4, :] = up_bias_s[:, 0:512]
@@ -161,14 +178,14 @@
     out_ref[...] = split(params_ref[...])
 
 
-def pack_params(place, after, merge, qv, up_bias, table):
-    operands = [in_hbm(array) for array in (merge, qv, up_bias, table)]
+def pack_params(place, after, *operands):
+    operands = [in_hbm(array) for array in operands]
     return pl.pallas_call(
         pack_params_body,
-        in_specs=[SCALARS] + [ANYWHERE] * 5,
+        in_specs=[SCALARS] + [ANYWHERE] * 6,
         out_specs=[RESIDENT] * 2,
-        out_shape=[shape_of((PARAMS, D), f32), shape_of((2 * PARAMS, D), bf16)],
-        scratch_shapes=[pltpu.VMEM(array.shape, f32) for array in operands] + [pltpu.SemaphoreType.DMA((4,))],
+        out_shape=[pltpu.VMEM((PARAMS, D), f32), pltpu.VMEM((2 * PARAMS, D), bf16)],
+        scratch_shapes=[pltpu.VMEM(array.shape, array.dtype) for array in operands] + [pltpu.SemaphoreType.DMA((5,))],
         cost_estimate=COST,
     )(place, after, *operands)
 
@@ -185,12 +202,33 @@
     )(*operands)
 
 
-def pack_qkv_body(place, qkv_ref, proj_ref, out):
+def pack_qkv_body(place, qkv_ref, proj_ref, *refs):
+    out, qkv_s, proj_s, sems = refs[-4:]
     core = place[0]
+    copies = [
+        pltpu.make_async_copy(qkv_ref.at[pl.ds(pl.multiple_of(768 * core, 256), 768), :], qkv_s, sems.at[0]),
+        pltpu.make_async_copy(proj_ref.at[pl.ds(pl.multiple_of(128 * core, 128), 128), :], proj_s, sems.at[1]),
+    ]
+    for copy in copies:
+        copy.start()
+    for copy in copies:
+        copy.wait()
     for side in range(2):
-        rows = pl.ds(pl.multiple_of(768 * core + 384 * side, 128), 384)
-        out[0:384, 256 * side : 256 * side + 256] = qkv_ref[rows, :]
-    out[384:512, :] = proj_ref[pl.ds(pl.multiple_of(128 * core, 128), 128), :]
+        out[0:384, 256 * side : 256 * side + 256] = qkv_s[384 * side : 384 * side + 384, :]
+    out[384:512, :] = proj_s[...]
+
+
+def pack_qkv(place, after, qkv, proj):
+    return pl.pallas_call(
+        pack_qkv_body,
+        in_specs=[SCALARS] + [ANYWHERE] * (2 + len(after)),
+        out_specs=RESIDENT,
+        out_shape=pltpu.VMEM((QKV_PACK + PROJ_PACK, D), bf16),
+        scratch_shapes=[
+            pltpu.VMEM((768, 256), bf16), pltpu.VMEM((128, D), bf16), pltpu.SemaphoreType.DMA((2,)),
+        ],
+        cost_estimate=COST,
+    )(place, in_hbm(qkv), in_hbm(proj), *after)
 
 
 def pack_feed_body(place, up_ref, down_ref, out):
@@ -216,7 +254,26 @@
     )(place, *after, *operands)
 
 
-def masks_body(place, window_ref, mask_ref, live_ref, stage):
+def nothing(array_ref, *refs):
+    pass
+
+
+def gate(array, *after):
+    return pl.pallas_call(
+        nothing,
+        in_specs=[RESIDENT] + [ANYWHERE] * len(after),
+        out_specs=RESIDENT,
+        out_shape=pltpu.VMEM(array.shape, array.dtype),
+        input_output_aliases={0: 0},
+        cost_estimate=COST,
+    )(array, *after)
+
+
+def masks_body(place, window_in, mask_ref, live_ref, stage, window_s, sem):
+    copy = pltpu.make_async_copy(window_in, window_s, sem)
+    copy.start()
+    copy.wait()
+    window_ref = window_s[...].reshape(1, window_s.shape[0])
     windows = mask_ref.shape[0]
     shards = window_ref.shape[1] // (windows * AREA)
     stage[...] = jnp.zeros_like(stage)
@@ -233,19 +290,21 @@
     added = jnp.where(keep, 0.0, MASKED_SCORE)
     for window in range(windows):
         mask_ref[window] = added[window : window + 1, :]
-        live_ref[AREA * window : AREA * (window + 1), :] = jnp.broadcast_to(live[window : window + 1, :], (AREA, 1))
+        live_ref[window] = jnp.broadcast_to(live[window : window + 1, :], (1, QUERIES))
 
 
 def masks_of(place, after, window_mask, count):
     windows = count // AREA
-    return plain_call_after(
-        masks_body,
-        [shape_of((windows, 1, QUERIES), f32), shape_of((count, 1), f32)],
-        place,
-        after,
-        (window_mask[None],),
-        scratch=[pltpu.VMEM((windows, QUERIES), jnp.int32)],
-    )
+    return pl.pallas_call(
+        lambda place, after, *refs: masks_body(place, *refs),
+        in_specs=[SCALARS, ANYWHERE, ANYWHERE],
+        out_specs=[RESIDENT] * 2,
+        out_shape=[pltpu.VMEM((windows, 1, QUERIES), f32)] * 2,
+        scratch_shapes=[
+            pltpu.VMEM((windows, QUERIES), jnp.int32), pltpu.VMEM(window_mask.shape, jnp.int32), pltpu.SemaphoreType.DMA,
+        ],
+        cost_estimate=COST,
+    )(place, after, in_hbm(window_mask))
 
 
 def section_norm_body(after, rows_ref, hat_ref, inverse_ref, rows_s, sems):
@@ -276,39 +335,13 @@
     )(after, in_hbm(rows))
 
 
-def turn_body(after, first_ref, hat_ref, first_out, hat_out, hat_copy):
-    columns = first_out.shape[0]
-    first_out[...] = first_ref[:, pl.ds(pl.multiple_of(columns * pl.program_id(0), 128), columns)].T
-    columns = hat_out.shape[0]
-    hat = hat_ref[:, pl.ds(pl.multiple_of(columns * pl.program_id(0), 128), columns)]
-    hat_out[...] = hat.T
-    hat_copy[...] = hat
-
-
-def turn(after, first, hat):
-    count = hat.shape[0]
-    steps = 4
-    return kernel_call(
-        turn_body,
-        (steps,),
-        [ANYWHERE, RESIDENT, RESIDENT],
-        [
-            pl.BlockSpec((D // steps, count), lambda i: (i, 0)),
-            pl.BlockSpec((MERGE_IN // steps, count), lambda i: (i, 0)),
-            pl.BlockSpec((count, MERGE_IN // steps), lambda i: (0, i)),
-        ],
-        [pltpu.HBM((D, count), bf16), pltpu.HBM((MERGE_IN, count), bf16), pltpu.HBM((count, MERGE_IN), bf16)],
-        room=16,
-    )(after, first, hat)
-
-
 def gain_rows(tp, params, others):
     return both_shards(tp, params[0:1], others[0:1], 1), both_shards(tp, params[1:2], others[1:2], 1)
 
 
 def merge_body(
-    place, hat_ref, own_ref, near_ref, far_ref, params_ref, others_ref, rows_ref,
-    merged_ref, first_ref, merge_ref, params_out_ref, column_ref,
+    place, hat_ref, own_ref, near_ref, far_ref, params_ref, others_ref, norm_gain, norm_bias,
+    merged_ref, first_ref, first_copy, merge_ref, params_out_ref, column_ref,
     merge_s, shift_s, gain_s,
 ):
 
@@ -345,27 +378,35 @@
     merged = mm(hat_ref[here, :] * gain_s[...], merge_s[...]) + shift_s[...]
     merged_ref[...] = merged
     hat, _ = normalize(merged)
-    first_ref[here, :] = (hat * rows_ref[0:1, :] + rows_ref[1:2, :]).astype(bf16)
-
-
-def merge_rows(place, hat, own, near, far, params, others, rows):
+    first = (hat * norm_gain[...] + norm_bias[...]).astype(bf16)
+    first_ref[here, :] = first
+    first_copy[...] = first
+
+
+def merge_rows(place, hat, own, near, far, params, others, gain, bias):
     count = hat.shape[0]
     return kernel_call(
         merge_body,
         (count // ROWS,),
         [
-            SCALARS, RESIDENT, RESIDENT, RESIDENT, RESIDENT, RESIDENT, RESIDENT, whole((2, D)),
+            SCALARS, RESIDENT, RESIDENT, RESIDENT, RESIDENT, RESIDENT, RESIDENT, RESIDENT, RESIDENT,
         ],
-        [by_rows(ROWS, D), RESIDENT, whole((MERGE_IN, D)), RESIDENT, whole((MERGE_IN, 128))],
         [
-            pltpu.HBM((count, D), f32), pltpu.VMEM((count, D), bf16), pltpu.HBM((MERGE_IN, D), bf16),
+            by_rows(ROWS, D), RESIDENT, by_rows(ROWS, D), whole((MERGE_IN, D)), RESIDENT,
+            whole((MERGE_IN, 128)),
+        ],
+        [
+            pltpu.HBM((count, D), f32), pltpu.VMEM((count, D), bf16), pltpu.HBM((count, D), bf16),
+            pltpu.HBM((MERGE_IN, D), bf16),
             shape_of((24, 2048), f32), pltpu.HBM((MERGE_IN, 128), f32),
         ],
-        [pltpu.VMEM((MERGE_IN, D), bf16), pltpu.VMEM((1, D), f32), pltpu.VMEM((1, MERGE_IN), bf16)],
+        [
+            pltpu.VMEM((MERGE_IN, D), bf16), pltpu.VMEM((1, D), f32), pltpu.VMEM((1, MERGE_IN), bf16),
+        ],
         flops=2 * count * D * MERGE_IN,
         moved=count * 10 * D + 4 * D * MERGE_IN,
         room=24,
-    )(place, hat, own, near, far, params, others, rows)
+    )(place, hat, own, near, far, params, others, gain, bias)
 
 
 def value_blocks(values, masks):
@@ -428,7 +469,7 @@
             out = mm(weights, jnp.concatenate(blocks, axis=0))
             inverse = 1.0 / out[:, QUAD:]
             both = out[:, :QUAD] * inverse
-            inverse_ref[w, :, columns] = inverse
+            inverse_ref[w, :, columns] = inverse.astype(bf16)
             padded_ref[w, :, columns] = both.astype(bf16)
             mixed[pl.ds(AREA * w, AREA), columns] = both[0:AREA]
     attended_ref[...] = mixed[...].astype(bf16)
@@ -449,7 +490,7 @@
         ],
         [
             pltpu.HBM((windows, QUERIES, 3 * D), bf16), pltpu.HBM((windows, QUADS, KEYS, LANES), bf16),
-            pltpu.HBM((count, D), bf16), pltpu.HBM((windows, KEYS, D), bf16), pltpu.HBM((windows, KEYS, D), f32),
+            pltpu.HBM((count, D), bf16), pltpu.HBM((windows, KEYS, D), bf16), pltpu.HBM((windows, KEYS, D), bf16),
             shape_of((3 * D, D), bf16),
         ],
         [pltpu.VMEM((ROWS + 32, D), f32), pltpu.VMEM((ROWS, D), f32)],
@@ -520,7 +561,11 @@
         residual_ref[here, :] = residual
         hat, _ = normalize(residual)
         second_ref[here, :] = (hat * norm_gain[...] + norm_bias[...]).astype(bf16)
-        branch = cotangent_ref[...].astype(f32) * live_ref[...]
+        row = lax.broadcasted_iota(jnp.int32, (ROWS, 1), 0)
+        live = live_ref[GROUP - 1, :, 0:1]
+        for window in range(GROUP - 2, -1, -1):
+            live = jnp.where(row < AREA * (window + 1), live_ref[window, :, 0:1], live)
+        branch = cotangent_ref[...].astype(f32) * live
         branch_ref[here, :] = branch.astype(bf16)
         sums_ref[7:8, :] += column_sum(branch)
 
@@ -549,7 +594,8 @@
         feed_own_body,
         (blocks + 1,),
         [
-            SCALARS, taken(D), taken(D), taken(D), taken(1), RESIDENT, RESIDENT, RESIDENT, RESIDENT, RESIDENT, RESIDENT, RESIDENT,
+            SCALARS, taken(D), taken(D), taken(D),
+            pl.BlockSpec((GROUP, 1, QUERIES), lambda i: (jnp.minimum(i, blocks - 1), 0, 0)), RESIDENT, RESIDENT, RESIDENT, RESIDENT, RESIDENT, RESIDENT, RESIDENT,
             RESIDENT, RESIDENT,
         ],
         [RESIDENT] * 9,
@@ -559,7 +605,7 @@
         [pltpu.VMEM((count, TILE), bf16)] * 2,
         room=OWN_ROOM,
     )(
-        place, in_hbm(attended), in_hbm(merged), in_hbm(cotangent), in_hbm(live), proj_bias, gain, bias, params, proj,
+        place, in_hbm(attended), in_hbm(merged), in_hbm(cotangent), live, proj_bias, gain, bias, params, proj,
         near, far, up, down,
     )
 
@@ -669,12 +715,19 @@
 
 def attend_back_body(
     after, attn_ref, qkv_in_ref, weights_ref, padded_ref, inverse_ref, proj_ref,
-    merged_ref, grad_residual_ref, qkv_ref, rows_ref,
-    stack_ref, low_ref, sums_ref, vectors_ref, position_ref,
-    stage, grads,
+    merged_ref, grad_residual_ref, qkv_ref, rows_ref, first_in,
+    stack_ref, low_ref, sums_ref, vectors_ref, position_ref, first_ref,
+    stage, grads, sem,
 ):
+    fetch = pltpu.make_async_copy(first_in, first_ref, sem)
+
+    @pl.when(pl.program_id(0) == pl.num_programs(0) - 1)
+    def _():
+        fetch.wait()
+
     @pl.when(pl.program_id(0) == 0)
     def _():
+        fetch.start()
         vectors_ref[...] = jnp.zeros_like(vectors_ref)
         sums_ref[...] = jnp.zeros_like(sums_ref)
         position_ref[...] = jnp.zeros_like(position_ref)
@@ -694,7 +747,7 @@
         for quad in range(QUADS):
             columns = slice(QUAD * quad, QUAD * (quad + 1))
             values = qkv_in_ref[w, :, 2 * D + QUAD * quad : 2 * D + QUAD * (quad + 1)]
-            grad = grad_attended[KEYS * w : KEYS * (w + 1), columns] * inverse_ref[w, :, columns]
+            grad = grad_attended[KEYS * w : KEYS * (w + 1), columns] * inverse_ref[w, :, columns].astype(f32)
             low = grad.astype(bf16)
             taken = (grad * padded_ref[w, :, columns].astype(f32)).astype(bf16)
             both = jnp.concatenate([low, -taken], axis=1)
@@ -730,7 +783,7 @@
     vectors_ref[2:3, :] += column_sum(low.astype(f32))
 
 
-def attend_back(after, attn, qkv_in, weights, padded, inverse, proj, merged, grad_residual, qkv, rows):
+def attend_back(after, attn, qkv_in, weights, padded, inverse, proj, merged, grad_residual, qkv, rows, first):
     count = attn.shape[0]
     return kernel_call(
         attend_back_body,
@@ -738,24 +791,36 @@
         [
             ANYWHERE, RESIDENT, by_windows((QUERIES, 3 * D)), by_windows((QUADS, KEYS, LANES)),
             by_windows((KEYS, D)), by_windows((KEYS, D)), RESIDENT, by_rows(ROWS, D), RESIDENT, RESIDENT, RESIDENT,
+            ANYWHERE,
         ],
-        [RESIDENT] * 5,
+        [RESIDENT] * 6,
         [
             pltpu.VMEM((count, 3 * D), bf16), pltpu.VMEM((count, D), bf16), shape_of((1, 3 * D), f32),
-            shape_of((8, D), f32), shape_of((QUADS, KEYS, LANES), f32),
+            shape_of((8, D), f32), shape_of((QUADS, KEYS, LANES), f32), pltpu.VMEM((count, D), bf16),
         ],
-        [pltpu.VMEM((ROWS + 32, D), f32), pltpu.VMEM((ROWS, 3 * D), f32)],
+        [pltpu.VMEM((ROWS + 32, D), f32), pltpu.VMEM((ROWS, 3 * D), f32), pltpu.SemaphoreType.DMA],
         room=AB_ROOM,
     )(
         after, attn, *[in_hbm(array) for array in (qkv_in, weights, padded, inverse)], proj, in_hbm(merged),
-        grad_residual, qkv, rows,
-    )
-
-
-def qkv_back_body(place, after, turned_ref, stack_ref, send_ref, keep_ref, qkv_s):
+        grad_residual, qkv, rows, in_hbm(first),
+    )
+
+
+def qkv_back_body(place, after, first_ref, stack_ref, hat_in, send_ref, keep_ref, hat_ref, qkv_s, turned_s, sem):
     part = pl.program_id(0)
+    fetch = pltpu.make_async_copy(hat_in, hat_ref, sem)
+
+    @pl.when(part == 0)
+    def _():
+        fetch.start()
+        turned_s[...] = first_ref[...].T
+
+    @pl.when(part == pl.num_programs(0) - 1)
+    def _():
+        fetch.wait()
+
     core, tp = place[0], place[3]
-    qkv_s[...] = mm(turned_ref[...], stack_ref[:, pl.ds(pl.multiple_of(D * part, D), D)]).astype(bf16)
+    qkv_s[...] = mm(turned_s[...], stack_ref[:, pl.ds(pl.multiple_of(D * part, D), D)]).astype(bf16)
     for target, half in ((send_ref, 1 - core), (keep_ref, core)):
         for other in range(2):
             shard = jnp.where(other == 0, tp, 1 - tp)
@@ -774,23 +839,21 @@
                 target[base + 256 : base + 384, 256:512] = block[128:256]
 
 
-def qkv_back(place, after, turned, stack):
+def qkv_back(place, after, first, stack, hat):
     count = stack.shape[0]
     return kernel_call(
         qkv_back_body,
         (3,),
-        [
-            SCALARS, ANYWHERE, RESIDENT, RESIDENT,
-        ],
-        [RESIDENT, RESIDENT],
-        [pltpu.VMEM((2 * QKV_PACK, D), bf16), pltpu.VMEM((2 * QKV_PACK, D), bf16)],
-        [pltpu.VMEM((D, D), bf16)],
+        [SCALARS, ANYWHERE, RESIDENT, RESIDENT, ANYWHERE],
+        [RESIDENT] * 3,
+        [pltpu.VMEM((2 * QKV_PACK, D), bf16)] * 2 + [pltpu.VMEM((count, MERGE_IN), bf16)],
+        [pltpu.VMEM((D, D), bf16), pltpu.VMEM((D, count), bf16), pltpu.SemaphoreType.DMA],
         room=12,
-    )(place, after, turned, stack)
+    )(place, after, first, stack, in_hbm(hat))
 
 
 def merge_back_body(
-    place, after, low_ref, turned_ref, merge_ref, params_ref, column_ref, feed_sums_ref, qkv_sums_ref, vectors_ref,
+    place, after, low_ref, hat_ref, merge_ref, params_ref, column_ref, feed_sums_ref, qkv_sums_ref, vectors_ref,
     position_ref,
     send_ref, keep_ref,
     fold_s, all_s, raw_s,
@@ -799,7 +862,7 @@
     total = vectors_ref[2:3, :]
     pair = jnp.concatenate([split(total), jnp.zeros((14, D), bf16)], axis=0)
     ones = jnp.ones((16, D), bf16)
-    raw_s[...] = mm(turned_ref[...], low_ref[...])
+    raw_s[...] = t_mm(hat_ref[...], low_ref[...])
     all_s[...] = jnp.zeros_like(all_s)
     all_s[0:2, :] = vectors_ref[0:2, :]
     all_s[2:6, :] = feed_sums_ref[4:8, :]
@@ -825,7 +888,7 @@
         target[2 * MERGE_PACK :, :] = split(all_s[pl.ds(pl.multiple_of(SUMS * half, SUMS), SUMS), :])
 
 
-def merge_back(place, after, low, turned, merge, params, column, feed_sums, sums, vectors, position):
+def merge_back(place, after, low, hat, merge, params, column, feed_sums, sums, vectors, position):
     pack = 2 * MERGE_PACK + 2 * SUMS
     return pl.pallas_call(
         merge_back_body,
@@ -837,7 +900,7 @@
         ],
         compiler_params=pltpu.CompilerParams(vmem_limit_bytes=20 * 1024 * 1024),
         cost_estimate=COST,
-    )(place, after, low, turned, merge, params, column, feed_sums, sums, vectors, position)
+    )(place, after, low, hat, merge, params, column, feed_sums, sums, vectors, position)
 
 
 def section_back_body(after, low_ref, hat_ref, inverse_ref, merge_ref, params_ref, out_ref, token_ref):
@@ -870,40 +933,43 @@
     return jnp.logical_and(lane == target, place < AREA).astype(f32)
 
 
-def expand_body(params_ref, place_ref, stage_s):
-    spread = spread_matrix().astype(bf16)
-    for head in range(HEADS):
-        stage = stage_s.at[head]
-        stage[96:KEYS, :] = jnp.zeros((KEYS - 96, 256), f32)
-        line = params_ref[8 + head : 9 + head, 0:384]
-        lines = jnp.concatenate(
-            [pltpu.roll(line, (384 - (WINDOW - 1) * (SIDE + 1) + x) % 384, 1) for x in range(WINDOW)]
-            + [jnp.zeros((6, 384), f32)],
-            axis=0,
-        )
-        for y in range(WINDOW):
-            moved = pltpu.roll(lines, SIDE * y, 1) if y else lines
-            stage[pl.ds(WINDOW * y, WINDOW), :] = moved[0:WINDOW, 0:256]
-        rows = stage[...]
+def expand_body(params_ref, hat_ref, place_ref, hat_copy, lines_s, out_s, sem):
+    save = pltpu.make_async_copy(hat_ref, hat_copy, sem)
+    save.start()
+    lane = lax.broadcasted_iota(jnp.int32, (384, QUERIES), 0)
+    patch = lax.broadcasted_iota(jnp.int32, (384, QUERIES), 1)
+    middle = (WINDOW - 1) * (SIDE + 1)
+    picked = jnp.logical_and(lane == middle - patch - (SIDE - WINDOW) * (patch // WINDOW), patch < AREA)
+    picked = picked.astype(f32).astype(bf16)
+    tables = params_ref[8 : 8 + HEADS, 0:384]
+    for place in range(AREA):
+        offset = SIDE * (place // WINDOW) + place % WINDOW
+        lines_s[HEADS * place : HEADS * (place + 1), :] = pltpu.roll(tables, (384 - offset) % 384, 1)
+    for begin in range(0, HEADS * AREA, ROWS):
+        here = slice(begin, begin + ROWS)
+        rows = lines_s[here, :]
         high = rows.astype(bf16)
         rest = rows - high.astype(f32)
-        middle = rest.astype(bf16)
-        low = (rest - middle.astype(f32)).astype(bf16)
-        block = mm_t(high, spread) + mm_t(middle, spread) + mm_t(low, spread)
-        block = jnp.concatenate([block, jnp.zeros((QUERIES - KEYS, QUERIES), f32)], axis=0).T[:KEYS]
-        place_ref[head // 4, :, QUERIES * (head % 4) : QUERIES * (head % 4 + 1)] = block
-
-
-def expand(params):
+        middle_part = rest.astype(bf16)
+        low = (rest - middle_part.astype(f32)).astype(bf16)
+        out_s[here, :] = mm(high, picked) + mm(middle_part, picked) + mm(low, picked)
+    for head in range(HEADS):
+        lanes = slice(QUERIES * (head % 4), QUERIES * (head % 4 + 1))
+        place_ref[head // 4, 0:AREA, lanes] = out_s[pl.ds(head, AREA, stride=HEADS), :]
+        place_ref[head // 4, AREA:KEYS, lanes] = jnp.zeros((KEYS - AREA, QUERIES), f32)
+    save.wait()
+
+
+def expand(params, hat):
     return kernel_call(
         expand_body,
         (1,),
-        [whole((24, 2048))],
-        whole((QUADS, KEYS, LANES)),
-        shape_of((QUADS, KEYS, LANES), f32),
-        [pltpu.VMEM((HEADS, KEYS, 256), f32)],
-        room=24,
-    )(params)
+        [RESIDENT, RESIDENT],
+        [RESIDENT, ANYWHERE],
+        [shape_of((QUADS, KEYS, LANES), f32), pltpu.HBM(hat.shape, bf16)],
+        [pltpu.VMEM((HEADS * AREA, 384), f32), pltpu.VMEM((HEADS * AREA, QUERIES), f32), pltpu.SemaphoreType.DMA],
+        room=16,
+    )(params, hat)
 
 
 def fold_place(place_ref, stage_s):
@@ -978,38 +1044,30 @@
     return ref.at[begin : begin + rows, :]
 
 
+FEED_BLOCKS = ((0, 256), (256, 64), (320, 256))
+
+
 def feed_first_body(
-    place, own_keep, own_got, other_keep, other_got, proj_keep, proj_got, down_y, up_x
-):
-    down_y[0:512, :] = added((other_keep, other_got), 0, 512).astype(bf16)
-    down_y[512:640, :] = added((proj_keep, proj_got), 128, 128).astype(bf16)
-    begin = 512 + 256 * (1 - place[1])
-    up_x[0:256, :] = added((own_keep, own_got), begin, 256).astype(bf16)
-    up_x[256:512, :] = added((other_keep, other_got), begin, 256).astype(bf16)
-
-
-def feed_second_body(
-    place, own_keep, own_got, other_keep, other_got, proj_keep, proj_got, down_shard, up_got, down_x, up_y, kept
+    place, own_keep, own_got, other_keep, other_got, proj_keep, proj_got, to_y, to_x, to_both, kept
 ):
     x = place[1]
-    for target, side in ((down_x, 1 - x), (kept, x)):
-        target[0:256, :] = added((own_keep, own_got, down_shard), 256 * side, 256).astype(bf16)
-        proj = (proj_keep, proj_got, part(down_shard, 512, 128))
-        target[256:320, :] = added(proj, 64 * side, 64).astype(bf16)
-    begin = 512 + 256 * x
-    up_y[...] = (added((other_keep, other_got), begin, 256) + up_got[256:512, :].astype(f32)).astype(bf16)
-    kept[320:576, :] = (added((own_keep, own_got), begin, 256) + up_got[0:256, :].astype(f32)).astype(bf16)
-
-
-def feed_third_body(place, kept, down_got, up_shard, *outs):
+    own, other = (own_keep, own_got), (other_keep, other_got)
+    for target, blocks, shard, side in (
+        (to_y, other, 1, x), (to_x, own, 0, 1 - x), (to_both, other, 1, 1 - x), (kept, own, 0, x)
+    ):
+        target[0:256, :] = added(blocks, 256 * side, 256).astype(bf16)
+        target[256:320, :] = added((proj_keep, proj_got), PROJ_PACK * shard + 64 * side, 64).astype(bf16)
+        target[320:576, :] = added(blocks, 512 + 256 * side, 256).astype(bf16)
+
+
+def feed_second_body(place, *refs):
+    blocks, outs = refs[:4], refs[4:]
     for step, out in enumerate(outs):
-        to = place[2] ^ step
         offset = 0
-        for ref, got, begin, size in ((kept, down_got, 0, 256), (kept, down_got, 256, 64), (kept, up_shard, 320, 256)):
+        for begin, size in FEED_BLOCKS:
             span = size // len(outs)
-            mine = part(ref, begin, size)
-            theirs = part(got, begin if got is down_got else 0, size)
-            out[offset : offset + span, :] = added((mine, theirs), to * span, span).astype(bf16)
+            to = begin + (place[2] ^ step) * span
+            out[offset : offset + span, :] = added(blocks, to, span).astype(bf16)
             offset += span
 
 
@@ -1023,23 +1081,28 @@
         refs[-1][rows * index : rows * (index + 1), :] = ref[...]
 
 
-def last_first_body(place, keep, got, qkv_keep, qkv_got, to_y, to_x, to_both, kept, sums_s):
+def qkv_first_body(place, keep, got, to_y, to_x, to_both, kept):
+    x = place[1]
+    for target, other, side in ((to_y, 1, x), (to_x, 0, 1 - x), (to_both, 1, 1 - x), (kept, 0, x)):
+        target[...] = added((keep, got), QKV_PACK * other + 192 * side, 192).astype(bf16)
+
+
+def merge_first_body(place, keep, got, to_y, to_x, to_both, kept, sums_s):
     x = place[1]
     sums_s[...] = joined(keep[512:544, :]) + joined(got[512:544, :])
     for target, other, side in ((to_y, 1, x), (to_x, 0, 1 - x), (to_both, 1, 1 - x), (kept, 0, x)):
-        target[0:192, :] = added((qkv_keep, qkv_got), QKV_PACK * other + 192 * side, 192).astype(bf16)
-        target[192:320, :] = added((keep, got), MERGE_PACK * other + 128 * side, 128).astype(bf16)
-        target[320:336, :] = split(sums_s[pl.ds(pl.multiple_of(8 * side, 8), 8), :])
-
-
-def last_second_body(place, *refs):
+        target[0:128, :] = added((keep, got), MERGE_PACK * other + 128 * side, 128).astype(bf16)
+        target[128:144, :] = split(sums_s[pl.ds(pl.multiple_of(8 * side, 8), 8), :])
+
+
+def last_second_body(place, qkv_sum, *refs):
     blocks, outs = refs[:4], refs[4:]
-    vectors = split(sum(joined(ref[320:336, :]) for ref in blocks))
+    vectors = split(sum(joined(ref[128:144, :]) for ref in blocks))
     wide, narrow = 192 // len(outs), 128 // len(outs)
     for step, out in enumerate(outs):
         to = place[2] ^ step
-        out[0:wide, :] = added(blocks, to * wide, wide).astype(bf16)
-        out[wide : wide + narrow, :] = added(blocks, 192 + to * narrow, narrow).astype(bf16)
+        out[0:wide, :] = added((qkv_sum,), to * wide, wide).astype(bf16)
+        out[wide : wide + narrow, :] = added(blocks, to * narrow, narrow).astype(bf16)
         out[wide + narrow :, :] = vectors
 
 
@@ -1092,12 +1155,10 @@
     )
 
 
-def last_unpack_body(along, place, mine, other, qkv_ref, merge_ref, *refs):
+def last_unpack_body(along, place, mine, beside, core_mine, core_beside, qkv_ref, merge_ref, *refs):
     vectors, stage, all_s = refs[:-2], refs[-2], refs[-1]
-    half = mine.shape[0] // 2
-    rows = half - 16
-    for target, ref in ((place[0], mine), (1 - place[0], other)):
-        near, far = ref.at[0:half, :], ref.at[half:, :]
+    rows = mine.shape[0] - 16
+    for target, near, far in ((place[0], mine, beside), (1 - place[0], core_mine, core_beside)):
         in_order(place, near, far, stage, (QKV_PACK, MERGE_PACK), along)
         for side, ref in ((place[1], near), (1 - place[1], far)):
             all_s[pl.ds(pl.multiple_of(SUMS * target + 8 * side, 8), 8), :] = joined(ref[rows:, :])
@@ -1125,11 +1186,11 @@
     refs[10][...] = sums[pl.ds(pl.multiple_of(16 + 8 * tp, 8), 8), 0 : SIDE * SIDE]
 
 
-def last_unpack(along, place, mine, other):
+def last_unpack(along, place, *parts):
     outs = plain_call(
         partial(last_unpack_body, along),
         [pltpu.HBM(shape, f32) if shape[-2] >= 128 else shape_of(shape, f32) for shape in [(3, D, D // 2), (MERGE_IN // 2, D)] + VECTORS],
-        (place, mine, other),
+        (place, *parts),
         scratch=[pltpu.VMEM((QKV_PACK + MERGE_PACK, D), bf16), pltpu.VMEM((2 * SUMS, D), f32)],
     )
     return outs[0], outs[1], outs[2:]
@@ -1229,18 +1290,16 @@
     ring = Ring(place, rows_size)
     if fast:
         flat_qkv = qkv_weight.reshape(3 * D, D // 2)
-        (merge_piece,) = plain_call(pack_merge_body, [shape_of((256, D), bf16)], (place, merge_weight))
+        merge_piece = pack_merge(place, merge_weight)
         merge_near = ring.y(merge_piece)
         params, piece = pack_params(
-            place, merge_piece, jnp.concatenate([merge_gain, merge_bias]).astype(f32)[None], qv_bias, up_bias[None], bias_table.T
+            place, merge_piece, merge_gain, merge_bias, qv_bias, up_bias[None], bias_table.T
         )
         others = ring.y(piece)
-        mask, live = masks_of(place, piece, window_mask, count)
-        hat, inverse = section_norm(mask, section_rows)
-        (qkv_piece,) = plain_call_after(
-            pack_qkv_body, [shape_of((QKV_PACK + PROJ_PACK, D), bf16)], place, (others, merge_near, hat), (flat_qkv, proj_weight)
-        )
+        mask, live = masks_of(place, params, window_mask, count)
+        qkv_piece = gate(pack_qkv(place, (mask,), flat_qkv, proj_weight), others, merge_near)
         qkv_near = ring.y(qkv_piece)
+        hat, inverse = section_norm(qkv_piece, section_rows)
         merge_far = ring.core(merge_near)
         kernel_place = place
     else:
@@ -1255,11 +1314,10 @@
         own_mask = lax.dynamic_slice_in_dim(window_mask, tp * count, count, 0)
         mask, live = masks_of(kernel_place, params, own_mask, count)
 
-    merged, first, merge_full, params, column = merge_rows(
-        kernel_place, hat, merge_weight, merge_near, merge_far, params, others, jnp.stack([norm1_gain, norm1_bias])
-    )
-    position = expand(params)
-    turned_first, turned_hat, hat = turn(position, first, hat)
+    merged, first, first_copy, merge_full, params, column = merge_rows(
+        kernel_place, hat, merge_weight, merge_near, merge_far, params, others, norm1_gain[None], norm1_bias[None]
+    )
+    position, hat = expand(params, hat)
     if fast:
         (feed_piece,) = plain_call_after(
             pack_feed_body, [shape_of((FEED_PACK, D), bf16)], place, (position, qkv_near), (up_weight, down_weight)
@@ -1289,65 +1347,64 @@
     if fast:
         own_got, other_got, proj_got = ring.core(own_send), ring.core(other_send), ring.core(proj_send)
         feed_keeps = (own_keep, own_got, other_keep, other_got, proj_keep, proj_got)
-        down_y, up_x = stage(feed_first_body, place, feed_sums, (640, 512), *feed_keeps)
-        down_shard, up_got = ring.y(down_y), ring.x(up_x)
-        after = up_x
-    stack, low, sums, vectors, position_grad = attend_back(
+        to_y, to_x, to_both, feed_kept = stage(feed_first_body, place, feed_sums, (576,) * 4, *feed_keeps)
+        feed_from = (ring.y(to_y), ring.x(to_x), ring.xy(to_both))
+        after = to_y
+    stack, low, sums, vectors, position_grad, first_near = attend_back(
         after, attn, qkv_rows, weights, padded, inverse_sums, proj_full, merged, grad_residual, qkv_full,
-        norm1_gain[None],
-    )
-    after = sums
-    if fast:
-        down_x, up_y, feed_kept = stage(
-            feed_second_body, place, sums, (320, 256, 576), *feed_keeps, down_shard, up_got
-        )
-        down_got, up_shard = ring.x(down_x), ring.y(up_y)
-        after = up_y
-    qkv_send, qkv_keep = qkv_back(kernel_place, after, turned_first, stack)
+        norm1_gain[None], first_copy,
+    )
+    qkv_send, qkv_keep, hat_near = qkv_back(kernel_place, sums, first_near, stack, hat)
     after = sums
     if fast:
         along = ring.along
         qkv_got = ring.core(qkv_send)
         span = 576 // along
         feed_parts = stage(
-            feed_third_body, place, qkv_send, (span,) * along, feed_kept, down_got, up_shard, cost=LONG
+            feed_second_body, place, qkv_send, (span,) * along, feed_kept, *feed_from, cost=LONG
         )
         feed_got = [ring.z(feed_parts[step], step) for step in range(1, along)]
-        after = feed_parts[0]
+        to_y, to_x, to_both, qkv_kept = stage(
+            qkv_first_body, place, feed_parts[0], (192,) * 4, qkv_keep, qkv_got
+        )
+        qkv_from = (ring.y(to_y), ring.x(to_x), ring.xy(to_both))
+        after = to_y
     merge_send, merge_keep = merge_back(
-        kernel_place, after, low, turned_hat, merge_full, params, column, feed_sums, sums, vectors, position_grad
+        kernel_place, after, low, hat_near, merge_full, params, column, feed_sums, sums, vectors, position_grad
     )
     if fast:
         merge_got = ring.core(merge_send)
         (feed_total,) = stage(total_body, place, merge_send, (span,), feed_parts[0], *feed_got, cost=LONG)
         feed_all = [feed_total] + [ring.z(feed_total, step) for step in range(1, along)]
-        to_y, to_x, to_both, last_kept = stage(
-            last_first_body, place, feed_total, (336,) * 4, merge_keep, merge_got, qkv_keep, qkv_got,
-            scratch=[pltpu.VMEM((SUMS, D), f32)],
+        (qkv_sum,) = stage(total_body, place, feed_total, (192,), qkv_kept, *qkv_from)
+        to_y, to_x, to_both, merge_kept = stage(
+            merge_first_body, place, qkv_sum, (144,) * 4, merge_keep, merge_got, scratch=[pltpu.VMEM((SUMS, D), f32)]
         )
         last_span = 320 // along
         last_parts = stage(
-            last_second_body, place, to_y, (last_span + 16,) * along,
-            last_kept, ring.y(to_y), ring.x(to_x), ring.xy(to_both),
+            last_second_body, place, to_y, (last_span + 16,) * along, qkv_sum,
+            merge_kept, ring.y(to_y), ring.x(to_x), ring.xy(to_both),
         )
         last_got = [ring.z(last_parts[step], step) for step in range(1, along)]
-        (feed_mine,) = stage(beside_body, place, last_parts[0], (span * along,), *feed_all)
+        section_grad, token = section_back(last_parts[0], low, hat, inverse, merge_full, params)
+        (feed_mine,) = stage(beside_body, place, token, (span * along,), *feed_all)
         feed_beside = ring.x(feed_mine)
         last_total, vectors = stage(
             merge_total_body, place, feed_mine, (last_span, 16), *([last_parts[0]] + last_got), cost=LONG
         )
         last_all = [last_total] + [ring.z(last_total, step) for step in range(1, along)]
-        section_grad, token = section_back(last_total, low, hat, inverse, merge_full, params)
         (last_near,) = stage(
-            last_beside_body, place, (token, feed_beside), (336,), vectors, *last_all, cost=LONG
+            last_beside_body, place, feed_beside, (336,), vectors, *last_all, cost=LONG
         )
         last_far = ring.x(last_near)
         feed_cores = ring.core(feed_mine), ring.core(feed_beside)
         down_grad, up_grad, proj_grad, token = feed_unpack(
             along, place, last_near, (feed_mine, feed_beside, *feed_cores)
         )
-        (last_half,) = stage(beside_body, place, token, (672,), last_near, last_far)
-        qkv_grad, merge_grad, vectors = last_unpack(along, place, last_half, ring.core(last_half))
+        (last_far,) = stage(beside_body, place, token, (336,), last_far)
+        qkv_grad, merge_grad, vectors = last_unpack(
+            along, place, last_near, last_far, ring.core(last_near), ring.core(last_far)
+        )
     else:
         section_grad, _ = section_back(low, low, hat, inverse, merge_full, params)
         down_grad, up_grad, qkv_grad, proj_grad, merge_grad, vectors = sum_plainly(

time: 205 us -> 196 us (0.956)
  waiting for transfers between devices: 26.7 us -> 22.8 us
  local copies, waits for them, and re-layouts: 6.21 us -> 2.63 us
    ppermute x28 -> x29, waiting for transfers between devices: 18.5 us -> 14.2 us  [to(): lax.ppermute(array, 'rows', [(i, i ^ bits) for i in range(self.rows_size)])]
    ppermute x1 -> x3, waiting for transfers between devices: 2.74 us -> 6.06 us  [xy(): return lax.ppermute(array, ('rows', 'tp'), pairs)]
    ppermute x7, waiting for transfers between devices: 5.45 us -> 2.57 us  [y(): return lax.ppermute(array, 'tp', [(0, 1), (1, 0)])]
    ppermute x28 -> x29, starting transfers between devices: 28.6 us -> 27 us  [to(): lax.ppermute(array, 'rows', [(i, i ^ bits) for i in range(self.rows_size)])]
    unnamed x70 -> x54, local copies, waits for them, and re-layouts: 4.12 us -> 2.63 us
    pallas_call x14 -> x13, Pallas kernels: 17 us -> 16.3 us  [plain_call_after(): pl.pallas_call(without_after, in_specs=[SCALARS] + [pl.BlockSpec(memory_s...]
    pallas_call x4 -> x7, Pallas kernels: 14.5 us -> 14.3 us  [the longest x1 5.77 us: qkv_back(): kernel_call(qkv_back_body, (3,), [SCALARS, ANYWHERE, RESIDENT, RESIDENT,...]
  transfers between devices with their start and end apart: 36 -> 39, of which waited for: 10 -> 12; matrix products, arithmetic and copies ran while one was open for 1% -> 0% of each run, Pallas kernels for 57% -> 61%
where the time goes in v1:
time: 196 us; the launch traced here: 193 us
  Pallas kernels  125 us (64%)
  starting transfers between devices  40.7 us (21%)
  waiting for transfers between devices  22.8 us (12%)
  local copies, waits for them, and re-layouts  2.63 us (1%)
    ppermute x29, starting transfers between devices, to(): lax.ppermute(array, 'rows', [(i, i ^ bits) for i in range(self.rows_size)])  27 us
    pallas_call x1, Pallas kernels, attend_back(): kernel_call(attend_back_body, (count // ROWS,), [ANYWHERE, RESIDENT, by_w...  18.6 us
    pallas_call x13, Pallas kernels, plain_call_after(): pl.pallas_call(without_after, in_specs=[SCALARS] + [pl.BlockSpec(memory_s...  16.3 us
    pallas_call x2, Pallas kernels, feed_middle(): pl.pallas_call(partial(feed_middle_body, own), in_specs=[SCALARS] + [RESI...  14.5 us
    ppermute x29, waiting for transfers between devices, to(): lax.ppermute(array, 'rows', [(i, i ^ bits) for i in range(self.rows_size)])  14.2 us
    pallas_call x1, Pallas kernels, feed_near(): kernel_call(feed_near_body, (blocks + 1,), [SCALARS] + [RESIDENT] * 9 + [...  13.1 us
    pallas_call x1, Pallas kernels, attend(): kernel_call(attend_body, (count // ROWS,), [SCALARS, RESIDENT, RESIDENT,...  12.5 us
    pallas_call x1, Pallas kernels, feed_own(): kernel_call(feed_own_body, (blocks + 1,), [SCALARS, taken(D), taken(D), t...  12.2 us
  transfers between devices with their start and end apart: 39, of which 12 were waited for; matrix products, arithmetic and copies ran while one was open for 0% of the time, Pallas kernels for 61%

profile of v1, /device:TPU:0, one launch (start us, length us, event | category | flops | bytes accessed | tf_op | source)
XLA Modules:
  0.0 192.9 jit_solution(12213280194325977412)
XLA Ops:
  1.2 1.6 shard_map.322.after
  2.9 3.0 %collective-permute-start.1 = (bf16[256,512]{1,0:T(8,128)(2,1)S(1)}, bf16[256,512]{1,0:T(8,128)(2,1)S(1)}, u32[]{:S(2)}, u32[]{:S(2)}) collective-permute-start(bf16[256,512]{1,0:T(8,128)(2,1)S(1)} %shard_map.322.after), channel_id=1, source_target_pairs={{0,1},{1,0},{2,3},{3,2},{4,5},{5,4},{6,7},{7,6},{8,9},{9,8},{10,11... | collective-permute-start | bytes 786440 | tf_op jit(solution)/shard_map/ppermute | solution.py:1017
  5.9 1.5 shard_map.323
  7.4 0.6 copy-done.13
  8.1 0.6 collective-permute-start
  8.7 1.6 shard_map.324
  10.3 0.6 copy-done.17
  10.9 1.9 shard_map.325.array_ref
  12.9 0.6 copy-done.15
  13.6 0.7 copy-done.9
  14.3 1.7 collective-permute-start.3
  16.0 3.0 %shard_map.327 = (bf16[1600,1024]{1,0:T(8,128)(2,1)S(1)}, f32[1600,1]{1,0:T(8,128)S(1)}) custom-call(bf16[512,512]{1,0:T(8,128)(2,1)S(1)} %shard_map.326.after, bf16[1600,1024]{1,0:T(8,128)(2,1)} %rows_ref.1), custom_call_target="tpu_custom_call" | custom-call | flops 1 | bytes 1 | tf_op jit(solution)/shard_map/pallas_call | solution.py:327
  19.1 6.0 %shard_map.328 = (f32[1600,512]{1,0:T(8,128)}, bf16[1600,512]{1,0:T(8,128)(2,1)S(1)}, bf16[1600,512]{1,0:T(8,128)(2,1)}, bf16[1024,512]{1,0:T(8,128)(2,1)}, f32[24,2048]{1,0:T(8,128)S(1)}, /*index=5*/f32[1024,128]{1,0:T(8,128)}) custom-call(s32[4]{0:T(128)S(1)} %copy-done.12, bf16[1600,1024]{1,0:T(8,128)(2,1)S(1)} %get-tuple-element.117.hat_ref, ...), custom_call_target="tpu_custom_call" | custom-call | flops 1 | bytes 1 | tf_op jit(solution)/shard_map/pallas_call | solution.py:388
  25.2 1.9 shard_map.329
  27.5 0.6 shard_map.333
  28.2 1.3 collective-permute-start.5
  29.5 1.9 collective-permute-done.4.far_ref
  31.4 12.5 %shard_map.330 = (bf16[16,128,1536]{2,1,0:T(8,128)(2,1)}, bf16[16,4,112,512]{3,2,1,0:T(8,128)(2,1)}, bf16[1600,512]{1,0:T(8,128)(2,1)}, bf16[16,112,512]{2,1,0:T...) custom-call(s32[4]{0:T(128)S(1)} %copy-done.12, ...), custom_call_target="tpu_custom_call" | custom-call | flops 1 | bytes 1 | tf_op jit(solution)/shard_map/pallas_call | solution.py:481
  43.9 12.2 %shard_map.331 = (f32[1600,512]{1,0:T(8,128)S(1)}, f32[1600,512]{1,0:T(8,128)S(1)}, f32[1600,512]{1,0:T(8,128)S(1)}, bf16[1600,512]{1,0:T(8,128)(2,1)S(1)}, bf16...) custom-call(s32[4]{0:T(128)S(1)} %copy-done.12, ...), custom_call_target="tpu_custom_call" | custom-call | flops 1 | bytes 1 | tf_op jit(solution)/shard_map/pallas_call | solution.py:593
  56.7 6.9 %shard_map.332 = (f32[1600,512]{1,0:T(8,128)S(1)}, f32[1600,512]{1,0:T(8,128)S(1)}, bf16[1024,512]{1,0:T(8,128)(2,1)S(1)}, f32[8,512]{1,0:T(8,128)S(1)}) custom-call(s32[4]{0:T(128)S(1)} %copy-done.12, bf16[1600,512]{1,0:T(8,128)(2,1)S(1)} %get-tuple-element.125.second_ref, ...), custom_call_target="tpu_custom_call", output_to_operand_aliasing={{0}: (4, {}), {1}: (5, {})} | custom-call | flops 999999995904 | bytes 1 | tf_op jit(solution)/shard_map/pallas_call | solution.py:634
  63.7 7.6 %shard_map.334 = (f32[1600,512]{1,0:T(8,128)S(1)}, f32[1600,512]{1,0:T(8,128)S(1)}, bf16[1024,512]{1,0:T(8,128)(2,1)S(1)}, f32[8,512]{1,0:T(8,128)S(1)}) custom-call(s32[4]{0:T(128)S(1)} %copy-done.12, bf16[1600,512]{1,0:T(8,128)(2,1)S(1)} %get-tuple-element.125.second_ref, ...), custom_call_target="tpu_custom_call", output_to_operand_aliasing={{0}: (4, {}), {1}: (5, {})} | custom-call | flops 1 | bytes 1 | tf_op jit(solution)/shard_map/pallas_call | solution.py:634
  71.5 13.1 %shard_map.335 = (bf16[1600,512]{1,0:T(8,128)(2,1)}, f32[1600,512]{1,0:T(8,128)S(1)}, bf16[1600,512]{1,0:T(8,128)(2,1)S(1)}, bf16[1024,512]{1,0:T(8,128)(2,1)S(1...) custom-call(s32[4]{0:T(128)S(1)} %copy-done.12, ...), custom_call_target="tpu_custom_call" | custom-call | flops 1 | bytes 1 | tf_op jit(solution)/shard_map/pallas_call | solution.py:699
  85.1 1.2 collective-permute-done.9.refs_6_
  86.2 1.8 shard_map.336
  88.0 1.6 collective-permute-start.11
  89.6 0.7 collective-permute-start.12
  90.3 1.3 collective-permute-start.10
  91.6 18.6 %shard_map.337 = (bf16[1600,1536]{1,0:T(8,128)(2,1)S(1)}, bf16[1600,512]{1,0:T(8,128)(2,1)S(1)}, f32[1,1536]{1,0:T(1,128)S(1)}, f32[8,512]{1,0:T(8,128)S(1)}, f3...) custom-call(bf16[576,512]{1,0:T(8,128)(2,1)S(1)} %get-tuple-element.145.after, ...), custom_call_target="tpu_custom_call" | custom-call | flops 1 | bytes 1 | tf_op jit(solution)/shard_map/pallas_call | solution.py:788
  110.2 5.8 %shard_map.338 = (bf16[768,512]{1,0:T(8,128)(2,1)}, bf16[768,512]{1,0:T(8,128)(2,1)S(1)}, bf16[1600,1024]{1,0:T(8,128)(2,1)S(1)}) custom-call(s32[4]{0:T(128)S(1)} %copy-done.12, f32[1,1536]{1,0:T(1,128)S(1)} %get-tuple-element.155.after.qkv_sums_ref, bf16[1600,512]{1,0:T(8,128)(2,1)S(1)} %get-tuple-element.156.first_ref, ...), custom_call_target="tpu_custom_call" | custom-call | flops 1 | bytes 1 | tf_op jit(solution)/shard_map/pallas_call | solution.py:844
  116.6 1.4 collective-permute-done.10.refs_2_
  118.0 0.8 shard_map.339
  118.8 1.6 collective-permute-start.14
  120.5 2.6 %collective-permute-start.15 = (bf16[144,512]{1,0:T(8,128)(2,1)S(1)}, bf16[144,512]{1,0:T(8,128)(2,1)S(1)}, u32[]{:S(2)}, u32[]{:S(2)}) collective-permute-start(bf16[144,512]{1,0:T(8,128)(2,1)S(1)} %get-tuple-element.174), channel_id=1, source_target_pairs={{0,16},{2,18},{4,20},{6,22},{8,24},{10,26},{12,28},{14,30},{16,0},... | collective-permute-start | bytes 442376 | tf_op jit(solution)/shard_map/ppermute | solution.py:1005
  123.3 2.0 %shard_map.340 = (bf16[192,512]{1,0:T(8,128)(2,1)}, bf16[192,512]{1,0:T(8,128)(2,1)}, bf16[192,512]{1,0:T(8,128)(2,1)}, bf16[192,512]{1,0:T(8,128)(2,1)S(1)}) custom-call(s32[4]{0:T(128)S(1)} %copy-done.12, bf16[144,512]{1,0:T(8,128)(2,1)S(1)} %get-tuple-element.163.refs_0_.refs_1_, bf16[768,512]{1,0:T(8,128)(2,1)S(1)} %get-tuple-element.164.refs_1_, ...), custom_call_target="tpu_custom_call" | custom-call | flops 1 | bytes 1 | tf_op jit(solution)/shard_map/pallas_call | solution.py:246
  125.3 1.5 collective-permute-start.18
  126.8 1.3 collective-permute-start.17
  128.1 5.2 %shard_map.341 = (bf16[544,512]{1,0:T(8,128)(2,1)}, bf16[544,512]{1,0:T(8,128)(2,1)S(1)}) custom-call(s32[4]{0:T(128)S(1)} %copy-done.12, bf16[192,512]{1,0:T(8,128)(2,1)} %get-tuple-element.165.after, bf16[1600,512]{1,0:T(8,128)(2,1)S(1)} %get-tuple-element.166.low_ref, bf16[1600,1024]{1,0:T(8,128)(2,1)S(1)} %get-tuple-element.167.hat_ref, ...), custom_call_target="tpu_custom_call" | custom-call | flops 1 | bytes 1 | tf_op jit(solution)/shard_map/pallas_call | solution.py:893
  133.3 0.7 collective-permute-start.19
  134.0 0.6 shard_map.342.refs_0_.refs_1_
  134.6 5.5 %collective-permute-done.19.refs_4_ = bf16[192,512]{1,0:T(8,128)(2,1)} collective-permute-done((bf16[192,512]{1,0:T(8,128)(2,1)}, bf16[192,512]{1,0:T(8,128)(2,1)}, u32[]{:S(2)}, u32[]{:S(2)}) %collective-permute-start.19) | collective-permute-done | bytes 196640 | tf_op jit(solution)/shard_map/ppermute | solution.py:1021
  140.1 1.2 shard_map.343.refs_0_.refs_1_
  141.4 1.2 shard_map.344
  142.6 0.6 collective-permute-start.22
  143.2 1.7 collective-permute-start.23
  144.9 1.3 collective-permute-start.21
  146.2 3.6 %collective-permute-start.26 = (bf16[144,512]{1,0:T(8,128)(2,1)S(1)}, bf16[144,512]{1,0:T(8,128)(2,1)S(1)}, u32[]{:S(2)}, u32[]{:S(2)}) collective-permute-start(bf16[144,512]{1,0:T(8,128)(2,1)S(1)} %shard_map.342.refs_0_.refs_1_), channel_id=1, source_target_pairs={{0,24},{2,26},{4,28},{6,30},{8,16},{10,18},{12,20},{14,22},{16,8},... | collective-permute-start | bytes 442376 | tf_op jit(solution)/shard_map/ppermute | solution.py:1005
  149.8 0.8 collective-permute-start.24
  150.6 0.6 collective-permute-done.21.refs_3_
  151.2 0.6 shard_map.345
  151.8 0.7 collective-permute-start.28
  152.6 3.5 %collective-permute-start.29 = (bf16[96,512]{1,0:T(8,128)(2,1)S(1)}, bf16[96,512]{1,0:T(8,128)(2,1)S(1)}, u32[]{:S(2)}, u32[]{:S(2)}) collective-permute-start(bf16[96,512]{1,0:T(8,128)(2,1)S(1)} %get-tuple-element.189), channel_id=1, source_target_pairs={{0,16},{2,18},{4,20},{6,22},{8,24},{10,26},{12,28},{14,30},{16,0},... | collective-permute-start | bytes 294920 | tf_op jit(solution)/shard_map/ppermute | solution.py:1005
  156.1 2.5 %collective-permute-start.30 = (bf16[96,512]{1,0:T(8,128)(2,1)S(1)}, bf16[96,512]{1,0:T(8,128)(2,1)S(1)}, u32[]{:S(2)}, u32[]{:S(2)}) collective-permute-start(bf16[96,512]{1,0:T(8,128)(2,1)S(1)} %get-tuple-element.190), channel_id=1, source_target_pairs={{0,24},{2,26},{4,28},{6,30},{8,16},{10,18},{12,20},{14,22},{16,8},... | collective-permute-start | bytes 294920 | tf_op jit(solution)/shard_map/ppermute | solution.py:1005
  158.5 6.8 %shard_map.346 = (bf16[1600,1024]{1,0:T(8,128)(2,1)}, f32[8,128]{1,0:T(8,128)S(1)}) custom-call(bf16[96,512]{1,0:T(8,128)(2,1)S(1)} %get-tuple-element.184.after.refs_1_, bf16[1600,512]{1,0:T(8,128)(2,1)} %copy-done, bf16[1600,1024]{1,0:T(8,128)(2,1)} %get-tuple-element.158.hat_in.hat_ref, f32[1600,1]{1,0:T(8,128)S(1)} %get-tuple-element.185.inverse_ref, ...), custom_call_target="tpu_custom_call" | custom-call | flops 1 | bytes 1 | tf_op jit(solution)/shard_map/pallas_call | solution.py:914
  165.3 1.4 shard_map.347.refs_0_.refs_1_
  167.3 0.6 shard_map.348
  167.9 1.9 collective-permute-start.33
  169.7 1.3 collective-permute-start.32
  171.0 1.3 collective-permute-start.31
  172.3 4.6 %collective-permute-done.27.refs_0_.refs_2_ = bf16[576,512]{1,0:T(8,128)(2,1)} collective-permute-done((bf16[576,512]{1,0:T(8,128)(2,1)}, bf16[576,512]{1,0:T(8,128)(2,1)}, u32[]{:S(2)}, u32[]{:S(2)}) %collective-permute-start.27) | collective-permute-done | bytes 589856 | tf_op jit(solution)/shard_map/ppermute | solution.py:1005
  177.5 1.5 collective-permute-start.36
  179.3 4.2 %shard_map.350 = (f32[1024,512]{1,0:T(8,128)}, f32[512,1024]{1,0:T(8,128)}, f32[256,512]{1,0:T(8,128)}, f32[8,128]{1,0:T(8,128)S(1)}) custom-call(s32[4]{0:T(128)S(1)} %copy-done.12, bf16[336,512]{1,0:T(8,128)(2,1)S(1)} %shard_map.349.refs_0_.mine, bf16[576,512]{1,0:T(8,128)(2,1)} %shard_map.347.refs_0_.refs_1_, ...), custom_call_target="tpu_custom_call" | custom-call | flops 1 | bytes 1 | tf_op jit(solution)/shard_map/pallas_call | solution.py:246
  183.5 4.6 %collective-permute-done.36.refs_1_ = bf16[336,512]{1,0:T(8,128)(2,1)S(1)} collective-permute-done((bf16[336,512]{1,0:T(8,128)(2,1)S(1)}, bf16[336,512]{1,0:T(8,128)(2,1)S(1)}, u32[]{:S(2)}, u32[]{:S(2)}) %collective-permute-start.36) | collective-permute-done | bytes 344096 | tf_op jit(solution)/shard_map/ppermute | solution.py:1005
  188.7 1.6 collective-permute-done.38.core_beside
  190.3 2.3 %shard_map.352 = (f32[3,512,256]{2,1,0:T(8,128)}, f32[512,512]{1,0:T(8,128)}, f32[1,512]{1,0:T(1,128)}, f32[1,512]{1,0:T(1,128)}, f32[1,512]{1,0:T(1,128)}, /*in...) custom-call(s32[4]{0:T(128)S(1)} %copy-done.12, ...), custom_call_target="tpu_custom_call" | custom-call | flops 1 | bytes 1 | tf_op jit(solution)/shard_map/pallas_call | solution.py:194
  (100 shorter events, 5.4 us)
Async XLA Ops:
  2.9 3.0 %copy-start.8 = (bf16[256,512]{1,0:T(8,128)(2,1)}, bf16[256,512]{1,0:T(8,128)(2,1)S(1)}, u32[]{:S(2)}) copy-start(bf16[256,512]{1,0:T(8,128)(2,1)S(1)} %shard_map.322.after) | copy-start | bytes 786436
  2.9 10.0 %collective-permute-start.1 = (bf16[256,512]{1,0:T(8,128)(2,1)S(1)}, bf16[256,512]{1,0:T(8,128)(2,1)S(1)}, u32[]{:S(2)}, u32[]{:S(2)}) collective-permute-start(bf16[256,512]{1,0:T(8,128)(2,1)S(1)} %shard_map.322.after), channel_id=1, source_target_pairs={{0,1},{1,0},{2,3},{3,2},{4,5},{5,4},{6,7},{7,6},{8,9},{9,8},{10,11... | collective-permute-start | bytes 786440 | tf_op jit(solution)/shard_map/ppermute | solution.py:1017
  7.4 0.6 copy-start.13
  8.1 4.9 %collective-permute-start = (bf16[32,512]{1,0:T(8,128)(2,1)S(1)}, bf16[32,512]{1,0:T(8,128)(2,1)S(1)}, u32[]{:S(2)}, u32[]{:S(2)}) collective-permute-start(bf16[32,512]{1,0:T(8,128)(2,1)S(1)} %get-tuple-element.116), channel_id=1, source_target_pairs={{0,1},{1,0},{2,3},{3,2},{4,5},{5,4},{6,7},{7,6},{8,9},{9,8},{10,11... | collective-permute-start | bytes 98312 | tf_op jit(solution)/shard_map/ppermute | solution.py:1017
  10.9 8.1 %copy-start.6 = (bf16[512,512]{1,0:T(8,128)(2,1)S(1)}, bf16[512,512]{1,0:T(8,128)(2,1)}, u32[]{:S(2)}) copy-start(bf16[512,512]{1,0:T(8,128)(2,1)} %own_ref.1) | copy-start | bytes 1572868
  10.9 8.1 %copy-start.12 = (s32[4]{0:T(128)S(1)}, s32[4]{0:T(128)}, u32[]{:S(2)}) copy-start(s32[4]{0:T(128)} %pad_add_fusion.place) | copy-start | bytes 52
  10.9 8.2 %copy-start.14 = (f32[16,512]{1,0:T(8,128)S(1)}, f32[16,512]{1,0:T(8,128)}, u32[]{:S(2)}) copy-start(f32[16,512]{1,0:T(8,128)} %copy-done.13) | copy-start | bytes 98308
  10.9 8.2 %copy-start.22 = (f32[512]{0:T(512)S(1)}, f32[512]{0:T(512)}, u32[]{:S(2)}) copy-start(f32[512]{0:T(512)} %param.25) | copy-start | bytes 6148
  10.9 8.2 %copy-start.23 = (f32[512]{0:T(512)S(1)}, f32[512]{0:T(512)}, u32[]{:S(2)}) copy-start(f32[512]{0:T(512)} %param.26) | copy-start | bytes 6148
  13.6 0.7 copy-start.9
  14.3 4.8 %copy-start.10 = (bf16[256,512]{1,0:T(8,128)(2,1)S(1)}, bf16[256,512]{1,0:T(8,128)(2,1)}, u32[]{:S(2)}) copy-start(bf16[256,512]{1,0:T(8,128)(2,1)} %copy-done.9) | copy-start | bytes 786436
  14.3 4.8 %copy-start.16 = (bf16[32,512]{1,0:T(8,128)(2,1)S(1)}, bf16[32,512]{1,0:T(8,128)(2,1)}, u32[]{:S(2)}) copy-start(bf16[32,512]{1,0:T(8,128)(2,1)} %copy-done.15) | copy-start | bytes 98308
  14.3 13.3 %collective-permute-start.3 = (bf16[512,512]{1,0:T(8,128)(2,1)S(1)}, bf16[512,512]{1,0:T(8,128)(2,1)S(1)}, u32[]{:S(2)}, u32[]{:S(2)}) collective-permute-start(bf16[512,512]{1,0:T(8,128)(2,1)S(1)} %shard_map.326.after), channel_id=1, source_target_pairs={{0,1},{1,0},{2,3},{3,2},{4,5},{5,4},{6,7},{7,6},{8,9},{9,8},{10,11... | collective-permute-start | bytes 1572872 | tf_op jit(solution)/shard_map/ppermute | solution.py:1017
  16.0 3.0 %collective-permute-start.2 = (bf16[256,512]{1,0:T(8,128)(2,1)}, bf16[256,512]{1,0:T(8,128)(2,1)S(1)}, u32[]{:S(2)}, u32[]{:S(2)}) collective-permute-start(bf16[256,512]{1,0:T(8,128)(2,1)} %copy-done.9), channel_id=1, source_target_pairs={{0,2},{2,0},{4,6},{6,4},{8,10},{10,8},{12,14},{14,12},{16,18},{18,... | collective-permute-start | bytes 786440 | tf_op jit(solution)/shard_map/ppermute | solution.py:1005
  19.1 8.4 %copy-start.1 = (bf16[512,1024]{1,0:T(8,128)(2,1)S(1)}, bf16[512,1024]{1,0:T(8,128)(2,1)}, u32[]{:S(2)}) copy-start(bf16[512,1024]{1,0:T(8,128)(2,1)} %refs_2_.1) | copy-start | bytes 3145732
  19.1 8.4 %copy-start.2 = (bf16[1024,512]{1,0:T(8,128)(2,1)S(1)}, bf16[1024,512]{1,0:T(8,128)(2,1)}, u32[]{:S(2)}) copy-start(bf16[1024,512]{1,0:T(8,128)(2,1)} %refs_3_.1) | copy-start | bytes 3145732
  25.2 6.3 %copy-start.5 = (bf16[3,512,256]{2,1,0:T(8,128)(2,1)S(1)}, bf16[3,512,256]{2,1,0:T(8,128)(2,1)}, u32[]{:S(2)}) copy-start(bf16[3,512,256]{2,1,0:T(8,128)(2,1)} %param.27) | copy-start | bytes 2359300
  25.2 6.3 %copy-start.18 = (f32[16,1,128]{2,1,0:T(1,128)S(1)}, f32[16,1,128]{2,1,0:T(1,128)}, u32[]{:S(2)}) copy-start(f32[16,1,128]{2,1,0:T(1,128)} %copy-done.17) | copy-start | bytes 24580
  28.2 15.7 %copy-start.7 = (bf16[256,512]{1,0:T(8,128)(2,1)S(1)}, bf16[256,512]{1,0:T(8,128)(2,1)}, u32[]{:S(2)}) copy-start(bf16[256,512]{1,0:T(8,128)(2,1)} %proj_own.1) | copy-start | bytes 786436
  28.2 15.7 %copy-start.21 = (f32[512]{0:T(512)S(1)}, f32[512]{0:T(512)}, u32[]{:S(2)}) copy-start(f32[512]{0:T(512)} %param.32) | copy-start | bytes 6148
  28.2 15.7 %copy-start.24 = (f32[512]{0:T(512)S(1)}, f32[512]{0:T(512)}, u32[]{:S(2)}) copy-start(f32[512]{0:T(512)} %param.31) | copy-start | bytes 6148
  28.2 15.7 %copy-start.25 = (f32[512]{0:T(512)S(1)}, f32[512]{0:T(512)}, u32[]{:S(2)}) copy-start(f32[512]{0:T(512)} %param.33) | copy-start | bytes 6148
  28.2 28.2 %collective-permute-start.5 = (bf16[1024,512]{1,0:T(8,128)(2,1)S(1)}, bf16[1024,512]{1,0:T(8,128)(2,1)}, u32[]{:S(2)}, u32[]{:S(2)}) collective-permute-start(bf16[1024,512]{1,0:T(8,128)(2,1)S(1)} %shard_map.333), channel_id=1, source_target_pairs={{0,1},{1,0},{2,3},{3,2},{4,5},{5,4},{6,7},{7,6},{8,9},{9,8},{10,11... | collective-permute-start | bytes 3145736 | tf_op jit(solution)/shard_map/ppermute | solution.py:1017
  29.5 1.9 collective-permute-start.4
  56.2 28.9 %collective-permute-start.7 = (bf16[1024,512]{1,0:T(8,128)(2,1)}, bf16[1024,512]{1,0:T(8,128)(2,1)}, u32[]{:S(2)}, u32[]{:S(2)}) collective-permute-start(bf16[1024,512]{1,0:T(8,128)(2,1)} %get-tuple-element.140), channel_id=1, source_target_pairs={{0,2},{2,0},{4,6},{6,4},{8,10},{10,8},{12,14},{14,12},{16,18},{18,... | collective-permute-start | bytes 3145736 | tf_op jit(solution)/shard_map/ppermute | solution.py:1005
  56.4 7.3 %collective-permute-start.6 = (bf16[1024,512]{1,0:T(8,128)(2,1)}, bf16[1024,512]{1,0:T(8,128)(2,1)}, u32[]{:S(2)}, u32[]{:S(2)}) collective-permute-start(bf16[1024,512]{1,0:T(8,128)(2,1)} %collective-permute-done.5.near_ref), channel_id=1, source_target_pairs={{0,2},{2,0},{4,6},{6,4},{8,10},{10,8},{12,14},{14,12},{16,18},{18,... | collective-permute-start | bytes 3145736 | tf_op jit(solution)/shard_map/ppermute | solution.py:1005
  63.7 7.8 %copy-start.26 = (f32[512]{0:T(512)S(1)}, f32[512]{0:T(512)}, u32[]{:S(2)}) copy-start(f32[512]{0:T(512)} %param.37) | copy-start | bytes 6148
  71.3 14.9 %collective-permute-start.8 = (bf16[1024,512]{1,0:T(8,128)(2,1)S(1)}, bf16[1024,512]{1,0:T(8,128)(2,1)S(1)}, u32[]{:S(2)}, u32[]{:S(2)}) collective-permute-start(bf16[1024,512]{1,0:T(8,128)(2,1)S(1)} %get-tuple-element.142), channel_id=1, source_target_pairs={{0,2},{2,0},{4,6},{6,4},{8,10},{10,8},{12,14},{14,12},{16,18},{18,... | collective-permute-start | bytes 3145736 | tf_op jit(solution)/shard_map/ppermute | solution.py:1005
  84.6 1.6 collective-permute-start.9
  88.0 28.0 %collective-permute-start.11 = (bf16[576,512]{1,0:T(8,128)(2,1)S(1)}, bf16[576,512]{1,0:T(8,128)(2,1)S(1)}, u32[]{:S(2)}, u32[]{:S(2)}) collective-permute-start(bf16[576,512]{1,0:T(8,128)(2,1)S(1)} %get-tuple-element.161), channel_id=1, source_target_pairs={{0,4},{2,6},{4,0},{6,2},{8,12},{10,14},{12,8},{14,10},{16,20},{18,... | collective-permute-start | bytes 1769480 | tf_op jit(solution)/shard_map/ppermute | solution.py:1005
  89.6 27.0 %collective-permute-start.12 = (bf16[576,512]{1,0:T(8,128)(2,1)S(1)}, bf16[576,512]{1,0:T(8,128)(2,1)S(1)}, u32[]{:S(2)}, u32[]{:S(2)}) collective-permute-start(bf16[576,512]{1,0:T(8,128)(2,1)S(1)} %get-tuple-element.162), channel_id=1, source_target_pairs={{0,5},{1,4},{2,7},{3,6},{4,1},{5,0},{6,3},{7,2},{8,13},{9,12},{10,... | collective-permute-start | bytes 1769480 | tf_op jit(solution)/shard_map/ppermute | solution.py:1021
  90.3 27.7 %collective-permute-start.10 = (bf16[576,512]{1,0:T(8,128)(2,1)S(1)}, bf16[576,512]{1,0:T(8,128)(2,1)S(1)}, u32[]{:S(2)}, u32[]{:S(2)}) collective-permute-start(bf16[576,512]{1,0:T(8,128)(2,1)S(1)} %get-tuple-element.145.after), channel_id=1, source_target_pairs={{0,1},{1,0},{2,3},{3,2},{4,5},{5,4},{6,7},{7,6},{8,9},{9,8},{10,11... | collective-permute-start | bytes 1769480 | tf_op jit(solution)/shard_map/ppermute | solution.py:1017
  110.2 5.8 %copy-start.19 = (f32[1,1536]{1,0:T(1,128)}, f32[1,1536]{1,0:T(1,128)S(1)}, u32[]{:S(2)}) copy-start(f32[1,1536]{1,0:T(1,128)S(1)} %get-tuple-element.155.after.qkv_sums_ref) | copy-start | bytes 18436
  110.2 17.9 %copy-start = (bf16[1600,512]{1,0:T(8,128)(2,1)}, bf16[1600,512]{1,0:T(8,128)(2,1)S(1)}, u32[]{:S(2)}) copy-start(bf16[1600,512]{1,0:T(8,128)(2,1)S(1)} %get-tuple-element.166.low_ref) | copy-start | bytes 4915204
  116.0 7.3 %collective-permute-start.13 = (bf16[768,512]{1,0:T(8,128)(2,1)}, bf16[768,512]{1,0:T(8,128)(2,1)}, u32[]{:S(2)}, u32[]{:S(2)}) collective-permute-start(bf16[768,512]{1,0:T(8,128)(2,1)} %get-tuple-element.159.refs_0_), channel_id=1, source_target_pairs={{0,2},{2,0},{4,6},{6,4},{8,10},{10,8},{12,14},{14,12},{16,18},{18,... | collective-permute-start | bytes 2359304 | tf_op jit(solution)/shard_map/ppermute | solution.py:1005
  118.0 10.1 %copy-start.3 = (bf16[1024,512]{1,0:T(8,128)(2,1)S(1)}, bf16[1024,512]{1,0:T(8,128)(2,1)}, u32[]{:S(2)}) copy-start(bf16[1024,512]{1,0:T(8,128)(2,1)} %get-tuple-element.168.merge_ref) | copy-start | bytes 3145732
  118.0 10.1 %copy-start.11 = (f32[1024,128]{1,0:T(8,128)S(1)}, f32[1024,128]{1,0:T(8,128)}, u32[]{:S(2)}) copy-start(f32[1024,128]{1,0:T(8,128)} %get-tuple-element.169.column_ref) | copy-start | bytes 1572868
  118.0 10.1 %copy-start.20 = (f32[1,1536]{1,0:T(1,128)S(1)}, f32[1,1536]{1,0:T(1,128)}, u32[]{:S(2)}) copy-start(f32[1,1536]{1,0:T(1,128)} %copy-done.19) | copy-start | bytes 18436
  118.8 14.4 %collective-permute-start.14 = (bf16[144,512]{1,0:T(8,128)(2,1)S(1)}, bf16[144,512]{1,0:T(8,128)(2,1)S(1)}, u32[]{:S(2)}, u32[]{:S(2)}) collective-permute-start(bf16[144,512]{1,0:T(8,128)(2,1)S(1)} %get-tuple-element.173), channel_id=1, source_target_pairs={{0,8},{2,10},{4,12},{6,14},{8,0},{10,2},{12,4},{14,6},{16,24},{18,... | collective-permute-start | bytes 442376 | tf_op jit(solution)/shard_map/ppermute | solution.py:1005
  120.5 13.5 %collective-permute-start.15 = (bf16[144,512]{1,0:T(8,128)(2,1)S(1)}, bf16[144,512]{1,0:T(8,128)(2,1)S(1)}, u32[]{:S(2)}, u32[]{:S(2)}) collective-permute-start(bf16[144,512]{1,0:T(8,128)(2,1)S(1)} %get-tuple-element.174), channel_id=1, source_target_pairs={{0,16},{2,18},{4,20},{6,22},{8,24},{10,26},{12,28},{14,30},{16,0},... | collective-permute-start | bytes 442376 | tf_op jit(solution)/shard_map/ppermute | solution.py:1005
  123.1 10.9 %collective-permute-start.16 = (bf16[144,512]{1,0:T(8,128)(2,1)S(1)}, bf16[144,512]{1,0:T(8,128)(2,1)S(1)}, u32[]{:S(2)}, u32[]{:S(2)}) collective-permute-start(bf16[144,512]{1,0:T(8,128)(2,1)S(1)} %get-tuple-element.175), channel_id=1, source_target_pairs={{0,24},{2,26},{4,28},{6,30},{8,16},{10,18},{12,20},{14,22},{16,8},... | collective-permute-start | bytes 442376 | tf_op jit(solution)/shard_map/ppermute | solution.py:1005
  125.3 9.3 %collective-permute-start.18 = (bf16[192,512]{1,0:T(8,128)(2,1)}, bf16[192,512]{1,0:T(8,128)(2,1)}, u32[]{:S(2)}, u32[]{:S(2)}) collective-permute-start(bf16[192,512]{1,0:T(8,128)(2,1)} %get-tuple-element.177), channel_id=1, source_target_pairs={{0,4},{2,6},{4,0},{6,2},{8,12},{10,14},{12,8},{14,10},{16,20},{18,... | collective-permute-start | bytes 589832 | tf_op jit(solution)/shard_map/ppermute | solution.py:1005
  126.8 13.3 %collective-permute-start.17 = (bf16[192,512]{1,0:T(8,128)(2,1)}, bf16[192,512]{1,0:T(8,128)(2,1)}, u32[]{:S(2)}, u32[]{:S(2)}) collective-permute-start(bf16[192,512]{1,0:T(8,128)(2,1)} %get-tuple-element.165.after), channel_id=1, source_target_pairs={{0,1},{1,0},{2,3},{3,2},{4,5},{5,4},{6,7},{7,6},{8,9},{9,8},{10,11... | collective-permute-start | bytes 589832 | tf_op jit(solution)/shard_map/ppermute | solution.py:1017
  133.3 6.9 %collective-permute-start.19 = (bf16[192,512]{1,0:T(8,128)(2,1)}, bf16[192,512]{1,0:T(8,128)(2,1)}, u32[]{:S(2)}, u32[]{:S(2)}) collective-permute-start(bf16[192,512]{1,0:T(8,128)(2,1)} %get-tuple-element.178), channel_id=1, source_target_pairs={{0,5},{1,4},{2,7},{3,6},{4,1},{5,0},{6,3},{7,2},{8,13},{9,12},{10,... | collective-permute-start | bytes 589832 | tf_op jit(solution)/shard_map/ppermute | solution.py:1021
  134.0 7.4 %collective-permute-start.20 = (bf16[544,512]{1,0:T(8,128)(2,1)}, bf16[544,512]{1,0:T(8,128)(2,1)}, u32[]{:S(2)}, u32[]{:S(2)}) collective-permute-start(bf16[544,512]{1,0:T(8,128)(2,1)} %get-tuple-element.172.refs_0_), channel_id=1, source_target_pairs={{0,2},{2,0},{4,6},{6,4},{8,10},{10,8},{12,14},{14,12},{16,18},{18,... | collective-permute-start | bytes 1671176 | tf_op jit(solution)/shard_map/ppermute | solution.py:1005
  134.6 23.9 %copy-start.4 = (bf16[1024,512]{1,0:T(8,128)(2,1)S(1)}, bf16[1024,512]{1,0:T(8,128)(2,1)}, u32[]{:S(2)}) copy-start(bf16[1024,512]{1,0:T(8,128)(2,1)} %get-tuple-element.168.merge_ref) | copy-start | bytes 3145732
  142.6 7.2 %collective-permute-start.22 = (bf16[144,512]{1,0:T(8,128)(2,1)S(1)}, bf16[144,512]{1,0:T(8,128)(2,1)S(1)}, u32[]{:S(2)}, u32[]{:S(2)}) collective-permute-start(bf16[144,512]{1,0:T(8,128)(2,1)S(1)} %get-tuple-element.182), channel_id=1, source_target_pairs={{0,4},{2,6},{4,0},{6,2},{8,12},{10,14},{12,8},{14,10},{16,20},{18,... | collective-permute-start | bytes 442376 | tf_op jit(solution)/shard_map/ppermute | solution.py:1005
  143.2 7.4 %collective-permute-start.23 = (bf16[144,512]{1,0:T(8,128)(2,1)S(1)}, bf16[144,512]{1,0:T(8,128)(2,1)S(1)}, u32[]{:S(2)}, u32[]{:S(2)}) collective-permute-start(bf16[144,512]{1,0:T(8,128)(2,1)S(1)} %get-tuple-element.183), channel_id=1, source_target_pairs={{0,5},{1,4},{2,7},{3,6},{4,1},{5,0},{6,3},{7,2},{8,13},{9,12},{10,... | collective-permute-start | bytes 442376 | tf_op jit(solution)/shard_map/ppermute | solution.py:1021
  144.9 6.3 %collective-permute-start.21 = (bf16[144,512]{1,0:T(8,128)(2,1)S(1)}, bf16[144,512]{1,0:T(8,128)(2,1)S(1)}, u32[]{:S(2)}, u32[]{:S(2)}) collective-permute-start(bf16[144,512]{1,0:T(8,128)(2,1)S(1)} %get-tuple-element.180.refs_0_), channel_id=1, source_target_pairs={{0,1},{1,0},{2,3},{3,2},{4,5},{5,4},{6,7},{7,6},{8,9},{9,8},{10,11... | collective-permute-start | bytes 442376 | tf_op jit(solution)/shard_map/ppermute | solution.py:1017
  146.2 9.9 %collective-permute-start.26 = (bf16[144,512]{1,0:T(8,128)(2,1)S(1)}, bf16[144,512]{1,0:T(8,128)(2,1)S(1)}, u32[]{:S(2)}, u32[]{:S(2)}) collective-permute-start(bf16[144,512]{1,0:T(8,128)(2,1)S(1)} %shard_map.342.refs_0_.refs_1_), channel_id=1, source_target_pairs={{0,24},{2,26},{4,28},{6,30},{8,16},{10,18},{12,20},{14,22},{16,8},... | collective-permute-start | bytes 442376 | tf_op jit(solution)/shard_map/ppermute | solution.py:1005
  149.8 15.5 %collective-permute-start.25 = (bf16[144,512]{1,0:T(8,128)(2,1)S(1)}, bf16[144,512]{1,0:T(8,128)(2,1)S(1)}, u32[]{:S(2)}, u32[]{:S(2)}) collective-permute-start(bf16[144,512]{1,0:T(8,128)(2,1)S(1)} %shard_map.342.refs_0_.refs_1_), channel_id=1, source_target_pairs={{0,16},{2,18},{4,20},{6,22},{8,24},{10,26},{12,28},{14,30},{16,0},... | collective-permute-start | bytes 442376 | tf_op jit(solution)/shard_map/ppermute | solution.py:1005
  149.8 15.5 %collective-permute-start.24 = (bf16[144,512]{1,0:T(8,128)(2,1)S(1)}, bf16[144,512]{1,0:T(8,128)(2,1)S(1)}, u32[]{:S(2)}, u32[]{:S(2)}) collective-permute-start(bf16[144,512]{1,0:T(8,128)(2,1)S(1)} %shard_map.342.refs_0_.refs_1_), channel_id=1, source_target_pairs={{0,8},{2,10},{4,12},{6,14},{8,0},{10,2},{12,4},{14,6},{16,24},{18,... | collective-permute-start | bytes 442376 | tf_op jit(solution)/shard_map/ppermute | solution.py:1005
  151.8 15.4 %collective-permute-start.28 = (bf16[96,512]{1,0:T(8,128)(2,1)S(1)}, bf16[96,512]{1,0:T(8,128)(2,1)S(1)}, u32[]{:S(2)}, u32[]{:S(2)}) collective-permute-start(bf16[96,512]{1,0:T(8,128)(2,1)S(1)} %get-tuple-element.188), channel_id=1, source_target_pairs={{0,8},{2,10},{4,12},{6,14},{8,0},{10,2},{12,4},{14,6},{16,24},{18,... | collective-permute-start | bytes 294920 | tf_op jit(solution)/shard_map/ppermute | solution.py:1005
  152.6 14.7 %collective-permute-start.29 = (bf16[96,512]{1,0:T(8,128)(2,1)S(1)}, bf16[96,512]{1,0:T(8,128)(2,1)S(1)}, u32[]{:S(2)}, u32[]{:S(2)}) collective-permute-start(bf16[96,512]{1,0:T(8,128)(2,1)S(1)} %get-tuple-element.189), channel_id=1, source_target_pairs={{0,16},{2,18},{4,20},{6,22},{8,24},{10,26},{12,28},{14,30},{16,0},... | collective-permute-start | bytes 294920 | tf_op jit(solution)/shard_map/ppermute | solution.py:1005
  156.1 11.2 %collective-permute-start.30 = (bf16[96,512]{1,0:T(8,128)(2,1)S(1)}, bf16[96,512]{1,0:T(8,128)(2,1)S(1)}, u32[]{:S(2)}, u32[]{:S(2)}) collective-permute-start(bf16[96,512]{1,0:T(8,128)(2,1)S(1)} %get-tuple-element.190), channel_id=1, source_target_pairs={{0,24},{2,26},{4,28},{6,30},{8,16},{10,18},{12,20},{14,22},{16,8},... | collective-permute-start | bytes 294920 | tf_op jit(solution)/shard_map/ppermute | solution.py:1005
  166.7 10.2 %collective-permute-start.27 = (bf16[576,512]{1,0:T(8,128)(2,1)}, bf16[576,512]{1,0:T(8,128)(2,1)}, u32[]{:S(2)}, u32[]{:S(2)}) collective-permute-start(bf16[576,512]{1,0:T(8,128)(2,1)} %shard_map.347.refs_0_.refs_1_), channel_id=1, source_target_pairs={{0,4},{2,6},{4,0},{6,2},{8,12},{10,14},{12,8},{14,10},{16,20},{18,... | collective-permute-start | bytes 1769480 | tf_op jit(solution)/shard_map/ppermute | solution.py:1005
  167.9 9.1 %collective-permute-start.33 = (bf16[80,512]{1,0:T(8,128)(2,1)S(1)}, bf16[80,512]{1,0:T(8,128)(2,1)S(1)}, u32[]{:S(2)}, u32[]{:S(2)}) collective-permute-start(bf16[80,512]{1,0:T(8,128)(2,1)S(1)} %get-tuple-element.192.refs_2_), channel_id=1, source_target_pairs={{0,24},{2,26},{4,28},{6,30},{8,16},{10,18},{12,20},{14,22},{16,8},... | collective-permute-start | bytes 245768 | tf_op jit(solution)/shard_map/ppermute | solution.py:1005
  169.7 7.2 %collective-permute-start.32 = (bf16[80,512]{1,0:T(8,128)(2,1)S(1)}, bf16[80,512]{1,0:T(8,128)(2,1)S(1)}, u32[]{:S(2)}, u32[]{:S(2)}) collective-permute-start(bf16[80,512]{1,0:T(8,128)(2,1)S(1)} %get-tuple-element.192.refs_2_), channel_id=1, source_target_pairs={{0,16},{2,18},{4,20},{6,22},{8,24},{10,26},{12,28},{14,30},{16,0},... | collective-permute-start | bytes 245768 | tf_op jit(solution)/shard_map/ppermute | solution.py:1005
  171.0 5.9 %collective-permute-start.31 = (bf16[80,512]{1,0:T(8,128)(2,1)S(1)}, bf16[80,512]{1,0:T(8,128)(2,1)S(1)}, u32[]{:S(2)}, u32[]{:S(2)}) collective-permute-start(bf16[80,512]{1,0:T(8,128)(2,1)S(1)} %get-tuple-element.192.refs_2_), channel_id=1, source_target_pairs={{0,8},{2,10},{4,12},{6,14},{8,0},{10,2},{12,4},{14,6},{16,24},{18,... | collective-permute-start | bytes 245768 | tf_op jit(solution)/shard_map/ppermute | solution.py:1005
  172.3 6.7 %collective-permute-start.34 = (bf16[576,512]{1,0:T(8,128)(2,1)}, bf16[576,512]{1,0:T(8,128)(2,1)}, u32[]{:S(2)}, u32[]{:S(2)}) collective-permute-start(bf16[576,512]{1,0:T(8,128)(2,1)} %shard_map.347.refs_0_.refs_1_), channel_id=1, source_target_pairs={{0,2},{2,0},{4,6},{6,4},{8,10},{10,8},{12,14},{14,12},{16,18},{18,... | collective-permute-start | bytes 1769480 | tf_op jit(solution)/shard_map/ppermute | solution.py:1005
  176.9 2.3 %collective-permute-start.35 = (bf16[576,512]{1,0:T(8,128)(2,1)}, bf16[576,512]{1,0:T(8,128)(2,1)}, u32[]{:S(2)}, u32[]{:S(2)}) collective-permute-start(bf16[576,512]{1,0:T(8,128)(2,1)} %collective-permute-done.27.refs_0_.refs_2_), channel_id=1, source_target_pairs={{0,2},{2,0},{4,6},{6,4},{8,10},{10,8},{12,14},{14,12},{16,18},{18,... | collective-permute-start | bytes 1769480 | tf_op jit(solution)/shard_map/ppermute | solution.py:1005
  177.5 10.5 %collective-permute-start.36 = (bf16[336,512]{1,0:T(8,128)(2,1)S(1)}, bf16[336,512]{1,0:T(8,128)(2,1)S(1)}, u32[]{:S(2)}, u32[]{:S(2)}) collective-permute-start(bf16[336,512]{1,0:T(8,128)(2,1)S(1)} %shard_map.349.refs_0_.mine), channel_id=1, source_target_pairs={{0,4},{2,6},{4,0},{6,2},{8,12},{10,14},{12,8},{14,10},{16,20},{18,... | collective-permute-start | bytes 1032200 | tf_op jit(solution)/shard_map/ppermute | solution.py:1005
  179.0 9.7 %collective-permute-start.37 = (bf16[336,512]{1,0:T(8,128)(2,1)S(1)}, bf16[336,512]{1,0:T(8,128)(2,1)S(1)}, u32[]{:S(2)}, u32[]{:S(2)}) collective-permute-start(bf16[336,512]{1,0:T(8,128)(2,1)S(1)} %shard_map.349.refs_0_.mine), channel_id=1, source_target_pairs={{0,2},{2,0},{4,6},{6,4},{8,10},{10,8},{12,14},{14,12},{16,18},{18,... | collective-permute-start | bytes 1032200 | tf_op jit(solution)/shard_map/ppermute | solution.py:1005
  188.6 1.7 collective-permute-start.38
  (2 other events, 1.2 us)

commit v2 on v1

--- a/solution.py
+++ b/solution.py
@@ -110,7 +110,7 @@
 QKV_PACK = 384
 PROJ_PACK = 128
 MERGE_PACK = 256
-STAGE_ROOM = 16
+STAGE_ROOM = 9
 COST = pl.CostEstimate(flops=1, bytes_accessed=1, transcendentals=0)
 LONG = pl.CostEstimate(flops=10**12, bytes_accessed=1, transcendentals=0)
 SUMS = 16
@@ -151,6 +151,7 @@
         out_specs=RESIDENT,
         out_shape=pltpu.VMEM((256, D), bf16),
         scratch_shapes=[pltpu.SemaphoreType.DMA],
+        compiler_params=pltpu.CompilerParams(vmem_limit_bytes=4 * 1024 * 1024),
         cost_estimate=COST,
     )(place, in_hbm(merge))
 
@@ -186,6 +187,7 @@
         out_specs=[RESIDENT] * 2,
         out_shape=[pltpu.VMEM((PARAMS, D), f32), pltpu.VMEM((2 * PARAMS, D), bf16)],
         scratch_shapes=[pltpu.VMEM(array.shape, array.dtype) for array in operands] + [pltpu.SemaphoreType.DMA((5,))],
+        compiler_params=pltpu.CompilerParams(vmem_limit_bytes=4 * 1024 * 1024),
         cost_estimate=COST,
     )(place, after, *operands)
 
@@ -227,6 +229,7 @@
         scratch_shapes=[
             pltpu.VMEM((768, 256), bf16), pltpu.VMEM((128, D), bf16), pltpu.SemaphoreType.DMA((2,)),
         ],
+        compiler_params=pltpu.CompilerParams(vmem_limit_bytes=4 * 1024 * 1024),
         cost_estimate=COST,
     )(place, in_hbm(qkv), in_hbm(proj), *after)
 
@@ -265,6 +268,7 @@
         out_specs=RESIDENT,
         out_shape=pltpu.VMEM(array.shape, array.dtype),
         input_output_aliases={0: 0},
+        compiler_params=pltpu.CompilerParams(vmem_limit_bytes=4 * 1024 * 1024),
         cost_estimate=COST,
     )(array, *after)
 
@@ -303,6 +307,7 @@
         scratch_shapes=[
             pltpu.VMEM((windows, QUERIES), jnp.int32), pltpu.VMEM(window_mask.shape, jnp.int32), pltpu.SemaphoreType.DMA,
         ],
+        compiler_params=pltpu.CompilerParams(vmem_limit_bytes=4 * 1024 * 1024),
         cost_estimate=COST,
     )(place, after, in_hbm(window_mask))
 
@@ -405,7 +410,7 @@
         ],
         flops=2 * count * D * MERGE_IN,
         moved=count * 10 * D + 4 * D * MERGE_IN,
-        room=24,
+        room=14,
     )(place, hat, own, near, far, params, others, gain, bias)
 
 
@@ -510,12 +515,22 @@
 FEED_ROWS = 400
 OWN_ROOM = 18
 OTHER_ROOM = 12
-AB_ROOM = 20
+AB_ROOM = 18
 NEAR_ROOM = 20
 
 
 def feed_tile(up, down, bias, second_ref, turned_ref, branch_ref, total_s, back_s, active_s, raise_s, target, first):
     sums = jnp.zeros((1, TILE), f32)
+
+    def add_products(here, active, grad_raised):
+        total_s[here, :] += mm(active, down)
+        back = mm_t(grad_raised, up)
+        if first:
+            back_s[here, :] = back
+        else:
+            back_s[here, :] += back
+
+    last = None
     for begin in range(0, second_ref.shape[0], FEED_ROWS):
         here = slice(begin, begin + FEED_ROWS)
         value, slope = gelu_parts(mm(second_ref[here, :], up) + bias)
@@ -524,23 +539,19 @@
         active_s[here, :] = active
         raise_s[here, :] = grad_raised
         sums += column_sum(grad_raised.astype(f32))
-        out = mm(active, down)
-        back = mm_t(grad_raised, up)
-        if first:
-            total_s[here, :] = out
-            back_s[here, :] = back
-        else:
-            total_s[here, :] += out
-            back_s[here, :] += back
+        if last is not None:
+            add_products(*last)
+        last = here, active, grad_raised
+    add_products(*last)
     target[0:512, :] = t_mm(active_s[...], branch_ref[...]).astype(bf16)
     target[512:1024, :] = mm(turned_ref[...], raise_s[...]).astype(bf16)
     return sums
 
 
 def feed_own_body(
-    place, attended_ref, merged_ref, cotangent_ref, live_ref, proj_bias, norm_gain, norm_bias, params_ref,
+    place, attended_ref, merged_ref, cotangent_ref, live_ref, proj_bias, norm_gain, norm_bias, down_bias, params_ref,
     proj_own, near_ref, far_ref, up_own, down_own,
-    residual_ref, total_ref, back_ref, second_ref, turned_ref, branch_ref, send_ref, sums_ref, proj_ref,
+    hat_ref, inverse_ref, total_ref, back_ref, second_ref, turned_ref, branch_ref, send_ref, sums_ref, proj_ref,
     active_s, raise_s,
 ):
     step = pl.program_id(0)
@@ -558,8 +569,10 @@
     def _():
         here = pl.ds(pl.multiple_of(step * ROWS, 16), ROWS)
         residual = merged_ref[...] + mm(attended_ref[...], proj_ref[...]) + proj_bias[...]
-        residual_ref[here, :] = residual
-        hat, _ = normalize(residual)
+        total_ref[here, :] = residual + down_bias[...]
+        hat, inverse = normalize(residual)
+        hat_ref[here, :] = hat
+        inverse_ref[here, :] = inverse
         second_ref[here, :] = (hat * norm_gain[...] + norm_bias[...]).astype(bf16)
         row = lax.broadcasted_iota(jnp.int32, (ROWS, 1), 0)
         live = live_ref[GROUP - 1, :, 0:1]
@@ -595,17 +608,17 @@
         (blocks + 1,),
         [
             SCALARS, taken(D), taken(D), taken(D),
-            pl.BlockSpec((GROUP, 1, QUERIES), lambda i: (jnp.minimum(i, blocks - 1), 0, 0)), RESIDENT, RESIDENT, RESIDENT, RESIDENT, RESIDENT, RESIDENT, RESIDENT,
+            pl.BlockSpec((GROUP, 1, QUERIES), lambda i: (jnp.minimum(i, blocks - 1), 0, 0)), RESIDENT, RESIDENT, RESIDENT, RESIDENT, RESIDENT, RESIDENT, RESIDENT, RESIDENT,
             RESIDENT, RESIDENT,
         ],
-        [RESIDENT] * 9,
-        [pltpu.VMEM((count, D), f32)] * 3
+        [RESIDENT] * 10,
+        [pltpu.VMEM((count, D), f32), pltpu.VMEM((count, 1), f32)] + [pltpu.VMEM((count, D), f32)] * 2
         + [pltpu.VMEM((count, D), bf16), pltpu.VMEM((D, count), bf16), pltpu.VMEM((count, D), bf16)]
         + [pltpu.VMEM((FEED_PACK, D), bf16), shape_of((8, D), f32), shape_of((D, D), bf16)],
         [pltpu.VMEM((count, TILE), bf16)] * 2,
         room=OWN_ROOM,
     )(
-        place, in_hbm(attended), in_hbm(merged), in_hbm(cotangent), live, proj_bias, gain, bias, params, proj,
+        place, in_hbm(attended), in_hbm(merged), in_hbm(cotangent), live, proj_bias, gain, bias, down_bias, params, proj,
         near, far, up, down,
     )
 
@@ -644,7 +657,7 @@
 
 
 def feed_near_body(
-    place, residual_ref, second_ref, turned_ref, branch_ref, total_in, back_in, down_bias, norm_gain, params_ref,
+    place, hat_ref, inverse_ref, second_ref, turned_ref, branch_ref, total_in, back_in, norm_gain, params_ref,
     sums_in, near_ref, attended_ref,
     out_ref, grad_residual_ref, attn_ref, keep_ref, proj_send, proj_keep, sums_ref,
     total_s, back_s, active_s, raise_s, attended_s, proj_s, sem,
@@ -657,6 +670,7 @@
     def _():
         fetch.start()
         sums_ref[...] = sums_in[...]
+        total_s[...] = jnp.zeros_like(total_s)
         shard = 2 * (1 - tp) + core
         bias = params_ref[2:3, pl.ds(pl.multiple_of(TILE * shard, TILE), TILE)]
         sums_ref[pl.ds(shard, 1), :] = feed_tile(
@@ -667,9 +681,8 @@
     @pl.when(step >= 1)
     def _():
         here = pl.ds(pl.multiple_of((step - 1) * ROWS, 16), ROWS)
-        residual = residual_ref[here, :]
-        out_ref[...] = (residual + down_bias[...] + total_in[here, :] + total_s[here, :]).astype(bf16)
-        hat, inverse = normalize(residual)
+        out_ref[...] = (total_in[here, :] + total_s[here, :]).astype(bf16)
+        hat, inverse = hat_ref[here, :], inverse_ref[here, :]
         grad_second = back_in[here, :] + back_s[here, :]
         grad_residual = branch_ref[here, :].astype(f32) + norm_back(grad_second * norm_gain[...], hat, inverse)
         grad_residual_ref[here, :] = grad_residual
@@ -689,8 +702,8 @@
                 target[PROJ_PACK * other : PROJ_PACK * (other + 1), :] = proj_s[rows, :]
 
 
-def feed_near(place, residual, second, turned, branch, total, back, down_bias, gain, params, sums, near, attended):
-    count = residual.shape[0]
+def feed_near(place, hat, inverse, second, turned, branch, total, back, gain, params, sums, near, attended):
+    count = hat.shape[0]
     blocks = count // ROWS
 
     def given(columns):
@@ -709,7 +722,7 @@
         + [pltpu.VMEM((count, D), bf16), pltpu.VMEM((D, D), bf16), pltpu.SemaphoreType.DMA],
         room=NEAR_ROOM,
     )(
-        place, residual, second, turned, branch, total, back, down_bias, gain, params, sums, near, in_hbm(attended)
+        place, hat, inverse, second, turned, branch, total, back, gain, params, sums, near, in_hbm(attended)
     )
 
 
@@ -848,7 +861,7 @@
         [RESIDENT] * 3,
         [pltpu.VMEM((2 * QKV_PACK, D), bf16)] * 2 + [pltpu.VMEM((count, MERGE_IN), bf16)],
         [pltpu.VMEM((D, D), bf16), pltpu.VMEM((D, count), bf16), pltpu.SemaphoreType.DMA],
-        room=12,
+        room=9,
     )(place, after, first, stack, in_hbm(hat))
 
 
@@ -898,7 +911,7 @@
         scratch_shapes=[
             pltpu.VMEM((HEADS, KEYS, 256), f32), pltpu.VMEM((32, D), f32), pltpu.VMEM((MERGE_IN, D), f32),
         ],
-        compiler_params=pltpu.CompilerParams(vmem_limit_bytes=20 * 1024 * 1024),
+        compiler_params=pltpu.CompilerParams(vmem_limit_bytes=14 * 1024 * 1024),
         cost_estimate=COST,
     )(place, after, low, hat, merge, params, column, feed_sums, sums, vectors, position)
 
@@ -922,7 +935,7 @@
         [pltpu.HBM((count, MERGE_IN), bf16), shape_of((8, 128), f32)],
         flops=2 * count * D * MERGE_IN,
         moved=count * 5 * MERGE_IN,
-        room=24,
+        room=16,
     )(after, in_hbm(low), in_hbm(hat), inverse, merge, params)
 
 
@@ -1151,7 +1164,7 @@
         after,
         parts,
         scratch=[pltpu.VMEM((FEED_PACK + PROJ_PACK, D), bf16)],
-        room=24,
+        room=14,
     )
 
 
@@ -1329,7 +1342,7 @@
         kernel_place, first, flat_qkv, qkv_near, qkv_far, params, position, mask
     )
     rows = [row[None] for row in (proj_bias, norm2_gain, norm2_bias, down_bias)]
-    residual, total, back, second, turned, branch, own_send, feed_sums, proj_full = feed_own(
+    second_hat, second_inverse, total, back, second, turned, branch, own_send, feed_sums, proj_full = feed_own(
         kernel_place, attended, merged, cotangent, live, *rows, params, proj_weight, qkv_near, qkv_far,
         up_weight, down_weight,
     )
@@ -1340,7 +1353,7 @@
         False, kernel_place, second, turned, branch, total, back, params, feed_sums, (feed_far_piece,)
     )
     block_out, grad_residual, attn, other_keep, proj_send, proj_keep, feed_sums = feed_near(
-        kernel_place, residual, second, turned, branch, total, back, rows[3], rows[1], params, feed_sums, feed_near_piece,
+        kernel_place, second_hat, second_inverse, second, turned, branch, total, back, rows[1], params, feed_sums, feed_near_piece,
         attended,
     )
     after = feed_sums
@@ -1380,21 +1393,21 @@
         to_y, to_x, to_both, merge_kept = stage(
             merge_first_body, place, qkv_sum, (144,) * 4, merge_keep, merge_got, scratch=[pltpu.VMEM((SUMS, D), f32)]
         )
+        (feed_mine,) = stage(beside_body, place, to_y, (span * along,), *feed_all)
+        feed_beside = ring.x(feed_mine)
         last_span = 320 // along
         last_parts = stage(
-            last_second_body, place, to_y, (last_span + 16,) * along, qkv_sum,
+            last_second_body, place, feed_mine, (last_span + 16,) * along, qkv_sum,
             merge_kept, ring.y(to_y), ring.x(to_x), ring.xy(to_both),
         )
         last_got = [ring.z(last_parts[step], step) for step in range(1, along)]
-        section_grad, token = section_back(last_parts[0], low, hat, inverse, merge_full, params)
-        (feed_mine,) = stage(beside_body, place, token, (span * along,), *feed_all)
-        feed_beside = ring.x(feed_mine)
         last_total, vectors = stage(
-            merge_total_body, place, feed_mine, (last_span, 16), *([last_parts[0]] + last_got), cost=LONG
+            merge_total_body, place, last_parts[0], (last_span, 16), *([last_parts[0]] + last_got), cost=LONG
         )
         last_all = [last_total] + [ring.z(last_total, step) for step in range(1, along)]
+        section_grad, token = section_back(last_total, low, hat, inverse, merge_full, params)
         (last_near,) = stage(
-            last_beside_body, place, feed_beside, (336,), vectors, *last_all, cost=LONG
+            last_beside_body, place, (token, feed_beside), (336,), vectors, *last_all, cost=LONG
         )
         last_far = ring.x(last_near)
         feed_cores = ring.core(feed_mine), ring.core(feed_beside)

time: 196 us -> 192 us (0.980)
  local copies, waits for them, and re-layouts: 2.63 us -> 0.1 us
  waiting for transfers between devices: 22.8 us -> 25.1 us
  Pallas kernels: 125 us -> 123 us
    ppermute x3, waiting for transfers between devices: 6.06 us -> 2.58 us  [xy(): return lax.ppermute(array, ('rows', 'tp'), pairs)]
    ppermute x29, waiting for transfers between devices: 14.2 us -> 17.6 us  [to(): lax.ppermute(array, 'rows', [(i, i ^ bits) for i in range(self.rows_size)])]
    unnamed x54 -> x38, local copies, waits for them, and re-layouts: 2.63 us -> 0.1 us
    ppermute x7, waiting for transfers between devices: 2.57 us -> 4.9 us  [y(): return lax.ppermute(array, 'tp', [(0, 1), (1, 0)])]
where the time goes in v2:
time: 192 us; the launch traced here: 189 us
  Pallas kernels  123 us (64%)
  starting transfers between devices  39.4 us (21%)
  waiting for transfers between devices  25.1 us (13%)
    ppermute x29, starting transfers between devices, to(): lax.ppermute(array, 'rows', [(i, i ^ bits) for i in range(self.rows_size)])  26.1 us
    pallas_call x1, Pallas kernels, attend_back(): kernel_call(attend_back_body, (count // ROWS,), [ANYWHERE, RESIDENT, by_w...  18.5 us
    ppermute x29, waiting for transfers between devices, to(): lax.ppermute(array, 'rows', [(i, i ^ bits) for i in range(self.rows_size)])  17.6 us
    pallas_call x13, Pallas kernels, plain_call_after(): pl.pallas_call(without_after, in_specs=[SCALARS] + [pl.BlockSpec(memory_s...  16.3 us
    pallas_call x2, Pallas kernels, feed_middle(): pl.pallas_call(partial(feed_middle_body, own), in_specs=[SCALARS] + [RESI...  13.9 us
    pallas_call x1, Pallas kernels, feed_near(): kernel_call(feed_near_body, (blocks + 1,), [SCALARS] + [RESIDENT] * 9 + [...  12.7 us
    pallas_call x1, Pallas kernels, attend(): kernel_call(attend_body, (count // ROWS,), [SCALARS, RESIDENT, RESIDENT,...  12.4 us
    pallas_call x1, Pallas kernels, feed_own(): kernel_call(feed_own_body, (blocks + 1,), [SCALARS, taken(D), taken(D), t...  12.1 us
  transfers between devices with their start and end apart: 39, of which 12 were waited for; matrix products, arithmetic and copies ran while one was open for 0% of the time, Pallas kernels for 61%

profile of v2, /device:TPU:0, one launch (start us, length us, event | category | flops | bytes accessed | tf_op | source)
XLA Modules:
  0.0 188.9 jit_solution(10862508010158925210)
XLA Ops:
  0.7 1.5 shard_map.322.after
  2.3 3.0 %collective-permute-start.1 = (bf16[256,512]{1,0:T(8,128)(2,1)S(1)}, bf16[256,512]{1,0:T(8,128)(2,1)S(1)}, u32[]{:S(2)}, u32[]{:S(2)}) collective-permute-start(bf16[256,512]{1,0:T(8,128)(2,1)S(1)} %shard_map.322.after), channel_id=1, source_target_pairs={{0,1},{1,0},{2,3},{3,2},{4,5},{5,4},{6,7},{7,6},{8,9},{9,8},{10,11... | collective-permute-start | bytes 786440 | tf_op jit(solution)/shard_map/ppermute | solution.py:1030
  5.3 1.4 shard_map.323
  6.8 1.5 shard_map.324
  8.3 1.6 shard_map.325.array_ref
  9.9 2.4 %collective-permute-done.refs_0_.others_ref = bf16[32,512]{1,0:T(8,128)(2,1)S(1)} collective-permute-done((bf16[32,512]{1,0:T(8,128)(2,1)S(1)}, bf16[32,512]{1,0:T(8,128)(2,1)S(1)}, u32[]{:S(2)}, u32[]{:S(2)}) %collective-permute-start) | collective-permute-done | bytes 32800 | tf_op jit(solution)/shard_map/ppermute | solution.py:1030
  12.3 1.7 collective-permute-start.3
  14.0 3.0 %shard_map.327 = (bf16[1600,1024]{1,0:T(8,128)(2,1)S(1)}, f32[1600,1]{1,0:T(8,128)S(1)}) custom-call(bf16[512,512]{1,0:T(8,128)(2,1)S(1)} %shard_map.326.after, bf16[1600,1024]{1,0:T(8,128)(2,1)} %rows_ref.1), custom_call_target="tpu_custom_call" | custom-call | flops 1 | bytes 1 | tf_op jit(solution)/shard_map/pallas_call | solution.py:332
  17.1 6.0 %shard_map.328 = (f32[1600,512]{1,0:T(8,128)}, bf16[1600,512]{1,0:T(8,128)(2,1)S(1)}, bf16[1600,512]{1,0:T(8,128)(2,1)}, bf16[1024,512]{1,0:T(8,128)(2,1)}, f32[24,2048]{1,0:T(8,128)S(1)}, /*index=5*/f32[1024,128]{1,0:T(8,128)}) custom-call(s32[4]{0:T(128)S(1)} %pad_add_fusion.place, bf16[1600,1024]{1,0:T(8,128)(2,1)S(1)} %get-tuple-element.118.hat_ref, ...), custom_call_target="tpu_custom_call" | custom-call | flops 1 | bytes 1 | tf_op jit(solution)/shard_map/pallas_call | solution.py:393
  23.1 1.9 %shard_map.329 = (f32[4,112,512]{2,1,0:T(8,128)S(1)}, bf16[1600,1024]{1,0:T(8,128)(2,1)}) custom-call(f32[24,2048]{1,0:T(8,128)S(1)} %get-tuple-element.120.params_ref, bf16[1600,1024]{1,0:T(8,128)(2,1)S(1)} %get-tuple-element.118.hat_ref), custom_call_target="tpu_custom_call" | custom-call | flops 1 | bytes 1 | tf_op jit(solution)/shard_map/pallas_call | solution.py:977
  25.4 0.6 shard_map.333
  26.1 1.5 collective-permute-start.5
  27.6 1.9 %collective-permute-done.4.far_ref = bf16[512,512]{1,0:T(8,128)(2,1)S(1)} collective-permute-done((bf16[512,512]{1,0:T(8,128)(2,1)S(1)}, bf16[512,512]{1,0:T(8,128)(2,1)S(1)}, u32[]{:S(2)}, u32[]{:S(2)}) %collective-permute-start.4) | collective-permute-done | bytes 524320 | tf_op jit(solution)/shard_map/ppermute | solution.py:1018
  29.5 12.4 %shard_map.330 = (bf16[16,128,1536]{2,1,0:T(8,128)(2,1)}, bf16[16,4,112,512]{3,2,1,0:T(8,128)(2,1)}, bf16[1600,512]{1,0:T(8,128)(2,1)}, bf16[16,112,512]{2,1,0:T...) custom-call(s32[4]{0:T(128)S(1)} %pad_add_fusion.place, ...), custom_call_target="tpu_custom_call" | custom-call | flops 1 | bytes 1 | tf_op jit(solution)/shard_map/pallas_call | solution.py:486
  41.9 12.1 %shard_map.331 = (f32[1600,512]{1,0:T(8,128)S(1)}, f32[1600,1]{1,0:T(8,128)S(1)}, f32[1600,512]{1,0:T(8,128)S(1)}, f32[1600,512]{1,0:T(8,128)S(1)}, bf16[1600,51...) custom-call(s32[4]{0:T(128)S(1)} %pad_add_fusion.place, ...), custom_call_target="tpu_custom_call" | custom-call | flops 1 | bytes 1 | tf_op jit(solution)/shard_map/pallas_call | solution.py:606
  54.7 6.6 %shard_map.332 = (f32[1600,512]{1,0:T(8,128)S(1)}, f32[1600,512]{1,0:T(8,128)S(1)}, bf16[1024,512]{1,0:T(8,128)(2,1)S(1)}, f32[8,512]{1,0:T(8,128)S(1)}) custom-call(s32[4]{0:T(128)S(1)} %pad_add_fusion.place, bf16[1600,512]{1,0:T(8,128)(2,1)S(1)} %get-tuple-element.127.second_ref, ...), custom_call_target="tpu_custom_call", output_to_operand_aliasing={{0}: (4, {}), {1}: (5, {})} | custom-call | flops 999999995904 | bytes 1 | tf_op jit(solution)/shard_map/pallas_call | solution.py:647
  61.2 7.3 %shard_map.334 = (f32[1600,512]{1,0:T(8,128)S(1)}, f32[1600,512]{1,0:T(8,128)S(1)}, bf16[1024,512]{1,0:T(8,128)(2,1)S(1)}, f32[8,512]{1,0:T(8,128)S(1)}) custom-call(s32[4]{0:T(128)S(1)} %pad_add_fusion.place, bf16[1600,512]{1,0:T(8,128)(2,1)S(1)} %get-tuple-element.127.second_ref, ...), custom_call_target="tpu_custom_call", output_to_operand_aliasing={{0}: (4, {}), {1}: (5, {})} | custom-call | flops 1 | bytes 1 | tf_op jit(solution)/shard_map/pallas_call | solution.py:647
  68.7 12.7 %shard_map.335 = (bf16[1600,512]{1,0:T(8,128)(2,1)}, f32[1600,512]{1,0:T(8,128)S(1)}, bf16[1600,512]{1,0:T(8,128)(2,1)S(1)}, bf16[1024,512]{1,0:T(8,128)(2,1)S(1...) custom-call(s32[4]{0:T(128)S(1)} %pad_add_fusion.place, ...), custom_call_target="tpu_custom_call" | custom-call | flops 1 | bytes 1 | tf_op jit(solution)/shard_map/pallas_call | solution.py:712
  81.9 1.2 collective-permute-done.9.refs_6_
  83.1 1.8 shard_map.336
  84.8 1.6 collective-permute-start.11
  86.4 0.6 collective-permute-start.12
  87.0 1.4 collective-permute-start.10
  88.4 18.5 %shard_map.337 = (bf16[1600,1536]{1,0:T(8,128)(2,1)S(1)}, bf16[1600,512]{1,0:T(8,128)(2,1)S(1)}, f32[1,1536]{1,0:T(1,128)S(1)}, f32[8,512]{1,0:T(8,128)S(1)}, f3...) custom-call(bf16[576,512]{1,0:T(8,128)(2,1)S(1)} %get-tuple-element.147.after, ...), custom_call_target="tpu_custom_call" | custom-call | flops 1 | bytes 1 | tf_op jit(solution)/shard_map/pallas_call | solution.py:801
  107.0 5.7 %shard_map.338 = (bf16[768,512]{1,0:T(8,128)(2,1)}, bf16[768,512]{1,0:T(8,128)(2,1)S(1)}, bf16[1600,1024]{1,0:T(8,128)(2,1)S(1)}) custom-call(s32[4]{0:T(128)S(1)} %pad_add_fusion.place, f32[1,1536]{1,0:T(1,128)S(1)} %get-tuple-element.157.after.qkv_sums_ref, bf16[1600,512]{1,0:T(8,128)(2,1)S(1)} %get-tuple-element.158.first_ref, ...), custom_call_target="tpu_custom_call" | custom-call | flops 1 | bytes 1 | tf_op jit(solution)/shard_map/pallas_call | solution.py:857
  113.3 1.4 collective-permute-done.10.refs_2_
  114.7 0.8 shard_map.339
  115.5 1.5 collective-permute-start.14
  117.0 2.6 %collective-permute-start.15 = (bf16[144,512]{1,0:T(8,128)(2,1)S(1)}, bf16[144,512]{1,0:T(8,128)(2,1)S(1)}, u32[]{:S(2)}, u32[]{:S(2)}) collective-permute-start(bf16[144,512]{1,0:T(8,128)(2,1)S(1)} %get-tuple-element.176), channel_id=1, source_target_pairs={{0,16},{2,18},{4,20},{6,22},{8,24},{10,26},{12,28},{14,30},{16,0},... | collective-permute-start | bytes 442376 | tf_op jit(solution)/shard_map/ppermute | solution.py:1018
  120.0 2.0 %shard_map.340 = (bf16[192,512]{1,0:T(8,128)(2,1)}, bf16[192,512]{1,0:T(8,128)(2,1)}, bf16[192,512]{1,0:T(8,128)(2,1)}, bf16[192,512]{1,0:T(8,128)(2,1)S(1)}) custom-call(s32[4]{0:T(128)S(1)} %pad_add_fusion.place, bf16[144,512]{1,0:T(8,128)(2,1)S(1)} %get-tuple-element.165.refs_0_.refs_1_, bf16[768,512]{1,0:T(8,128)(2,1)S(1)} %get-tuple-element.166.refs_1_, ...), custom_call_target="tpu_custom_call" | custom-call | flops 1 | bytes 1 | tf_op jit(solution)/shard_map/pallas_call | solution.py:249
  122.0 1.4 collective-permute-start.18
  123.4 1.5 collective-permute-start.17
  124.9 5.2 %shard_map.341 = (bf16[544,512]{1,0:T(8,128)(2,1)}, bf16[544,512]{1,0:T(8,128)(2,1)S(1)}) custom-call(s32[4]{0:T(128)S(1)} %pad_add_fusion.place, bf16[192,512]{1,0:T(8,128)(2,1)} %get-tuple-element.167.after, bf16[1600,512]{1,0:T(8,128)(2,1)S(1)} %get-tuple-element.168.low_ref, bf16[1600,1024]{1,0:T(8,128)(2,1)S(1)} %get-tuple-element.169.hat_ref, ...), custom_call_target="tpu_custom_call" | custom-call | flops 1 | bytes 1 | tf_op jit(solution)/shard_map/pallas_call | solution.py:906
  130.1 0.6 collective-permute-start.19
  130.6 0.6 shard_map.342.refs_0_.refs_1_
  131.3 3.6 %collective-permute-start.23 = (bf16[144,512]{1,0:T(8,128)(2,1)S(1)}, bf16[144,512]{1,0:T(8,128)(2,1)S(1)}, u32[]{:S(2)}, u32[]{:S(2)}) collective-permute-start(bf16[144,512]{1,0:T(8,128)(2,1)S(1)} %shard_map.342.refs_0_.refs_1_), channel_id=1, source_target_pairs={{0,24},{2,26},{4,28},{6,30},{8,16},{10,18},{12,20},{14,22},{16,8},... | collective-permute-start | bytes 442376 | tf_op jit(solution)/shard_map/ppermute | solution.py:1018
  134.9 2.1 %collective-permute-done.19.refs_4_ = bf16[192,512]{1,0:T(8,128)(2,1)} collective-permute-done((bf16[192,512]{1,0:T(8,128)(2,1)}, bf16[192,512]{1,0:T(8,128)(2,1)}, u32[]{:S(2)}, u32[]{:S(2)}) %collective-permute-start.19) | collective-permute-done | bytes 196640 | tf_op jit(solution)/shard_map/ppermute | solution.py:1034
  136.9 0.7 collective-permute-start.21
  137.6 1.2 shard_map.343.refs_0_.refs_1_
  138.9 1.2 shard_map.344
  140.1 0.6 collective-permute-start.25
  140.7 1.4 collective-permute-start.26
  142.2 1.5 collective-permute-start.24
  143.7 3.5 %collective-permute-done.22.refs_3_ = bf16[144,512]{1,0:T(8,128)(2,1)S(1)} collective-permute-done((bf16[144,512]{1,0:T(8,128)(2,1)S(1)}, bf16[144,512]{1,0:T(8,128)(2,1)S(1)}, u32[]{:S(2)}, u32[]{:S(2)}) %collective-permute-start.22) | collective-permute-done | bytes 147488 | tf_op jit(solution)/shard_map/ppermute | solution.py:1018
  147.2 1.4 shard_map.345.refs_0_.refs_1_
  148.6 0.8 collective-permute-done.24.refs_3_
  149.3 0.6 shard_map.346
  150.0 1.8 collective-permute-start.27
  151.8 2.3 %collective-permute-start.28 = (bf16[96,512]{1,0:T(8,128)(2,1)S(1)}, bf16[96,512]{1,0:T(8,128)(2,1)S(1)}, u32[]{:S(2)}, u32[]{:S(2)}) collective-permute-start(bf16[96,512]{1,0:T(8,128)(2,1)S(1)} %get-tuple-element.188), channel_id=1, source_target_pairs={{0,16},{2,18},{4,20},{6,22},{8,24},{10,26},{12,28},{14,30},{16,0},... | collective-permute-start | bytes 294920 | tf_op jit(solution)/shard_map/ppermute | solution.py:1018
  154.4 1.5 collective-permute-start.30
  155.9 5.0 %collective-permute-done.28.refs_3_ = bf16[96,512]{1,0:T(8,128)(2,1)S(1)} collective-permute-done((bf16[96,512]{1,0:T(8,128)(2,1)S(1)}, bf16[96,512]{1,0:T(8,128)(2,1)S(1)}, u32[]{:S(2)}, u32[]{:S(2)}) %collective-permute-start.28) | collective-permute-done | bytes 98336 | tf_op jit(solution)/shard_map/ppermute | solution.py:1018
  161.0 0.6 shard_map.347
  161.6 2.5 %collective-permute-start.33 = (bf16[80,512]{1,0:T(8,128)(2,1)S(1)}, bf16[80,512]{1,0:T(8,128)(2,1)S(1)}, u32[]{:S(2)}, u32[]{:S(2)}) collective-permute-start(bf16[80,512]{1,0:T(8,128)(2,1)S(1)} %get-tuple-element.190.after.refs_3_), channel_id=1, source_target_pairs={{0,24},{2,26},{4,28},{6,30},{8,16},{10,18},{12,20},{14,22},{16,8},... | collective-permute-start | bytes 245768 | tf_op jit(solution)/shard_map/ppermute | solution.py:1018
  164.1 0.6 collective-permute-start.32
  164.7 1.3 collective-permute-start.31
  166.0 6.8 %shard_map.348 = (bf16[1600,1024]{1,0:T(8,128)(2,1)}, f32[8,128]{1,0:T(8,128)S(1)}) custom-call(bf16[80,512]{1,0:T(8,128)(2,1)S(1)} %get-tuple-element.190.after.refs_3_, bf16[1600,512]{1,0:T(8,128)(2,1)} %copy-done.3, bf16[1600,1024]{1,0:T(8,128)(2,1)} %get-tuple-element.160.hat_in.hat_ref, f32[1600,1]{1,0:T(8,128)S(1)} %get-tuple-element.191.inverse_ref, ...), custom_call_target="tpu_custom_call" | custom-call | flops 1 | bytes 1 | tf_op jit(solution)/shard_map/pallas_call | solution.py:927
  172.8 0.5 collective-permute-start.35
  173.4 0.6 shard_map.349.refs_0_.mine
  173.9 1.5 collective-permute-start.36
  175.5 4.2 %shard_map.350 = (f32[1024,512]{1,0:T(8,128)}, f32[512,1024]{1,0:T(8,128)}, f32[256,512]{1,0:T(8,128)}, f32[8,128]{1,0:T(8,128)S(1)}) custom-call(s32[4]{0:T(128)S(1)} %pad_add_fusion.place, bf16[336,512]{1,0:T(8,128)(2,1)S(1)} %shard_map.349.refs_0_.mine, bf16[576,512]{1,0:T(8,128)(2,1)} %shard_map.345.refs_0_.refs_1_, ...), custom_call_target="tpu_custom_call" | custom-call | flops 1 | bytes 1 | tf_op jit(solution)/shard_map/pallas_call | solution.py:249
  179.7 4.3 %collective-permute-done.36.refs_1_ = bf16[336,512]{1,0:T(8,128)(2,1)S(1)} collective-permute-done((bf16[336,512]{1,0:T(8,128)(2,1)S(1)}, bf16[336,512]{1,0:T(8,128)(2,1)S(1)}, u32[]{:S(2)}, u32[]{:S(2)}) %collective-permute-start.36) | collective-permute-done | bytes 344096 | tf_op jit(solution)/shard_map/ppermute | solution.py:1018
  184.0 0.6 shard_map.351.beside
  184.6 1.6 collective-permute-done.38.core_beside
  186.3 2.3 %shard_map.352 = (f32[3,512,256]{2,1,0:T(8,128)}, f32[512,512]{1,0:T(8,128)}, f32[1,512]{1,0:T(1,128)}, f32[1,512]{1,0:T(1,128)}, f32[1,512]{1,0:T(1,128)}, /*in...) custom-call(s32[4]{0:T(128)S(1)} %pad_add_fusion.place, ...), custom_call_target="tpu_custom_call" | custom-call | flops 1 | bytes 1 | tf_op jit(solution)/shard_map/pallas_call | solution.py:196
  (84 shorter events, 3.3 us)
Async XLA Ops:
  2.3 10.0 %collective-permute-start.1 = (bf16[256,512]{1,0:T(8,128)(2,1)S(1)}, bf16[256,512]{1,0:T(8,128)(2,1)S(1)}, u32[]{:S(2)}, u32[]{:S(2)}) collective-permute-start(bf16[256,512]{1,0:T(8,128)(2,1)S(1)} %shard_map.322.after), channel_id=1, source_target_pairs={{0,1},{1,0},{2,3},{3,2},{4,5},{5,4},{6,7},{7,6},{8,9},{9,8},{10,11... | collective-permute-start | bytes 786440 | tf_op jit(solution)/shard_map/ppermute | solution.py:1030
  6.7 5.6 %collective-permute-start = (bf16[32,512]{1,0:T(8,128)(2,1)S(1)}, bf16[32,512]{1,0:T(8,128)(2,1)S(1)}, u32[]{:S(2)}, u32[]{:S(2)}) collective-permute-start(bf16[32,512]{1,0:T(8,128)(2,1)S(1)} %get-tuple-element.117), channel_id=1, source_target_pairs={{0,1},{1,0},{2,3},{3,2},{4,5},{5,4},{6,7},{7,6},{8,9},{9,8},{10,11... | collective-permute-start | bytes 98312 | tf_op jit(solution)/shard_map/ppermute | solution.py:1030
  8.2 8.8 %copy-start.9 = (bf16[512,512]{1,0:T(8,128)(2,1)S(1)}, bf16[512,512]{1,0:T(8,128)(2,1)}, u32[]{:S(2)}) copy-start(bf16[512,512]{1,0:T(8,128)(2,1)} %own_ref.1) | copy-start | bytes 1572868
  8.3 8.8 %copy-start.13 = (f32[512]{0:T(512)S(1)}, f32[512]{0:T(512)}, u32[]{:S(2)}) copy-start(f32[512]{0:T(512)} %param.25) | copy-start | bytes 6148
  8.3 8.8 %copy-start.15 = (f32[512]{0:T(512)S(1)}, f32[512]{0:T(512)}, u32[]{:S(2)}) copy-start(f32[512]{0:T(512)} %param.26) | copy-start | bytes 6148
  12.3 13.1 %collective-permute-start.3 = (bf16[512,512]{1,0:T(8,128)(2,1)S(1)}, bf16[512,512]{1,0:T(8,128)(2,1)S(1)}, u32[]{:S(2)}, u32[]{:S(2)}) collective-permute-start(bf16[512,512]{1,0:T(8,128)(2,1)S(1)} %shard_map.326.after), channel_id=1, source_target_pairs={{0,1},{1,0},{2,3},{3,2},{4,5},{5,4},{6,7},{7,6},{8,9},{9,8},{10,11... | collective-permute-start | bytes 1572872 | tf_op jit(solution)/shard_map/ppermute | solution.py:1030
  14.0 3.0 %collective-permute-start.2 = (bf16[256,512]{1,0:T(8,128)(2,1)S(1)}, bf16[256,512]{1,0:T(8,128)(2,1)S(1)}, u32[]{:S(2)}, u32[]{:S(2)}) collective-permute-start(bf16[256,512]{1,0:T(8,128)(2,1)S(1)} %collective-permute-done.1.refs_1_.near_ref), channel_id=1, source_target_pairs={{0,2},{2,0},{4,6},{6,4},{8,10},{10,8},{12,14},{14,12},{16,18},{18,... | collective-permute-start | bytes 786440 | tf_op jit(solution)/shard_map/ppermute | solution.py:1018
  17.1 8.3 %copy-start.4 = (bf16[512,1024]{1,0:T(8,128)(2,1)S(1)}, bf16[512,1024]{1,0:T(8,128)(2,1)}, u32[]{:S(2)}) copy-start(bf16[512,1024]{1,0:T(8,128)(2,1)} %refs_2_.1) | copy-start | bytes 3145732
  17.1 8.3 %copy-start.5 = (bf16[1024,512]{1,0:T(8,128)(2,1)S(1)}, bf16[1024,512]{1,0:T(8,128)(2,1)}, u32[]{:S(2)}) copy-start(bf16[1024,512]{1,0:T(8,128)(2,1)} %refs_3_.1) | copy-start | bytes 3145732
  23.1 45.6 %copy-start = (f32[24,2048]{1,0:T(8,128)}, f32[24,2048]{1,0:T(8,128)S(1)}, u32[]{:S(2)}) copy-start(f32[24,2048]{1,0:T(8,128)S(1)} %get-tuple-element.120.params_ref) | copy-start | bytes 589828
  23.1 6.4 %copy-start.8 = (bf16[3,512,256]{2,1,0:T(8,128)(2,1)S(1)}, bf16[3,512,256]{2,1,0:T(8,128)(2,1)}, u32[]{:S(2)}) copy-start(bf16[3,512,256]{2,1,0:T(8,128)(2,1)} %param.27) | copy-start | bytes 2359300
  26.0 15.9 %copy-start.10 = (bf16[256,512]{1,0:T(8,128)(2,1)S(1)}, bf16[256,512]{1,0:T(8,128)(2,1)}, u32[]{:S(2)}) copy-start(bf16[256,512]{1,0:T(8,128)(2,1)} %proj_own.1) | copy-start | bytes 786436
  26.0 15.9 %copy-start.12 = (f32[512]{0:T(512)S(1)}, f32[512]{0:T(512)}, u32[]{:S(2)}) copy-start(f32[512]{0:T(512)} %param.32) | copy-start | bytes 6148
  26.1 15.9 %copy-start.16 = (f32[512]{0:T(512)S(1)}, f32[512]{0:T(512)}, u32[]{:S(2)}) copy-start(f32[512]{0:T(512)} %param.31) | copy-start | bytes 6148
  26.1 15.9 %copy-start.17 = (f32[512]{0:T(512)S(1)}, f32[512]{0:T(512)}, u32[]{:S(2)}) copy-start(f32[512]{0:T(512)} %param.33) | copy-start | bytes 6148
  26.1 15.9 %copy-start.18 = (f32[512]{0:T(512)S(1)}, f32[512]{0:T(512)}, u32[]{:S(2)}) copy-start(f32[512]{0:T(512)} %param.37) | copy-start | bytes 6148
  26.1 28.2 %collective-permute-start.5 = (bf16[1024,512]{1,0:T(8,128)(2,1)S(1)}, bf16[1024,512]{1,0:T(8,128)(2,1)}, u32[]{:S(2)}, u32[]{:S(2)}) collective-permute-start(bf16[1024,512]{1,0:T(8,128)(2,1)S(1)} %shard_map.333), channel_id=1, source_target_pairs={{0,1},{1,0},{2,3},{3,2},{4,5},{5,4},{6,7},{7,6},{8,9},{9,8},{10,11... | collective-permute-start | bytes 3145736 | tf_op jit(solution)/shard_map/ppermute | solution.py:1030
  27.6 1.9 %collective-permute-start.4 = (bf16[512,512]{1,0:T(8,128)(2,1)S(1)}, bf16[512,512]{1,0:T(8,128)(2,1)S(1)}, u32[]{:S(2)}, u32[]{:S(2)}) collective-permute-start(bf16[512,512]{1,0:T(8,128)(2,1)S(1)} %collective-permute-done.3.near_ref.refs_1_), channel_id=1, source_target_pairs={{0,2},{2,0},{4,6},{6,4},{8,10},{10,8},{12,14},{14,12},{16,18},{18,... | collective-permute-start | bytes 1572872 | tf_op jit(solution)/shard_map/ppermute | solution.py:1018
  54.1 27.8 %collective-permute-start.7 = (bf16[1024,512]{1,0:T(8,128)(2,1)}, bf16[1024,512]{1,0:T(8,128)(2,1)}, u32[]{:S(2)}, u32[]{:S(2)}) collective-permute-start(bf16[1024,512]{1,0:T(8,128)(2,1)} %get-tuple-element.142), channel_id=1, source_target_pairs={{0,2},{2,0},{4,6},{6,4},{8,10},{10,8},{12,14},{14,12},{16,18},{18,... | collective-permute-start | bytes 3145736 | tf_op jit(solution)/shard_map/ppermute | solution.py:1018
  54.3 6.9 %collective-permute-start.6 = (bf16[1024,512]{1,0:T(8,128)(2,1)}, bf16[1024,512]{1,0:T(8,128)(2,1)}, u32[]{:S(2)}, u32[]{:S(2)}) collective-permute-start(bf16[1024,512]{1,0:T(8,128)(2,1)} %collective-permute-done.5.near_ref), channel_id=1, source_target_pairs={{0,2},{2,0},{4,6},{6,4},{8,10},{10,8},{12,14},{14,12},{16,18},{18,... | collective-permute-start | bytes 3145736 | tf_op jit(solution)/shard_map/ppermute | solution.py:1018
  68.5 14.5 %collective-permute-start.8 = (bf16[1024,512]{1,0:T(8,128)(2,1)S(1)}, bf16[1024,512]{1,0:T(8,128)(2,1)S(1)}, u32[]{:S(2)}, u32[]{:S(2)}) collective-permute-start(bf16[1024,512]{1,0:T(8,128)(2,1)S(1)} %get-tuple-element.144), channel_id=1, source_target_pairs={{0,2},{2,0},{4,6},{6,4},{8,10},{10,8},{12,14},{14,12},{16,18},{18,... | collective-permute-start | bytes 3145736 | tf_op jit(solution)/shard_map/ppermute | solution.py:1018
  81.4 7.0 %copy-start.14 = (f32[512]{0:T(512)S(1)}, f32[512]{0:T(512)}, u32[]{:S(2)}) copy-start(f32[512]{0:T(512)} %param.25) | copy-start | bytes 6148
  81.4 1.6 collective-permute-start.9
  84.8 28.0 %collective-permute-start.11 = (bf16[576,512]{1,0:T(8,128)(2,1)S(1)}, bf16[576,512]{1,0:T(8,128)(2,1)S(1)}, u32[]{:S(2)}, u32[]{:S(2)}) collective-permute-start(bf16[576,512]{1,0:T(8,128)(2,1)S(1)} %get-tuple-element.163), channel_id=1, source_target_pairs={{0,4},{2,6},{4,0},{6,2},{8,12},{10,14},{12,8},{14,10},{16,20},{18,... | collective-permute-start | bytes 1769480 | tf_op jit(solution)/shard_map/ppermute | solution.py:1018
  86.4 26.9 %collective-permute-start.12 = (bf16[576,512]{1,0:T(8,128)(2,1)S(1)}, bf16[576,512]{1,0:T(8,128)(2,1)S(1)}, u32[]{:S(2)}, u32[]{:S(2)}) collective-permute-start(bf16[576,512]{1,0:T(8,128)(2,1)S(1)} %get-tuple-element.164), channel_id=1, source_target_pairs={{0,5},{1,4},{2,7},{3,6},{4,1},{5,0},{6,3},{7,2},{8,13},{9,12},{10,... | collective-permute-start | bytes 1769480 | tf_op jit(solution)/shard_map/ppermute | solution.py:1034
  87.0 27.7 %collective-permute-start.10 = (bf16[576,512]{1,0:T(8,128)(2,1)S(1)}, bf16[576,512]{1,0:T(8,128)(2,1)S(1)}, u32[]{:S(2)}, u32[]{:S(2)}) collective-permute-start(bf16[576,512]{1,0:T(8,128)(2,1)S(1)} %get-tuple-element.147.after), channel_id=1, source_target_pairs={{0,1},{1,0},{2,3},{3,2},{4,5},{5,4},{6,7},{7,6},{8,9},{9,8},{10,11... | collective-permute-start | bytes 1769480 | tf_op jit(solution)/shard_map/ppermute | solution.py:1030
  107.0 17.9 %copy-start.3 = (bf16[1600,512]{1,0:T(8,128)(2,1)}, bf16[1600,512]{1,0:T(8,128)(2,1)S(1)}, u32[]{:S(2)}) copy-start(bf16[1600,512]{1,0:T(8,128)(2,1)S(1)} %get-tuple-element.168.low_ref) | copy-start | bytes 4915204
  112.7 7.2 %collective-permute-start.13 = (bf16[768,512]{1,0:T(8,128)(2,1)}, bf16[768,512]{1,0:T(8,128)(2,1)}, u32[]{:S(2)}, u32[]{:S(2)}) collective-permute-start(bf16[768,512]{1,0:T(8,128)(2,1)} %get-tuple-element.161.refs_0_), channel_id=1, source_target_pairs={{0,2},{2,0},{4,6},{6,4},{8,10},{10,8},{12,14},{14,12},{16,18},{18,... | collective-permute-start | bytes 2359304 | tf_op jit(solution)/shard_map/ppermute | solution.py:1018
  114.6 10.2 %copy-start.1 = (f32[24,2048]{1,0:T(8,128)S(1)}, f32[24,2048]{1,0:T(8,128)}, u32[]{:S(2)}) copy-start(f32[24,2048]{1,0:T(8,128)} %copy-done) | copy-start | bytes 589828
  114.7 10.2 %copy-start.6 = (bf16[1024,512]{1,0:T(8,128)(2,1)S(1)}, bf16[1024,512]{1,0:T(8,128)(2,1)}, u32[]{:S(2)}) copy-start(bf16[1024,512]{1,0:T(8,128)(2,1)} %get-tuple-element.170.merge_ref) | copy-start | bytes 3145732
  114.7 10.2 %copy-start.11 = (f32[1024,128]{1,0:T(8,128)S(1)}, f32[1024,128]{1,0:T(8,128)}, u32[]{:S(2)}) copy-start(f32[1024,128]{1,0:T(8,128)} %get-tuple-element.171.column_ref) | copy-start | bytes 1572868
  115.5 14.6 %collective-permute-start.14 = (bf16[144,512]{1,0:T(8,128)(2,1)S(1)}, bf16[144,512]{1,0:T(8,128)(2,1)S(1)}, u32[]{:S(2)}, u32[]{:S(2)}) collective-permute-start(bf16[144,512]{1,0:T(8,128)(2,1)S(1)} %get-tuple-element.175), channel_id=1, source_target_pairs={{0,8},{2,10},{4,12},{6,14},{8,0},{10,2},{12,4},{14,6},{16,24},{18,... | collective-permute-start | bytes 442376 | tf_op jit(solution)/shard_map/ppermute | solution.py:1018
  117.0 13.6 %collective-permute-start.15 = (bf16[144,512]{1,0:T(8,128)(2,1)S(1)}, bf16[144,512]{1,0:T(8,128)(2,1)S(1)}, u32[]{:S(2)}, u32[]{:S(2)}) collective-permute-start(bf16[144,512]{1,0:T(8,128)(2,1)S(1)} %get-tuple-element.176), channel_id=1, source_target_pairs={{0,16},{2,18},{4,20},{6,22},{8,24},{10,26},{12,28},{14,30},{16,0},... | collective-permute-start | bytes 442376 | tf_op jit(solution)/shard_map/ppermute | solution.py:1018
  119.6 11.0 %collective-permute-start.16 = (bf16[144,512]{1,0:T(8,128)(2,1)S(1)}, bf16[144,512]{1,0:T(8,128)(2,1)S(1)}, u32[]{:S(2)}, u32[]{:S(2)}) collective-permute-start(bf16[144,512]{1,0:T(8,128)(2,1)S(1)} %get-tuple-element.177), channel_id=1, source_target_pairs={{0,24},{2,26},{4,28},{6,30},{8,16},{10,18},{12,20},{14,22},{16,8},... | collective-permute-start | bytes 442376 | tf_op jit(solution)/shard_map/ppermute | solution.py:1018
  122.0 12.9 %collective-permute-start.18 = (bf16[192,512]{1,0:T(8,128)(2,1)}, bf16[192,512]{1,0:T(8,128)(2,1)}, u32[]{:S(2)}, u32[]{:S(2)}) collective-permute-start(bf16[192,512]{1,0:T(8,128)(2,1)} %get-tuple-element.179), channel_id=1, source_target_pairs={{0,4},{2,6},{4,0},{6,2},{8,12},{10,14},{12,8},{14,10},{16,20},{18,... | collective-permute-start | bytes 589832 | tf_op jit(solution)/shard_map/ppermute | solution.py:1018
  123.4 14.3 %collective-permute-start.17 = (bf16[192,512]{1,0:T(8,128)(2,1)}, bf16[192,512]{1,0:T(8,128)(2,1)}, u32[]{:S(2)}, u32[]{:S(2)}) collective-permute-start(bf16[192,512]{1,0:T(8,128)(2,1)} %get-tuple-element.167.after), channel_id=1, source_target_pairs={{0,1},{1,0},{2,3},{3,2},{4,5},{5,4},{6,7},{7,6},{8,9},{9,8},{10,11... | collective-permute-start | bytes 589832 | tf_op jit(solution)/shard_map/ppermute | solution.py:1030
  130.1 6.9 %collective-permute-start.19 = (bf16[192,512]{1,0:T(8,128)(2,1)}, bf16[192,512]{1,0:T(8,128)(2,1)}, u32[]{:S(2)}, u32[]{:S(2)}) collective-permute-start(bf16[192,512]{1,0:T(8,128)(2,1)} %get-tuple-element.180), channel_id=1, source_target_pairs={{0,5},{1,4},{2,7},{3,6},{4,1},{5,0},{6,3},{7,2},{8,13},{9,12},{10,... | collective-permute-start | bytes 589832 | tf_op jit(solution)/shard_map/ppermute | solution.py:1034
  130.6 8.2 %collective-permute-start.20 = (bf16[544,512]{1,0:T(8,128)(2,1)}, bf16[544,512]{1,0:T(8,128)(2,1)}, u32[]{:S(2)}, u32[]{:S(2)}) collective-permute-start(bf16[544,512]{1,0:T(8,128)(2,1)} %get-tuple-element.174.refs_0_), channel_id=1, source_target_pairs={{0,2},{2,0},{4,6},{6,4},{8,10},{10,8},{12,14},{14,12},{16,18},{18,... | collective-permute-start | bytes 1671176 | tf_op jit(solution)/shard_map/ppermute | solution.py:1018
  131.3 10.9 %collective-permute-start.23 = (bf16[144,512]{1,0:T(8,128)(2,1)S(1)}, bf16[144,512]{1,0:T(8,128)(2,1)S(1)}, u32[]{:S(2)}, u32[]{:S(2)}) collective-permute-start(bf16[144,512]{1,0:T(8,128)(2,1)S(1)} %shard_map.342.refs_0_.refs_1_), channel_id=1, source_target_pairs={{0,24},{2,26},{4,28},{6,30},{8,16},{10,18},{12,20},{14,22},{16,8},... | collective-permute-start | bytes 442376 | tf_op jit(solution)/shard_map/ppermute | solution.py:1018
  134.8 12.3 %collective-permute-start.22 = (bf16[144,512]{1,0:T(8,128)(2,1)S(1)}, bf16[144,512]{1,0:T(8,128)(2,1)S(1)}, u32[]{:S(2)}, u32[]{:S(2)}) collective-permute-start(bf16[144,512]{1,0:T(8,128)(2,1)S(1)} %shard_map.342.refs_0_.refs_1_), channel_id=1, source_target_pairs={{0,16},{2,18},{4,20},{6,22},{8,24},{10,26},{12,28},{14,30},{16,0},... | collective-permute-start | bytes 442376 | tf_op jit(solution)/shard_map/ppermute | solution.py:1018
  136.9 10.2 %collective-permute-start.21 = (bf16[144,512]{1,0:T(8,128)(2,1)S(1)}, bf16[144,512]{1,0:T(8,128)(2,1)S(1)}, u32[]{:S(2)}, u32[]{:S(2)}) collective-permute-start(bf16[144,512]{1,0:T(8,128)(2,1)S(1)} %shard_map.342.refs_0_.refs_1_), channel_id=1, source_target_pairs={{0,8},{2,10},{4,12},{6,14},{8,0},{10,2},{12,4},{14,6},{16,24},{18,... | collective-permute-start | bytes 442376 | tf_op jit(solution)/shard_map/ppermute | solution.py:1018
  140.1 8.5 %collective-permute-start.25 = (bf16[144,512]{1,0:T(8,128)(2,1)S(1)}, bf16[144,512]{1,0:T(8,128)(2,1)S(1)}, u32[]{:S(2)}, u32[]{:S(2)}) collective-permute-start(bf16[144,512]{1,0:T(8,128)(2,1)S(1)} %get-tuple-element.184), channel_id=1, source_target_pairs={{0,4},{2,6},{4,0},{6,2},{8,12},{10,14},{12,8},{14,10},{16,20},{18,... | collective-permute-start | bytes 442376 | tf_op jit(solution)/shard_map/ppermute | solution.py:1018
  140.7 7.9 %collective-permute-start.26 = (bf16[144,512]{1,0:T(8,128)(2,1)S(1)}, bf16[144,512]{1,0:T(8,128)(2,1)S(1)}, u32[]{:S(2)}, u32[]{:S(2)}) collective-permute-start(bf16[144,512]{1,0:T(8,128)(2,1)S(1)} %get-tuple-element.185), channel_id=1, source_target_pairs={{0,5},{1,4},{2,7},{3,6},{4,1},{5,0},{6,3},{7,2},{8,13},{9,12},{10,... | collective-permute-start | bytes 442376 | tf_op jit(solution)/shard_map/ppermute | solution.py:1034
  142.2 7.2 %collective-permute-start.24 = (bf16[144,512]{1,0:T(8,128)(2,1)S(1)}, bf16[144,512]{1,0:T(8,128)(2,1)S(1)}, u32[]{:S(2)}, u32[]{:S(2)}) collective-permute-start(bf16[144,512]{1,0:T(8,128)(2,1)S(1)} %get-tuple-element.182.refs_0_), channel_id=1, source_target_pairs={{0,1},{1,0},{2,3},{3,2},{4,5},{5,4},{6,7},{7,6},{8,9},{9,8},{10,11... | collective-permute-start | bytes 442376 | tf_op jit(solution)/shard_map/ppermute | solution.py:1030
  150.0 5.9 %collective-permute-start.27 = (bf16[96,512]{1,0:T(8,128)(2,1)S(1)}, bf16[96,512]{1,0:T(8,128)(2,1)S(1)}, u32[]{:S(2)}, u32[]{:S(2)}) collective-permute-start(bf16[96,512]{1,0:T(8,128)(2,1)S(1)} %get-tuple-element.187), channel_id=1, source_target_pairs={{0,8},{2,10},{4,12},{6,14},{8,0},{10,2},{12,4},{14,6},{16,24},{18,... | collective-permute-start | bytes 294920 | tf_op jit(solution)/shard_map/ppermute | solution.py:1018
  151.8 9.2 %collective-permute-start.28 = (bf16[96,512]{1,0:T(8,128)(2,1)S(1)}, bf16[96,512]{1,0:T(8,128)(2,1)S(1)}, u32[]{:S(2)}, u32[]{:S(2)}) collective-permute-start(bf16[96,512]{1,0:T(8,128)(2,1)S(1)} %get-tuple-element.188), channel_id=1, source_target_pairs={{0,16},{2,18},{4,20},{6,22},{8,24},{10,26},{12,28},{14,30},{16,0},... | collective-permute-start | bytes 294920 | tf_op jit(solution)/shard_map/ppermute | solution.py:1018
  154.1 6.9 %collective-permute-start.29 = (bf16[96,512]{1,0:T(8,128)(2,1)S(1)}, bf16[96,512]{1,0:T(8,128)(2,1)S(1)}, u32[]{:S(2)}, u32[]{:S(2)}) collective-permute-start(bf16[96,512]{1,0:T(8,128)(2,1)S(1)} %get-tuple-element.189), channel_id=1, source_target_pairs={{0,24},{2,26},{4,28},{6,30},{8,16},{10,18},{12,20},{14,22},{16,8},... | collective-permute-start | bytes 294920 | tf_op jit(solution)/shard_map/ppermute | solution.py:1018
  154.4 18.4 %collective-permute-start.30 = (bf16[576,512]{1,0:T(8,128)(2,1)}, bf16[576,512]{1,0:T(8,128)(2,1)}, u32[]{:S(2)}, u32[]{:S(2)}) collective-permute-start(bf16[576,512]{1,0:T(8,128)(2,1)} %shard_map.345.refs_0_.refs_1_), channel_id=1, source_target_pairs={{0,4},{2,6},{4,0},{6,2},{8,12},{10,14},{12,8},{14,10},{16,20},{18,... | collective-permute-start | bytes 1769480 | tf_op jit(solution)/shard_map/ppermute | solution.py:1018
  161.0 5.1 %copy-start.2 = (f32[24,2048]{1,0:T(8,128)S(1)}, f32[24,2048]{1,0:T(8,128)}, u32[]{:S(2)}) copy-start(f32[24,2048]{1,0:T(8,128)} %copy-done) | copy-start | bytes 589828
  161.0 5.1 %copy-start.7 = (bf16[1024,512]{1,0:T(8,128)(2,1)S(1)}, bf16[1024,512]{1,0:T(8,128)(2,1)}, u32[]{:S(2)}) copy-start(bf16[1024,512]{1,0:T(8,128)(2,1)} %get-tuple-element.170.merge_ref) | copy-start | bytes 3145732
  161.6 11.8 %collective-permute-start.33 = (bf16[80,512]{1,0:T(8,128)(2,1)S(1)}, bf16[80,512]{1,0:T(8,128)(2,1)S(1)}, u32[]{:S(2)}, u32[]{:S(2)}) collective-permute-start(bf16[80,512]{1,0:T(8,128)(2,1)S(1)} %get-tuple-element.190.after.refs_3_), channel_id=1, source_target_pairs={{0,24},{2,26},{4,28},{6,30},{8,16},{10,18},{12,20},{14,22},{16,8},... | collective-permute-start | bytes 245768 | tf_op jit(solution)/shard_map/ppermute | solution.py:1018
  164.1 9.3 %collective-permute-start.32 = (bf16[80,512]{1,0:T(8,128)(2,1)S(1)}, bf16[80,512]{1,0:T(8,128)(2,1)S(1)}, u32[]{:S(2)}, u32[]{:S(2)}) collective-permute-start(bf16[80,512]{1,0:T(8,128)(2,1)S(1)} %get-tuple-element.190.after.refs_3_), channel_id=1, source_target_pairs={{0,16},{2,18},{4,20},{6,22},{8,24},{10,26},{12,28},{14,30},{16,0},... | collective-permute-start | bytes 245768 | tf_op jit(solution)/shard_map/ppermute | solution.py:1018
  164.7 8.6 %collective-permute-start.31 = (bf16[80,512]{1,0:T(8,128)(2,1)S(1)}, bf16[80,512]{1,0:T(8,128)(2,1)S(1)}, u32[]{:S(2)}, u32[]{:S(2)}) collective-permute-start(bf16[80,512]{1,0:T(8,128)(2,1)S(1)} %get-tuple-element.190.after.refs_3_), channel_id=1, source_target_pairs={{0,8},{2,10},{4,12},{6,14},{8,0},{10,2},{12,4},{14,6},{16,24},{18,... | collective-permute-start | bytes 245768 | tf_op jit(solution)/shard_map/ppermute | solution.py:1018
  166.0 9.4 %collective-permute-start.34 = (bf16[576,512]{1,0:T(8,128)(2,1)}, bf16[576,512]{1,0:T(8,128)(2,1)}, u32[]{:S(2)}, u32[]{:S(2)}) collective-permute-start(bf16[576,512]{1,0:T(8,128)(2,1)} %shard_map.345.refs_0_.refs_1_), channel_id=1, source_target_pairs={{0,2},{2,0},{4,6},{6,4},{8,10},{10,8},{12,14},{14,12},{16,18},{18,... | collective-permute-start | bytes 1769480 | tf_op jit(solution)/shard_map/ppermute | solution.py:1018
  172.8 2.6 %collective-permute-start.35 = (bf16[576,512]{1,0:T(8,128)(2,1)}, bf16[576,512]{1,0:T(8,128)(2,1)}, u32[]{:S(2)}, u32[]{:S(2)}) collective-permute-start(bf16[576,512]{1,0:T(8,128)(2,1)} %collective-permute-done.30.refs_1_.refs_2_), channel_id=1, source_target_pairs={{0,2},{2,0},{4,6},{6,4},{8,10},{10,8},{12,14},{14,12},{16,18},{18,... | collective-permute-start | bytes 1769480 | tf_op jit(solution)/shard_map/ppermute | solution.py:1018
  173.9 10.1 %collective-permute-start.36 = (bf16[336,512]{1,0:T(8,128)(2,1)S(1)}, bf16[336,512]{1,0:T(8,128)(2,1)S(1)}, u32[]{:S(2)}, u32[]{:S(2)}) collective-permute-start(bf16[336,512]{1,0:T(8,128)(2,1)S(1)} %shard_map.349.refs_0_.mine), channel_id=1, source_target_pairs={{0,4},{2,6},{4,0},{6,2},{8,12},{10,14},{12,8},{14,10},{16,20},{18,... | collective-permute-start | bytes 1032200 | tf_op jit(solution)/shard_map/ppermute | solution.py:1018
  175.5 9.2 %collective-permute-start.37 = (bf16[336,512]{1,0:T(8,128)(2,1)S(1)}, bf16[336,512]{1,0:T(8,128)(2,1)S(1)}, u32[]{:S(2)}, u32[]{:S(2)}) collective-permute-start(bf16[336,512]{1,0:T(8,128)(2,1)S(1)} %shard_map.349.refs_0_.mine), channel_id=1, source_target_pairs={{0,2},{2,0},{4,6},{6,4},{8,10},{10,8},{12,14},{14,12},{16,18},{18,... | collective-permute-start | bytes 1032200 | tf_op jit(solution)/shard_map/ppermute | solution.py:1018
  184.6 1.7 collective-permute-start.38

commit v3 on v2

--- a/solution.py
+++ b/solution.py
@@ -477,7 +477,7 @@
             inverse_ref[w, :, columns] = inverse.astype(bf16)
             padded_ref[w, :, columns] = both.astype(bf16)
             mixed[pl.ds(AREA * w, AREA), columns] = both[0:AREA]
-    attended_ref[...] = mixed[...].astype(bf16)
+    attended_ref[...] = mixed[pl.ds(0, ROWS), :].astype(bf16)
 
 
 def attend(place, first, own, near, far, params, position, mask):
@@ -498,7 +498,7 @@
             pltpu.HBM((count, D), bf16), pltpu.HBM((windows, KEYS, D), bf16), pltpu.HBM((windows, KEYS, D), bf16),
             shape_of((3 * D, D), bf16),
         ],
-        [pltpu.VMEM((ROWS + 32, D), f32), pltpu.VMEM((ROWS, D), f32)],
+        [pltpu.VMEM((ROWS + 32, D), f32), pltpu.VMEM((ROWS + 8, D), f32)],
         flops=2 * count * D * (3 * D + 4 * AREA),
         moved=count * 10 * D + windows * QUADS * KEYS * LANES * 2,
         room=20,
@@ -779,7 +779,7 @@
             grad_values = turned_products(jnp.concatenate([low, empty], axis=0).T[:, :KEYS], weights_ref[w, quad])
             for part, grad in enumerate((grad_queries, grad_keys, grad_values)):
                 grads[to, D * part + QUAD * quad : D * part + QUAD * (quad + 1)] = grad[0:AREA]
-    stack = grads[...].astype(bf16)
+    stack = grads[pl.ds(0, ROWS), :].astype(bf16)
     stack_ref[here, :] = stack
     sums_ref[...] += column_sum(stack.astype(f32))
     grad_first = (
@@ -811,7 +811,7 @@
             pltpu.VMEM((count, 3 * D), bf16), pltpu.VMEM((count, D), bf16), shape_of((1, 3 * D), f32),
             shape_of((8, D), f32), shape_of((QUADS, KEYS, LANES), f32), pltpu.VMEM((count, D), bf16),
         ],
-        [pltpu.VMEM((ROWS + 32, D), f32), pltpu.VMEM((ROWS, 3 * D), f32), pltpu.SemaphoreType.DMA],
+        [pltpu.VMEM((ROWS + 32, D), f32), pltpu.VMEM((ROWS + 8, 3 * D), f32), pltpu.SemaphoreType.DMA],
         room=AB_ROOM,
     )(
         after, attn, *[in_hbm(array) for array in (qkv_in, weights, padded, inverse)], proj, in_hbm(merged),
@@ -966,6 +966,7 @@
         middle_part = rest.astype(bf16)
         low = (rest - middle_part.astype(f32)).astype(bf16)
         out_s[here, :] = mm(high, picked) + mm(middle_part, picked) + mm(low, picked)
+    out_s[HEADS * AREA :, :] = jnp.zeros((8 * HEADS, QUERIES), f32)
     for head in range(HEADS):
         lanes = slice(QUERIES * (head % 4), QUERIES * (head % 4 + 1))
         place_ref[head // 4, 0:AREA, lanes] = out_s[pl.ds(head, AREA, stride=HEADS), :]
@@ -980,7 +981,7 @@
         [RESIDENT, RESIDENT],
         [RESIDENT, ANYWHERE],
         [shape_of((QUADS, KEYS, LANES), f32), pltpu.HBM(hat.shape, bf16)],
-        [pltpu.VMEM((HEADS * AREA, 384), f32), pltpu.VMEM((HEADS * AREA, QUERIES), f32), pltpu.SemaphoreType.DMA],
+        [pltpu.VMEM((HEADS * AREA, 384), f32), pltpu.VMEM((HEADS * (AREA + 8), QUERIES), f32), pltpu.SemaphoreType.DMA],
         room=16,
     )(params, hat)
 
@@ -1057,20 +1058,33 @@
     return ref.at[begin : begin + rows, :]
 
 
-FEED_BLOCKS = ((0, 256), (256, 64), (320, 256))
-
-
-def feed_first_body(
-    place, own_keep, own_got, other_keep, other_got, proj_keep, proj_got, to_y, to_x, to_both, kept
-):
+FEED_BLOCKS = ((0, 256), (256, 256), (512, 64))
+
+
+def feed_first_body(place, own_keep, own_got, other_keep, other_got, to_y, to_x, to_both, kept):
     x = place[1]
     own, other = (own_keep, own_got), (other_keep, other_got)
-    for target, blocks, shard, side in (
-        (to_y, other, 1, x), (to_x, own, 0, 1 - x), (to_both, other, 1, 1 - x), (kept, own, 0, x)
-    ):
+    for target, blocks, side in ((to_y, other, x), (to_x, own, 1 - x), (to_both, other, 1 - x), (kept, own, x)):
         target[0:256, :] = added(blocks, 256 * side, 256).astype(bf16)
-        target[256:320, :] = added((proj_keep, proj_got), PROJ_PACK * shard + 64 * side, 64).astype(bf16)
-        target[320:576, :] = added(blocks, 512 + 256 * side, 256).astype(bf16)
+        target[256:512, :] = added(blocks, 512 + 256 * side, 256).astype(bf16)
+
+
+def feed_proj_body(place, keep, got, *refs):
+    x = place[1]
+    for target, shard, side in zip(refs[-4:], (1, 0, 1, 0), (x, 1 - x, 1 - x, x)):
+        target[512:576, :] = added((keep, got), PROJ_PACK * shard + 64 * side, 64).astype(bf16)
+
+
+def feed_proj(place, keep, got, outs):
+    return pl.pallas_call(
+        feed_proj_body,
+        in_specs=[SCALARS] + [RESIDENT] * 6,
+        out_specs=[RESIDENT] * 4,
+        out_shape=[pltpu.VMEM(out.shape, bf16) for out in outs],
+        input_output_aliases={3: 0, 4: 1, 5: 2, 6: 3},
+        compiler_params=pltpu.CompilerParams(vmem_limit_bytes=STAGE_ROOM * 1024 * 1024),
+        cost_estimate=COST,
+    )(place, keep, got, *outs)
 
 
 def feed_second_body(place, *refs):
@@ -1149,11 +1163,11 @@
 def feed_unpack_body(along, place, near, far, core_near, core_far, down_ref, up_ref, proj_ref, token_ref, stage):
     token_ref[...] = jnp.zeros_like(token_ref)
     for target, mine, beside in ((place[0], near, far), (1 - place[0], core_near, core_far)):
-        in_order(place, mine, beside, stage, (512, PROJ_PACK, 512), along)
+        in_order(place, mine, beside, stage, (512, 512, PROJ_PACK), along)
         wide = pl.ds(pl.multiple_of(512 * target, 512), 512)
         down_ref[wide, :] = stage[0:512, :].astype(f32)
-        proj_ref[pl.ds(pl.multiple_of(128 * target, 128), 128), :] = stage[512:640, :].astype(f32)
-        up_ref[:, wide] = stage[640:1152, :].astype(f32)
+        proj_ref[pl.ds(pl.multiple_of(128 * target, 128), 128), :] = stage[1024:1152, :].astype(f32)
+        up_ref[:, wide] = stage[512:1024, :].astype(f32)
 
 
 def feed_unpack(along, place, after, parts):
@@ -1359,8 +1373,8 @@
     after = feed_sums
     if fast:
         own_got, other_got, proj_got = ring.core(own_send), ring.core(other_send), ring.core(proj_send)
-        feed_keeps = (own_keep, own_got, other_keep, other_got, proj_keep, proj_got)
-        to_y, to_x, to_both, feed_kept = stage(feed_first_body, place, feed_sums, (576,) * 4, *feed_keeps)
+        outs = stage(feed_first_body, place, feed_sums, (576,) * 4, own_keep, own_got, other_keep, other_got)
+        to_y, to_x, to_both, feed_kept = feed_proj(place, proj_keep, proj_got, outs)
         feed_from = (ring.y(to_y), ring.x(to_x), ring.xy(to_both))
         after = to_y
     stack, low, sums, vectors, position_grad, first_near = attend_back(

time: 192 us -> 192 us (level)
  waiting for transfers between devices: 25.1 us -> 22.6 us
  transfers between devices with their start and end apart: 39 -> 39, of which waited for: 12 -> 10; matrix products, arithmetic and copies ran while one was open for 0% -> 0% of each run, Pallas kernels for 61% -> 63%
where the time goes in v3:
time: 192 us; the launch traced here: 188 us
  Pallas kernels  124 us (65%)
  starting transfers between devices  40.3 us (21%)
  waiting for transfers between devices  22.6 us (12%)
    ppermute x29, starting transfers between devices, to(): lax.ppermute(array, 'rows', [(i, i ^ bits) for i in range(self.rows_size)])  27.2 us
    pallas_call x1, Pallas kernels, attend_back(): kernel_call(attend_back_body, (count // ROWS,), [ANYWHERE, RESIDENT, by_w...  18.5 us
    pallas_call x13, Pallas kernels, plain_call_after(): pl.pallas_call(without_after, in_specs=[SCALARS] + [pl.BlockSpec(memory_s...  16.3 us
    ppermute x29, waiting for transfers between devices, to(): lax.ppermute(array, 'rows', [(i, i ^ bits) for i in range(self.rows_size)])  16.2 us
    pallas_call x2, Pallas kernels, feed_middle(): pl.pallas_call(partial(feed_middle_body, own), in_specs=[SCALARS] + [RESI...  13.9 us
    pallas_call x1, Pallas kernels, feed_near(): kernel_call(feed_near_body, (blocks + 1,), [SCALARS] + [RESIDENT] * 9 + [...  12.7 us
    pallas_call x1, Pallas kernels, attend(): kernel_call(attend_body, (count // ROWS,), [SCALARS, RESIDENT, RESIDENT,...  12.4 us
    pallas_call x1, Pallas kernels, feed_own(): kernel_call(feed_own_body, (blocks + 1,), [SCALARS, taken(D), taken(D), t...  12.1 us
  transfers between devices with their start and end apart: 39, of which 10 were waited for; matrix products, arithmetic and copies ran while one was open for 0% of the time, Pallas kernels for 63%

profile of v3, /device:TPU:0, one launch (start us, length us, event | category | flops | bytes accessed | tf_op | source)
XLA Modules:
  0.0 188.4 jit_solution(5140043712596542635)
XLA Ops:
  0.7 1.5 shard_map.322.after
  2.3 3.0 %collective-permute-start.1 = (bf16[256,512]{1,0:T(8,128)(2,1)S(1)}, bf16[256,512]{1,0:T(8,128)(2,1)S(1)}, u32[]{:S(2)}, u32[]{:S(2)}) collective-permute-start(bf16[256,512]{1,0:T(8,128)(2,1)S(1)} %shard_map.322.after), channel_id=1, source_target_pairs={{0,1},{1,0},{2,3},{3,2},{4,5},{5,4},{6,7},{7,6},{8,9},{9,8},{10,11... | collective-permute-start | bytes 786440 | tf_op jit(solution)/shard_map/ppermute | solution.py:1031
  5.3 1.4 shard_map.323
  6.8 1.5 shard_map.324
  8.3 1.6 shard_map.325.array_ref
  9.9 2.4 %collective-permute-done.refs_0_.others_ref = bf16[32,512]{1,0:T(8,128)(2,1)S(1)} collective-permute-done((bf16[32,512]{1,0:T(8,128)(2,1)S(1)}, bf16[32,512]{1,0:T(8,128)(2,1)S(1)}, u32[]{:S(2)}, u32[]{:S(2)}) %collective-permute-start) | collective-permute-done | bytes 32800 | tf_op jit(solution)/shard_map/ppermute | solution.py:1031
  12.3 1.7 collective-permute-start.3
  14.0 3.0 %shard_map.327 = (bf16[1600,1024]{1,0:T(8,128)(2,1)S(1)}, f32[1600,1]{1,0:T(8,128)S(1)}) custom-call(bf16[512,512]{1,0:T(8,128)(2,1)S(1)} %shard_map.326.after, bf16[1600,1024]{1,0:T(8,128)(2,1)} %rows_ref.1), custom_call_target="tpu_custom_call" | custom-call | flops 1 | bytes 1 | tf_op jit(solution)/shard_map/pallas_call | solution.py:332
  17.1 6.0 %shard_map.328 = (f32[1600,512]{1,0:T(8,128)}, bf16[1600,512]{1,0:T(8,128)(2,1)S(1)}, bf16[1600,512]{1,0:T(8,128)(2,1)}, bf16[1024,512]{1,0:T(8,128)(2,1)}, f32[24,2048]{1,0:T(8,128)S(1)}, /*index=5*/f32[1024,128]{1,0:T(8,128)}) custom-call(s32[4]{0:T(128)S(1)} %pad_add_fusion.place, bf16[1600,1024]{1,0:T(8,128)(2,1)S(1)} %get-tuple-element.122.hat_ref, ...), custom_call_target="tpu_custom_call" | custom-call | flops 1 | bytes 1 | tf_op jit(solution)/shard_map/pallas_call | solution.py:393
  23.1 2.5 %shard_map.329 = (f32[4,112,512]{2,1,0:T(8,128)S(1)}, bf16[1600,1024]{1,0:T(8,128)(2,1)}) custom-call(f32[24,2048]{1,0:T(8,128)S(1)} %get-tuple-element.124.params_ref, bf16[1600,1024]{1,0:T(8,128)(2,1)S(1)} %get-tuple-element.122.hat_ref), custom_call_target="tpu_custom_call" | custom-call | flops 1 | bytes 1 | tf_op jit(solution)/shard_map/pallas_call | solution.py:978
  25.6 0.6 shard_map.333
  26.3 1.3 collective-permute-start.5
  27.6 1.9 %collective-permute-done.4.far_ref = bf16[512,512]{1,0:T(8,128)(2,1)S(1)} collective-permute-done((bf16[512,512]{1,0:T(8,128)(2,1)S(1)}, bf16[512,512]{1,0:T(8,128)(2,1)S(1)}, u32[]{:S(2)}, u32[]{:S(2)}) %collective-permute-start.4) | collective-permute-done | bytes 524320 | tf_op jit(solution)/shard_map/ppermute | solution.py:1019
  29.5 12.4 %shard_map.330 = (bf16[16,128,1536]{2,1,0:T(8,128)(2,1)}, bf16[16,4,112,512]{3,2,1,0:T(8,128)(2,1)}, bf16[1600,512]{1,0:T(8,128)(2,1)}, bf16[16,112,512]{2,1,0:T...) custom-call(s32[4]{0:T(128)S(1)} %pad_add_fusion.place, ...), custom_call_target="tpu_custom_call" | custom-call | flops 1 | bytes 1 | tf_op jit(solution)/shard_map/pallas_call | solution.py:486
  41.9 12.1 %shard_map.331 = (f32[1600,512]{1,0:T(8,128)S(1)}, f32[1600,1]{1,0:T(8,128)S(1)}, f32[1600,512]{1,0:T(8,128)S(1)}, f32[1600,512]{1,0:T(8,128)S(1)}, bf16[1600,51...) custom-call(s32[4]{0:T(128)S(1)} %pad_add_fusion.place, ...), custom_call_target="tpu_custom_call" | custom-call | flops 1 | bytes 1 | tf_op jit(solution)/shard_map/pallas_call | solution.py:606
  54.7 6.6 %shard_map.332 = (f32[1600,512]{1,0:T(8,128)S(1)}, f32[1600,512]{1,0:T(8,128)S(1)}, bf16[1024,512]{1,0:T(8,128)(2,1)S(1)}, f32[8,512]{1,0:T(8,128)S(1)}) custom-call(s32[4]{0:T(128)S(1)} %pad_add_fusion.place, bf16[1600,512]{1,0:T(8,128)(2,1)S(1)} %get-tuple-element.131.second_ref, ...), custom_call_target="tpu_custom_call", output_to_operand_aliasing={{0}: (4, {}), {1}: (5, {})} | custom-call | flops 999999995904 | bytes 1 | tf_op jit(solution)/shard_map/pallas_call | solution.py:647
  61.2 7.3 %shard_map.334 = (f32[1600,512]{1,0:T(8,128)S(1)}, f32[1600,512]{1,0:T(8,128)S(1)}, bf16[1024,512]{1,0:T(8,128)(2,1)S(1)}, f32[8,512]{1,0:T(8,128)S(1)}) custom-call(s32[4]{0:T(128)S(1)} %pad_add_fusion.place, bf16[1600,512]{1,0:T(8,128)(2,1)S(1)} %get-tuple-element.131.second_ref, ...), custom_call_target="tpu_custom_call", output_to_operand_aliasing={{0}: (4, {}), {1}: (5, {})} | custom-call | flops 1 | bytes 1 | tf_op jit(solution)/shard_map/pallas_call | solution.py:647
  68.7 12.7 %shard_map.335 = (bf16[1600,512]{1,0:T(8,128)(2,1)}, f32[1600,512]{1,0:T(8,128)S(1)}, bf16[1600,512]{1,0:T(8,128)(2,1)S(1)}, bf16[1024,512]{1,0:T(8,128)(2,1)S(1...) custom-call(s32[4]{0:T(128)S(1)} %pad_add_fusion.place, ...), custom_call_target="tpu_custom_call" | custom-call | flops 1 | bytes 1 | tf_op jit(solution)/shard_map/pallas_call | solution.py:712
  81.9 1.8 shard_map.336
  83.7 0.6 shard_map.337
  84.3 1.6 collective-permute-start.11
  85.8 0.8 collective-permute-start.12
  86.6 1.2 collective-permute-start.10
  87.8 18.5 %shard_map.338 = (bf16[1600,1536]{1,0:T(8,128)(2,1)S(1)}, bf16[1600,512]{1,0:T(8,128)(2,1)S(1)}, f32[1,1536]{1,0:T(1,128)S(1)}, f32[8,512]{1,0:T(8,128)S(1)}, f3...) custom-call(bf16[576,512]{1,0:T(8,128)(2,1)S(1)} %get-tuple-element.155.after, ...), custom_call_target="tpu_custom_call" | custom-call | flops 1 | bytes 1 | tf_op jit(solution)/shard_map/pallas_call | solution.py:801
  106.4 5.7 %shard_map.339 = (bf16[768,512]{1,0:T(8,128)(2,1)}, bf16[768,512]{1,0:T(8,128)(2,1)S(1)}, bf16[1600,1024]{1,0:T(8,128)(2,1)S(1)}) custom-call(s32[4]{0:T(128)S(1)} %pad_add_fusion.place, f32[1,1536]{1,0:T(1,128)S(1)} %get-tuple-element.165.after.qkv_sums_ref, bf16[1600,512]{1,0:T(8,128)(2,1)S(1)} %get-tuple-element.166.first_ref, ...), custom_call_target="tpu_custom_call" | custom-call | flops 1 | bytes 1 | tf_op jit(solution)/shard_map/pallas_call | solution.py:857
  112.2 0.6 collective-permute-done.12.refs_4_
  112.8 1.4 collective-permute-done.10.refs_2_
  114.2 0.8 shard_map.340
  115.0 1.6 collective-permute-start.14
  116.6 2.6 %collective-permute-start.15 = (bf16[144,512]{1,0:T(8,128)(2,1)S(1)}, bf16[144,512]{1,0:T(8,128)(2,1)S(1)}, u32[]{:S(2)}, u32[]{:S(2)}) collective-permute-start(bf16[144,512]{1,0:T(8,128)(2,1)S(1)} %get-tuple-element.184), channel_id=1, source_target_pairs={{0,16},{2,18},{4,20},{6,22},{8,24},{10,26},{12,28},{14,30},{16,0},... | collective-permute-start | bytes 442376 | tf_op jit(solution)/shard_map/ppermute | solution.py:1019
  119.5 2.0 %shard_map.341 = (bf16[192,512]{1,0:T(8,128)(2,1)}, bf16[192,512]{1,0:T(8,128)(2,1)}, bf16[192,512]{1,0:T(8,128)(2,1)}, bf16[192,512]{1,0:T(8,128)(2,1)S(1)}) custom-call(s32[4]{0:T(128)S(1)} %pad_add_fusion.place, bf16[144,512]{1,0:T(8,128)(2,1)S(1)} %get-tuple-element.173.refs_0_.refs_1_, bf16[768,512]{1,0:T(8,128)(2,1)S(1)} %get-tuple-element.174.refs_1_, ...), custom_call_target="tpu_custom_call" | custom-call | flops 1 | bytes 1 | tf_op jit(solution)/shard_map/pallas_call | solution.py:249
  121.5 1.5 collective-permute-start.18
  123.0 1.1 collective-permute-start.17
  124.1 5.1 %shard_map.342 = (bf16[544,512]{1,0:T(8,128)(2,1)}, bf16[544,512]{1,0:T(8,128)(2,1)S(1)}) custom-call(s32[4]{0:T(128)S(1)} %pad_add_fusion.place, bf16[192,512]{1,0:T(8,128)(2,1)} %get-tuple-element.175.after, bf16[1600,512]{1,0:T(8,128)(2,1)S(1)} %get-tuple-element.176.low_ref, bf16[1600,1024]{1,0:T(8,128)(2,1)S(1)} %get-tuple-element.177.hat_ref, ...), custom_call_target="tpu_custom_call" | custom-call | flops 1 | bytes 1 | tf_op jit(solution)/shard_map/pallas_call | solution.py:906
  129.3 0.9 collective-permute-start.19
  130.2 0.6 shard_map.343.refs_0_.refs_1_
  130.8 3.7 %collective-permute-start.23 = (bf16[144,512]{1,0:T(8,128)(2,1)S(1)}, bf16[144,512]{1,0:T(8,128)(2,1)S(1)}, u32[]{:S(2)}, u32[]{:S(2)}) collective-permute-start(bf16[144,512]{1,0:T(8,128)(2,1)S(1)} %shard_map.343.refs_0_.refs_1_), channel_id=1, source_target_pairs={{0,24},{2,26},{4,28},{6,30},{8,16},{10,18},{12,20},{14,22},{16,8},... | collective-permute-start | bytes 442376 | tf_op jit(solution)/shard_map/ppermute | solution.py:1019
  134.5 1.7 collective-permute-done.19.refs_4_
  136.1 0.7 collective-permute-start.21
  136.8 1.2 shard_map.344.refs_0_.refs_1_
  138.1 1.2 shard_map.345
  139.3 0.6 collective-permute-start.25
  139.9 1.8 collective-permute-start.26
  141.8 1.1 collective-permute-start.24
  142.9 3.8 %collective-permute-done.22.refs_3_ = bf16[144,512]{1,0:T(8,128)(2,1)S(1)} collective-permute-done((bf16[144,512]{1,0:T(8,128)(2,1)S(1)}, bf16[144,512]{1,0:T(8,128)(2,1)S(1)}, u32[]{:S(2)}, u32[]{:S(2)}) %collective-permute-start.22) | collective-permute-done | bytes 147488 | tf_op jit(solution)/shard_map/ppermute | solution.py:1019
  146.7 1.4 shard_map.346.refs_0_.refs_1_
  148.5 0.6 shard_map.347
  149.2 2.1 %collective-permute-start.27 = (bf16[96,512]{1,0:T(8,128)(2,1)S(1)}, bf16[96,512]{1,0:T(8,128)(2,1)S(1)}, u32[]{:S(2)}, u32[]{:S(2)}) collective-permute-start(bf16[96,512]{1,0:T(8,128)(2,1)S(1)} %get-tuple-element.195), channel_id=1, source_target_pairs={{0,8},{2,10},{4,12},{6,14},{8,0},{10,2},{12,4},{14,6},{16,24},{18,... | collective-permute-start | bytes 294920 | tf_op jit(solution)/shard_map/ppermute | solution.py:1019
  151.2 2.0 %collective-permute-start.28 = (bf16[96,512]{1,0:T(8,128)(2,1)S(1)}, bf16[96,512]{1,0:T(8,128)(2,1)S(1)}, u32[]{:S(2)}, u32[]{:S(2)}) collective-permute-start(bf16[96,512]{1,0:T(8,128)(2,1)S(1)} %get-tuple-element.196), channel_id=1, source_target_pairs={{0,16},{2,18},{4,20},{6,22},{8,24},{10,26},{12,28},{14,30},{16,0},... | collective-permute-start | bytes 294920 | tf_op jit(solution)/shard_map/ppermute | solution.py:1019
  153.7 1.7 collective-permute-start.30
  155.4 4.7 %collective-permute-done.28.refs_3_ = bf16[96,512]{1,0:T(8,128)(2,1)S(1)} collective-permute-done((bf16[96,512]{1,0:T(8,128)(2,1)S(1)}, bf16[96,512]{1,0:T(8,128)(2,1)S(1)}, u32[]{:S(2)}, u32[]{:S(2)}) %collective-permute-start.28) | collective-permute-done | bytes 98336 | tf_op jit(solution)/shard_map/ppermute | solution.py:1019
  160.2 0.6 shard_map.348
  160.8 2.5 %collective-permute-start.33 = (bf16[80,512]{1,0:T(8,128)(2,1)S(1)}, bf16[80,512]{1,0:T(8,128)(2,1)S(1)}, u32[]{:S(2)}, u32[]{:S(2)}) collective-permute-start(bf16[80,512]{1,0:T(8,128)(2,1)S(1)} %get-tuple-element.198.after.refs_3_), channel_id=1, source_target_pairs={{0,24},{2,26},{4,28},{6,30},{8,16},{10,18},{12,20},{14,22},{16,8},... | collective-permute-start | bytes 245768 | tf_op jit(solution)/shard_map/ppermute | solution.py:1019
  163.3 0.6 collective-permute-start.32
  163.9 1.3 collective-permute-start.31
  165.2 6.8 %shard_map.349 = (bf16[1600,1024]{1,0:T(8,128)(2,1)}, f32[8,128]{1,0:T(8,128)S(1)}) custom-call(bf16[80,512]{1,0:T(8,128)(2,1)S(1)} %get-tuple-element.198.after.refs_3_, bf16[1600,512]{1,0:T(8,128)(2,1)} %copy-done.3, bf16[1600,1024]{1,0:T(8,128)(2,1)} %get-tuple-element.168.hat_in.hat_ref, f32[1600,1]{1,0:T(8,128)S(1)} %get-tuple-element.199.inverse_ref, ...), custom_call_target="tpu_custom_call" | custom-call | flops 1 | bytes 1 | tf_op jit(solution)/shard_map/pallas_call | solution.py:927
  172.0 0.5 collective-permute-start.35
  172.6 0.6 shard_map.350.refs_0_.mine
  173.1 2.2 %collective-permute-start.36 = (bf16[336,512]{1,0:T(8,128)(2,1)S(1)}, bf16[336,512]{1,0:T(8,128)(2,1)S(1)}, u32[]{:S(2)}, u32[]{:S(2)}) collective-permute-start(bf16[336,512]{1,0:T(8,128)(2,1)S(1)} %shard_map.350.refs_0_.mine), channel_id=1, source_target_pairs={{0,4},{2,6},{4,0},{6,2},{8,12},{10,14},{12,8},{14,10},{16,20},{18,... | collective-permute-start | bytes 1032200 | tf_op jit(solution)/shard_map/ppermute | solution.py:1019
  175.3 4.2 %shard_map.351 = (f32[1024,512]{1,0:T(8,128)}, f32[512,1024]{1,0:T(8,128)}, f32[256,512]{1,0:T(8,128)}, f32[8,128]{1,0:T(8,128)S(1)}) custom-call(s32[4]{0:T(128)S(1)} %pad_add_fusion.place, bf16[336,512]{1,0:T(8,128)(2,1)S(1)} %shard_map.350.refs_0_.mine, bf16[576,512]{1,0:T(8,128)(2,1)} %shard_map.346.refs_0_.refs_1_, ...), custom_call_target="tpu_custom_call" | custom-call | flops 1 | bytes 1 | tf_op jit(solution)/shard_map/pallas_call | solution.py:249
  179.5 4.0 %collective-permute-done.36.refs_1_ = bf16[336,512]{1,0:T(8,128)(2,1)S(1)} collective-permute-done((bf16[336,512]{1,0:T(8,128)(2,1)S(1)}, bf16[336,512]{1,0:T(8,128)(2,1)S(1)}, u32[]{:S(2)}, u32[]{:S(2)}) %collective-permute-start.36) | collective-permute-done | bytes 344096 | tf_op jit(solution)/shard_map/ppermute | solution.py:1019
  183.5 0.6 shard_map.352.beside
  184.2 1.6 collective-permute-done.38.core_beside
  185.8 2.3 %shard_map.353 = (f32[3,512,256]{2,1,0:T(8,128)}, f32[512,512]{1,0:T(8,128)}, f32[1,512]{1,0:T(1,128)}, f32[1,512]{1,0:T(1,128)}, f32[1,512]{1,0:T(1,128)}, /*in...) custom-call(s32[4]{0:T(128)S(1)} %pad_add_fusion.place, ...), custom_call_target="tpu_custom_call" | custom-call | flops 1 | bytes 1 | tf_op jit(solution)/shard_map/pallas_call | solution.py:196
  (85 shorter events, 2.8 us)
Async XLA Ops:
  2.3 10.0 %collective-permute-start.1 = (bf16[256,512]{1,0:T(8,128)(2,1)S(1)}, bf16[256,512]{1,0:T(8,128)(2,1)S(1)}, u32[]{:S(2)}, u32[]{:S(2)}) collective-permute-start(bf16[256,512]{1,0:T(8,128)(2,1)S(1)} %shard_map.322.after), channel_id=1, source_target_pairs={{0,1},{1,0},{2,3},{3,2},{4,5},{5,4},{6,7},{7,6},{8,9},{9,8},{10,11... | collective-permute-start | bytes 786440 | tf_op jit(solution)/shard_map/ppermute | solution.py:1031
  6.7 5.6 %collective-permute-start = (bf16[32,512]{1,0:T(8,128)(2,1)S(1)}, bf16[32,512]{1,0:T(8,128)(2,1)S(1)}, u32[]{:S(2)}, u32[]{:S(2)}) collective-permute-start(bf16[32,512]{1,0:T(8,128)(2,1)S(1)} %get-tuple-element.121), channel_id=1, source_target_pairs={{0,1},{1,0},{2,3},{3,2},{4,5},{5,4},{6,7},{7,6},{8,9},{9,8},{10,11... | collective-permute-start | bytes 98312 | tf_op jit(solution)/shard_map/ppermute | solution.py:1031
  8.2 8.8 %copy-start.9 = (bf16[512,512]{1,0:T(8,128)(2,1)S(1)}, bf16[512,512]{1,0:T(8,128)(2,1)}, u32[]{:S(2)}) copy-start(bf16[512,512]{1,0:T(8,128)(2,1)} %own_ref.1) | copy-start | bytes 1572868
  8.3 8.8 %copy-start.13 = (f32[512]{0:T(512)S(1)}, f32[512]{0:T(512)}, u32[]{:S(2)}) copy-start(f32[512]{0:T(512)} %param.25) | copy-start | bytes 6148
  8.3 8.8 %copy-start.15 = (f32[512]{0:T(512)S(1)}, f32[512]{0:T(512)}, u32[]{:S(2)}) copy-start(f32[512]{0:T(512)} %param.26) | copy-start | bytes 6148
  12.3 13.3 %collective-permute-start.3 = (bf16[512,512]{1,0:T(8,128)(2,1)S(1)}, bf16[512,512]{1,0:T(8,128)(2,1)S(1)}, u32[]{:S(2)}, u32[]{:S(2)}) collective-permute-start(bf16[512,512]{1,0:T(8,128)(2,1)S(1)} %shard_map.326.after), channel_id=1, source_target_pairs={{0,1},{1,0},{2,3},{3,2},{4,5},{5,4},{6,7},{7,6},{8,9},{9,8},{10,11... | collective-permute-start | bytes 1572872 | tf_op jit(solution)/shard_map/ppermute | solution.py:1031
  14.0 3.0 %collective-permute-start.2 = (bf16[256,512]{1,0:T(8,128)(2,1)S(1)}, bf16[256,512]{1,0:T(8,128)(2,1)S(1)}, u32[]{:S(2)}, u32[]{:S(2)}) collective-permute-start(bf16[256,512]{1,0:T(8,128)(2,1)S(1)} %collective-permute-done.1.refs_1_.near_ref), channel_id=1, source_target_pairs={{0,2},{2,0},{4,6},{6,4},{8,10},{10,8},{12,14},{14,12},{16,18},{18,... | collective-permute-start | bytes 786440 | tf_op jit(solution)/shard_map/ppermute | solution.py:1019
  17.1 8.5 %copy-start.4 = (bf16[512,1024]{1,0:T(8,128)(2,1)S(1)}, bf16[512,1024]{1,0:T(8,128)(2,1)}, u32[]{:S(2)}) copy-start(bf16[512,1024]{1,0:T(8,128)(2,1)} %refs_2_.1) | copy-start | bytes 3145732
  17.1 8.5 %copy-start.5 = (bf16[1024,512]{1,0:T(8,128)(2,1)S(1)}, bf16[1024,512]{1,0:T(8,128)(2,1)}, u32[]{:S(2)}) copy-start(bf16[1024,512]{1,0:T(8,128)(2,1)} %refs_3_.1) | copy-start | bytes 3145732
  23.1 45.6 %copy-start = (f32[24,2048]{1,0:T(8,128)}, f32[24,2048]{1,0:T(8,128)S(1)}, u32[]{:S(2)}) copy-start(f32[24,2048]{1,0:T(8,128)S(1)} %get-tuple-element.124.params_ref) | copy-start | bytes 589828
  23.1 6.4 %copy-start.8 = (bf16[3,512,256]{2,1,0:T(8,128)(2,1)S(1)}, bf16[3,512,256]{2,1,0:T(8,128)(2,1)}, u32[]{:S(2)}) copy-start(bf16[3,512,256]{2,1,0:T(8,128)(2,1)} %param.27) | copy-start | bytes 2359300
  26.3 15.7 %copy-start.10 = (bf16[256,512]{1,0:T(8,128)(2,1)S(1)}, bf16[256,512]{1,0:T(8,128)(2,1)}, u32[]{:S(2)}) copy-start(bf16[256,512]{1,0:T(8,128)(2,1)} %proj_own.1) | copy-start | bytes 786436
  26.3 15.6 %copy-start.12 = (f32[512]{0:T(512)S(1)}, f32[512]{0:T(512)}, u32[]{:S(2)}) copy-start(f32[512]{0:T(512)} %param.32) | copy-start | bytes 6148
  26.3 15.6 %copy-start.16 = (f32[512]{0:T(512)S(1)}, f32[512]{0:T(512)}, u32[]{:S(2)}) copy-start(f32[512]{0:T(512)} %param.31) | copy-start | bytes 6148
  26.3 15.6 %copy-start.17 = (f32[512]{0:T(512)S(1)}, f32[512]{0:T(512)}, u32[]{:S(2)}) copy-start(f32[512]{0:T(512)} %param.33) | copy-start | bytes 6148
  26.3 15.6 %copy-start.18 = (f32[512]{0:T(512)S(1)}, f32[512]{0:T(512)}, u32[]{:S(2)}) copy-start(f32[512]{0:T(512)} %param.37) | copy-start | bytes 6148
  26.3 28.0 %collective-permute-start.5 = (bf16[1024,512]{1,0:T(8,128)(2,1)S(1)}, bf16[1024,512]{1,0:T(8,128)(2,1)}, u32[]{:S(2)}, u32[]{:S(2)}) collective-permute-start(bf16[1024,512]{1,0:T(8,128)(2,1)S(1)} %shard_map.333), channel_id=1, source_target_pairs={{0,1},{1,0},{2,3},{3,2},{4,5},{5,4},{6,7},{7,6},{8,9},{9,8},{10,11... | collective-permute-start | bytes 3145736 | tf_op jit(solution)/shard_map/ppermute | solution.py:1031
  27.6 1.9 %collective-permute-start.4 = (bf16[512,512]{1,0:T(8,128)(2,1)S(1)}, bf16[512,512]{1,0:T(8,128)(2,1)S(1)}, u32[]{:S(2)}, u32[]{:S(2)}) collective-permute-start(bf16[512,512]{1,0:T(8,128)(2,1)S(1)} %collective-permute-done.3.near_ref.refs_1_), channel_id=1, source_target_pairs={{0,2},{2,0},{4,6},{6,4},{8,10},{10,8},{12,14},{14,12},{16,18},{18,... | collective-permute-start | bytes 1572872 | tf_op jit(solution)/shard_map/ppermute | solution.py:1019
  54.1 27.8 %collective-permute-start.8 = (bf16[1024,512]{1,0:T(8,128)(2,1)}, bf16[1024,512]{1,0:T(8,128)(2,1)}, u32[]{:S(2)}, u32[]{:S(2)}) collective-permute-start(bf16[1024,512]{1,0:T(8,128)(2,1)} %get-tuple-element.148), channel_id=1, source_target_pairs={{0,2},{2,0},{4,6},{6,4},{8,10},{10,8},{12,14},{14,12},{16,18},{18,... | collective-permute-start | bytes 3145736 | tf_op jit(solution)/shard_map/ppermute | solution.py:1019
  54.3 6.9 %collective-permute-start.6 = (bf16[1024,512]{1,0:T(8,128)(2,1)}, bf16[1024,512]{1,0:T(8,128)(2,1)}, u32[]{:S(2)}, u32[]{:S(2)}) collective-permute-start(bf16[1024,512]{1,0:T(8,128)(2,1)} %collective-permute-done.5.near_ref), channel_id=1, source_target_pairs={{0,2},{2,0},{4,6},{6,4},{8,10},{10,8},{12,14},{14,12},{16,18},{18,... | collective-permute-start | bytes 3145736 | tf_op jit(solution)/shard_map/ppermute | solution.py:1019
  68.5 13.3 %collective-permute-start.9 = (bf16[1024,512]{1,0:T(8,128)(2,1)S(1)}, bf16[1024,512]{1,0:T(8,128)(2,1)S(1)}, u32[]{:S(2)}, u32[]{:S(2)}) collective-permute-start(bf16[1024,512]{1,0:T(8,128)(2,1)S(1)} %get-tuple-element.150), channel_id=1, source_target_pairs={{0,2},{2,0},{4,6},{6,4},{8,10},{10,8},{12,14},{14,12},{16,18},{18,... | collective-permute-start | bytes 3145736 | tf_op jit(solution)/shard_map/ppermute | solution.py:1019
  81.4 2.2 %collective-permute-start.7 = (bf16[256,512]{1,0:T(8,128)(2,1)S(1)}, bf16[256,512]{1,0:T(8,128)(2,1)S(1)}, u32[]{:S(2)}, u32[]{:S(2)}) collective-permute-start(bf16[256,512]{1,0:T(8,128)(2,1)S(1)} %get-tuple-element.145), channel_id=1, source_target_pairs={{0,2},{2,0},{4,6},{6,4},{8,10},{10,8},{12,14},{14,12},{16,18},{18,... | collective-permute-start | bytes 786440 | tf_op jit(solution)/shard_map/ppermute | solution.py:1019
  81.9 6.0 %copy-start.14 = (f32[512]{0:T(512)S(1)}, f32[512]{0:T(512)}, u32[]{:S(2)}) copy-start(f32[512]{0:T(512)} %param.25) | copy-start | bytes 6148
  84.3 28.0 %collective-permute-start.11 = (bf16[576,512]{1,0:T(8,128)(2,1)S(1)}, bf16[576,512]{1,0:T(8,128)(2,1)S(1)}, u32[]{:S(2)}, u32[]{:S(2)}) collective-permute-start(bf16[576,512]{1,0:T(8,128)(2,1)S(1)} %get-tuple-element.171), channel_id=1, source_target_pairs={{0,4},{2,6},{4,0},{6,2},{8,12},{10,14},{12,8},{14,10},{16,20},{18,... | collective-permute-start | bytes 1769480 | tf_op jit(solution)/shard_map/ppermute | solution.py:1019
  85.8 27.0 %collective-permute-start.12 = (bf16[576,512]{1,0:T(8,128)(2,1)S(1)}, bf16[576,512]{1,0:T(8,128)(2,1)S(1)}, u32[]{:S(2)}, u32[]{:S(2)}) collective-permute-start(bf16[576,512]{1,0:T(8,128)(2,1)S(1)} %get-tuple-element.172), channel_id=1, source_target_pairs={{0,5},{1,4},{2,7},{3,6},{4,1},{5,0},{6,3},{7,2},{8,13},{9,12},{10,... | collective-permute-start | bytes 1769480 | tf_op jit(solution)/shard_map/ppermute | solution.py:1035
  86.6 27.5 %collective-permute-start.10 = (bf16[576,512]{1,0:T(8,128)(2,1)S(1)}, bf16[576,512]{1,0:T(8,128)(2,1)S(1)}, u32[]{:S(2)}, u32[]{:S(2)}) collective-permute-start(bf16[576,512]{1,0:T(8,128)(2,1)S(1)} %get-tuple-element.155.after), channel_id=1, source_target_pairs={{0,1},{1,0},{2,3},{3,2},{4,5},{5,4},{6,7},{7,6},{8,9},{9,8},{10,11... | collective-permute-start | bytes 1769480 | tf_op jit(solution)/shard_map/ppermute | solution.py:1031
  106.4 17.7 %copy-start.3 = (bf16[1600,512]{1,0:T(8,128)(2,1)}, bf16[1600,512]{1,0:T(8,128)(2,1)S(1)}, u32[]{:S(2)}) copy-start(bf16[1600,512]{1,0:T(8,128)(2,1)S(1)} %get-tuple-element.176.low_ref) | copy-start | bytes 4915204
  112.1 7.3 %collective-permute-start.13 = (bf16[768,512]{1,0:T(8,128)(2,1)}, bf16[768,512]{1,0:T(8,128)(2,1)}, u32[]{:S(2)}, u32[]{:S(2)}) collective-permute-start(bf16[768,512]{1,0:T(8,128)(2,1)} %get-tuple-element.169.refs_0_), channel_id=1, source_target_pairs={{0,2},{2,0},{4,6},{6,4},{8,10},{10,8},{12,14},{14,12},{16,18},{18,... | collective-permute-start | bytes 2359304 | tf_op jit(solution)/shard_map/ppermute | solution.py:1019
  114.2 9.9 %copy-start.1 = (f32[24,2048]{1,0:T(8,128)S(1)}, f32[24,2048]{1,0:T(8,128)}, u32[]{:S(2)}) copy-start(f32[24,2048]{1,0:T(8,128)} %copy-done) | copy-start | bytes 589828
  114.2 9.9 %copy-start.6 = (bf16[1024,512]{1,0:T(8,128)(2,1)S(1)}, bf16[1024,512]{1,0:T(8,128)(2,1)}, u32[]{:S(2)}) copy-start(bf16[1024,512]{1,0:T(8,128)(2,1)} %get-tuple-element.178.merge_ref) | copy-start | bytes 3145732
  114.2 9.9 %copy-start.11 = (f32[1024,128]{1,0:T(8,128)S(1)}, f32[1024,128]{1,0:T(8,128)}, u32[]{:S(2)}) copy-start(f32[1024,128]{1,0:T(8,128)} %get-tuple-element.179.column_ref) | copy-start | bytes 1572868
  115.0 14.2 %collective-permute-start.14 = (bf16[144,512]{1,0:T(8,128)(2,1)S(1)}, bf16[144,512]{1,0:T(8,128)(2,1)S(1)}, u32[]{:S(2)}, u32[]{:S(2)}) collective-permute-start(bf16[144,512]{1,0:T(8,128)(2,1)S(1)} %get-tuple-element.183), channel_id=1, source_target_pairs={{0,8},{2,10},{4,12},{6,14},{8,0},{10,2},{12,4},{14,6},{16,24},{18,... | collective-permute-start | bytes 442376 | tf_op jit(solution)/shard_map/ppermute | solution.py:1019
  116.6 13.5 %collective-permute-start.15 = (bf16[144,512]{1,0:T(8,128)(2,1)S(1)}, bf16[144,512]{1,0:T(8,128)(2,1)S(1)}, u32[]{:S(2)}, u32[]{:S(2)}) collective-permute-start(bf16[144,512]{1,0:T(8,128)(2,1)S(1)} %get-tuple-element.184), channel_id=1, source_target_pairs={{0,16},{2,18},{4,20},{6,22},{8,24},{10,26},{12,28},{14,30},{16,0},... | collective-permute-start | bytes 442376 | tf_op jit(solution)/shard_map/ppermute | solution.py:1019
  119.2 10.9 %collective-permute-start.16 = (bf16[144,512]{1,0:T(8,128)(2,1)S(1)}, bf16[144,512]{1,0:T(8,128)(2,1)S(1)}, u32[]{:S(2)}, u32[]{:S(2)}) collective-permute-start(bf16[144,512]{1,0:T(8,128)(2,1)S(1)} %get-tuple-element.185), channel_id=1, source_target_pairs={{0,24},{2,26},{4,28},{6,30},{8,16},{10,18},{12,20},{14,22},{16,8},... | collective-permute-start | bytes 442376 | tf_op jit(solution)/shard_map/ppermute | solution.py:1019
  121.5 13.0 %collective-permute-start.18 = (bf16[192,512]{1,0:T(8,128)(2,1)}, bf16[192,512]{1,0:T(8,128)(2,1)}, u32[]{:S(2)}, u32[]{:S(2)}) collective-permute-start(bf16[192,512]{1,0:T(8,128)(2,1)} %get-tuple-element.187), channel_id=1, source_target_pairs={{0,4},{2,6},{4,0},{6,2},{8,12},{10,14},{12,8},{14,10},{16,20},{18,... | collective-permute-start | bytes 589832 | tf_op jit(solution)/shard_map/ppermute | solution.py:1019
  123.0 13.8 %collective-permute-start.17 = (bf16[192,512]{1,0:T(8,128)(2,1)}, bf16[192,512]{1,0:T(8,128)(2,1)}, u32[]{:S(2)}, u32[]{:S(2)}) collective-permute-start(bf16[192,512]{1,0:T(8,128)(2,1)} %get-tuple-element.175.after), channel_id=1, source_target_pairs={{0,1},{1,0},{2,3},{3,2},{4,5},{5,4},{6,7},{7,6},{8,9},{9,8},{10,11... | collective-permute-start | bytes 589832 | tf_op jit(solution)/shard_map/ppermute | solution.py:1031
  129.3 6.9 %collective-permute-start.19 = (bf16[192,512]{1,0:T(8,128)(2,1)}, bf16[192,512]{1,0:T(8,128)(2,1)}, u32[]{:S(2)}, u32[]{:S(2)}) collective-permute-start(bf16[192,512]{1,0:T(8,128)(2,1)} %get-tuple-element.188), channel_id=1, source_target_pairs={{0,5},{1,4},{2,7},{3,6},{4,1},{5,0},{6,3},{7,2},{8,13},{9,12},{10,... | collective-permute-start | bytes 589832 | tf_op jit(solution)/shard_map/ppermute | solution.py:1035
  130.2 7.9 %collective-permute-start.20 = (bf16[544,512]{1,0:T(8,128)(2,1)}, bf16[544,512]{1,0:T(8,128)(2,1)}, u32[]{:S(2)}, u32[]{:S(2)}) collective-permute-start(bf16[544,512]{1,0:T(8,128)(2,1)} %get-tuple-element.182.refs_0_), channel_id=1, source_target_pairs={{0,2},{2,0},{4,6},{6,4},{8,10},{10,8},{12,14},{14,12},{16,18},{18,... | collective-permute-start | bytes 1671176 | tf_op jit(solution)/shard_map/ppermute | solution.py:1019
  130.8 11.0 %collective-permute-start.23 = (bf16[144,512]{1,0:T(8,128)(2,1)S(1)}, bf16[144,512]{1,0:T(8,128)(2,1)S(1)}, u32[]{:S(2)}, u32[]{:S(2)}) collective-permute-start(bf16[144,512]{1,0:T(8,128)(2,1)S(1)} %shard_map.343.refs_0_.refs_1_), channel_id=1, source_target_pairs={{0,24},{2,26},{4,28},{6,30},{8,16},{10,18},{12,20},{14,22},{16,8},... | collective-permute-start | bytes 442376 | tf_op jit(solution)/shard_map/ppermute | solution.py:1019
  134.5 12.2 %collective-permute-start.22 = (bf16[144,512]{1,0:T(8,128)(2,1)S(1)}, bf16[144,512]{1,0:T(8,128)(2,1)S(1)}, u32[]{:S(2)}, u32[]{:S(2)}) collective-permute-start(bf16[144,512]{1,0:T(8,128)(2,1)S(1)} %shard_map.343.refs_0_.refs_1_), channel_id=1, source_target_pairs={{0,16},{2,18},{4,20},{6,22},{8,24},{10,26},{12,28},{14,30},{16,0},... | collective-permute-start | bytes 442376 | tf_op jit(solution)/shard_map/ppermute | solution.py:1019
  136.1 10.6 %collective-permute-start.21 = (bf16[144,512]{1,0:T(8,128)(2,1)S(1)}, bf16[144,512]{1,0:T(8,128)(2,1)S(1)}, u32[]{:S(2)}, u32[]{:S(2)}) collective-permute-start(bf16[144,512]{1,0:T(8,128)(2,1)S(1)} %shard_map.343.refs_0_.refs_1_), channel_id=1, source_target_pairs={{0,8},{2,10},{4,12},{6,14},{8,0},{10,2},{12,4},{14,6},{16,24},{18,... | collective-permute-start | bytes 442376 | tf_op jit(solution)/shard_map/ppermute | solution.py:1019
  139.3 8.8 %collective-permute-start.25 = (bf16[144,512]{1,0:T(8,128)(2,1)S(1)}, bf16[144,512]{1,0:T(8,128)(2,1)S(1)}, u32[]{:S(2)}, u32[]{:S(2)}) collective-permute-start(bf16[144,512]{1,0:T(8,128)(2,1)S(1)} %get-tuple-element.192), channel_id=1, source_target_pairs={{0,4},{2,6},{4,0},{6,2},{8,12},{10,14},{12,8},{14,10},{16,20},{18,... | collective-permute-start | bytes 442376 | tf_op jit(solution)/shard_map/ppermute | solution.py:1019
  139.9 8.2 %collective-permute-start.26 = (bf16[144,512]{1,0:T(8,128)(2,1)S(1)}, bf16[144,512]{1,0:T(8,128)(2,1)S(1)}, u32[]{:S(2)}, u32[]{:S(2)}) collective-permute-start(bf16[144,512]{1,0:T(8,128)(2,1)S(1)} %get-tuple-element.193), channel_id=1, source_target_pairs={{0,5},{1,4},{2,7},{3,6},{4,1},{5,0},{6,3},{7,2},{8,13},{9,12},{10,... | collective-permute-start | bytes 442376 | tf_op jit(solution)/shard_map/ppermute | solution.py:1035
  141.8 6.8 %collective-permute-start.24 = (bf16[144,512]{1,0:T(8,128)(2,1)S(1)}, bf16[144,512]{1,0:T(8,128)(2,1)S(1)}, u32[]{:S(2)}, u32[]{:S(2)}) collective-permute-start(bf16[144,512]{1,0:T(8,128)(2,1)S(1)} %get-tuple-element.190.refs_0_), channel_id=1, source_target_pairs={{0,1},{1,0},{2,3},{3,2},{4,5},{5,4},{6,7},{7,6},{8,9},{9,8},{10,11... | collective-permute-start | bytes 442376 | tf_op jit(solution)/shard_map/ppermute | solution.py:1031
  149.2 6.3 %collective-permute-start.27 = (bf16[96,512]{1,0:T(8,128)(2,1)S(1)}, bf16[96,512]{1,0:T(8,128)(2,1)S(1)}, u32[]{:S(2)}, u32[]{:S(2)}) collective-permute-start(bf16[96,512]{1,0:T(8,128)(2,1)S(1)} %get-tuple-element.195), channel_id=1, source_target_pairs={{0,8},{2,10},{4,12},{6,14},{8,0},{10,2},{12,4},{14,6},{16,24},{18,... | collective-permute-start | bytes 294920 | tf_op jit(solution)/shard_map/ppermute | solution.py:1019
  151.2 8.9 %collective-permute-start.28 = (bf16[96,512]{1,0:T(8,128)(2,1)S(1)}, bf16[96,512]{1,0:T(8,128)(2,1)S(1)}, u32[]{:S(2)}, u32[]{:S(2)}) collective-permute-start(bf16[96,512]{1,0:T(8,128)(2,1)S(1)} %get-tuple-element.196), channel_id=1, source_target_pairs={{0,16},{2,18},{4,20},{6,22},{8,24},{10,26},{12,28},{14,30},{16,0},... | collective-permute-start | bytes 294920 | tf_op jit(solution)/shard_map/ppermute | solution.py:1019
  153.3 6.9 %collective-permute-start.29 = (bf16[96,512]{1,0:T(8,128)(2,1)S(1)}, bf16[96,512]{1,0:T(8,128)(2,1)S(1)}, u32[]{:S(2)}, u32[]{:S(2)}) collective-permute-start(bf16[96,512]{1,0:T(8,128)(2,1)S(1)} %get-tuple-element.197), channel_id=1, source_target_pairs={{0,24},{2,26},{4,28},{6,30},{8,16},{10,18},{12,20},{14,22},{16,8},... | collective-permute-start | bytes 294920 | tf_op jit(solution)/shard_map/ppermute | solution.py:1019
  153.7 18.4 %collective-permute-start.30 = (bf16[576,512]{1,0:T(8,128)(2,1)}, bf16[576,512]{1,0:T(8,128)(2,1)}, u32[]{:S(2)}, u32[]{:S(2)}) collective-permute-start(bf16[576,512]{1,0:T(8,128)(2,1)} %shard_map.346.refs_0_.refs_1_), channel_id=1, source_target_pairs={{0,4},{2,6},{4,0},{6,2},{8,12},{10,14},{12,8},{14,10},{16,20},{18,... | collective-permute-start | bytes 1769480 | tf_op jit(solution)/shard_map/ppermute | solution.py:1019
  160.2 5.1 %copy-start.2 = (f32[24,2048]{1,0:T(8,128)S(1)}, f32[24,2048]{1,0:T(8,128)}, u32[]{:S(2)}) copy-start(f32[24,2048]{1,0:T(8,128)} %copy-done) | copy-start | bytes 589828
  160.2 5.1 %copy-start.7 = (bf16[1024,512]{1,0:T(8,128)(2,1)S(1)}, bf16[1024,512]{1,0:T(8,128)(2,1)}, u32[]{:S(2)}) copy-start(bf16[1024,512]{1,0:T(8,128)(2,1)} %get-tuple-element.178.merge_ref) | copy-start | bytes 3145732
  160.8 11.8 %collective-permute-start.33 = (bf16[80,512]{1,0:T(8,128)(2,1)S(1)}, bf16[80,512]{1,0:T(8,128)(2,1)S(1)}, u32[]{:S(2)}, u32[]{:S(2)}) collective-permute-start(bf16[80,512]{1,0:T(8,128)(2,1)S(1)} %get-tuple-element.198.after.refs_3_), channel_id=1, source_target_pairs={{0,24},{2,26},{4,28},{6,30},{8,16},{10,18},{12,20},{14,22},{16,8},... | collective-permute-start | bytes 245768 | tf_op jit(solution)/shard_map/ppermute | solution.py:1019
  163.3 9.3 %collective-permute-start.32 = (bf16[80,512]{1,0:T(8,128)(2,1)S(1)}, bf16[80,512]{1,0:T(8,128)(2,1)S(1)}, u32[]{:S(2)}, u32[]{:S(2)}) collective-permute-start(bf16[80,512]{1,0:T(8,128)(2,1)S(1)} %get-tuple-element.198.after.refs_3_), channel_id=1, source_target_pairs={{0,16},{2,18},{4,20},{6,22},{8,24},{10,26},{12,28},{14,30},{16,0},... | collective-permute-start | bytes 245768 | tf_op jit(solution)/shard_map/ppermute | solution.py:1019
  163.9 8.6 %collective-permute-start.31 = (bf16[80,512]{1,0:T(8,128)(2,1)S(1)}, bf16[80,512]{1,0:T(8,128)(2,1)S(1)}, u32[]{:S(2)}, u32[]{:S(2)}) collective-permute-start(bf16[80,512]{1,0:T(8,128)(2,1)S(1)} %get-tuple-element.198.after.refs_3_), channel_id=1, source_target_pairs={{0,8},{2,10},{4,12},{6,14},{8,0},{10,2},{12,4},{14,6},{16,24},{18,... | collective-permute-start | bytes 245768 | tf_op jit(solution)/shard_map/ppermute | solution.py:1019
  165.2 10.1 %collective-permute-start.34 = (bf16[576,512]{1,0:T(8,128)(2,1)}, bf16[576,512]{1,0:T(8,128)(2,1)}, u32[]{:S(2)}, u32[]{:S(2)}) collective-permute-start(bf16[576,512]{1,0:T(8,128)(2,1)} %shard_map.346.refs_0_.refs_1_), channel_id=1, source_target_pairs={{0,2},{2,0},{4,6},{6,4},{8,10},{10,8},{12,14},{14,12},{16,18},{18,... | collective-permute-start | bytes 1769480 | tf_op jit(solution)/shard_map/ppermute | solution.py:1019
  172.0 3.3 %collective-permute-start.35 = (bf16[576,512]{1,0:T(8,128)(2,1)}, bf16[576,512]{1,0:T(8,128)(2,1)}, u32[]{:S(2)}, u32[]{:S(2)}) collective-permute-start(bf16[576,512]{1,0:T(8,128)(2,1)} %collective-permute-done.30.refs_1_.refs_2_), channel_id=1, source_target_pairs={{0,2},{2,0},{4,6},{6,4},{8,10},{10,8},{12,14},{14,12},{16,18},{18,... | collective-permute-start | bytes 1769480 | tf_op jit(solution)/shard_map/ppermute | solution.py:1019
  173.1 10.4 %collective-permute-start.36 = (bf16[336,512]{1,0:T(8,128)(2,1)S(1)}, bf16[336,512]{1,0:T(8,128)(2,1)S(1)}, u32[]{:S(2)}, u32[]{:S(2)}) collective-permute-start(bf16[336,512]{1,0:T(8,128)(2,1)S(1)} %shard_map.350.refs_0_.mine), channel_id=1, source_target_pairs={{0,4},{2,6},{4,0},{6,2},{8,12},{10,14},{12,8},{14,10},{16,20},{18,... | collective-permute-start | bytes 1032200 | tf_op jit(solution)/shard_map/ppermute | solution.py:1019
  175.3 8.9 %collective-permute-start.37 = (bf16[336,512]{1,0:T(8,128)(2,1)S(1)}, bf16[336,512]{1,0:T(8,128)(2,1)S(1)}, u32[]{:S(2)}, u32[]{:S(2)}) collective-permute-start(bf16[336,512]{1,0:T(8,128)(2,1)S(1)} %shard_map.350.refs_0_.mine), channel_id=1, source_target_pairs={{0,2},{2,0},{4,6},{6,4},{8,10},{10,8},{12,14},{14,12},{16,18},{18,... | collective-permute-start | bytes 1032200 | tf_op jit(solution)/shard_map/ppermute | solution.py:1019
  184.1 1.7 collective-permute-start.38

commit v4 on v3

--- a/solution.py
+++ b/solution.py
@@ -922,21 +922,30 @@
     out_ref[...] = norm_back(scaled, hat_ref[...].astype(f32), inverse_ref[...]).astype(bf16)
 
 
-def section_back(after, low, hat, inverse, merge, params):
+def section_back(after, out, low, hat, inverse, merge, params, begin, steps):
     count = low.shape[0]
-    return kernel_call(
-        section_back_body,
-        (count // ROWS,),
-        [
-            pl.BlockSpec(memory_space=pl.ANY), by_rows(ROWS, D), by_rows(ROWS, MERGE_IN), by_rows(ROWS, 1),
-            whole((MERGE_IN, D)), whole((24, 2048)),
-        ],
-        [by_rows(ROWS, MERGE_IN), whole((8, 128))],
-        [pltpu.HBM((count, MERGE_IN), bf16), shape_of((8, 128), f32)],
-        flops=2 * count * D * MERGE_IN,
-        moved=count * 5 * MERGE_IN,
-        room=16,
-    )(after, in_hbm(low), in_hbm(hat), inverse, merge, params)
+
+    def rows_at(columns):
+        return pl.BlockSpec((ROWS, columns), lambda i: (i + begin, 0))
+
+    first = out is None
+
+    def body(*refs):
+        section_back_body(*(refs if first else refs[1:]))
+
+    return pl.pallas_call(
+        body,
+        grid=(steps,),
+        in_specs=([] if first else [ANYWHERE])
+        + [ANYWHERE, rows_at(D), rows_at(MERGE_IN), rows_at(1), whole((MERGE_IN, D)), whole((24, 2048))],
+        out_specs=[rows_at(MERGE_IN), whole((8, 128))],
+        out_shape=[pltpu.HBM((count, MERGE_IN), bf16), shape_of((8, 128), f32)],
+        input_output_aliases={} if first else {0: 0},
+        compiler_params=pltpu.CompilerParams(
+            dimension_semantics=("arbitrary",), vmem_limit_bytes=16 * 1024 * 1024
+        ),
+        cost_estimate=COST,
+    )(*([] if first else [out]), after, in_hbm(low), in_hbm(hat), inverse, merge, params)
 
 
 def spread_matrix():
@@ -1419,21 +1428,25 @@
             merge_total_body, place, last_parts[0], (last_span, 16), *([last_parts[0]] + last_got), cost=LONG
         )
         last_all = [last_total] + [ring.z(last_total, step) for step in range(1, along)]
-        section_grad, token = section_back(last_total, low, hat, inverse, merge_full, params)
+        steps = count // ROWS
+        section_grad, token = section_back(last_total, None, low, hat, inverse, merge_full, params, 0, steps // 2)
         (last_near,) = stage(
             last_beside_body, place, (token, feed_beside), (336,), vectors, *last_all, cost=LONG
         )
         last_far = ring.x(last_near)
         feed_cores = ring.core(feed_mine), ring.core(feed_beside)
+        section_grad, token = section_back(
+            last_near, section_grad, low, hat, inverse, merge_full, params, steps // 2, steps - steps // 2
+        )
         down_grad, up_grad, proj_grad, token = feed_unpack(
-            along, place, last_near, (feed_mine, feed_beside, *feed_cores)
+            along, place, token, (feed_mine, feed_beside, *feed_cores)
         )
         (last_far,) = stage(beside_body, place, token, (336,), last_far)
         qkv_grad, merge_grad, vectors = last_unpack(
             along, place, last_near, last_far, ring.core(last_near), ring.core(last_far)
         )
     else:
-        section_grad, _ = section_back(low, low, hat, inverse, merge_full, params)
+        section_grad, _ = section_back(low, None, low, hat, inverse, merge_full, params, 0, count // ROWS)
         down_grad, up_grad, qkv_grad, proj_grad, merge_grad, vectors = sum_plainly(
             tp_size, (own_send, own_keep, other_send, other_keep), (proj_send, proj_keep), (qkv_send, qkv_keep),
             (merge_send, merge_keep),

time: 192 us -> 189 us (0.984)
  waiting for transfers between devices: 22.6 us -> 18.2 us
    ppermute x29, waiting for transfers between devices: 16.2 us -> 11.8 us  [to(): lax.ppermute(array, 'rows', [(i, i ^ bits) for i in range(self.rows_size)])]
    pallas_call x1 -> x2, Pallas kernels: 6.8 us -> 8.31 us  [section_back(): pl.pallas_call(body, grid=(steps,), in_specs=([] if first else [ANYWHERE]...]
  transfers between devices with their start and end apart: 39 -> 39, of which waited for: 10 -> 9; matrix products, arithmetic and copies ran while one was open for 0% -> 0% of each run, Pallas kernels for 63% -> 64%
where the time goes in v4:
time: 189 us; the launch traced here: 186 us
  Pallas kernels  125 us (66%)
  starting transfers between devices  40.7 us (22%)
  waiting for transfers between devices  18.2 us (10%)
    ppermute x29, starting transfers between devices, to(): lax.ppermute(array, 'rows', [(i, i ^ bits) for i in range(self.rows_size)])  27.7 us
    pallas_call x1, Pallas kernels, attend_back(): kernel_call(attend_back_body, (count // ROWS,), [ANYWHERE, RESIDENT, by_w...  18.5 us
    pallas_call x13, Pallas kernels, plain_call_after(): pl.pallas_call(without_after, in_specs=[SCALARS] + [pl.BlockSpec(memory_s...  16.2 us
    pallas_call x2, Pallas kernels, feed_middle(): pl.pallas_call(partial(feed_middle_body, own), in_specs=[SCALARS] + [RESI...  13.9 us
    pallas_call x1, Pallas kernels, feed_near(): kernel_call(feed_near_body, (blocks + 1,), [SCALARS] + [RESIDENT] * 9 + [...  12.7 us
    pallas_call x1, Pallas kernels, attend(): kernel_call(attend_body, (count // ROWS,), [SCALARS, RESIDENT, RESIDENT,...  12.4 us
    pallas_call x1, Pallas kernels, feed_own(): kernel_call(feed_own_body, (blocks + 1,), [SCALARS, taken(D), taken(D), t...  12.1 us
    ppermute x29, waiting for transfers between devices, to(): lax.ppermute(array, 'rows', [(i, i ^ bits) for i in range(self.rows_size)])  11.8 us
  transfers between devices with their start and end apart: 39, of which 9 were waited for; matrix products, arithmetic and copies ran while one was open for 0% of the time, Pallas kernels for 64%

profile of v4, /device:TPU:0, one launch (start us, length us, event | category | flops | bytes accessed | tf_op | source)
XLA Modules:
  0.0 185.9 jit_solution(13273559815437285588)
XLA Ops:
  0.7 1.5 shard_map.322.after
  2.3 3.0 %collective-permute-start.1 = (bf16[256,512]{1,0:T(8,128)(2,1)S(1)}, bf16[256,512]{1,0:T(8,128)(2,1)S(1)}, u32[]{:S(2)}, u32[]{:S(2)}) collective-permute-start(bf16[256,512]{1,0:T(8,128)(2,1)S(1)} %shard_map.322.after), channel_id=1, source_target_pairs={{0,1},{1,0},{2,3},{3,2},{4,5},{5,4},{6,7},{7,6},{8,9},{9,8},{10,11... | collective-permute-start | bytes 786440 | tf_op jit(solution)/shard_map/ppermute | solution.py:1040
  5.3 1.4 shard_map.323
  6.8 1.5 shard_map.324
  8.3 1.6 shard_map.325.array_ref
  9.9 2.4 %collective-permute-done.refs_0_.others_ref = bf16[32,512]{1,0:T(8,128)(2,1)S(1)} collective-permute-done((bf16[32,512]{1,0:T(8,128)(2,1)S(1)}, bf16[32,512]{1,0:T(8,128)(2,1)S(1)}, u32[]{:S(2)}, u32[]{:S(2)}) %collective-permute-start) | collective-permute-done | bytes 32800 | tf_op jit(solution)/shard_map/ppermute | solution.py:1040
  12.3 1.7 collective-permute-start.3
  14.0 3.0 %shard_map.327 = (bf16[1600,1024]{1,0:T(8,128)(2,1)S(1)}, f32[1600,1]{1,0:T(8,128)S(1)}) custom-call(bf16[512,512]{1,0:T(8,128)(2,1)S(1)} %shard_map.326.after, bf16[1600,1024]{1,0:T(8,128)(2,1)} %rows_ref.1), custom_call_target="tpu_custom_call" | custom-call | flops 1 | bytes 1 | tf_op jit(solution)/shard_map/pallas_call | solution.py:332
  17.1 6.0 %shard_map.328 = (f32[1600,512]{1,0:T(8,128)}, bf16[1600,512]{1,0:T(8,128)(2,1)S(1)}, bf16[1600,512]{1,0:T(8,128)(2,1)}, bf16[1024,512]{1,0:T(8,128)(2,1)}, f32[24,2048]{1,0:T(8,128)S(1)}, /*index=5*/f32[1024,128]{1,0:T(8,128)}) custom-call(s32[4]{0:T(128)S(1)} %pad_add_fusion.place, bf16[1600,1024]{1,0:T(8,128)(2,1)S(1)} %get-tuple-element.124.hat_ref, ...), custom_call_target="tpu_custom_call" | custom-call | flops 1 | bytes 1 | tf_op jit(solution)/shard_map/pallas_call | solution.py:393
  23.1 2.5 %shard_map.329 = (f32[4,112,512]{2,1,0:T(8,128)S(1)}, bf16[1600,1024]{1,0:T(8,128)(2,1)}) custom-call(f32[24,2048]{1,0:T(8,128)S(1)} %get-tuple-element.126.params_ref.refs_5_.refs_6_, bf16[1600,1024]{1,0:T(8,128)(2,1)S(1)} %get-tuple-element.124.hat_ref), custom_call_target="tpu_custom_call" | custom-call | flops 1 | bytes 1 | tf_op jit(solution)/shard_map/pallas_call | solution.py:987
  25.6 0.6 shard_map.333
  26.3 1.3 collective-permute-start.5
  27.6 1.9 %collective-permute-done.4.far_ref = bf16[512,512]{1,0:T(8,128)(2,1)S(1)} collective-permute-done((bf16[512,512]{1,0:T(8,128)(2,1)S(1)}, bf16[512,512]{1,0:T(8,128)(2,1)S(1)}, u32[]{:S(2)}, u32[]{:S(2)}) %collective-permute-start.4) | collective-permute-done | bytes 524320 | tf_op jit(solution)/shard_map/ppermute | solution.py:1028
  29.5 12.4 %shard_map.330 = (bf16[16,128,1536]{2,1,0:T(8,128)(2,1)}, bf16[16,4,112,512]{3,2,1,0:T(8,128)(2,1)}, bf16[1600,512]{1,0:T(8,128)(2,1)}, bf16[16,112,512]{2,1,0:T...) custom-call(s32[4]{0:T(128)S(1)} %pad_add_fusion.place, ...), custom_call_target="tpu_custom_call" | custom-call | flops 1 | bytes 1 | tf_op jit(solution)/shard_map/pallas_call | solution.py:486
  41.9 12.1 %shard_map.331 = (f32[1600,512]{1,0:T(8,128)S(1)}, f32[1600,1]{1,0:T(8,128)S(1)}, f32[1600,512]{1,0:T(8,128)S(1)}, f32[1600,512]{1,0:T(8,128)S(1)}, bf16[1600,51...) custom-call(s32[4]{0:T(128)S(1)} %pad_add_fusion.place, ...), custom_call_target="tpu_custom_call" | custom-call | flops 1 | bytes 1 | tf_op jit(solution)/shard_map/pallas_call | solution.py:606
  54.7 6.6 %shard_map.332 = (f32[1600,512]{1,0:T(8,128)S(1)}, f32[1600,512]{1,0:T(8,128)S(1)}, bf16[1024,512]{1,0:T(8,128)(2,1)S(1)}, f32[8,512]{1,0:T(8,128)S(1)}) custom-call(s32[4]{0:T(128)S(1)} %pad_add_fusion.place, bf16[1600,512]{1,0:T(8,128)(2,1)S(1)} %get-tuple-element.133.second_ref, ...), custom_call_target="tpu_custom_call", output_to_operand_aliasing={{0}: (4, {}), {1}: (5, {})} | custom-call | flops 999999995904 | bytes 1 | tf_op jit(solution)/shard_map/pallas_call | solution.py:647
  61.2 7.3 %shard_map.334 = (f32[1600,512]{1,0:T(8,128)S(1)}, f32[1600,512]{1,0:T(8,128)S(1)}, bf16[1024,512]{1,0:T(8,128)(2,1)S(1)}, f32[8,512]{1,0:T(8,128)S(1)}) custom-call(s32[4]{0:T(128)S(1)} %pad_add_fusion.place, bf16[1600,512]{1,0:T(8,128)(2,1)S(1)} %get-tuple-element.133.second_ref, ...), custom_call_target="tpu_custom_call", output_to_operand_aliasing={{0}: (4, {}), {1}: (5, {})} | custom-call | flops 1 | bytes 1 | tf_op jit(solution)/shard_map/pallas_call | solution.py:647
  68.7 12.7 %shard_map.335 = (bf16[1600,512]{1,0:T(8,128)(2,1)}, f32[1600,512]{1,0:T(8,128)S(1)}, bf16[1600,512]{1,0:T(8,128)(2,1)S(1)}, bf16[1024,512]{1,0:T(8,128)(2,1)S(1...) custom-call(s32[4]{0:T(128)S(1)} %pad_add_fusion.place, ...), custom_call_target="tpu_custom_call" | custom-call | flops 1 | bytes 1 | tf_op jit(solution)/shard_map/pallas_call | solution.py:712
  81.9 1.8 shard_map.336
  83.7 0.6 shard_map.337
  84.3 1.6 collective-permute-start.11
  85.8 0.8 collective-permute-start.12
  86.6 1.2 collective-permute-start.10
  87.8 18.5 %shard_map.338 = (bf16[1600,1536]{1,0:T(8,128)(2,1)S(1)}, bf16[1600,512]{1,0:T(8,128)(2,1)S(1)}, f32[1,1536]{1,0:T(1,128)S(1)}, f32[8,512]{1,0:T(8,128)S(1)}, f3...) custom-call(bf16[576,512]{1,0:T(8,128)(2,1)S(1)} %get-tuple-element.157.after, ...), custom_call_target="tpu_custom_call" | custom-call | flops 1 | bytes 1 | tf_op jit(solution)/shard_map/pallas_call | solution.py:801
  106.4 5.7 %shard_map.339 = (bf16[768,512]{1,0:T(8,128)(2,1)}, bf16[768,512]{1,0:T(8,128)(2,1)S(1)}, bf16[1600,1024]{1,0:T(8,128)(2,1)S(1)}) custom-call(s32[4]{0:T(128)S(1)} %pad_add_fusion.place, f32[1,1536]{1,0:T(1,128)S(1)} %get-tuple-element.167.after.qkv_sums_ref, bf16[1600,512]{1,0:T(8,128)(2,1)S(1)} %get-tuple-element.168.first_ref, ...), custom_call_target="tpu_custom_call" | custom-call | flops 1 | bytes 1 | tf_op jit(solution)/shard_map/pallas_call | solution.py:857
  112.2 0.6 collective-permute-done.12.refs_4_
  112.8 1.4 collective-permute-done.10.refs_2_
  114.2 0.8 shard_map.340
  115.0 1.6 collective-permute-start.14
  116.7 2.6 %collective-permute-start.15 = (bf16[144,512]{1,0:T(8,128)(2,1)S(1)}, bf16[144,512]{1,0:T(8,128)(2,1)S(1)}, u32[]{:S(2)}, u32[]{:S(2)}) collective-permute-start(bf16[144,512]{1,0:T(8,128)(2,1)S(1)} %get-tuple-element.186), channel_id=1, source_target_pairs={{0,16},{2,18},{4,20},{6,22},{8,24},{10,26},{12,28},{14,30},{16,0},... | collective-permute-start | bytes 442376 | tf_op jit(solution)/shard_map/ppermute | solution.py:1028
  119.5 2.0 %shard_map.341 = (bf16[192,512]{1,0:T(8,128)(2,1)}, bf16[192,512]{1,0:T(8,128)(2,1)}, bf16[192,512]{1,0:T(8,128)(2,1)}, bf16[192,512]{1,0:T(8,128)(2,1)S(1)}) custom-call(s32[4]{0:T(128)S(1)} %pad_add_fusion.place, bf16[144,512]{1,0:T(8,128)(2,1)S(1)} %get-tuple-element.175.refs_0_.refs_1_, bf16[768,512]{1,0:T(8,128)(2,1)S(1)} %get-tuple-element.176.refs_1_, ...), custom_call_target="tpu_custom_call" | custom-call | flops 1 | bytes 1 | tf_op jit(solution)/shard_map/pallas_call | solution.py:249
  121.5 1.5 collective-permute-start.18
  123.0 1.1 collective-permute-start.17
  124.1 5.1 %shard_map.342 = (bf16[544,512]{1,0:T(8,128)(2,1)}, bf16[544,512]{1,0:T(8,128)(2,1)S(1)}) custom-call(s32[4]{0:T(128)S(1)} %pad_add_fusion.place, bf16[192,512]{1,0:T(8,128)(2,1)} %get-tuple-element.177.after, bf16[1600,512]{1,0:T(8,128)(2,1)S(1)} %get-tuple-element.178.low_ref.refs_1_.refs_2_, bf16[1600,1024]{1,0:T(8,128)(2,1)S(1)} %get-tuple-element.179.hat_ref, ...), custom_call_target="tpu_custom_call" | custom-call | flops 1 | bytes 1 | tf_op jit(solution)/shard_map/pallas_call | solution.py:906
  129.2 0.9 collective-permute-start.19
  130.2 0.6 shard_map.343.refs_0_.refs_1_
  130.8 3.7 %collective-permute-start.23 = (bf16[144,512]{1,0:T(8,128)(2,1)S(1)}, bf16[144,512]{1,0:T(8,128)(2,1)S(1)}, u32[]{:S(2)}, u32[]{:S(2)}) collective-permute-start(bf16[144,512]{1,0:T(8,128)(2,1)S(1)} %shard_map.343.refs_0_.refs_1_), channel_id=1, source_target_pairs={{0,24},{2,26},{4,28},{6,30},{8,16},{10,18},{12,20},{14,22},{16,8},... | collective-permute-start | bytes 442376 | tf_op jit(solution)/shard_map/ppermute | solution.py:1028
  134.5 1.7 collective-permute-done.19.refs_4_
  136.1 0.7 collective-permute-start.21
  136.8 1.2 shard_map.344.refs_0_.refs_1_
  138.0 1.2 shard_map.345
  139.3 0.6 collective-permute-start.25
  139.9 1.9 %collective-permute-start.26 = (bf16[144,512]{1,0:T(8,128)(2,1)S(1)}, bf16[144,512]{1,0:T(8,128)(2,1)S(1)}, u32[]{:S(2)}, u32[]{:S(2)}) collective-permute-start(bf16[144,512]{1,0:T(8,128)(2,1)S(1)} %get-tuple-element.195), channel_id=1, source_target_pairs={{0,5},{1,4},{2,7},{3,6},{4,1},{5,0},{6,3},{7,2},{8,13},{9,12},{10,... | collective-permute-start | bytes 442376 | tf_op jit(solution)/shard_map/ppermute | solution.py:1044
  141.8 1.1 collective-permute-start.24
  142.8 3.9 %collective-permute-done.22.refs_3_ = bf16[144,512]{1,0:T(8,128)(2,1)S(1)} collective-permute-done((bf16[144,512]{1,0:T(8,128)(2,1)S(1)}, bf16[144,512]{1,0:T(8,128)(2,1)S(1)}, u32[]{:S(2)}, u32[]{:S(2)}) %collective-permute-start.22) | collective-permute-done | bytes 147488 | tf_op jit(solution)/shard_map/ppermute | solution.py:1028
  146.7 1.4 shard_map.346.refs_0_.refs_1_
  148.5 0.6 shard_map.347
  149.1 2.1 %collective-permute-start.27 = (bf16[96,512]{1,0:T(8,128)(2,1)S(1)}, bf16[96,512]{1,0:T(8,128)(2,1)S(1)}, u32[]{:S(2)}, u32[]{:S(2)}) collective-permute-start(bf16[96,512]{1,0:T(8,128)(2,1)S(1)} %get-tuple-element.197), channel_id=1, source_target_pairs={{0,8},{2,10},{4,12},{6,14},{8,0},{10,2},{12,4},{14,6},{16,24},{18,... | collective-permute-start | bytes 294920 | tf_op jit(solution)/shard_map/ppermute | solution.py:1028
  151.3 2.0 %collective-permute-start.28 = (bf16[96,512]{1,0:T(8,128)(2,1)S(1)}, bf16[96,512]{1,0:T(8,128)(2,1)S(1)}, u32[]{:S(2)}, u32[]{:S(2)}) collective-permute-start(bf16[96,512]{1,0:T(8,128)(2,1)S(1)} %get-tuple-element.198), channel_id=1, source_target_pairs={{0,16},{2,18},{4,20},{6,22},{8,24},{10,26},{12,28},{14,30},{16,0},... | collective-permute-start | bytes 294920 | tf_op jit(solution)/shard_map/ppermute | solution.py:1028
  153.7 1.7 collective-permute-start.30
  155.4 4.7 %collective-permute-done.28.refs_3_ = bf16[96,512]{1,0:T(8,128)(2,1)S(1)} collective-permute-done((bf16[96,512]{1,0:T(8,128)(2,1)S(1)}, bf16[96,512]{1,0:T(8,128)(2,1)S(1)}, u32[]{:S(2)}, u32[]{:S(2)}) %collective-permute-start.28) | collective-permute-done | bytes 98336 | tf_op jit(solution)/shard_map/ppermute | solution.py:1028
  160.1 0.6 shard_map.348
  160.7 2.5 %collective-permute-start.33 = (bf16[80,512]{1,0:T(8,128)(2,1)S(1)}, bf16[80,512]{1,0:T(8,128)(2,1)S(1)}, u32[]{:S(2)}, u32[]{:S(2)}) collective-permute-start(bf16[80,512]{1,0:T(8,128)(2,1)S(1)} %get-tuple-element.200.refs_0_.refs_3_), channel_id=1, source_target_pairs={{0,24},{2,26},{4,28},{6,30},{8,16},{10,18},{12,20},{14,22},{16,8},... | collective-permute-start | bytes 245768 | tf_op jit(solution)/shard_map/ppermute | solution.py:1028
  163.2 0.6 collective-permute-start.32
  163.8 1.3 collective-permute-start.31
  165.1 4.2 %shard_map.349 = (bf16[1600,1024]{1,0:T(8,128)(2,1)}, f32[8,128]{1,0:T(8,128)S(1)}) custom-call(bf16[80,512]{1,0:T(8,128)(2,1)S(1)} %get-tuple-element.200.refs_0_.refs_3_, bf16[1600,512]{1,0:T(8,128)(2,1)} %copy-done, bf16[1600,1024]{1,0:T(8,128)(2,1)} %get-tuple-element.170.hat_in.refs_2_.refs_3_, f32[1600,1]{1,0:T(8,128)S(1)} %get-tuple-element.201.refs_3_.refs_4_, ...), custom_call_target="tpu_custom_call" | custom-call | flops 1 | bytes 1 | tf_op jit(solution)/shard_map/pallas_call | solution.py:936
  169.8 0.6 shard_map.350.refs_1_.mine
  170.4 2.2 %collective-permute-start.36 = (bf16[336,512]{1,0:T(8,128)(2,1)S(1)}, bf16[336,512]{1,0:T(8,128)(2,1)S(1)}, u32[]{:S(2)}, u32[]{:S(2)}) collective-permute-start(bf16[336,512]{1,0:T(8,128)(2,1)S(1)} %shard_map.350.refs_1_.mine), channel_id=1, source_target_pairs={{0,4},{2,6},{4,0},{6,2},{8,12},{10,14},{12,8},{14,10},{16,20},{18,... | collective-permute-start | bytes 1032200 | tf_op jit(solution)/shard_map/ppermute | solution.py:1028
  172.6 4.2 %shard_map.351 = (bf16[1600,1024]{1,0:T(8,128)(2,1)}, f32[8,128]{1,0:T(8,128)S(1)}) custom-call(bf16[1600,1024]{1,0:T(8,128)(2,1)} %get-tuple-element.202.refs_0_, bf16[336,512]{1,0:T(8,128)(2,1)S(1)} %shard_map.350.refs_1_.mine, bf16[1600,512]{1,0:T(8,128)(2,1)} %copy-done, ...), custom_call_target="tpu_custom_call", output_to_operand_aliasing={{0}: (0, {})} | custom-call | flops 1 | bytes 1 | tf_op jit(solution)/shard_map/pallas_call | solution.py:936
  176.7 4.2 %shard_map.352 = (f32[1024,512]{1,0:T(8,128)}, f32[512,1024]{1,0:T(8,128)}, f32[256,512]{1,0:T(8,128)}, f32[8,128]{1,0:T(8,128)S(1)}) custom-call(s32[4]{0:T(128)S(1)} %pad_add_fusion.place, f32[8,128]{1,0:T(8,128)S(1)} %get-tuple-element.206.refs_0_, bf16[576,512]{1,0:T(8,128)(2,1)} %shard_map.346.refs_0_.refs_1_, ...), custom_call_target="tpu_custom_call" | custom-call | flops 1 | bytes 1 | tf_op jit(solution)/shard_map/pallas_call | solution.py:249
  180.9 0.6 shard_map.353.beside
  181.5 0.6 collective-permute-start.38
  182.1 1.3 collective-permute-done.38.core_beside
  183.3 2.3 %shard_map.354 = (f32[3,512,256]{2,1,0:T(8,128)}, f32[512,512]{1,0:T(8,128)}, f32[1,512]{1,0:T(1,128)}, f32[1,512]{1,0:T(1,128)}, f32[1,512]{1,0:T(1,128)}, /*in...) custom-call(s32[4]{0:T(128)S(1)} %pad_add_fusion.place, ...), custom_call_target="tpu_custom_call" | custom-call | flops 1 | bytes 1 | tf_op jit(solution)/shard_map/pallas_call | solution.py:196
  (86 shorter events, 3.2 us)
Async XLA Ops:
  2.3 10.0 %collective-permute-start.1 = (bf16[256,512]{1,0:T(8,128)(2,1)S(1)}, bf16[256,512]{1,0:T(8,128)(2,1)S(1)}, u32[]{:S(2)}, u32[]{:S(2)}) collective-permute-start(bf16[256,512]{1,0:T(8,128)(2,1)S(1)} %shard_map.322.after), channel_id=1, source_target_pairs={{0,1},{1,0},{2,3},{3,2},{4,5},{5,4},{6,7},{7,6},{8,9},{9,8},{10,11... | collective-permute-start | bytes 786440 | tf_op jit(solution)/shard_map/ppermute | solution.py:1040
  6.7 5.6 %collective-permute-start = (bf16[32,512]{1,0:T(8,128)(2,1)S(1)}, bf16[32,512]{1,0:T(8,128)(2,1)S(1)}, u32[]{:S(2)}, u32[]{:S(2)}) collective-permute-start(bf16[32,512]{1,0:T(8,128)(2,1)S(1)} %get-tuple-element.123), channel_id=1, source_target_pairs={{0,1},{1,0},{2,3},{3,2},{4,5},{5,4},{6,7},{7,6},{8,9},{9,8},{10,11... | collective-permute-start | bytes 98312 | tf_op jit(solution)/shard_map/ppermute | solution.py:1040
  8.2 8.8 %copy-start.9 = (bf16[512,512]{1,0:T(8,128)(2,1)S(1)}, bf16[512,512]{1,0:T(8,128)(2,1)}, u32[]{:S(2)}) copy-start(bf16[512,512]{1,0:T(8,128)(2,1)} %own_ref.1) | copy-start | bytes 1572868
  8.3 8.8 %copy-start.13 = (f32[512]{0:T(512)S(1)}, f32[512]{0:T(512)}, u32[]{:S(2)}) copy-start(f32[512]{0:T(512)} %param.25) | copy-start | bytes 6148
  8.3 8.8 %copy-start.15 = (f32[512]{0:T(512)S(1)}, f32[512]{0:T(512)}, u32[]{:S(2)}) copy-start(f32[512]{0:T(512)} %param.26) | copy-start | bytes 6148
  12.3 13.3 %collective-permute-start.3 = (bf16[512,512]{1,0:T(8,128)(2,1)S(1)}, bf16[512,512]{1,0:T(8,128)(2,1)S(1)}, u32[]{:S(2)}, u32[]{:S(2)}) collective-permute-start(bf16[512,512]{1,0:T(8,128)(2,1)S(1)} %shard_map.326.after), channel_id=1, source_target_pairs={{0,1},{1,0},{2,3},{3,2},{4,5},{5,4},{6,7},{7,6},{8,9},{9,8},{10,11... | collective-permute-start | bytes 1572872 | tf_op jit(solution)/shard_map/ppermute | solution.py:1040
  14.0 3.0 %collective-permute-start.2 = (bf16[256,512]{1,0:T(8,128)(2,1)S(1)}, bf16[256,512]{1,0:T(8,128)(2,1)S(1)}, u32[]{:S(2)}, u32[]{:S(2)}) collective-permute-start(bf16[256,512]{1,0:T(8,128)(2,1)S(1)} %collective-permute-done.1.refs_1_.near_ref), channel_id=1, source_target_pairs={{0,2},{2,0},{4,6},{6,4},{8,10},{10,8},{12,14},{14,12},{16,18},{18,... | collective-permute-start | bytes 786440 | tf_op jit(solution)/shard_map/ppermute | solution.py:1028
  17.1 8.5 %copy-start.6 = (bf16[512,1024]{1,0:T(8,128)(2,1)S(1)}, bf16[512,1024]{1,0:T(8,128)(2,1)}, u32[]{:S(2)}) copy-start(bf16[512,1024]{1,0:T(8,128)(2,1)} %refs_2_.1) | copy-start | bytes 3145732
  17.1 8.5 %copy-start.7 = (bf16[1024,512]{1,0:T(8,128)(2,1)S(1)}, bf16[1024,512]{1,0:T(8,128)(2,1)}, u32[]{:S(2)}) copy-start(bf16[1024,512]{1,0:T(8,128)(2,1)} %refs_3_.1) | copy-start | bytes 3145732
  23.1 45.6 %copy-start.1 = (f32[24,2048]{1,0:T(8,128)}, f32[24,2048]{1,0:T(8,128)S(1)}, u32[]{:S(2)}) copy-start(f32[24,2048]{1,0:T(8,128)S(1)} %get-tuple-element.126.params_ref.refs_5_.refs_6_) | copy-start | bytes 589828
  23.1 6.4 %copy-start.8 = (bf16[3,512,256]{2,1,0:T(8,128)(2,1)S(1)}, bf16[3,512,256]{2,1,0:T(8,128)(2,1)}, u32[]{:S(2)}) copy-start(bf16[3,512,256]{2,1,0:T(8,128)(2,1)} %param.27) | copy-start | bytes 2359300
  26.3 15.6 %copy-start.10 = (bf16[256,512]{1,0:T(8,128)(2,1)S(1)}, bf16[256,512]{1,0:T(8,128)(2,1)}, u32[]{:S(2)}) copy-start(bf16[256,512]{1,0:T(8,128)(2,1)} %proj_own.1) | copy-start | bytes 786436
  26.3 15.6 %copy-start.12 = (f32[512]{0:T(512)S(1)}, f32[512]{0:T(512)}, u32[]{:S(2)}) copy-start(f32[512]{0:T(512)} %param.32) | copy-start | bytes 6148
  26.3 15.6 %copy-start.16 = (f32[512]{0:T(512)S(1)}, f32[512]{0:T(512)}, u32[]{:S(2)}) copy-start(f32[512]{0:T(512)} %param.31) | copy-start | bytes 6148
  26.3 15.6 %copy-start.17 = (f32[512]{0:T(512)S(1)}, f32[512]{0:T(512)}, u32[]{:S(2)}) copy-start(f32[512]{0:T(512)} %param.33) | copy-start | bytes 6148
  26.3 15.6 %copy-start.18 = (f32[512]{0:T(512)S(1)}, f32[512]{0:T(512)}, u32[]{:S(2)}) copy-start(f32[512]{0:T(512)} %param.37) | copy-start | bytes 6148
  26.3 28.0 %collective-permute-start.5 = (bf16[1024,512]{1,0:T(8,128)(2,1)S(1)}, bf16[1024,512]{1,0:T(8,128)(2,1)}, u32[]{:S(2)}, u32[]{:S(2)}) collective-permute-start(bf16[1024,512]{1,0:T(8,128)(2,1)S(1)} %shard_map.333), channel_id=1, source_target_pairs={{0,1},{1,0},{2,3},{3,2},{4,5},{5,4},{6,7},{7,6},{8,9},{9,8},{10,11... | collective-permute-start | bytes 3145736 | tf_op jit(solution)/shard_map/ppermute | solution.py:1040
  27.6 1.9 %collective-permute-start.4 = (bf16[512,512]{1,0:T(8,128)(2,1)S(1)}, bf16[512,512]{1,0:T(8,128)(2,1)S(1)}, u32[]{:S(2)}, u32[]{:S(2)}) collective-permute-start(bf16[512,512]{1,0:T(8,128)(2,1)S(1)} %collective-permute-done.3.near_ref.refs_1_), channel_id=1, source_target_pairs={{0,2},{2,0},{4,6},{6,4},{8,10},{10,8},{12,14},{14,12},{16,18},{18,... | collective-permute-start | bytes 1572872 | tf_op jit(solution)/shard_map/ppermute | solution.py:1028
  54.1 27.8 %collective-permute-start.8 = (bf16[1024,512]{1,0:T(8,128)(2,1)}, bf16[1024,512]{1,0:T(8,128)(2,1)}, u32[]{:S(2)}, u32[]{:S(2)}) collective-permute-start(bf16[1024,512]{1,0:T(8,128)(2,1)} %get-tuple-element.150), channel_id=1, source_target_pairs={{0,2},{2,0},{4,6},{6,4},{8,10},{10,8},{12,14},{14,12},{16,18},{18,... | collective-permute-start | bytes 3145736 | tf_op jit(solution)/shard_map/ppermute | solution.py:1028
  54.3 6.9 %collective-permute-start.6 = (bf16[1024,512]{1,0:T(8,128)(2,1)}, bf16[1024,512]{1,0:T(8,128)(2,1)}, u32[]{:S(2)}, u32[]{:S(2)}) collective-permute-start(bf16[1024,512]{1,0:T(8,128)(2,1)} %collective-permute-done.5.near_ref), channel_id=1, source_target_pairs={{0,2},{2,0},{4,6},{6,4},{8,10},{10,8},{12,14},{14,12},{16,18},{18,... | collective-permute-start | bytes 3145736 | tf_op jit(solution)/shard_map/ppermute | solution.py:1028
  68.5 13.3 %collective-permute-start.9 = (bf16[1024,512]{1,0:T(8,128)(2,1)S(1)}, bf16[1024,512]{1,0:T(8,128)(2,1)S(1)}, u32[]{:S(2)}, u32[]{:S(2)}) collective-permute-start(bf16[1024,512]{1,0:T(8,128)(2,1)S(1)} %get-tuple-element.152), channel_id=1, source_target_pairs={{0,2},{2,0},{4,6},{6,4},{8,10},{10,8},{12,14},{14,12},{16,18},{18,... | collective-permute-start | bytes 3145736 | tf_op jit(solution)/shard_map/ppermute | solution.py:1028
  81.4 2.2 %collective-permute-start.7 = (bf16[256,512]{1,0:T(8,128)(2,1)S(1)}, bf16[256,512]{1,0:T(8,128)(2,1)S(1)}, u32[]{:S(2)}, u32[]{:S(2)}) collective-permute-start(bf16[256,512]{1,0:T(8,128)(2,1)S(1)} %get-tuple-element.147), channel_id=1, source_target_pairs={{0,2},{2,0},{4,6},{6,4},{8,10},{10,8},{12,14},{14,12},{16,18},{18,... | collective-permute-start | bytes 786440 | tf_op jit(solution)/shard_map/ppermute | solution.py:1028
  81.9 6.0 %copy-start.14 = (f32[512]{0:T(512)S(1)}, f32[512]{0:T(512)}, u32[]{:S(2)}) copy-start(f32[512]{0:T(512)} %param.25) | copy-start | bytes 6148
  84.3 28.0 %collective-permute-start.11 = (bf16[576,512]{1,0:T(8,128)(2,1)S(1)}, bf16[576,512]{1,0:T(8,128)(2,1)S(1)}, u32[]{:S(2)}, u32[]{:S(2)}) collective-permute-start(bf16[576,512]{1,0:T(8,128)(2,1)S(1)} %get-tuple-element.173), channel_id=1, source_target_pairs={{0,4},{2,6},{4,0},{6,2},{8,12},{10,14},{12,8},{14,10},{16,20},{18,... | collective-permute-start | bytes 1769480 | tf_op jit(solution)/shard_map/ppermute | solution.py:1028
  85.8 27.0 %collective-permute-start.12 = (bf16[576,512]{1,0:T(8,128)(2,1)S(1)}, bf16[576,512]{1,0:T(8,128)(2,1)S(1)}, u32[]{:S(2)}, u32[]{:S(2)}) collective-permute-start(bf16[576,512]{1,0:T(8,128)(2,1)S(1)} %get-tuple-element.174), channel_id=1, source_target_pairs={{0,5},{1,4},{2,7},{3,6},{4,1},{5,0},{6,3},{7,2},{8,13},{9,12},{10,... | collective-permute-start | bytes 1769480 | tf_op jit(solution)/shard_map/ppermute | solution.py:1044
  86.6 27.5 %collective-permute-start.10 = (bf16[576,512]{1,0:T(8,128)(2,1)S(1)}, bf16[576,512]{1,0:T(8,128)(2,1)S(1)}, u32[]{:S(2)}, u32[]{:S(2)}) collective-permute-start(bf16[576,512]{1,0:T(8,128)(2,1)S(1)} %get-tuple-element.157.after), channel_id=1, source_target_pairs={{0,1},{1,0},{2,3},{3,2},{4,5},{5,4},{6,7},{7,6},{8,9},{9,8},{10,11... | collective-permute-start | bytes 1769480 | tf_op jit(solution)/shard_map/ppermute | solution.py:1040
  106.4 17.7 %copy-start = (bf16[1600,512]{1,0:T(8,128)(2,1)}, bf16[1600,512]{1,0:T(8,128)(2,1)S(1)}, u32[]{:S(2)}) copy-start(bf16[1600,512]{1,0:T(8,128)(2,1)S(1)} %get-tuple-element.178.low_ref.refs_1_.refs_2_) | copy-start | bytes 4915204
  112.1 7.3 %collective-permute-start.13 = (bf16[768,512]{1,0:T(8,128)(2,1)}, bf16[768,512]{1,0:T(8,128)(2,1)}, u32[]{:S(2)}, u32[]{:S(2)}) collective-permute-start(bf16[768,512]{1,0:T(8,128)(2,1)} %get-tuple-element.171.refs_0_), channel_id=1, source_target_pairs={{0,2},{2,0},{4,6},{6,4},{8,10},{10,8},{12,14},{14,12},{16,18},{18,... | collective-permute-start | bytes 2359304 | tf_op jit(solution)/shard_map/ppermute | solution.py:1028
  114.2 9.9 %copy-start.2 = (f32[24,2048]{1,0:T(8,128)S(1)}, f32[24,2048]{1,0:T(8,128)}, u32[]{:S(2)}) copy-start(f32[24,2048]{1,0:T(8,128)} %copy-done.1) | copy-start | bytes 589828
  114.2 9.9 %copy-start.4 = (bf16[1024,512]{1,0:T(8,128)(2,1)S(1)}, bf16[1024,512]{1,0:T(8,128)(2,1)}, u32[]{:S(2)}) copy-start(bf16[1024,512]{1,0:T(8,128)(2,1)} %get-tuple-element.180.merge_ref.refs_4_.refs_5_) | copy-start | bytes 3145732
  114.2 9.9 %copy-start.11 = (f32[1024,128]{1,0:T(8,128)S(1)}, f32[1024,128]{1,0:T(8,128)}, u32[]{:S(2)}) copy-start(f32[1024,128]{1,0:T(8,128)} %get-tuple-element.181.column_ref) | copy-start | bytes 1572868
  115.0 14.2 %collective-permute-start.14 = (bf16[144,512]{1,0:T(8,128)(2,1)S(1)}, bf16[144,512]{1,0:T(8,128)(2,1)S(1)}, u32[]{:S(2)}, u32[]{:S(2)}) collective-permute-start(bf16[144,512]{1,0:T(8,128)(2,1)S(1)} %get-tuple-element.185), channel_id=1, source_target_pairs={{0,8},{2,10},{4,12},{6,14},{8,0},{10,2},{12,4},{14,6},{16,24},{18,... | collective-permute-start | bytes 442376 | tf_op jit(solution)/shard_map/ppermute | solution.py:1028
  116.7 13.5 %collective-permute-start.15 = (bf16[144,512]{1,0:T(8,128)(2,1)S(1)}, bf16[144,512]{1,0:T(8,128)(2,1)S(1)}, u32[]{:S(2)}, u32[]{:S(2)}) collective-permute-start(bf16[144,512]{1,0:T(8,128)(2,1)S(1)} %get-tuple-element.186), channel_id=1, source_target_pairs={{0,16},{2,18},{4,20},{6,22},{8,24},{10,26},{12,28},{14,30},{16,0},... | collective-permute-start | bytes 442376 | tf_op jit(solution)/shard_map/ppermute | solution.py:1028
  119.3 10.9 %collective-permute-start.16 = (bf16[144,512]{1,0:T(8,128)(2,1)S(1)}, bf16[144,512]{1,0:T(8,128)(2,1)S(1)}, u32[]{:S(2)}, u32[]{:S(2)}) collective-permute-start(bf16[144,512]{1,0:T(8,128)(2,1)S(1)} %get-tuple-element.187), channel_id=1, source_target_pairs={{0,24},{2,26},{4,28},{6,30},{8,16},{10,18},{12,20},{14,22},{16,8},... | collective-permute-start | bytes 442376 | tf_op jit(solution)/shard_map/ppermute | solution.py:1028
  121.5 13.0 %collective-permute-start.18 = (bf16[192,512]{1,0:T(8,128)(2,1)}, bf16[192,512]{1,0:T(8,128)(2,1)}, u32[]{:S(2)}, u32[]{:S(2)}) collective-permute-start(bf16[192,512]{1,0:T(8,128)(2,1)} %get-tuple-element.189), channel_id=1, source_target_pairs={{0,4},{2,6},{4,0},{6,2},{8,12},{10,14},{12,8},{14,10},{16,20},{18,... | collective-permute-start | bytes 589832 | tf_op jit(solution)/shard_map/ppermute | solution.py:1028
  123.0 13.8 %collective-permute-start.17 = (bf16[192,512]{1,0:T(8,128)(2,1)}, bf16[192,512]{1,0:T(8,128)(2,1)}, u32[]{:S(2)}, u32[]{:S(2)}) collective-permute-start(bf16[192,512]{1,0:T(8,128)(2,1)} %get-tuple-element.177.after), channel_id=1, source_target_pairs={{0,1},{1,0},{2,3},{3,2},{4,5},{5,4},{6,7},{7,6},{8,9},{9,8},{10,11... | collective-permute-start | bytes 589832 | tf_op jit(solution)/shard_map/ppermute | solution.py:1040
  129.2 6.9 %collective-permute-start.19 = (bf16[192,512]{1,0:T(8,128)(2,1)}, bf16[192,512]{1,0:T(8,128)(2,1)}, u32[]{:S(2)}, u32[]{:S(2)}) collective-permute-start(bf16[192,512]{1,0:T(8,128)(2,1)} %get-tuple-element.190), channel_id=1, source_target_pairs={{0,5},{1,4},{2,7},{3,6},{4,1},{5,0},{6,3},{7,2},{8,13},{9,12},{10,... | collective-permute-start | bytes 589832 | tf_op jit(solution)/shard_map/ppermute | solution.py:1044
  130.1 7.9 %collective-permute-start.20 = (bf16[544,512]{1,0:T(8,128)(2,1)}, bf16[544,512]{1,0:T(8,128)(2,1)}, u32[]{:S(2)}, u32[]{:S(2)}) collective-permute-start(bf16[544,512]{1,0:T(8,128)(2,1)} %get-tuple-element.184.refs_0_), channel_id=1, source_target_pairs={{0,2},{2,0},{4,6},{6,4},{8,10},{10,8},{12,14},{14,12},{16,18},{18,... | collective-permute-start | bytes 1671176 | tf_op jit(solution)/shard_map/ppermute | solution.py:1028
  130.8 11.0 %collective-permute-start.23 = (bf16[144,512]{1,0:T(8,128)(2,1)S(1)}, bf16[144,512]{1,0:T(8,128)(2,1)S(1)}, u32[]{:S(2)}, u32[]{:S(2)}) collective-permute-start(bf16[144,512]{1,0:T(8,128)(2,1)S(1)} %shard_map.343.refs_0_.refs_1_), channel_id=1, source_target_pairs={{0,24},{2,26},{4,28},{6,30},{8,16},{10,18},{12,20},{14,22},{16,8},... | collective-permute-start | bytes 442376 | tf_op jit(solution)/shard_map/ppermute | solution.py:1028
  134.5 12.2 %collective-permute-start.22 = (bf16[144,512]{1,0:T(8,128)(2,1)S(1)}, bf16[144,512]{1,0:T(8,128)(2,1)S(1)}, u32[]{:S(2)}, u32[]{:S(2)}) collective-permute-start(bf16[144,512]{1,0:T(8,128)(2,1)S(1)} %shard_map.343.refs_0_.refs_1_), channel_id=1, source_target_pairs={{0,16},{2,18},{4,20},{6,22},{8,24},{10,26},{12,28},{14,30},{16,0},... | collective-permute-start | bytes 442376 | tf_op jit(solution)/shard_map/ppermute | solution.py:1028
  136.1 10.6 %collective-permute-start.21 = (bf16[144,512]{1,0:T(8,128)(2,1)S(1)}, bf16[144,512]{1,0:T(8,128)(2,1)S(1)}, u32[]{:S(2)}, u32[]{:S(2)}) collective-permute-start(bf16[144,512]{1,0:T(8,128)(2,1)S(1)} %shard_map.343.refs_0_.refs_1_), channel_id=1, source_target_pairs={{0,8},{2,10},{4,12},{6,14},{8,0},{10,2},{12,4},{14,6},{16,24},{18,... | collective-permute-start | bytes 442376 | tf_op jit(solution)/shard_map/ppermute | solution.py:1028
  139.3 8.8 %collective-permute-start.25 = (bf16[144,512]{1,0:T(8,128)(2,1)S(1)}, bf16[144,512]{1,0:T(8,128)(2,1)S(1)}, u32[]{:S(2)}, u32[]{:S(2)}) collective-permute-start(bf16[144,512]{1,0:T(8,128)(2,1)S(1)} %get-tuple-element.194), channel_id=1, source_target_pairs={{0,4},{2,6},{4,0},{6,2},{8,12},{10,14},{12,8},{14,10},{16,20},{18,... | collective-permute-start | bytes 442376 | tf_op jit(solution)/shard_map/ppermute | solution.py:1028
  139.9 8.2 %collective-permute-start.26 = (bf16[144,512]{1,0:T(8,128)(2,1)S(1)}, bf16[144,512]{1,0:T(8,128)(2,1)S(1)}, u32[]{:S(2)}, u32[]{:S(2)}) collective-permute-start(bf16[144,512]{1,0:T(8,128)(2,1)S(1)} %get-tuple-element.195), channel_id=1, source_target_pairs={{0,5},{1,4},{2,7},{3,6},{4,1},{5,0},{6,3},{7,2},{8,13},{9,12},{10,... | collective-permute-start | bytes 442376 | tf_op jit(solution)/shard_map/ppermute | solution.py:1044
  141.8 6.8 %collective-permute-start.24 = (bf16[144,512]{1,0:T(8,128)(2,1)S(1)}, bf16[144,512]{1,0:T(8,128)(2,1)S(1)}, u32[]{:S(2)}, u32[]{:S(2)}) collective-permute-start(bf16[144,512]{1,0:T(8,128)(2,1)S(1)} %get-tuple-element.192.refs_0_), channel_id=1, source_target_pairs={{0,1},{1,0},{2,3},{3,2},{4,5},{5,4},{6,7},{7,6},{8,9},{9,8},{10,11... | collective-permute-start | bytes 442376 | tf_op jit(solution)/shard_map/ppermute | solution.py:1040
  149.1 6.2 %collective-permute-start.27 = (bf16[96,512]{1,0:T(8,128)(2,1)S(1)}, bf16[96,512]{1,0:T(8,128)(2,1)S(1)}, u32[]{:S(2)}, u32[]{:S(2)}) collective-permute-start(bf16[96,512]{1,0:T(8,128)(2,1)S(1)} %get-tuple-element.197), channel_id=1, source_target_pairs={{0,8},{2,10},{4,12},{6,14},{8,0},{10,2},{12,4},{14,6},{16,24},{18,... | collective-permute-start | bytes 294920 | tf_op jit(solution)/shard_map/ppermute | solution.py:1028
  151.3 8.8 %collective-permute-start.28 = (bf16[96,512]{1,0:T(8,128)(2,1)S(1)}, bf16[96,512]{1,0:T(8,128)(2,1)S(1)}, u32[]{:S(2)}, u32[]{:S(2)}) collective-permute-start(bf16[96,512]{1,0:T(8,128)(2,1)S(1)} %get-tuple-element.198), channel_id=1, source_target_pairs={{0,16},{2,18},{4,20},{6,22},{8,24},{10,26},{12,28},{14,30},{16,0},... | collective-permute-start | bytes 294920 | tf_op jit(solution)/shard_map/ppermute | solution.py:1028
  153.2 6.8 %collective-permute-start.29 = (bf16[96,512]{1,0:T(8,128)(2,1)S(1)}, bf16[96,512]{1,0:T(8,128)(2,1)S(1)}, u32[]{:S(2)}, u32[]{:S(2)}) collective-permute-start(bf16[96,512]{1,0:T(8,128)(2,1)S(1)} %get-tuple-element.199), channel_id=1, source_target_pairs={{0,24},{2,26},{4,28},{6,30},{8,16},{10,18},{12,20},{14,22},{16,8},... | collective-permute-start | bytes 294920 | tf_op jit(solution)/shard_map/ppermute | solution.py:1028
  153.7 15.6 %collective-permute-start.30 = (bf16[576,512]{1,0:T(8,128)(2,1)}, bf16[576,512]{1,0:T(8,128)(2,1)}, u32[]{:S(2)}, u32[]{:S(2)}) collective-permute-start(bf16[576,512]{1,0:T(8,128)(2,1)} %shard_map.346.refs_0_.refs_1_), channel_id=1, source_target_pairs={{0,4},{2,6},{4,0},{6,2},{8,12},{10,14},{12,8},{14,10},{16,20},{18,... | collective-permute-start | bytes 1769480 | tf_op jit(solution)/shard_map/ppermute | solution.py:1028
  160.1 5.1 %copy-start.3 = (f32[24,2048]{1,0:T(8,128)S(1)}, f32[24,2048]{1,0:T(8,128)}, u32[]{:S(2)}) copy-start(f32[24,2048]{1,0:T(8,128)} %copy-done.1) | copy-start | bytes 589828
  160.1 5.1 %copy-start.5 = (bf16[1024,512]{1,0:T(8,128)(2,1)S(1)}, bf16[1024,512]{1,0:T(8,128)(2,1)}, u32[]{:S(2)}) copy-start(bf16[1024,512]{1,0:T(8,128)(2,1)} %get-tuple-element.180.merge_ref.refs_4_.refs_5_) | copy-start | bytes 3145732
  160.7 9.1 %collective-permute-start.33 = (bf16[80,512]{1,0:T(8,128)(2,1)S(1)}, bf16[80,512]{1,0:T(8,128)(2,1)S(1)}, u32[]{:S(2)}, u32[]{:S(2)}) collective-permute-start(bf16[80,512]{1,0:T(8,128)(2,1)S(1)} %get-tuple-element.200.refs_0_.refs_3_), channel_id=1, source_target_pairs={{0,24},{2,26},{4,28},{6,30},{8,16},{10,18},{12,20},{14,22},{16,8},... | collective-permute-start | bytes 245768 | tf_op jit(solution)/shard_map/ppermute | solution.py:1028
  163.2 6.6 %collective-permute-start.32 = (bf16[80,512]{1,0:T(8,128)(2,1)S(1)}, bf16[80,512]{1,0:T(8,128)(2,1)S(1)}, u32[]{:S(2)}, u32[]{:S(2)}) collective-permute-start(bf16[80,512]{1,0:T(8,128)(2,1)S(1)} %get-tuple-element.200.refs_0_.refs_3_), channel_id=1, source_target_pairs={{0,16},{2,18},{4,20},{6,22},{8,24},{10,26},{12,28},{14,30},{16,0},... | collective-permute-start | bytes 245768 | tf_op jit(solution)/shard_map/ppermute | solution.py:1028
  163.8 6.0 %collective-permute-start.31 = (bf16[80,512]{1,0:T(8,128)(2,1)S(1)}, bf16[80,512]{1,0:T(8,128)(2,1)S(1)}, u32[]{:S(2)}, u32[]{:S(2)}) collective-permute-start(bf16[80,512]{1,0:T(8,128)(2,1)S(1)} %get-tuple-element.200.refs_0_.refs_3_), channel_id=1, source_target_pairs={{0,8},{2,10},{4,12},{6,14},{8,0},{10,2},{12,4},{14,6},{16,24},{18,... | collective-permute-start | bytes 245768 | tf_op jit(solution)/shard_map/ppermute | solution.py:1028
  165.1 11.6 %collective-permute-start.34 = (bf16[576,512]{1,0:T(8,128)(2,1)}, bf16[576,512]{1,0:T(8,128)(2,1)}, u32[]{:S(2)}, u32[]{:S(2)}) collective-permute-start(bf16[576,512]{1,0:T(8,128)(2,1)} %shard_map.346.refs_0_.refs_1_), channel_id=1, source_target_pairs={{0,2},{2,0},{4,6},{6,4},{8,10},{10,8},{12,14},{14,12},{16,18},{18,... | collective-permute-start | bytes 1769480 | tf_op jit(solution)/shard_map/ppermute | solution.py:1028
  169.3 7.4 %collective-permute-start.35 = (bf16[576,512]{1,0:T(8,128)(2,1)}, bf16[576,512]{1,0:T(8,128)(2,1)}, u32[]{:S(2)}, u32[]{:S(2)}) collective-permute-start(bf16[576,512]{1,0:T(8,128)(2,1)} %collective-permute-done.30.refs_1_.refs_2_), channel_id=1, source_target_pairs={{0,2},{2,0},{4,6},{6,4},{8,10},{10,8},{12,14},{14,12},{16,18},{18,... | collective-permute-start | bytes 1769480 | tf_op jit(solution)/shard_map/ppermute | solution.py:1028
  170.4 10.5 %collective-permute-start.36 = (bf16[336,512]{1,0:T(8,128)(2,1)S(1)}, bf16[336,512]{1,0:T(8,128)(2,1)S(1)}, u32[]{:S(2)}, u32[]{:S(2)}) collective-permute-start(bf16[336,512]{1,0:T(8,128)(2,1)S(1)} %shard_map.350.refs_1_.mine), channel_id=1, source_target_pairs={{0,4},{2,6},{4,0},{6,2},{8,12},{10,14},{12,8},{14,10},{16,20},{18,... | collective-permute-start | bytes 1032200 | tf_op jit(solution)/shard_map/ppermute | solution.py:1028
  172.6 9.5 %collective-permute-start.37 = (bf16[336,512]{1,0:T(8,128)(2,1)S(1)}, bf16[336,512]{1,0:T(8,128)(2,1)S(1)}, u32[]{:S(2)}, u32[]{:S(2)}) collective-permute-start(bf16[336,512]{1,0:T(8,128)(2,1)S(1)} %shard_map.350.refs_1_.mine), channel_id=1, source_target_pairs={{0,2},{2,0},{4,6},{6,4},{8,10},{10,8},{12,14},{14,12},{16,18},{18,... | collective-permute-start | bytes 1032200 | tf_op jit(solution)/shard_map/ppermute | solution.py:1028
  181.5 1.8 collective-permute-start.38

commit v5 on v4

--- a/solution.py
+++ b/solution.py
@@ -1424,14 +1424,14 @@
             merge_kept, ring.y(to_y), ring.x(to_x), ring.xy(to_both),
         )
         last_got = [ring.z(last_parts[step], step) for step in range(1, along)]
+        steps = count // ROWS
+        section_grad, token = section_back(last_parts[0], None, low, hat, inverse, merge_full, params, 0, steps // 2)
         last_total, vectors = stage(
-            merge_total_body, place, last_parts[0], (last_span, 16), *([last_parts[0]] + last_got), cost=LONG
+            merge_total_body, place, token, (last_span, 16), *([last_parts[0]] + last_got), cost=LONG
         )
         last_all = [last_total] + [ring.z(last_total, step) for step in range(1, along)]
-        steps = count // ROWS
-        section_grad, token = section_back(last_total, None, low, hat, inverse, merge_full, params, 0, steps // 2)
         (last_near,) = stage(
-            last_beside_body, place, (token, feed_beside), (336,), vectors, *last_all, cost=LONG
+            last_beside_body, place, feed_beside, (336,), vectors, *last_all, cost=LONG
         )
         last_far = ring.x(last_near)
         feed_cores = ring.core(feed_mine), ring.core(feed_beside)

time: 189 us -> 189 us (level)
  transfers between devices with their start and end apart: 39 -> 39, of which waited for: 9 -> 12; matrix products, arithmetic and copies ran while one was open for 0% -> 0% of each run, Pallas kernels for 64% -> 65%
where the time goes in v5:
time: 189 us; the launch traced here: 186 us
  Pallas kernels  125 us (66%)
  starting transfers between devices  39.9 us (21%)
  waiting for transfers between devices  18.6 us (10%)
    ppermute x29, starting transfers between devices, to(): lax.ppermute(array, 'rows', [(i, i ^ bits) for i in range(self.rows_size)])  26.8 us
    pallas_call x1, Pallas kernels, attend_back(): kernel_call(attend_back_body, (count // ROWS,), [ANYWHERE, RESIDENT, by_w...  18.5 us
    pallas_call x13, Pallas kernels, plain_call_after(): pl.pallas_call(without_after, in_specs=[SCALARS] + [pl.BlockSpec(memory_s...  16.2 us
    pallas_call x2, Pallas kernels, feed_middle(): pl.pallas_call(partial(feed_middle_body, own), in_specs=[SCALARS] + [RESI...  13.9 us
    pallas_call x1, Pallas kernels, feed_near(): kernel_call(feed_near_body, (blocks + 1,), [SCALARS] + [RESIDENT] * 9 + [...  12.7 us
    pallas_call x1, Pallas kernels, attend(): kernel_call(attend_body, (count // ROWS,), [SCALARS, RESIDENT, RESIDENT,...  12.4 us
    ppermute x29, waiting for transfers between devices, to(): lax.ppermute(array, 'rows', [(i, i ^ bits) for i in range(self.rows_size)])  12.2 us
    pallas_call x1, Pallas kernels, feed_own(): kernel_call(feed_own_body, (blocks + 1,), [SCALARS, taken(D), taken(D), t...  12.1 us
  transfers between devices with their start and end apart: 39, of which 12 were waited for; matrix products, arithmetic and copies ran while one was open for 0% of the time, Pallas kernels for 65%

profile of v5, /device:TPU:0, one launch (start us, length us, event | category | flops | bytes accessed | tf_op | source)
XLA Modules:
  0.0 185.5 jit_solution(11443144035209849458)
XLA Ops:
  0.7 1.5 shard_map.322.after
  2.3 3.0 %collective-permute-start.1 = (bf16[256,512]{1,0:T(8,128)(2,1)S(1)}, bf16[256,512]{1,0:T(8,128)(2,1)S(1)}, u32[]{:S(2)}, u32[]{:S(2)}) collective-permute-start(bf16[256,512]{1,0:T(8,128)(2,1)S(1)} %shard_map.322.after), channel_id=1, source_target_pairs={{0,1},{1,0},{2,3},{3,2},{4,5},{5,4},{6,7},{7,6},{8,9},{9,8},{10,11... | collective-permute-start | bytes 786440 | tf_op jit(solution)/shard_map/ppermute | solution.py:1040
  5.3 1.4 shard_map.323
  6.8 1.5 shard_map.324
  8.3 1.6 shard_map.325.array_ref
  9.9 2.4 %collective-permute-done.refs_0_.others_ref = bf16[32,512]{1,0:T(8,128)(2,1)S(1)} collective-permute-done((bf16[32,512]{1,0:T(8,128)(2,1)S(1)}, bf16[32,512]{1,0:T(8,128)(2,1)S(1)}, u32[]{:S(2)}, u32[]{:S(2)}) %collective-permute-start) | collective-permute-done | bytes 32800 | tf_op jit(solution)/shard_map/ppermute | solution.py:1040
  12.3 1.7 collective-permute-start.3
  14.0 3.0 %shard_map.327 = (bf16[1600,1024]{1,0:T(8,128)(2,1)S(1)}, f32[1600,1]{1,0:T(8,128)S(1)}) custom-call(bf16[512,512]{1,0:T(8,128)(2,1)S(1)} %shard_map.326.after, bf16[1600,1024]{1,0:T(8,128)(2,1)} %rows_ref.1), custom_call_target="tpu_custom_call" | custom-call | flops 1 | bytes 1 | tf_op jit(solution)/shard_map/pallas_call | solution.py:332
  17.1 6.0 %shard_map.328 = (f32[1600,512]{1,0:T(8,128)}, bf16[1600,512]{1,0:T(8,128)(2,1)S(1)}, bf16[1600,512]{1,0:T(8,128)(2,1)}, bf16[1024,512]{1,0:T(8,128)(2,1)}, f32[24,2048]{1,0:T(8,128)S(1)}, /*index=5*/f32[1024,128]{1,0:T(8,128)}) custom-call(s32[4]{0:T(128)S(1)} %pad_add_fusion.place, bf16[1600,1024]{1,0:T(8,128)(2,1)S(1)} %get-tuple-element.124.hat_ref, ...), custom_call_target="tpu_custom_call" | custom-call | flops 1 | bytes 1 | tf_op jit(solution)/shard_map/pallas_call | solution.py:393
  23.1 2.5 %shard_map.329 = (f32[4,112,512]{2,1,0:T(8,128)S(1)}, bf16[1600,1024]{1,0:T(8,128)(2,1)}) custom-call(f32[24,2048]{1,0:T(8,128)S(1)} %get-tuple-element.126.params_ref.refs_5_.refs_6_, bf16[1600,1024]{1,0:T(8,128)(2,1)S(1)} %get-tuple-element.124.hat_ref), custom_call_target="tpu_custom_call" | custom-call | flops 1 | bytes 1 | tf_op jit(solution)/shard_map/pallas_call | solution.py:987
  25.6 0.6 shard_map.333
  26.3 1.3 collective-permute-start.5
  27.6 1.9 %collective-permute-done.4.far_ref = bf16[512,512]{1,0:T(8,128)(2,1)S(1)} collective-permute-done((bf16[512,512]{1,0:T(8,128)(2,1)S(1)}, bf16[512,512]{1,0:T(8,128)(2,1)S(1)}, u32[]{:S(2)}, u32[]{:S(2)}) %collective-permute-start.4) | collective-permute-done | bytes 524320 | tf_op jit(solution)/shard_map/ppermute | solution.py:1028
  29.5 12.4 %shard_map.330 = (bf16[16,128,1536]{2,1,0:T(8,128)(2,1)}, bf16[16,4,112,512]{3,2,1,0:T(8,128)(2,1)}, bf16[1600,512]{1,0:T(8,128)(2,1)}, bf16[16,112,512]{2,1,0:T...) custom-call(s32[4]{0:T(128)S(1)} %pad_add_fusion.place, ...), custom_call_target="tpu_custom_call" | custom-call | flops 1 | bytes 1 | tf_op jit(solution)/shard_map/pallas_call | solution.py:486
  41.9 12.1 %shard_map.331 = (f32[1600,512]{1,0:T(8,128)S(1)}, f32[1600,1]{1,0:T(8,128)S(1)}, f32[1600,512]{1,0:T(8,128)S(1)}, f32[1600,512]{1,0:T(8,128)S(1)}, bf16[1600,51...) custom-call(s32[4]{0:T(128)S(1)} %pad_add_fusion.place, ...), custom_call_target="tpu_custom_call" | custom-call | flops 1 | bytes 1 | tf_op jit(solution)/shard_map/pallas_call | solution.py:606
  54.7 6.6 %shard_map.332 = (f32[1600,512]{1,0:T(8,128)S(1)}, f32[1600,512]{1,0:T(8,128)S(1)}, bf16[1024,512]{1,0:T(8,128)(2,1)S(1)}, f32[8,512]{1,0:T(8,128)S(1)}) custom-call(s32[4]{0:T(128)S(1)} %pad_add_fusion.place, bf16[1600,512]{1,0:T(8,128)(2,1)S(1)} %get-tuple-element.133.second_ref, ...), custom_call_target="tpu_custom_call", output_to_operand_aliasing={{0}: (4, {}), {1}: (5, {})} | custom-call | flops 999999995904 | bytes 1 | tf_op jit(solution)/shard_map/pallas_call | solution.py:647
  61.2 7.3 %shard_map.334 = (f32[1600,512]{1,0:T(8,128)S(1)}, f32[1600,512]{1,0:T(8,128)S(1)}, bf16[1024,512]{1,0:T(8,128)(2,1)S(1)}, f32[8,512]{1,0:T(8,128)S(1)}) custom-call(s32[4]{0:T(128)S(1)} %pad_add_fusion.place, bf16[1600,512]{1,0:T(8,128)(2,1)S(1)} %get-tuple-element.133.second_ref, ...), custom_call_target="tpu_custom_call", output_to_operand_aliasing={{0}: (4, {}), {1}: (5, {})} | custom-call | flops 1 | bytes 1 | tf_op jit(solution)/shard_map/pallas_call | solution.py:647
  68.7 12.7 %shard_map.335 = (bf16[1600,512]{1,0:T(8,128)(2,1)}, f32[1600,512]{1,0:T(8,128)S(1)}, bf16[1600,512]{1,0:T(8,128)(2,1)S(1)}, bf16[1024,512]{1,0:T(8,128)(2,1)S(1...) custom-call(s32[4]{0:T(128)S(1)} %pad_add_fusion.place, ...), custom_call_target="tpu_custom_call" | custom-call | flops 1 | bytes 1 | tf_op jit(solution)/shard_map/pallas_call | solution.py:712
  81.9 1.8 shard_map.336
  83.7 0.6 shard_map.337
  84.3 1.6 collective-permute-start.11
  85.8 0.8 collective-permute-start.12
  86.6 1.2 collective-permute-start.10
  87.8 18.5 %shard_map.338 = (bf16[1600,1536]{1,0:T(8,128)(2,1)S(1)}, bf16[1600,512]{1,0:T(8,128)(2,1)S(1)}, f32[1,1536]{1,0:T(1,128)S(1)}, f32[8,512]{1,0:T(8,128)S(1)}, f3...) custom-call(bf16[576,512]{1,0:T(8,128)(2,1)S(1)} %get-tuple-element.157.after, ...), custom_call_target="tpu_custom_call" | custom-call | flops 1 | bytes 1 | tf_op jit(solution)/shard_map/pallas_call | solution.py:801
  106.4 5.7 %shard_map.339 = (bf16[768,512]{1,0:T(8,128)(2,1)}, bf16[768,512]{1,0:T(8,128)(2,1)S(1)}, bf16[1600,1024]{1,0:T(8,128)(2,1)S(1)}) custom-call(s32[4]{0:T(128)S(1)} %pad_add_fusion.place, f32[1,1536]{1,0:T(1,128)S(1)} %get-tuple-element.167.after.qkv_sums_ref, bf16[1600,512]{1,0:T(8,128)(2,1)S(1)} %get-tuple-element.168.first_ref, ...), custom_call_target="tpu_custom_call" | custom-call | flops 1 | bytes 1 | tf_op jit(solution)/shard_map/pallas_call | solution.py:857
  112.2 0.6 collective-permute-done.12.refs_4_
  112.8 1.4 collective-permute-done.10.refs_2_
  114.2 0.8 shard_map.340
  115.0 1.6 collective-permute-start.14
  116.7 2.6 %collective-permute-start.15 = (bf16[144,512]{1,0:T(8,128)(2,1)S(1)}, bf16[144,512]{1,0:T(8,128)(2,1)S(1)}, u32[]{:S(2)}, u32[]{:S(2)}) collective-permute-start(bf16[144,512]{1,0:T(8,128)(2,1)S(1)} %get-tuple-element.186), channel_id=1, source_target_pairs={{0,16},{2,18},{4,20},{6,22},{8,24},{10,26},{12,28},{14,30},{16,0},... | collective-permute-start | bytes 442376 | tf_op jit(solution)/shard_map/ppermute | solution.py:1028
  119.5 2.0 %shard_map.341 = (bf16[192,512]{1,0:T(8,128)(2,1)}, bf16[192,512]{1,0:T(8,128)(2,1)}, bf16[192,512]{1,0:T(8,128)(2,1)}, bf16[192,512]{1,0:T(8,128)(2,1)S(1)}) custom-call(s32[4]{0:T(128)S(1)} %pad_add_fusion.place, bf16[144,512]{1,0:T(8,128)(2,1)S(1)} %get-tuple-element.175.refs_0_.refs_1_, bf16[768,512]{1,0:T(8,128)(2,1)S(1)} %get-tuple-element.176.refs_1_, ...), custom_call_target="tpu_custom_call" | custom-call | flops 1 | bytes 1 | tf_op jit(solution)/shard_map/pallas_call | solution.py:249
  121.5 1.5 collective-permute-start.18
  123.0 1.1 collective-permute-start.17
  124.1 5.1 %shard_map.342 = (bf16[544,512]{1,0:T(8,128)(2,1)}, bf16[544,512]{1,0:T(8,128)(2,1)S(1)}) custom-call(s32[4]{0:T(128)S(1)} %pad_add_fusion.place, bf16[192,512]{1,0:T(8,128)(2,1)} %get-tuple-element.177.after, bf16[1600,512]{1,0:T(8,128)(2,1)S(1)} %get-tuple-element.178.low_ref.refs_1_.refs_2_, bf16[1600,1024]{1,0:T(8,128)(2,1)S(1)} %get-tuple-element.179.hat_ref, ...), custom_call_target="tpu_custom_call" | custom-call | flops 1 | bytes 1 | tf_op jit(solution)/shard_map/pallas_call | solution.py:906
  129.2 0.9 collective-permute-start.19
  130.2 0.6 shard_map.343.refs_0_.refs_1_
  130.8 3.7 %collective-permute-start.23 = (bf16[144,512]{1,0:T(8,128)(2,1)S(1)}, bf16[144,512]{1,0:T(8,128)(2,1)S(1)}, u32[]{:S(2)}, u32[]{:S(2)}) collective-permute-start(bf16[144,512]{1,0:T(8,128)(2,1)S(1)} %shard_map.343.refs_0_.refs_1_), channel_id=1, source_target_pairs={{0,24},{2,26},{4,28},{6,30},{8,16},{10,18},{12,20},{14,22},{16,8},... | collective-permute-start | bytes 442376 | tf_op jit(solution)/shard_map/ppermute | solution.py:1028
  134.5 1.6 collective-permute-done.19.refs_4_
  136.1 0.7 collective-permute-start.21
  136.8 1.2 shard_map.344.refs_0_.refs_1_
  138.0 1.2 shard_map.345
  139.3 0.6 collective-permute-start.25
  139.9 1.9 %collective-permute-start.26 = (bf16[144,512]{1,0:T(8,128)(2,1)S(1)}, bf16[144,512]{1,0:T(8,128)(2,1)S(1)}, u32[]{:S(2)}, u32[]{:S(2)}) collective-permute-start(bf16[144,512]{1,0:T(8,128)(2,1)S(1)} %get-tuple-element.195), channel_id=1, source_target_pairs={{0,5},{1,4},{2,7},{3,6},{4,1},{5,0},{6,3},{7,2},{8,13},{9,12},{10,... | collective-permute-start | bytes 442376 | tf_op jit(solution)/shard_map/ppermute | solution.py:1044
  141.8 1.1 collective-permute-start.24
  142.8 3.9 %collective-permute-done.22.refs_3_ = bf16[144,512]{1,0:T(8,128)(2,1)S(1)} collective-permute-done((bf16[144,512]{1,0:T(8,128)(2,1)S(1)}, bf16[144,512]{1,0:T(8,128)(2,1)S(1)}, u32[]{:S(2)}, u32[]{:S(2)}) %collective-permute-start.22) | collective-permute-done | bytes 147488 | tf_op jit(solution)/shard_map/ppermute | solution.py:1028
  146.7 1.4 shard_map.346.refs_0_.refs_1_
  148.5 0.6 shard_map.347
  149.2 2.1 %collective-permute-start.28 = (bf16[96,512]{1,0:T(8,128)(2,1)S(1)}, bf16[96,512]{1,0:T(8,128)(2,1)S(1)}, u32[]{:S(2)}, u32[]{:S(2)}) collective-permute-start(bf16[96,512]{1,0:T(8,128)(2,1)S(1)} %get-tuple-element.200), channel_id=1, source_target_pairs={{0,8},{2,10},{4,12},{6,14},{8,0},{10,2},{12,4},{14,6},{16,24},{18,... | collective-permute-start | bytes 294920 | tf_op jit(solution)/shard_map/ppermute | solution.py:1028
  151.3 2.0 %collective-permute-start.29 = (bf16[96,512]{1,0:T(8,128)(2,1)S(1)}, bf16[96,512]{1,0:T(8,128)(2,1)S(1)}, u32[]{:S(2)}, u32[]{:S(2)}) collective-permute-start(bf16[96,512]{1,0:T(8,128)(2,1)S(1)} %get-tuple-element.201), channel_id=1, source_target_pairs={{0,16},{2,18},{4,20},{6,22},{8,24},{10,26},{12,28},{14,30},{16,0},... | collective-permute-start | bytes 294920 | tf_op jit(solution)/shard_map/ppermute | solution.py:1028
  153.7 1.7 collective-permute-start.27
  155.4 4.1 %shard_map.348 = (bf16[1600,1024]{1,0:T(8,128)(2,1)}, f32[8,128]{1,0:T(8,128)S(1)}) custom-call(bf16[96,512]{1,0:T(8,128)(2,1)S(1)} %get-tuple-element.196.refs_0_.refs_1_, bf16[1600,512]{1,0:T(8,128)(2,1)} %copy-done, bf16[1600,1024]{1,0:T(8,128)(2,1)} %get-tuple-element.170.hat_in.refs_2_.refs_3_, f32[1600,1]{1,0:T(8,128)S(1)} %get-tuple-element.197.refs_3_.refs_4_, ...), custom_call_target="tpu_custom_call" | custom-call | flops 1 | bytes 1 | tf_op jit(solution)/shard_map/pallas_call | solution.py:936
  160.1 0.6 shard_map.349
  160.7 2.7 %collective-permute-start.33 = (bf16[80,512]{1,0:T(8,128)(2,1)S(1)}, bf16[80,512]{1,0:T(8,128)(2,1)S(1)}, u32[]{:S(2)}, u32[]{:S(2)}) collective-permute-start(bf16[80,512]{1,0:T(8,128)(2,1)S(1)} %get-tuple-element.204.refs_2_), channel_id=1, source_target_pairs={{0,24},{2,26},{4,28},{6,30},{8,16},{10,18},{12,20},{14,22},{16,8},... | collective-permute-start | bytes 245768 | tf_op jit(solution)/shard_map/ppermute | solution.py:1028
  163.8 1.3 collective-permute-start.31
  165.1 2.2 %collective-permute-done.27.refs_0_.refs_2_ = bf16[576,512]{1,0:T(8,128)(2,1)} collective-permute-done((bf16[576,512]{1,0:T(8,128)(2,1)}, bf16[576,512]{1,0:T(8,128)(2,1)}, u32[]{:S(2)}, u32[]{:S(2)}) %collective-permute-start.27) | collective-permute-done | bytes 589856 | tf_op jit(solution)/shard_map/ppermute | solution.py:1028
  167.5 2.3 %collective-permute-done.32.refs_4_ = bf16[80,512]{1,0:T(8,128)(2,1)S(1)} collective-permute-done((bf16[80,512]{1,0:T(8,128)(2,1)S(1)}, bf16[80,512]{1,0:T(8,128)(2,1)S(1)}, u32[]{:S(2)}, u32[]{:S(2)}) %collective-permute-start.32) | collective-permute-done | bytes 81952 | tf_op jit(solution)/shard_map/ppermute | solution.py:1028
  169.7 0.6 shard_map.350.refs_1_.mine
  170.3 1.8 collective-permute-start.36
  172.1 4.1 %shard_map.351 = (bf16[1600,1024]{1,0:T(8,128)(2,1)}, f32[8,128]{1,0:T(8,128)S(1)}) custom-call(bf16[1600,1024]{1,0:T(8,128)(2,1)} %get-tuple-element.198.refs_0_, bf16[336,512]{1,0:T(8,128)(2,1)S(1)} %shard_map.350.refs_1_.mine, bf16[1600,512]{1,0:T(8,128)(2,1)} %copy-done, ...), custom_call_target="tpu_custom_call", output_to_operand_aliasing={{0}: (0, {})} | custom-call | flops 1 | bytes 1 | tf_op jit(solution)/shard_map/pallas_call | solution.py:936
  176.3 4.2 %shard_map.352 = (f32[1024,512]{1,0:T(8,128)}, f32[512,1024]{1,0:T(8,128)}, f32[256,512]{1,0:T(8,128)}, f32[8,128]{1,0:T(8,128)S(1)}) custom-call(s32[4]{0:T(128)S(1)} %pad_add_fusion.place, f32[8,128]{1,0:T(8,128)S(1)} %get-tuple-element.206.refs_0_, bf16[576,512]{1,0:T(8,128)(2,1)} %shard_map.346.refs_0_.refs_1_, ...), custom_call_target="tpu_custom_call" | custom-call | flops 1 | bytes 1 | tf_op jit(solution)/shard_map/pallas_call | solution.py:249
  180.5 0.6 shard_map.353.beside
  181.1 0.6 collective-permute-start.38
  181.6 1.3 collective-permute-done.38.core_beside
  182.9 2.3 %shard_map.354 = (f32[3,512,256]{2,1,0:T(8,128)}, f32[512,512]{1,0:T(8,128)}, f32[1,512]{1,0:T(1,128)}, f32[1,512]{1,0:T(1,128)}, f32[1,512]{1,0:T(1,128)}, /*in...) custom-call(s32[4]{0:T(128)S(1)} %pad_add_fusion.place, ...), custom_call_target="tpu_custom_call" | custom-call | flops 1 | bytes 1 | tf_op jit(solution)/shard_map/pallas_call | solution.py:196
  (86 shorter events, 3.8 us)
Async XLA Ops:
  2.3 10.0 %collective-permute-start.1 = (bf16[256,512]{1,0:T(8,128)(2,1)S(1)}, bf16[256,512]{1,0:T(8,128)(2,1)S(1)}, u32[]{:S(2)}, u32[]{:S(2)}) collective-permute-start(bf16[256,512]{1,0:T(8,128)(2,1)S(1)} %shard_map.322.after), channel_id=1, source_target_pairs={{0,1},{1,0},{2,3},{3,2},{4,5},{5,4},{6,7},{7,6},{8,9},{9,8},{10,11... | collective-permute-start | bytes 786440 | tf_op jit(solution)/shard_map/ppermute | solution.py:1040
  6.7 5.6 %collective-permute-start = (bf16[32,512]{1,0:T(8,128)(2,1)S(1)}, bf16[32,512]{1,0:T(8,128)(2,1)S(1)}, u32[]{:S(2)}, u32[]{:S(2)}) collective-permute-start(bf16[32,512]{1,0:T(8,128)(2,1)S(1)} %get-tuple-element.123), channel_id=1, source_target_pairs={{0,1},{1,0},{2,3},{3,2},{4,5},{5,4},{6,7},{7,6},{8,9},{9,8},{10,11... | collective-permute-start | bytes 98312 | tf_op jit(solution)/shard_map/ppermute | solution.py:1040
  8.2 8.8 %copy-start.9 = (bf16[512,512]{1,0:T(8,128)(2,1)S(1)}, bf16[512,512]{1,0:T(8,128)(2,1)}, u32[]{:S(2)}) copy-start(bf16[512,512]{1,0:T(8,128)(2,1)} %own_ref.1) | copy-start | bytes 1572868
  8.3 8.8 %copy-start.13 = (f32[512]{0:T(512)S(1)}, f32[512]{0:T(512)}, u32[]{:S(2)}) copy-start(f32[512]{0:T(512)} %param.25) | copy-start | bytes 6148
  8.3 8.8 %copy-start.15 = (f32[512]{0:T(512)S(1)}, f32[512]{0:T(512)}, u32[]{:S(2)}) copy-start(f32[512]{0:T(512)} %param.26) | copy-start | bytes 6148
  12.3 13.3 %collective-permute-start.3 = (bf16[512,512]{1,0:T(8,128)(2,1)S(1)}, bf16[512,512]{1,0:T(8,128)(2,1)S(1)}, u32[]{:S(2)}, u32[]{:S(2)}) collective-permute-start(bf16[512,512]{1,0:T(8,128)(2,1)S(1)} %shard_map.326.after), channel_id=1, source_target_pairs={{0,1},{1,0},{2,3},{3,2},{4,5},{5,4},{6,7},{7,6},{8,9},{9,8},{10,11... | collective-permute-start | bytes 1572872 | tf_op jit(solution)/shard_map/ppermute | solution.py:1040
  14.0 3.0 %collective-permute-start.2 = (bf16[256,512]{1,0:T(8,128)(2,1)S(1)}, bf16[256,512]{1,0:T(8,128)(2,1)S(1)}, u32[]{:S(2)}, u32[]{:S(2)}) collective-permute-start(bf16[256,512]{1,0:T(8,128)(2,1)S(1)} %collective-permute-done.1.refs_1_.near_ref), channel_id=1, source_target_pairs={{0,2},{2,0},{4,6},{6,4},{8,10},{10,8},{12,14},{14,12},{16,18},{18,... | collective-permute-start | bytes 786440 | tf_op jit(solution)/shard_map/ppermute | solution.py:1028
  17.1 8.5 %copy-start.6 = (bf16[512,1024]{1,0:T(8,128)(2,1)S(1)}, bf16[512,1024]{1,0:T(8,128)(2,1)}, u32[]{:S(2)}) copy-start(bf16[512,1024]{1,0:T(8,128)(2,1)} %refs_2_.1) | copy-start | bytes 3145732
  17.1 8.5 %copy-start.7 = (bf16[1024,512]{1,0:T(8,128)(2,1)S(1)}, bf16[1024,512]{1,0:T(8,128)(2,1)}, u32[]{:S(2)}) copy-start(bf16[1024,512]{1,0:T(8,128)(2,1)} %refs_3_.1) | copy-start | bytes 3145732
  23.1 45.6 %copy-start.1 = (f32[24,2048]{1,0:T(8,128)}, f32[24,2048]{1,0:T(8,128)S(1)}, u32[]{:S(2)}) copy-start(f32[24,2048]{1,0:T(8,128)S(1)} %get-tuple-element.126.params_ref.refs_5_.refs_6_) | copy-start | bytes 589828
  23.1 6.4 %copy-start.8 = (bf16[3,512,256]{2,1,0:T(8,128)(2,1)S(1)}, bf16[3,512,256]{2,1,0:T(8,128)(2,1)}, u32[]{:S(2)}) copy-start(bf16[3,512,256]{2,1,0:T(8,128)(2,1)} %param.27) | copy-start | bytes 2359300
  26.3 15.6 %copy-start.10 = (bf16[256,512]{1,0:T(8,128)(2,1)S(1)}, bf16[256,512]{1,0:T(8,128)(2,1)}, u32[]{:S(2)}) copy-start(bf16[256,512]{1,0:T(8,128)(2,1)} %proj_own.1) | copy-start | bytes 786436
  26.3 15.6 %copy-start.12 = (f32[512]{0:T(512)S(1)}, f32[512]{0:T(512)}, u32[]{:S(2)}) copy-start(f32[512]{0:T(512)} %param.32) | copy-start | bytes 6148
  26.3 15.6 %copy-start.16 = (f32[512]{0:T(512)S(1)}, f32[512]{0:T(512)}, u32[]{:S(2)}) copy-start(f32[512]{0:T(512)} %param.31) | copy-start | bytes 6148
  26.3 15.6 %copy-start.17 = (f32[512]{0:T(512)S(1)}, f32[512]{0:T(512)}, u32[]{:S(2)}) copy-start(f32[512]{0:T(512)} %param.33) | copy-start | bytes 6148
  26.3 15.6 %copy-start.18 = (f32[512]{0:T(512)S(1)}, f32[512]{0:T(512)}, u32[]{:S(2)}) copy-start(f32[512]{0:T(512)} %param.37) | copy-start | bytes 6148
  26.3 28.0 %collective-permute-start.5 = (bf16[1024,512]{1,0:T(8,128)(2,1)S(1)}, bf16[1024,512]{1,0:T(8,128)(2,1)}, u32[]{:S(2)}, u32[]{:S(2)}) collective-permute-start(bf16[1024,512]{1,0:T(8,128)(2,1)S(1)} %shard_map.333), channel_id=1, source_target_pairs={{0,1},{1,0},{2,3},{3,2},{4,5},{5,4},{6,7},{7,6},{8,9},{9,8},{10,11... | collective-permute-start | bytes 3145736 | tf_op jit(solution)/shard_map/ppermute | solution.py:1040
  27.6 1.9 %collective-permute-start.4 = (bf16[512,512]{1,0:T(8,128)(2,1)S(1)}, bf16[512,512]{1,0:T(8,128)(2,1)S(1)}, u32[]{:S(2)}, u32[]{:S(2)}) collective-permute-start(bf16[512,512]{1,0:T(8,128)(2,1)S(1)} %collective-permute-done.3.near_ref.refs_1_), channel_id=1, source_target_pairs={{0,2},{2,0},{4,6},{6,4},{8,10},{10,8},{12,14},{14,12},{16,18},{18,... | collective-permute-start | bytes 1572872 | tf_op jit(solution)/shard_map/ppermute | solution.py:1028
  54.1 27.8 %collective-permute-start.8 = (bf16[1024,512]{1,0:T(8,128)(2,1)}, bf16[1024,512]{1,0:T(8,128)(2,1)}, u32[]{:S(2)}, u32[]{:S(2)}) collective-permute-start(bf16[1024,512]{1,0:T(8,128)(2,1)} %get-tuple-element.150), channel_id=1, source_target_pairs={{0,2},{2,0},{4,6},{6,4},{8,10},{10,8},{12,14},{14,12},{16,18},{18,... | collective-permute-start | bytes 3145736 | tf_op jit(solution)/shard_map/ppermute | solution.py:1028
  54.3 6.9 %collective-permute-start.6 = (bf16[1024,512]{1,0:T(8,128)(2,1)}, bf16[1024,512]{1,0:T(8,128)(2,1)}, u32[]{:S(2)}, u32[]{:S(2)}) collective-permute-start(bf16[1024,512]{1,0:T(8,128)(2,1)} %collective-permute-done.5.near_ref), channel_id=1, source_target_pairs={{0,2},{2,0},{4,6},{6,4},{8,10},{10,8},{12,14},{14,12},{16,18},{18,... | collective-permute-start | bytes 3145736 | tf_op jit(solution)/shard_map/ppermute | solution.py:1028
  68.5 13.3 %collective-permute-start.9 = (bf16[1024,512]{1,0:T(8,128)(2,1)S(1)}, bf16[1024,512]{1,0:T(8,128)(2,1)S(1)}, u32[]{:S(2)}, u32[]{:S(2)}) collective-permute-start(bf16[1024,512]{1,0:T(8,128)(2,1)S(1)} %get-tuple-element.152), channel_id=1, source_target_pairs={{0,2},{2,0},{4,6},{6,4},{8,10},{10,8},{12,14},{14,12},{16,18},{18,... | collective-permute-start | bytes 3145736 | tf_op jit(solution)/shard_map/ppermute | solution.py:1028
  81.4 2.2 %collective-permute-start.7 = (bf16[256,512]{1,0:T(8,128)(2,1)S(1)}, bf16[256,512]{1,0:T(8,128)(2,1)S(1)}, u32[]{:S(2)}, u32[]{:S(2)}) collective-permute-start(bf16[256,512]{1,0:T(8,128)(2,1)S(1)} %get-tuple-element.147), channel_id=1, source_target_pairs={{0,2},{2,0},{4,6},{6,4},{8,10},{10,8},{12,14},{14,12},{16,18},{18,... | collective-permute-start | bytes 786440 | tf_op jit(solution)/shard_map/ppermute | solution.py:1028
  81.9 6.0 %copy-start.14 = (f32[512]{0:T(512)S(1)}, f32[512]{0:T(512)}, u32[]{:S(2)}) copy-start(f32[512]{0:T(512)} %param.25) | copy-start | bytes 6148
  84.3 28.0 %collective-permute-start.11 = (bf16[576,512]{1,0:T(8,128)(2,1)S(1)}, bf16[576,512]{1,0:T(8,128)(2,1)S(1)}, u32[]{:S(2)}, u32[]{:S(2)}) collective-permute-start(bf16[576,512]{1,0:T(8,128)(2,1)S(1)} %get-tuple-element.173), channel_id=1, source_target_pairs={{0,4},{2,6},{4,0},{6,2},{8,12},{10,14},{12,8},{14,10},{16,20},{18,... | collective-permute-start | bytes 1769480 | tf_op jit(solution)/shard_map/ppermute | solution.py:1028
  85.8 27.0 %collective-permute-start.12 = (bf16[576,512]{1,0:T(8,128)(2,1)S(1)}, bf16[576,512]{1,0:T(8,128)(2,1)S(1)}, u32[]{:S(2)}, u32[]{:S(2)}) collective-permute-start(bf16[576,512]{1,0:T(8,128)(2,1)S(1)} %get-tuple-element.174), channel_id=1, source_target_pairs={{0,5},{1,4},{2,7},{3,6},{4,1},{5,0},{6,3},{7,2},{8,13},{9,12},{10,... | collective-permute-start | bytes 1769480 | tf_op jit(solution)/shard_map/ppermute | solution.py:1044
  86.6 27.5 %collective-permute-start.10 = (bf16[576,512]{1,0:T(8,128)(2,1)S(1)}, bf16[576,512]{1,0:T(8,128)(2,1)S(1)}, u32[]{:S(2)}, u32[]{:S(2)}) collective-permute-start(bf16[576,512]{1,0:T(8,128)(2,1)S(1)} %get-tuple-element.157.after), channel_id=1, source_target_pairs={{0,1},{1,0},{2,3},{3,2},{4,5},{5,4},{6,7},{7,6},{8,9},{9,8},{10,11... | collective-permute-start | bytes 1769480 | tf_op jit(solution)/shard_map/ppermute | solution.py:1040
  106.4 17.7 %copy-start = (bf16[1600,512]{1,0:T(8,128)(2,1)}, bf16[1600,512]{1,0:T(8,128)(2,1)S(1)}, u32[]{:S(2)}) copy-start(bf16[1600,512]{1,0:T(8,128)(2,1)S(1)} %get-tuple-element.178.low_ref.refs_1_.refs_2_) | copy-start | bytes 4915204
  112.1 7.3 %collective-permute-start.13 = (bf16[768,512]{1,0:T(8,128)(2,1)}, bf16[768,512]{1,0:T(8,128)(2,1)}, u32[]{:S(2)}, u32[]{:S(2)}) collective-permute-start(bf16[768,512]{1,0:T(8,128)(2,1)} %get-tuple-element.171.refs_0_), channel_id=1, source_target_pairs={{0,2},{2,0},{4,6},{6,4},{8,10},{10,8},{12,14},{14,12},{16,18},{18,... | collective-permute-start | bytes 2359304 | tf_op jit(solution)/shard_map/ppermute | solution.py:1028
  114.2 9.9 %copy-start.2 = (f32[24,2048]{1,0:T(8,128)S(1)}, f32[24,2048]{1,0:T(8,128)}, u32[]{:S(2)}) copy-start(f32[24,2048]{1,0:T(8,128)} %copy-done.1) | copy-start | bytes 589828
  114.2 9.9 %copy-start.4 = (bf16[1024,512]{1,0:T(8,128)(2,1)S(1)}, bf16[1024,512]{1,0:T(8,128)(2,1)}, u32[]{:S(2)}) copy-start(bf16[1024,512]{1,0:T(8,128)(2,1)} %get-tuple-element.180.merge_ref.refs_4_.refs_5_) | copy-start | bytes 3145732
  114.2 9.9 %copy-start.11 = (f32[1024,128]{1,0:T(8,128)S(1)}, f32[1024,128]{1,0:T(8,128)}, u32[]{:S(2)}) copy-start(f32[1024,128]{1,0:T(8,128)} %get-tuple-element.181.column_ref) | copy-start | bytes 1572868
  115.0 14.2 %collective-permute-start.14 = (bf16[144,512]{1,0:T(8,128)(2,1)S(1)}, bf16[144,512]{1,0:T(8,128)(2,1)S(1)}, u32[]{:S(2)}, u32[]{:S(2)}) collective-permute-start(bf16[144,512]{1,0:T(8,128)(2,1)S(1)} %get-tuple-element.185), channel_id=1, source_target_pairs={{0,8},{2,10},{4,12},{6,14},{8,0},{10,2},{12,4},{14,6},{16,24},{18,... | collective-permute-start | bytes 442376 | tf_op jit(solution)/shard_map/ppermute | solution.py:1028
  116.7 13.5 %collective-permute-start.15 = (bf16[144,512]{1,0:T(8,128)(2,1)S(1)}, bf16[144,512]{1,0:T(8,128)(2,1)S(1)}, u32[]{:S(2)}, u32[]{:S(2)}) collective-permute-start(bf16[144,512]{1,0:T(8,128)(2,1)S(1)} %get-tuple-element.186), channel_id=1, source_target_pairs={{0,16},{2,18},{4,20},{6,22},{8,24},{10,26},{12,28},{14,30},{16,0},... | collective-permute-start | bytes 442376 | tf_op jit(solution)/shard_map/ppermute | solution.py:1028
  119.3 10.9 %collective-permute-start.16 = (bf16[144,512]{1,0:T(8,128)(2,1)S(1)}, bf16[144,512]{1,0:T(8,128)(2,1)S(1)}, u32[]{:S(2)}, u32[]{:S(2)}) collective-permute-start(bf16[144,512]{1,0:T(8,128)(2,1)S(1)} %get-tuple-element.187), channel_id=1, source_target_pairs={{0,24},{2,26},{4,28},{6,30},{8,16},{10,18},{12,20},{14,22},{16,8},... | collective-permute-start | bytes 442376 | tf_op jit(solution)/shard_map/ppermute | solution.py:1028
  121.5 13.0 %collective-permute-start.18 = (bf16[192,512]{1,0:T(8,128)(2,1)}, bf16[192,512]{1,0:T(8,128)(2,1)}, u32[]{:S(2)}, u32[]{:S(2)}) collective-permute-start(bf16[192,512]{1,0:T(8,128)(2,1)} %get-tuple-element.189), channel_id=1, source_target_pairs={{0,4},{2,6},{4,0},{6,2},{8,12},{10,14},{12,8},{14,10},{16,20},{18,... | collective-permute-start | bytes 589832 | tf_op jit(solution)/shard_map/ppermute | solution.py:1028
  123.0 13.8 %collective-permute-start.17 = (bf16[192,512]{1,0:T(8,128)(2,1)}, bf16[192,512]{1,0:T(8,128)(2,1)}, u32[]{:S(2)}, u32[]{:S(2)}) collective-permute-start(bf16[192,512]{1,0:T(8,128)(2,1)} %get-tuple-element.177.after), channel_id=1, source_target_pairs={{0,1},{1,0},{2,3},{3,2},{4,5},{5,4},{6,7},{7,6},{8,9},{9,8},{10,11... | collective-permute-start | bytes 589832 | tf_op jit(solution)/shard_map/ppermute | solution.py:1040
  129.2 6.9 %collective-permute-start.19 = (bf16[192,512]{1,0:T(8,128)(2,1)}, bf16[192,512]{1,0:T(8,128)(2,1)}, u32[]{:S(2)}, u32[]{:S(2)}) collective-permute-start(bf16[192,512]{1,0:T(8,128)(2,1)} %get-tuple-element.190), channel_id=1, source_target_pairs={{0,5},{1,4},{2,7},{3,6},{4,1},{5,0},{6,3},{7,2},{8,13},{9,12},{10,... | collective-permute-start | bytes 589832 | tf_op jit(solution)/shard_map/ppermute | solution.py:1044
  130.1 7.9 %collective-permute-start.20 = (bf16[544,512]{1,0:T(8,128)(2,1)}, bf16[544,512]{1,0:T(8,128)(2,1)}, u32[]{:S(2)}, u32[]{:S(2)}) collective-permute-start(bf16[544,512]{1,0:T(8,128)(2,1)} %get-tuple-element.184.refs_0_), channel_id=1, source_target_pairs={{0,2},{2,0},{4,6},{6,4},{8,10},{10,8},{12,14},{14,12},{16,18},{18,... | collective-permute-start | bytes 1671176 | tf_op jit(solution)/shard_map/ppermute | solution.py:1028
  130.8 24.6 %copy-start.3 = (f32[24,2048]{1,0:T(8,128)S(1)}, f32[24,2048]{1,0:T(8,128)}, u32[]{:S(2)}) copy-start(f32[24,2048]{1,0:T(8,128)} %copy-done.1) | copy-start | bytes 589828
  130.8 24.6 %copy-start.5 = (bf16[1024,512]{1,0:T(8,128)(2,1)S(1)}, bf16[1024,512]{1,0:T(8,128)(2,1)}, u32[]{:S(2)}) copy-start(bf16[1024,512]{1,0:T(8,128)(2,1)} %get-tuple-element.180.merge_ref.refs_4_.refs_5_) | copy-start | bytes 3145732
  130.8 11.0 %collective-permute-start.23 = (bf16[144,512]{1,0:T(8,128)(2,1)S(1)}, bf16[144,512]{1,0:T(8,128)(2,1)S(1)}, u32[]{:S(2)}, u32[]{:S(2)}) collective-permute-start(bf16[144,512]{1,0:T(8,128)(2,1)S(1)} %shard_map.343.refs_0_.refs_1_), channel_id=1, source_target_pairs={{0,24},{2,26},{4,28},{6,30},{8,16},{10,18},{12,20},{14,22},{16,8},... | collective-permute-start | bytes 442376 | tf_op jit(solution)/shard_map/ppermute | solution.py:1028
  134.5 12.2 %collective-permute-start.22 = (bf16[144,512]{1,0:T(8,128)(2,1)S(1)}, bf16[144,512]{1,0:T(8,128)(2,1)S(1)}, u32[]{:S(2)}, u32[]{:S(2)}) collective-permute-start(bf16[144,512]{1,0:T(8,128)(2,1)S(1)} %shard_map.343.refs_0_.refs_1_), channel_id=1, source_target_pairs={{0,16},{2,18},{4,20},{6,22},{8,24},{10,26},{12,28},{14,30},{16,0},... | collective-permute-start | bytes 442376 | tf_op jit(solution)/shard_map/ppermute | solution.py:1028
  136.1 10.6 %collective-permute-start.21 = (bf16[144,512]{1,0:T(8,128)(2,1)S(1)}, bf16[144,512]{1,0:T(8,128)(2,1)S(1)}, u32[]{:S(2)}, u32[]{:S(2)}) collective-permute-start(bf16[144,512]{1,0:T(8,128)(2,1)S(1)} %shard_map.343.refs_0_.refs_1_), channel_id=1, source_target_pairs={{0,8},{2,10},{4,12},{6,14},{8,0},{10,2},{12,4},{14,6},{16,24},{18,... | collective-permute-start | bytes 442376 | tf_op jit(solution)/shard_map/ppermute | solution.py:1028
  139.3 8.8 %collective-permute-start.25 = (bf16[144,512]{1,0:T(8,128)(2,1)S(1)}, bf16[144,512]{1,0:T(8,128)(2,1)S(1)}, u32[]{:S(2)}, u32[]{:S(2)}) collective-permute-start(bf16[144,512]{1,0:T(8,128)(2,1)S(1)} %get-tuple-element.194), channel_id=1, source_target_pairs={{0,4},{2,6},{4,0},{6,2},{8,12},{10,14},{12,8},{14,10},{16,20},{18,... | collective-permute-start | bytes 442376 | tf_op jit(solution)/shard_map/ppermute | solution.py:1028
  139.9 8.2 %collective-permute-start.26 = (bf16[144,512]{1,0:T(8,128)(2,1)S(1)}, bf16[144,512]{1,0:T(8,128)(2,1)S(1)}, u32[]{:S(2)}, u32[]{:S(2)}) collective-permute-start(bf16[144,512]{1,0:T(8,128)(2,1)S(1)} %get-tuple-element.195), channel_id=1, source_target_pairs={{0,5},{1,4},{2,7},{3,6},{4,1},{5,0},{6,3},{7,2},{8,13},{9,12},{10,... | collective-permute-start | bytes 442376 | tf_op jit(solution)/shard_map/ppermute | solution.py:1044
  141.8 6.8 %collective-permute-start.24 = (bf16[144,512]{1,0:T(8,128)(2,1)S(1)}, bf16[144,512]{1,0:T(8,128)(2,1)S(1)}, u32[]{:S(2)}, u32[]{:S(2)}) collective-permute-start(bf16[144,512]{1,0:T(8,128)(2,1)S(1)} %get-tuple-element.192.refs_0_), channel_id=1, source_target_pairs={{0,1},{1,0},{2,3},{3,2},{4,5},{5,4},{6,7},{7,6},{8,9},{9,8},{10,11... | collective-permute-start | bytes 442376 | tf_op jit(solution)/shard_map/ppermute | solution.py:1040
  149.2 10.4 %collective-permute-start.28 = (bf16[96,512]{1,0:T(8,128)(2,1)S(1)}, bf16[96,512]{1,0:T(8,128)(2,1)S(1)}, u32[]{:S(2)}, u32[]{:S(2)}) collective-permute-start(bf16[96,512]{1,0:T(8,128)(2,1)S(1)} %get-tuple-element.200), channel_id=1, source_target_pairs={{0,8},{2,10},{4,12},{6,14},{8,0},{10,2},{12,4},{14,6},{16,24},{18,... | collective-permute-start | bytes 294920 | tf_op jit(solution)/shard_map/ppermute | solution.py:1028
  151.3 8.8 %collective-permute-start.29 = (bf16[96,512]{1,0:T(8,128)(2,1)S(1)}, bf16[96,512]{1,0:T(8,128)(2,1)S(1)}, u32[]{:S(2)}, u32[]{:S(2)}) collective-permute-start(bf16[96,512]{1,0:T(8,128)(2,1)S(1)} %get-tuple-element.201), channel_id=1, source_target_pairs={{0,16},{2,18},{4,20},{6,22},{8,24},{10,26},{12,28},{14,30},{16,0},... | collective-permute-start | bytes 294920 | tf_op jit(solution)/shard_map/ppermute | solution.py:1028
  153.3 6.8 %collective-permute-start.30 = (bf16[96,512]{1,0:T(8,128)(2,1)S(1)}, bf16[96,512]{1,0:T(8,128)(2,1)S(1)}, u32[]{:S(2)}, u32[]{:S(2)}) collective-permute-start(bf16[96,512]{1,0:T(8,128)(2,1)S(1)} %get-tuple-element.202), channel_id=1, source_target_pairs={{0,24},{2,26},{4,28},{6,30},{8,16},{10,18},{12,20},{14,22},{16,8},... | collective-permute-start | bytes 294920 | tf_op jit(solution)/shard_map/ppermute | solution.py:1028
  153.7 13.6 %collective-permute-start.27 = (bf16[576,512]{1,0:T(8,128)(2,1)}, bf16[576,512]{1,0:T(8,128)(2,1)}, u32[]{:S(2)}, u32[]{:S(2)}) collective-permute-start(bf16[576,512]{1,0:T(8,128)(2,1)} %shard_map.346.refs_0_.refs_1_), channel_id=1, source_target_pairs={{0,4},{2,6},{4,0},{6,2},{8,12},{10,14},{12,8},{14,10},{16,20},{18,... | collective-permute-start | bytes 1769480 | tf_op jit(solution)/shard_map/ppermute | solution.py:1028
  160.7 6.8 %collective-permute-start.33 = (bf16[80,512]{1,0:T(8,128)(2,1)S(1)}, bf16[80,512]{1,0:T(8,128)(2,1)S(1)}, u32[]{:S(2)}, u32[]{:S(2)}) collective-permute-start(bf16[80,512]{1,0:T(8,128)(2,1)S(1)} %get-tuple-element.204.refs_2_), channel_id=1, source_target_pairs={{0,24},{2,26},{4,28},{6,30},{8,16},{10,18},{12,20},{14,22},{16,8},... | collective-permute-start | bytes 245768 | tf_op jit(solution)/shard_map/ppermute | solution.py:1028
  163.4 6.3 %collective-permute-start.32 = (bf16[80,512]{1,0:T(8,128)(2,1)S(1)}, bf16[80,512]{1,0:T(8,128)(2,1)S(1)}, u32[]{:S(2)}, u32[]{:S(2)}) collective-permute-start(bf16[80,512]{1,0:T(8,128)(2,1)S(1)} %get-tuple-element.204.refs_2_), channel_id=1, source_target_pairs={{0,16},{2,18},{4,20},{6,22},{8,24},{10,26},{12,28},{14,30},{16,0},... | collective-permute-start | bytes 245768 | tf_op jit(solution)/shard_map/ppermute | solution.py:1028
  163.8 5.9 %collective-permute-start.31 = (bf16[80,512]{1,0:T(8,128)(2,1)S(1)}, bf16[80,512]{1,0:T(8,128)(2,1)S(1)}, u32[]{:S(2)}, u32[]{:S(2)}) collective-permute-start(bf16[80,512]{1,0:T(8,128)(2,1)S(1)} %get-tuple-element.204.refs_2_), channel_id=1, source_target_pairs={{0,8},{2,10},{4,12},{6,14},{8,0},{10,2},{12,4},{14,6},{16,24},{18,... | collective-permute-start | bytes 245768 | tf_op jit(solution)/shard_map/ppermute | solution.py:1028
  165.1 11.2 %collective-permute-start.34 = (bf16[576,512]{1,0:T(8,128)(2,1)}, bf16[576,512]{1,0:T(8,128)(2,1)}, u32[]{:S(2)}, u32[]{:S(2)}) collective-permute-start(bf16[576,512]{1,0:T(8,128)(2,1)} %shard_map.346.refs_0_.refs_1_), channel_id=1, source_target_pairs={{0,2},{2,0},{4,6},{6,4},{8,10},{10,8},{12,14},{14,12},{16,18},{18,... | collective-permute-start | bytes 1769480 | tf_op jit(solution)/shard_map/ppermute | solution.py:1028
  167.3 9.0 %collective-permute-start.35 = (bf16[576,512]{1,0:T(8,128)(2,1)}, bf16[576,512]{1,0:T(8,128)(2,1)}, u32[]{:S(2)}, u32[]{:S(2)}) collective-permute-start(bf16[576,512]{1,0:T(8,128)(2,1)} %collective-permute-done.27.refs_0_.refs_2_), channel_id=1, source_target_pairs={{0,2},{2,0},{4,6},{6,4},{8,10},{10,8},{12,14},{14,12},{16,18},{18,... | collective-permute-start | bytes 1769480 | tf_op jit(solution)/shard_map/ppermute | solution.py:1028
  170.3 10.2 %collective-permute-start.36 = (bf16[336,512]{1,0:T(8,128)(2,1)S(1)}, bf16[336,512]{1,0:T(8,128)(2,1)S(1)}, u32[]{:S(2)}, u32[]{:S(2)}) collective-permute-start(bf16[336,512]{1,0:T(8,128)(2,1)S(1)} %shard_map.350.refs_1_.mine), channel_id=1, source_target_pairs={{0,4},{2,6},{4,0},{6,2},{8,12},{10,14},{12,8},{14,10},{16,20},{18,... | collective-permute-start | bytes 1032200 | tf_op jit(solution)/shard_map/ppermute | solution.py:1028
  172.1 9.5 %collective-permute-start.37 = (bf16[336,512]{1,0:T(8,128)(2,1)S(1)}, bf16[336,512]{1,0:T(8,128)(2,1)S(1)}, u32[]{:S(2)}, u32[]{:S(2)}) collective-permute-start(bf16[336,512]{1,0:T(8,128)(2,1)S(1)} %shard_map.350.refs_1_.mine), channel_id=1, source_target_pairs={{0,2},{2,0},{4,6},{6,4},{8,10},{10,8},{12,14},{14,12},{16,18},{18,... | collective-permute-start | bytes 1032200 | tf_op jit(solution)/shard_map/ppermute | solution.py:1028
  181.1 1.9 collective-permute-start.38
